TPU v7x, 32 devices: a whole 2x2x4 slice. The times are simulated.
32 devices in a mesh: grp: 2 (over x), row: 16 (over z, y, core).
Axes of the slice: x: 2, y: 2, z: 4, core: 2. Of those that a mesh axis runs over, the one named last changes fastest.
Arguments:
- alignment_features: bfloat16 [192, 512, 256], P(('grp', 'row')), parts along dimension 0, may hold values from -6 to 6
- pairwise_features: bfloat16 [32, 128, 128, 128], P(('grp', 'row')), parts along dimension 0, may hold values from -6 to 6
- standardize_scaling: float32 [256], replicated, may hold values from 0.1 to 1.9
- standardize_additive: float32 [256], replicated, may hold values from -3 to 3
- first_factor_matrix: bfloat16 [256, 32], replicated, may hold values from -0.375 to 0.375
- first_factor_intercept: float32 [32], replicated, may hold values from -3 to 3
- second_factor_matrix: bfloat16 [256, 32], replicated, may hold values from -0.375 to 0.375
- second_factor_intercept: float32 [32], replicated, may hold values from -3 to 3
- final_matrix: bfloat16 [1024, 128], replicated, may hold values from -1 to 1
- final_intercept: float32 [128], replicated, may hold values from -3 to 3
Outputs:
- new_pair: bfloat16 [32, 128, 128, 128], P(('grp', 'row')), parts along dimension 0
There are 2 independent parts, one for each index of `grp`. A program takes and returns all parts, laid end to end along the dimension named above; an argument that names none is the same for every part. Nothing has to cross between parts.
All inputs are finite; a program needn't handle non-finite values.
Results may differ from a plain program's by a relative error of at most 0.0053.
Values may be sent and summed in bfloat16 or wider, within the bound.
No kernel may reach another device: no remote copies, remote signals or barrier semaphores. Data moves between devices by JAX's collectives and lax.ppermute only.
A program may use at most 128 MiB of HBM per device.

v0:
```python
import math

import jax
import jax.numpy as jnp
from jax import lax
from jax.sharding import PartitionSpec as P


def standardize_rows(computed_entries, standardize_scaling, standardize_additive):
    wide = computed_entries.astype(jnp.float32)
    center = wide - jnp.mean(wide, axis=-1, keepdims=True)
    variance = jnp.mean(center * center, axis=-1, keepdims=True)
    return (
        center * lax.rsqrt(variance + 1e-05) * standardize_scaling + standardize_additive
    ).astype(jnp.bfloat16)


def project_left_right(
    computed_entries,
    standardize_scaling,
    standardize_additive,
    first_factor_matrix,
    first_factor_intercept,
    second_factor_matrix,
    second_factor_intercept,
):
    seq_count, res_count, chans = computed_entries.shape
    standardized_alignment = standardize_rows(
        computed_entries, standardize_scaling, standardize_additive
    ).reshape(seq_count * res_count, chans)
    first_factor_mapped = (
        jnp.dot(standardized_alignment, first_factor_matrix, preferred_element_type=jnp.float32)
        + first_factor_intercept
    ).astype(jnp.bfloat16)
    second_factor_mapped = (
        jnp.dot(standardized_alignment, second_factor_matrix, preferred_element_type=jnp.float32)
        + second_factor_intercept
    ).astype(jnp.bfloat16)
    width = first_factor_matrix.shape[1]
    return jnp.stack(
        [
            first_factor_mapped.reshape(seq_count, res_count, width),
            second_factor_mapped.reshape(seq_count, res_count, width),
        ]
    )


def rows_per_block(row_count, col_count):
    for candidate in range(1, row_count + 1):
        if row_count % candidate == 0 and candidate * col_count >= 2048:
            return candidate
    return row_count


def tile_update(left_tile, right_tile, final_matrix, final_intercept):
    seq_total = left_tile.shape[0]
    row_count = left_tile.shape[1]
    col_count = right_tile.shape[1]
    width = left_tile.shape[2]
    chans_out = final_matrix.shape[1]
    block_rows = rows_per_block(row_count, col_count)
    block_count = row_count // block_rows
    left_blocks = left_tile.reshape(seq_total, block_count, block_rows, width).transpose(1, 0, 2, 3)
    final_cube = final_matrix.reshape(width, width, chans_out)

    def one_block(left_block):
        outer_mean = (
            jnp.einsum("sic,sje->icje", left_block, right_tile, preferred_element_type=jnp.float32)
            / seq_total
        )
        outer_mean = outer_mean.astype(jnp.bfloat16)
        update = (
            jnp.einsum("icje,cez->ijz", outer_mean, final_cube, preferred_element_type=jnp.float32)
            + final_intercept
        )
        return update

    return lax.map(one_block, left_blocks).reshape(row_count, col_count, chans_out)


def local(
    alignment_features,
    pairwise_features,
    standardize_scaling,
    standardize_additive,
    first_factor_matrix,
    first_factor_intercept,
    second_factor_matrix,
    second_factor_intercept,
    final_matrix,
    final_intercept,
):
    devices_row = lax.axis_size("row")
    side_count = math.isqrt(devices_row)
    tile_len = pairwise_features.shape[1]
    stacked_tiles = project_left_right(
        alignment_features,
        standardize_scaling,
        standardize_additive,
        first_factor_matrix,
        first_factor_intercept,
        second_factor_matrix,
        second_factor_intercept,
    )
    seq_here = stacked_tiles.shape[1]
    width = stacked_tiles.shape[3]
    left_blocks = (
        stacked_tiles[0].reshape(seq_here, side_count, tile_len, width).transpose(1, 0, 2, 3)
    )
    right_blocks = (
        stacked_tiles[1].reshape(seq_here, side_count, tile_len, width).transpose(1, 0, 2, 3)
    )
    shape_out = (side_count, side_count, seq_here, tile_len, width)
    left_slots = jnp.broadcast_to(left_blocks[:, None], shape_out)
    right_slots = jnp.broadcast_to(right_blocks[None, :], shape_out)
    slots = jnp.stack([left_slots, right_slots], axis=2).reshape(
        devices_row, 2, seq_here, tile_len, width
    )
    received = lax.all_to_all(slots, "row", split_axis=0, concat_axis=0, tiled=True)
    chosen = received.transpose(1, 0, 2, 3, 4).reshape(2, devices_row * seq_here, tile_len, width)
    update = tile_update(chosen[0], chosen[1], final_matrix, final_intercept)
    return (pairwise_features.astype(jnp.float32) + update[None]).astype(jnp.bfloat16)


def solution(mesh):
    placed = (
        P(("grp", "row"), None, None),
        P(("grp", "row"), None, None, None),
        P(),
        P(),
        P(),
        P(),
        P(),
        P(),
        P(),
        P(),
    )
    return jax.shard_map(
        local,
        mesh=mesh,
        in_specs=placed,
        out_specs=P(("grp", "row"), None, None, None),
        check_vma=False,
    )
```

profile of v0, /device:TPU:13, one launch (start us, length us, event | category | flops | bytes accessed | tf_op | source)
XLA Modules:
  0.0 105.7 jit_solution(15416802264877524901)
XLA Ops:
  0.0 0.0 copy-start
  0.0 0.0 copy-start.1
  0.0 0.0 copy-start.3
  0.0 0.0 copy-start.4
  0.0 0.0 copy-start.5
  0.0 2.0 %convert_reduce_fusion = f32[6,512]{1,0:T(8,128)S(1)} fusion(bf16[6,512,256]{2,1,0:T(8,128)(2,1)} %param.12), kind=kLoop, calls=%fused_computation.17 | loop fusion | flops 1569792 | bytes 1585152 | tf_op jit(solution)/shard_map/reduce_sum | solution.py:11
  2.1 2.3 %fusion.23 = f32[6,512]{1,0:T(8,128)S(1)} fusion(bf16[6,512,256]{2,1,0:T(8,128)(2,1)} %param.12, f32[6,512]{1,0:T(8,128)S(1)} %broadcast_multiply_fusion), kind=kLoop, calls=%fused_computation.24 | loop fusion | flops 3142656 | bytes 1597440 | tf_op jit(solution)/shard_map/reduce_sum | solution.py:12
  4.4 0.0 copy-start.2
  4.4 0.0 copy-start.6
  4.4 0.0 copy-done.1
  4.4 0.0 copy-done.3
  4.4 0.0 copy-done.4
  4.4 1.0 fusion.26
  5.4 0.0 copy-done
  5.5 0.0 copy-done.5
  5.5 0.6 fusion.21
  6.0 0.1 reshape_squeeze_stack_reshape.6
  6.2 0.0 copy-done.2
  6.2 0.0 copy-done.6
  6.2 0.6 fusion.22
  6.8 0.1 reshape_squeeze_stack_reshape.7
  7.0 0.1 stack_broadcast_in_dim.5
  7.1 0.1 stack_broadcast_in_dim.4
  7.3 1.3 %pad_maximum_fusion = bf16[4,4,2,6,128,32]{4,5,3,2,1,0:T(8,128)(2,1)} fusion(bf16[4,4,1,6,128,32]{4,5,3,2,1,0:T(8,128)(2,1)S(1)} %stack_broadcast_in_dim.5, bf16[4,4,1,6,128,32]{4,5,3,2,1,0:T(8,128)(2,1)S(1)} %stack_broadcast_in_dim.4), kind=kLoop, calls=%fused_computation.28 | loop fusion | flops 786432 | bytes 3145728 | tf_op jit(solution)/shard_map/stack | solution.py:116
  8.6 6.6 %all-to-all-start = ((bf16[16,2,6,128,32]{3,4,2,1,0:T(8,128)(2,1)}), bf16[16,2,6,128,32]{3,4,2,1,0:T(8,128)(2,1)S(1)}, u32[]{:S(2)}, u32[]{:S(2)}) async-start(bf16[16,2,6,128,32]{3,4,2,1,0:T(8,128)(2,1)} %bitcast.11), calls=%async_computation | async-start | bytes 3145728 | tf_op jit(solution)/shard_map/all_to_all | solution.py:119
  15.1 36.2 %all-to-all-done = bf16[16,2,6,128,32]{3,4,2,1,0:T(8,128)(2,1)S(1)} async-done(((bf16[16,2,6,128,32]{3,4,2,1,0:T(8,128)(2,1)}), bf16[16,2,6,128,32]{3,4,2,1,0:T(8,128)(2,1)S(1)}, u32[]{:S(2)}, u32[]{:S(2)}) %all-to-all-start) | async-done | bytes 1572896 | tf_op jit(solution)/shard_map/all_to_all | solution.py:119
  51.3 1.2 %fusion.27 = (bf16[1,16,6,128,32]{3,4,2,0,1:T(8,128)(2,1)S(1)}, bf16[1,16,6,128,32]{3,4,2,0,1:T(8,128)(2,1)}) fusion(bf16[2,16,6,128,32]{3,4,2,0,1:T(8,128)(2,1)S(1)} %bitcast.62), kind=kLoop, calls=%fused_computation.31 | loop fusion | bytes 3145728 | tf_op jit(solution)/shard_map/slice | solution.py:121
  52.5 1.2 %copy.21 = bf16[96,128,32]{1,0,2:T(8,128)(2,1)} copy(bf16[96,128,32]{1,2,0:T(8,128)(2,1)S(1)} %bitcast.63) | data formatting | bytes 1572864 | tf_op jit(solution)/shard_map/while | solution.py:78
  53.7 0.0 copy-start.7
  53.7 0.0 copy-start.8
  53.7 2.9 %copy.19 = bf16[1,16,6,128,32]{4,3,2,1,0:T(8,128)(2,1)S(1)} copy(bf16[1,16,6,128,32]{3,4,2,0,1:T(8,128)(2,1)} %get-tuple-element.63) | data formatting | bytes 1572864 | tf_op jit(solution)/shard_map/slice | solution.py:121
  56.6 4.1 %copy.20 = bf16[8,96,16,32]{1,3,2,0:T(8,128)(2,1)} copy(bf16[8,96,16,32]{3,2,0,1:T(8,128)(2,1)S(1)} %bitcast.60) | data formatting | bytes 1572864 | tf_op jit(solution)/shard_map/while | solution.py:78
  60.7 0.0 copy-done.7
  60.7 0.0 copy-done.8
  60.7 36.4 %while.10 = (s32[]{:T(128)}, f32[8,16,128,128]{3,2,1,0:T(8,128)}, bf16[8,96,16,32]{1,3,2,0:T(8,128)(2,1)}, bf16[96,128,32]{1,0,2:T(8,128)(2,1)}, bf16[32,32,128]...) while((s32[]{:T(128)}, f32[8,16,128,128]{3,2,1,0:T(8,128)}, bf16[8,96,16,32]{1,3,2,0:T(8,128)(2,1)}, ...), condition=%wide.region_3.4_spmd, body=%wide.region_2.3_spmd.sunk | while | flops 943980544 | bytes 2229845 | solution.py:78
  60.7 4.5 %fusion.39 = f32[8,16,128,128]{3,2,1,0:T(8,128)} fusion(f32[8,16,128,128]{3,2,1,0:T(8,128)} %get-tuple-element.109, s32[]{:T(128)S(6)} %copy.33, bf16[96,128,32]{1,0,2:T(8,128)(2,1)} %get-tuple-element.118, f32[128]{0:T(128)S(1)} %get-tuple-element.120, bf16[32,32,128,1]{2,1,0,3:T(8,128)(2,1)S(1)} %bitcast.67, ...), kind=kOutput, calls=%fused_computation.7.clone.1 | convolution fusion | flops 943980544 | bytes 2229760 | tf_op jit(solution)/shard_map/while/body/eval_jaxpr/icje,cez->ijz/dot_general | solution.py:73
  65.3 4.6 %fusion.39 = f32[8,16,128,128]{3,2,1,0:T(8,128)} fusion(f32[8,16,128,128]{3,2,1,0:T(8,128)} %get-tuple-element.109, s32[]{:T(128)S(6)} %copy.33, bf16[96,128,32]{1,0,2:T(8,128)(2,1)} %get-tuple-element.118, f32[128]{0:T(128)S(1)} %get-tuple-element.120, bf16[32,32,128,1]{2,1,0,3:T(8,128)(2,1)S(1)} %bitcast.67, ...), kind=kOutput, calls=%fused_computation.7.clone.1 | convolution fusion | flops 943980544 | bytes 2229760 | tf_op jit(solution)/shard_map/while/body/eval_jaxpr/icje,cez->ijz/dot_general | solution.py:73
  69.8 4.5 %fusion.39 = f32[8,16,128,128]{3,2,1,0:T(8,128)} fusion(f32[8,16,128,128]{3,2,1,0:T(8,128)} %get-tuple-element.109, s32[]{:T(128)S(6)} %copy.33, bf16[96,128,32]{1,0,2:T(8,128)(2,1)} %get-tuple-element.118, f32[128]{0:T(128)S(1)} %get-tuple-element.120, bf16[32,32,128,1]{2,1,0,3:T(8,128)(2,1)S(1)} %bitcast.67, ...), kind=kOutput, calls=%fused_computation.7.clone.1 | convolution fusion | flops 943980544 | bytes 2229760 | tf_op jit(solution)/shard_map/while/body/eval_jaxpr/icje,cez->ijz/dot_general | solution.py:73
  74.4 4.5 %fusion.39 = f32[8,16,128,128]{3,2,1,0:T(8,128)} fusion(f32[8,16,128,128]{3,2,1,0:T(8,128)} %get-tuple-element.109, s32[]{:T(128)S(6)} %copy.33, bf16[96,128,32]{1,0,2:T(8,128)(2,1)} %get-tuple-element.118, f32[128]{0:T(128)S(1)} %get-tuple-element.120, bf16[32,32,128,1]{2,1,0,3:T(8,128)(2,1)S(1)} %bitcast.67, ...), kind=kOutput, calls=%fused_computation.7.clone.1 | convolution fusion | flops 943980544 | bytes 2229760 | tf_op jit(solution)/shard_map/while/body/eval_jaxpr/icje,cez->ijz/dot_general | solution.py:73
  78.9 4.5 %fusion.39 = f32[8,16,128,128]{3,2,1,0:T(8,128)} fusion(f32[8,16,128,128]{3,2,1,0:T(8,128)} %get-tuple-element.109, s32[]{:T(128)S(6)} %copy.33, bf16[96,128,32]{1,0,2:T(8,128)(2,1)} %get-tuple-element.118, f32[128]{0:T(128)S(1)} %get-tuple-element.120, bf16[32,32,128,1]{2,1,0,3:T(8,128)(2,1)S(1)} %bitcast.67, ...), kind=kOutput, calls=%fused_computation.7.clone.1 | convolution fusion | flops 943980544 | bytes 2229760 | tf_op jit(solution)/shard_map/while/body/eval_jaxpr/icje,cez->ijz/dot_general | solution.py:73
  83.4 4.6 %fusion.39 = f32[8,16,128,128]{3,2,1,0:T(8,128)} fusion(f32[8,16,128,128]{3,2,1,0:T(8,128)} %get-tuple-element.109, s32[]{:T(128)S(6)} %copy.33, bf16[96,128,32]{1,0,2:T(8,128)(2,1)} %get-tuple-element.118, f32[128]{0:T(128)S(1)} %get-tuple-element.120, bf16[32,32,128,1]{2,1,0,3:T(8,128)(2,1)S(1)} %bitcast.67, ...), kind=kOutput, calls=%fused_computation.7.clone.1 | convolution fusion | flops 943980544 | bytes 2229760 | tf_op jit(solution)/shard_map/while/body/eval_jaxpr/icje,cez->ijz/dot_general | solution.py:73
  88.0 4.5 %fusion.39 = f32[8,16,128,128]{3,2,1,0:T(8,128)} fusion(f32[8,16,128,128]{3,2,1,0:T(8,128)} %get-tuple-element.109, s32[]{:T(128)S(6)} %copy.33, bf16[96,128,32]{1,0,2:T(8,128)(2,1)} %get-tuple-element.118, f32[128]{0:T(128)S(1)} %get-tuple-element.120, bf16[32,32,128,1]{2,1,0,3:T(8,128)(2,1)S(1)} %bitcast.67, ...), kind=kOutput, calls=%fused_computation.7.clone.1 | convolution fusion | flops 943980544 | bytes 2229760 | tf_op jit(solution)/shard_map/while/body/eval_jaxpr/icje,cez->ijz/dot_general | solution.py:73
  92.6 4.6 %fusion.39 = f32[8,16,128,128]{3,2,1,0:T(8,128)} fusion(f32[8,16,128,128]{3,2,1,0:T(8,128)} %get-tuple-element.109, s32[]{:T(128)S(6)} %copy.33, bf16[96,128,32]{1,0,2:T(8,128)(2,1)} %get-tuple-element.118, f32[128]{0:T(128)S(1)} %get-tuple-element.120, bf16[32,32,128,1]{2,1,0,3:T(8,128)(2,1)S(1)} %bitcast.67, ...), kind=kOutput, calls=%fused_computation.7.clone.1 | convolution fusion | flops 943980544 | bytes 2229760 | tf_op jit(solution)/shard_map/while/body/eval_jaxpr/icje,cez->ijz/dot_general | solution.py:73
  97.1 8.6 %fusion.18 = bf16[1,128,128,128]{3,2,1,0:T(8,128)(2,1)} fusion(bf16[1,128,128,128]{3,2,1,0:T(8,128)(2,1)} %param.13, f32[1,128,128,128]{3,2,1,0:T(8,128)} %bitcast.61), kind=kLoop, calls=%fused_computation.15 | loop fusion | flops 6291456 | bytes 16777216 | tf_op jit(solution)/shard_map/convert_element_type | solution.py:122
  (5 shorter events, 0.1 us)
Async XLA Ops:
  0.0 5.5 %copy-start = (bf16[256,32]{0,1:T(8,128)(2,1)S(1)}, bf16[256,32]{0,1:T(8,128)(2,1)}, u32[]{:S(2)}) copy-start(bf16[256,32]{0,1:T(8,128)(2,1)} %param.16) | copy-start | bytes 49156
  0.0 4.4 %copy-start.1 = (bf16[6,512,256]{2,1,0:T(8,128)(2,1)S(1)}, bf16[6,512,256]{2,1,0:T(8,128)(2,1)}, u32[]{:S(2)}) copy-start(bf16[6,512,256]{2,1,0:T(8,128)(2,1)} %param.12) | copy-start | bytes 4718596
  0.0 4.4 %copy-start.3 = (f32[256]{0:T(256)S(1)}, f32[256]{0:T(256)}, u32[]{:S(2)}) copy-start(f32[256]{0:T(256)} %param.15) | copy-start | bytes 3076
  0.0 4.4 %copy-start.4 = (f32[256]{0:T(256)S(1)}, f32[256]{0:T(256)}, u32[]{:S(2)}) copy-start(f32[256]{0:T(256)} %param.14) | copy-start | bytes 3076
  0.0 5.4 %copy-start.5 = (f32[32]{0:T(128)S(1)}, f32[32]{0:T(128)}, u32[]{:S(2)}) copy-start(f32[32]{0:T(128)} %param.17) | copy-start | bytes 388
  4.4 1.8 %copy-start.2 = (bf16[256,32]{0,1:T(8,128)(2,1)S(1)}, bf16[256,32]{0,1:T(8,128)(2,1)}, u32[]{:S(2)}) copy-start(bf16[256,32]{0,1:T(8,128)(2,1)} %param.18) | copy-start | bytes 49156
  4.4 1.8 %copy-start.6 = (f32[32]{0:T(128)S(1)}, f32[32]{0:T(128)}, u32[]{:S(2)}) copy-start(f32[32]{0:T(128)} %param.19) | copy-start | bytes 388
  8.6 42.7 %all-to-all-start = ((bf16[16,2,6,128,32]{3,4,2,1,0:T(8,128)(2,1)}), bf16[16,2,6,128,32]{3,4,2,1,0:T(8,128)(2,1)S(1)}, u32[]{:S(2)}, u32[]{:S(2)}) async-start(bf16[16,2,6,128,32]{3,4,2,1,0:T(8,128)(2,1)} %bitcast.11), calls=%async_computation | async-start | bytes 3145728 | tf_op jit(solution)/shard_map/all_to_all | solution.py:119
  53.7 7.0 %copy-start.7 = (bf16[1024,128]{1,0:T(8,128)(2,1)S(1)}, bf16[1024,128]{1,0:T(8,128)(2,1)}, u32[]{:S(2)}) copy-start(bf16[1024,128]{1,0:T(8,128)(2,1)} %param.20) | copy-start | bytes 786436
  53.7 7.0 %copy-start.8 = (f32[128]{0:T(128)S(1)}, f32[128]{0:T(128)}, u32[]{:S(2)}) copy-start(f32[128]{0:T(128)} %param.21) | copy-start | bytes 1540
where the time goes:
time: 106 us
  matrix products  37.5 us (35%)
  waiting for transfers between devices  36.2 us (34%)
  other arithmetic  15.2 us (14%)
  local copies, waits for them, and re-layouts  10.1 us (10%)
  starting transfers between devices  6.56 us (6%)
    dot_general x8, matrix products, one_block(): jnp.einsum('icje,cez->ijz', outer_mean, final_cube, preferred_element_typ...  36.4 us
    all_to_all x1, waiting for transfers between devices, local(): lax.all_to_all(slots, 'row', split_axis=0, concat_axis=0, tiled=True)  36.2 us
    convert_element_type x1, other arithmetic, local(): (pairwise_features.astype(jnp.float32) + update[None]).astype(jnp.bfloat16)  8.59 us
    all_to_all x1, starting transfers between devices, local(): lax.all_to_all(slots, 'row', split_axis=0, concat_axis=0, tiled=True)  6.56 us
    while x2, local copies, waits for them, and re-layouts, tile_update(): lax.map(one_block, left_blocks).reshape(row_count, col_count, chans_out)  5.33 us
    slice x2, local copies, waits for them, and re-layouts, local(): update = tile_update(chosen[0], chosen[1], final_matrix, final_intercept)  4.08 us
    reduce_sum x1, other arithmetic, standardize_rows(): variance = jnp.mean(center * center, axis=-1, keepdims=True)  2.32 us
  transfers between devices with their start and end apart: 1, of which 1 were waited for; matrix products, arithmetic and copies ran while one was open for 0% of the time, Pallas kernels for 0%

commit v1 on v0

v1 whole, which is shorter than its diff:
```python
import functools
import math

import jax
import jax.numpy as jnp
from jax import lax
from jax.experimental import pallas as pl
from jax.experimental.pallas import tpu as pltpu
from jax.sharding import PartitionSpec as P

LANES = 128
VMEM_BYTES = 48 * 1024 * 1024


def project_kernel(side, place_ref, x_ref, gain_ref, offset_ref, wl_ref, bl_ref, wr_ref, br_ref, *rest):
    left_out, right_out, normed_ref = rest[:side], rest[side : 2 * side], rest[2 * side]
    width = wr_ref.shape[0]
    tile = x_ref.shape[1] // side
    pack = LANES // width
    rows = tile // pack
    x = x_ref[0].astype(jnp.float32)
    center = x - jnp.mean(x, axis=-1, keepdims=True)
    variance = jnp.mean(center * center, axis=-1, keepdims=True)
    normed_ref[...] = (
        center * lax.rsqrt(variance + 1e-05) * gain_ref[...] + offset_ref[...]
    ).astype(jnp.bfloat16)
    lane_group = lax.broadcasted_iota(jnp.int32, wl_ref.shape, 1) // width
    wl = wl_ref[...]
    left_parts = [jnp.where(lane_group == h, wl, jnp.zeros_like(wl)) for h in range(pack)]
    for d in range(side):
        a = lax.rem(place_ref[0] + d, side)
        block = normed_ref[pl.ds(pl.multiple_of(a * tile, tile), tile), :]
        total = bl_ref[...]
        for h in range(pack):
            total = total + jnp.dot(
                block[h * rows : (h + 1) * rows], left_parts[h], preferred_element_type=jnp.float32
            )
        left_out[d][0] = total.astype(jnp.bfloat16)
        b = lax.rem(place_ref[1] + d, side)
        block = normed_ref[pl.ds(pl.multiple_of(b * tile, tile), tile), :]
        right = lax.dot_general(
            wr_ref[...], block, (((1,), (1,)), ((), ())), preferred_element_type=jnp.float32
        )
        right_out[d][0] = (right + br_ref[...]).astype(jnp.bfloat16)


def project(side, place, x, gain, offset, wl, bl, wr, br):
    seqs, residues, chans = x.shape
    width = wl.shape[1]
    pack = LANES // width
    tile = residues // side
    rows = tile // pack
    whole = lambda *shape: pl.BlockSpec(shape, lambda s, place: (0,) * len(shape))
    out_spec = [pl.BlockSpec((1, rows, LANES), lambda s, place: (s, 0, 0))] * side
    out_spec += [pl.BlockSpec((1, width, tile), lambda s, place: (s, 0, 0))] * side
    out = pl.pallas_call(
        functools.partial(project_kernel, side),
        grid_spec=pltpu.PrefetchScalarGridSpec(
            num_scalar_prefetch=1,
            grid=(seqs,),
            in_specs=[
                pl.BlockSpec((1, residues, chans), lambda s, place: (s, 0, 0)),
                whole(1, chans),
                whole(1, chans),
                whole(chans, LANES),
                whole(1, LANES),
                whole(width, chans),
                whole(width, 1),
            ],
            out_specs=out_spec,
            scratch_shapes=[pltpu.VMEM((residues, chans), jnp.bfloat16)],
        ),
        out_shape=[jax.ShapeDtypeStruct((seqs, rows, LANES), jnp.bfloat16)] * side
        + [jax.ShapeDtypeStruct((seqs, width, tile), jnp.bfloat16)] * side,
        compiler_params=pltpu.CompilerParams(vmem_limit_bytes=VMEM_BYTES),
        name="project",
    )(
        place,
        x,
        gain[None],
        offset[None],
        jnp.tile(wl, (1, pack)),
        jnp.tile(bl, pack)[None],
        wr.T,
        br[:, None],
    )
    return out[:side], out[side:]


def update_kernel(side, seqs, seq_total, *refs):
    left_refs, right_refs = refs[:side], refs[side : 2 * side]
    wt_ref, bias_ref, pair_ref, out_ref, left_wide, right_wide, right_flat, outer = refs[2 * side :]
    _, rows, lanes = left_refs[0].shape
    _, width, tile = right_refs[0].shape
    depth = right_flat.shape[0]
    pack, group = pair_ref.shape[0], pair_ref.shape[1]
    step = pl.program_id(0)

    @pl.when(step == 0)
    def _():
        part = side * seqs
        for dy in range(side):
            left_wide[dy * part * rows : (dy + 1) * part * rows] = (
                left_refs[dy][...].astype(jnp.float32).reshape(part * rows, lanes)
            )
            for dz in range(side):
                at = (dy * side + dz) * seqs
                right_wide[at * width : (at + seqs) * width] = (
                    right_refs[dz][dy * seqs : (dy + 1) * seqs]
                    .astype(jnp.float32)
                    .reshape(seqs * width, tile)
                )
        if depth > seq_total:
            left_wide[seq_total * rows :] = jnp.zeros(
                ((depth - seq_total) * rows, lanes), jnp.float32
            )
            right_wide[seq_total * width :] = jnp.zeros(
                ((depth - seq_total) * width, tile), jnp.float32
            )
        for e in range(width):
            right_flat[:, e * tile : (e + 1) * tile] = right_wide[
                pl.ds(e, depth, stride=width), :
            ].astype(jnp.bfloat16)

    for q in range(group):
        x = left_wide[pl.ds(step * group + q, depth, stride=rows), :]
        left = x.T.astype(jnp.bfloat16)
        for n in range(width // 2):
            both = jnp.dot(
                left, right_flat[:, 2 * n * tile : (2 * n + 2) * tile], preferred_element_type=jnp.float32
            ).astype(jnp.bfloat16)
            for k in range(2):
                e = 2 * n + k
                for h in range(pack):
                    outer[
                        q * (pack // 2) + h // 2,
                        e * width : (e + 1) * width,
                        (h % 2) * tile : (h % 2 + 1) * tile,
                    ] = both[h * width : (h + 1) * width, k * tile : (k + 1) * tile]
    for q in range(group):
        for g in range(pack // 2):
            update = jnp.dot(
                wt_ref[...], outer[q * (pack // 2) + g], preferred_element_type=jnp.float32
            )
            for k in range(2):
                h = 2 * g + k
                part = update[:, k * tile : (k + 1) * tile].T * (1.0 / seq_total) + bias_ref[...]
                out_ref[h, q] = (pair_ref[h, q].astype(jnp.float32) + part).astype(jnp.bfloat16)


def tile_update(side, seqs, left, right, pair, wt, bias):
    part, rows, lanes = left[0].shape
    _, width, tile = right[0].shape
    seq_total = part * side
    depth = -(-seq_total // LANES) * LANES
    chans = wt.shape[0]
    pack = tile // rows
    group = 4
    whole = lambda shape: pl.BlockSpec(shape, lambda g: (0,) * len(shape))
    pair_spec = pl.BlockSpec((pack, group, tile, chans), lambda g: (0, g, 0, 0))
    out = pl.pallas_call(
        functools.partial(update_kernel, side, seqs, seq_total),
        grid=(rows // group,),
        in_specs=[whole(x.shape) for x in left + right] + [whole(wt.shape), whole((1, chans)), pair_spec],
        out_specs=pair_spec,
        out_shape=jax.ShapeDtypeStruct((pack, rows, tile, chans), jnp.bfloat16),
        scratch_shapes=[
            pltpu.VMEM((depth * rows, lanes), jnp.float32),
            pltpu.VMEM((depth * width, tile), jnp.float32),
            pltpu.VMEM((depth, width * tile), jnp.bfloat16),
            pltpu.VMEM((group * pack // 2, width * width, 2 * tile), jnp.bfloat16),
        ],
        compiler_params=pltpu.CompilerParams(vmem_limit_bytes=VMEM_BYTES),
        name="tile_update",
    )(*left, *right, wt, bias[None], pair.reshape(pack, rows, tile, chans))
    return out.reshape(1, tile, tile, chans)


def local(
    alignment_features,
    pairwise_features,
    standardize_scaling,
    standardize_additive,
    first_factor_matrix,
    first_factor_intercept,
    second_factor_matrix,
    second_factor_intercept,
    final_matrix,
    final_intercept,
):
    devices = lax.axis_size("row")
    side = math.isqrt(devices)
    me = lax.axis_index("row")
    place = jnp.stack([me // side, me % side]).astype(jnp.int32)
    seqs = alignment_features.shape[0]
    width = first_factor_matrix.shape[1]
    left, right = project(
        side,
        place,
        alignment_features,
        standardize_scaling,
        standardize_additive,
        first_factor_matrix,
        first_factor_intercept,
        second_factor_matrix,
        second_factor_intercept,
    )

    def along_a(x, d):
        perm = [(i, (i // side + d) % side * side + i % side) for i in range(devices)]
        return lax.ppermute(x, "row", perm)

    def along_b(x, d):
        perm = [(i, i // side * side + (i % side + d) % side) for i in range(devices)]
        return lax.ppermute(x, "row", perm)

    left = jnp.concatenate([left[0]] + [along_a(left[d], d) for d in range(1, side)])
    right = jnp.concatenate([right[0]] + [along_b(right[d], d) for d in range(1, side)])
    left = [left] + [along_b(left, d) for d in range(1, side)]
    right = [right] + [along_a(right, d) for d in range(1, side)]
    wt = final_matrix.reshape(width, width, -1).transpose(2, 1, 0).reshape(-1, width * width)
    return tile_update(side, seqs, left, right, pairwise_features, wt, final_intercept)


def solution(mesh):
    placed = (
        P(("grp", "row"), None, None),
        P(("grp", "row"), None, None, None),
        P(),
        P(),
        P(),
        P(),
        P(),
        P(),
        P(),
        P(),
    )
    return jax.shard_map(
        local,
        mesh=mesh,
        in_specs=placed,
        out_specs=P(("grp", "row"), None, None, None),
        check_vma=False,
    )
```

time: 106 us -> 64.8 us (0.61)
  the two profiles are of different devices: /device:TPU:13 before, /device:TPU:0 now
where the time goes in v1:
time: 64.8 us; the launch traced here: 64.4 us
  Pallas kernels  23.4 us (36%)
  waiting for transfers between devices  16.9 us (26%)
  starting transfers between devices  14 us (22%)
  local copies, waits for them, and re-layouts  9.9 us (15%)
    pallas_call x1, Pallas kernels, tile_update(): pl.pallas_call(functools.partial(update_kernel, side, seqs, seq_total), g...  19.4 us
    ppermute x6, waiting for transfers between devices, along_a(): return lax.ppermute(x, 'row', perm)  13.2 us
    ppermute x6, starting transfers between devices, along_a(): return lax.ppermute(x, 'row', perm)  9.29 us
    unnamed x18, local copies, waits for them, and re-layouts  6.37 us
    ppermute x6, starting transfers between devices, along_b(): return lax.ppermute(x, 'row', perm)  4.73 us
    pallas_call x1, Pallas kernels, project(): pl.pallas_call(functools.partial(project_kernel, side), grid_spec=pltpu.P...  4.01 us
    ppermute x6, waiting for transfers between devices, along_b(): return lax.ppermute(x, 'row', perm)  3.68 us
  transfers between devices with their start and end apart: 12, of which 5 were waited for; matrix products, arithmetic and copies ran while one was open for 2% of the time, Pallas kernels for 0%

profile of v1, /device:TPU:0, one launch (start us, length us, event | category | flops | bytes accessed | tf_op | source)
XLA Modules:
  0.0 64.4 jit_solution(18304004499858237330)
XLA Ops:
  0.0 0.7 %tile.8 = f32[4,32]{1,0:T(4,128)S(1)} broadcast(f32[32]{0:T(128)} %param.15), dimensions={1} | broadcast | bytes 640 | tf_op jit(solution)/shard_map/tile | solution.py:83
  0.7 0.1 broadcast_in_dim_tile.3.bl_ref
  0.7 0.7 %copy.18.br_ref = f32[32,1]{1,0:T(8,128)S(1)} copy(f32[32,1]{0,1:T(1,128)} %bitcast.22) | data formatting | bytes 256 | tf_op jit(solution)/shard_map/broadcast_in_dim | solution.py:85
  1.5 0.7 %tile.6 = bf16[256,4,32]{0,2,1:T(8,128)(2,1)S(1)} broadcast(bf16[256,32]{0,1:T(8,128)(2,1)} %param.14), dimensions={0,2} | broadcast | bytes 81920 | tf_op jit(solution)/shard_map/tile | solution.py:82
  2.2 0.1 copy.17.wl_ref
  2.3 0.1 pad_add_fusion.place_ref
  2.4 0.0 copy-start.1
  2.4 1.4 %copy-done.1 = bf16[6,512,256]{2,1,0:T(8,128)(2,1)S(1)} copy-done((bf16[6,512,256]{2,1,0:T(8,128)(2,1)S(1)}, bf16[6,512,256]{2,1,0:T(8,128)(2,1)}, u32[]{:S(2)}) %copy-start.1) | copy-done | bytes 1572888
  3.8 0.0 copy-start.2
  3.8 0.7 %copy-done.2 = bf16[256,32]{0,1:T(8,128)(2,1)S(1)} copy-done((bf16[256,32]{0,1:T(8,128)(2,1)S(1)}, bf16[256,32]{0,1:T(8,128)(2,1)}, u32[]{:S(2)}) %copy-start.2) | copy-done | bytes 16408
  4.5 0.0 copy-start.3
  4.5 0.7 %copy-done.3 = f32[256]{0:T(256)S(1)} copy-done((f32[256]{0:T(256)S(1)}, f32[256]{0:T(256)}, u32[]{:S(2)}) %copy-start.3) | copy-done | bytes 1048
  5.2 0.0 copy-start.4
  5.2 0.7 %copy-done.4 = f32[256]{0:T(256)S(1)} copy-done((f32[256]{0:T(256)S(1)}, f32[256]{0:T(256)}, u32[]{:S(2)}) %copy-start.4) | copy-done | bytes 1048
  5.9 4.0 %project.1 = (bf16[6,32,128]{2,1,0:T(8,128)(2,1)S(1)}, bf16[6,32,128]{2,1,0:T(8,128)(2,1)S(1)}, bf16[6,32,128]{2,1,0:T(8,128)(2,1)S(1)}, bf16[6,32,128]{2,1,0:T(...) custom-call(s32[2]{0:T(128)S(1)} %pad_add_fusion.place_ref, ...), custom_call_target="tpu_custom_call" | custom-call | tf_op jit(solution)/shard_map/project/pallas_call | solution.py:56
  9.9 3.1 %collective-permute-start = (bf16[6,32,128]{2,1,0:T(8,128)(2,1)S(1)}, bf16[6,32,128]{2,1,0:T(8,128)(2,1)S(1)}, u32[]{:S(2)}, u32[]{:S(2)}) collective-permute-start(bf16[6,32,128]{2,1,0:T(8,128)(2,1)S(1)} %get-tuple-element.14), channel_id=1, source_target_pairs={{0,4},{1,5},{2,6},{3,7},{4,8},{5,9},{6,10},{7,11},{8,12},{9,13},{1... | collective-permute-start | bytes 147464 | tf_op jit(solution)/shard_map/ppermute | solution.py:211
  13.0 2.6 %collective-permute-start.1 = (bf16[6,32,128]{2,1,0:T(8,128)(2,1)S(1)}, bf16[6,32,128]{2,1,0:T(8,128)(2,1)S(1)}, u32[]{:S(2)}, u32[]{:S(2)}) collective-permute-start(bf16[6,32,128]{2,1,0:T(8,128)(2,1)S(1)} %get-tuple-element.15), channel_id=1, source_target_pairs={{0,8},{1,9},{2,10},{3,11},{4,12},{5,13},{6,14},{7,15},{8,0},{9,1},... | collective-permute-start | bytes 147464 | tf_op jit(solution)/shard_map/ppermute | solution.py:211
  15.6 1.3 %collective-permute-start.2 = (bf16[6,32,128]{2,1,0:T(8,128)(2,1)S(1)}, bf16[6,32,128]{2,1,0:T(8,128)(2,1)S(1)}, u32[]{:S(2)}, u32[]{:S(2)}) collective-permute-start(bf16[6,32,128]{2,1,0:T(8,128)(2,1)S(1)} %get-tuple-element.16), channel_id=1, source_target_pairs={{0,12},{1,13},{2,14},{3,15},{4,0},{5,1},{6,2},{7,3},{8,4},{9,5},{1... | collective-permute-start | bytes 147464 | tf_op jit(solution)/shard_map/ppermute | solution.py:211
  16.9 0.0 collective-permute-start.6
  16.9 1.6 %collective-permute-start.7 = (bf16[6,32,128]{2,1,0:T(8,128)(2,1)S(1)}, bf16[6,32,128]{2,1,0:T(8,128)(2,1)S(1)}, u32[]{:S(2)}, u32[]{:S(2)}) collective-permute-start(bf16[6,32,128]{2,1,0:T(8,128)(2,1)S(1)} %get-tuple-element.19), channel_id=1, source_target_pairs={{0,2},{1,3},{2,0},{3,1},{4,6},{5,7},{6,4},{7,5},{8,10},{9,11},{10,... | collective-permute-start | bytes 147464 | tf_op jit(solution)/shard_map/ppermute | solution.py:215
  18.5 1.9 %collective-permute-done.6 = bf16[6,32,128]{2,1,0:T(8,128)(2,1)S(1)} collective-permute-done((bf16[6,32,128]{2,1,0:T(8,128)(2,1)S(1)}, bf16[6,32,128]{2,1,0:T(8,128)(2,1)S(1)}, u32[]{:S(2)}, u32[]{:S(2)}) %collective-permute-start.6) | collective-permute-done | bytes 49184 | tf_op jit(solution)/shard_map/ppermute | solution.py:215
  20.5 0.0 collective-permute-start.8
  20.5 0.6 collective-permute-done.7
  21.1 1.1 %collective-permute-done.8 = bf16[6,32,128]{2,1,0:T(8,128)(2,1)S(1)} collective-permute-done((bf16[6,32,128]{2,1,0:T(8,128)(2,1)S(1)}, bf16[6,32,128]{2,1,0:T(8,128)(2,1)S(1)}, u32[]{:S(2)}, u32[]{:S(2)}) %collective-permute-start.8) | collective-permute-done | bytes 49184 | tf_op jit(solution)/shard_map/ppermute | solution.py:215
  22.2 0.5 collective-permute-start.11
  22.7 1.7 %collective-permute-start.10 = (bf16[24,32,128]{2,1,0:T(8,128)(2,1)S(1)}, bf16[24,32,128]{2,1,0:T(8,128)(2,1)S(1)}, u32[]{:S(2)}, u32[]{:S(2)}) collective-permute-start(bf16[24,32,128]{2,1,0:T(8,128)(2,1)S(1)} %constant_dynamic-update-slice_fusion.4.refs_4_), channel_id=1, source_target_pairs={{0,8},{1,9},{2,10},{3,11},{4,12},{5,13},{6,14},{7,15},{8,0},{9,1},... | collective-permute-start | bytes 589832 | tf_op jit(solution)/shard_map/ppermute | solution.py:211
  24.4 0.0 collective-permute-done
  24.4 0.1 collective-permute-start.9
  24.5 0.0 collective-permute-done.1
  24.5 0.0 collective-permute-done.2
  24.6 1.2 %collective-permute-start.5 = (bf16[24,32,128]{2,1,0:T(8,128)(2,1)S(1)}, bf16[24,32,128]{2,1,0:T(8,128)(2,1)S(1)}, u32[]{:S(2)}, u32[]{:S(2)}) collective-permute-start(bf16[24,32,128]{2,1,0:T(8,128)(2,1)S(1)} %constant_dynamic-update-slice_fusion.refs_0_), channel_id=1, source_target_pairs={{0,3},{1,0},{2,1},{3,2},{4,7},{5,4},{6,5},{7,6},{8,11},{9,8},{10,9... | collective-permute-start | bytes 589832 | tf_op jit(solution)/shard_map/ppermute | solution.py:215
  25.8 1.5 %collective-permute-start.4 = (bf16[24,32,128]{2,1,0:T(8,128)(2,1)S(1)}, bf16[24,32,128]{2,1,0:T(8,128)(2,1)S(1)}, u32[]{:S(2)}, u32[]{:S(2)}) collective-permute-start(bf16[24,32,128]{2,1,0:T(8,128)(2,1)S(1)} %constant_dynamic-update-slice_fusion.refs_0_), channel_id=1, source_target_pairs={{0,2},{1,3},{2,0},{3,1},{4,6},{5,7},{6,4},{7,5},{8,10},{9,11},{10,... | collective-permute-start | bytes 589832 | tf_op jit(solution)/shard_map/ppermute | solution.py:215
  27.3 2.1 %collective-permute-done.11.refs_7_ = bf16[24,32,128]{2,1,0:T(8,128)(2,1)S(1)} collective-permute-done((bf16[24,32,128]{2,1,0:T(8,128)(2,1)S(1)}, bf16[24,32,128]{2,1,0:T(8,128)(2,1)S(1)}, u32[]{:S(2)}, u32[]{:S(2)}) %collective-permute-start.11) | collective-permute-done | bytes 196640 | tf_op jit(solution)/shard_map/ppermute | solution.py:211
  29.4 0.5 collective-permute-start.3
  29.9 1.1 %copy.19 = bf16[128,32,32]{0,2,1:T(8,128)(2,1)S(1)} copy(bf16[128,32,32]{0,1,2:T(8,128)(2,1)} %bitcast.21) | data formatting | bytes 524288 | tf_op jit(solution)/shard_map/transpose | solution.py:221
  30.9 0.1 copy.20.refs_8_
  31.1 11.1 %collective-permute-done.10.refs_6_ = bf16[24,32,128]{2,1,0:T(8,128)(2,1)S(1)} collective-permute-done((bf16[24,32,128]{2,1,0:T(8,128)(2,1)S(1)}, bf16[24,32,128]{2,1,0:T(8,128)(2,1)S(1)}, u32[]{:S(2)}, u32[]{:S(2)}) %collective-permute-start.10) | collective-permute-done | bytes 196640 | tf_op jit(solution)/shard_map/ppermute | solution.py:211
  42.2 0.0 collective-permute-done.9.refs_5_
  42.2 0.0 collective-permute-done.5.refs_3_
  42.2 0.0 collective-permute-done.4.refs_2_
  42.2 0.0 collective-permute-done.3.refs_1_
  42.2 0.0 copy-start
  42.2 2.2 %copy-done = bf16[1,128,128,128]{3,2,1,0:T(8,128)(2,1)S(1)} copy-done((bf16[1,128,128,128]{3,2,1,0:T(8,128)(2,1)S(1)}, bf16[1,128,128,128]{3,2,1,0:T(8,128)(2,1)}, u32[]{:S(2)}) %copy-start) | copy-done | bytes 4194328
  44.4 0.0 copy-start.5
  44.4 0.7 %copy-done.5 = f32[128]{0:T(128)S(1)} copy-done((f32[128]{0:T(128)S(1)}, f32[128]{0:T(128)}, u32[]{:S(2)}) %copy-start.5) | copy-done | bytes 536
  45.0 19.4 %tile_update.1 = bf16[4,32,128,128]{3,2,1,0:T(8,128)(2,1)} custom-call(bf16[24,32,128]{2,1,0:T(8,128)(2,1)S(1)} %constant_dynamic-update-slice_fusion.refs_0_, bf16[24,32,128]{2,1,0:T(8,128)(2,1)S(1)} %collective-permute-done.3.refs_1_, bf16[24,32,128]{2,1,0:T(8,128)(2,1)S(1)} %collective-permute-done.4.refs_2_, ...), custom_call_target="tpu_custom_call" | custom-call | tf_op jit(solution)/shard_map/tile_update/pallas_call | solution.py:161
  (8 shorter events, 0.1 us)
Async XLA Ops:
  2.4 1.4 %copy-start.1 = (bf16[6,512,256]{2,1,0:T(8,128)(2,1)S(1)}, bf16[6,512,256]{2,1,0:T(8,128)(2,1)}, u32[]{:S(2)}) copy-start(bf16[6,512,256]{2,1,0:T(8,128)(2,1)} %x_ref.1) | copy-start | bytes 4718596
  3.8 0.7 %copy-start.2 = (bf16[256,32]{0,1:T(8,128)(2,1)S(1)}, bf16[256,32]{0,1:T(8,128)(2,1)}, u32[]{:S(2)}) copy-start(bf16[256,32]{0,1:T(8,128)(2,1)} %param.16) | copy-start | bytes 49156
  4.5 0.7 %copy-start.3 = (f32[256]{0:T(256)S(1)}, f32[256]{0:T(256)}, u32[]{:S(2)}) copy-start(f32[256]{0:T(256)} %param.12) | copy-start | bytes 3076
  5.2 0.7 %copy-start.4 = (f32[256]{0:T(256)S(1)}, f32[256]{0:T(256)}, u32[]{:S(2)}) copy-start(f32[256]{0:T(256)} %param.13) | copy-start | bytes 3076
  9.9 14.5 %collective-permute-start = (bf16[6,32,128]{2,1,0:T(8,128)(2,1)S(1)}, bf16[6,32,128]{2,1,0:T(8,128)(2,1)S(1)}, u32[]{:S(2)}, u32[]{:S(2)}) collective-permute-start(bf16[6,32,128]{2,1,0:T(8,128)(2,1)S(1)} %get-tuple-element.14), channel_id=1, source_target_pairs={{0,4},{1,5},{2,6},{3,7},{4,8},{5,9},{6,10},{7,11},{8,12},{9,13},{1... | collective-permute-start | bytes 147464 | tf_op jit(solution)/shard_map/ppermute | solution.py:211
  13.0 11.5 %collective-permute-start.1 = (bf16[6,32,128]{2,1,0:T(8,128)(2,1)S(1)}, bf16[6,32,128]{2,1,0:T(8,128)(2,1)S(1)}, u32[]{:S(2)}, u32[]{:S(2)}) collective-permute-start(bf16[6,32,128]{2,1,0:T(8,128)(2,1)S(1)} %get-tuple-element.15), channel_id=1, source_target_pairs={{0,8},{1,9},{2,10},{3,11},{4,12},{5,13},{6,14},{7,15},{8,0},{9,1},... | collective-permute-start | bytes 147464 | tf_op jit(solution)/shard_map/ppermute | solution.py:211
  15.6 8.9 %collective-permute-start.2 = (bf16[6,32,128]{2,1,0:T(8,128)(2,1)S(1)}, bf16[6,32,128]{2,1,0:T(8,128)(2,1)S(1)}, u32[]{:S(2)}, u32[]{:S(2)}) collective-permute-start(bf16[6,32,128]{2,1,0:T(8,128)(2,1)S(1)} %get-tuple-element.16), channel_id=1, source_target_pairs={{0,12},{1,13},{2,14},{3,15},{4,0},{5,1},{6,2},{7,3},{8,4},{9,5},{1... | collective-permute-start | bytes 147464 | tf_op jit(solution)/shard_map/ppermute | solution.py:211
  16.9 3.5 %collective-permute-start.6 = (bf16[6,32,128]{2,1,0:T(8,128)(2,1)S(1)}, bf16[6,32,128]{2,1,0:T(8,128)(2,1)S(1)}, u32[]{:S(2)}, u32[]{:S(2)}) collective-permute-start(bf16[6,32,128]{2,1,0:T(8,128)(2,1)S(1)} %get-tuple-element.18), channel_id=1, source_target_pairs={{0,1},{1,2},{2,3},{3,0},{4,5},{5,6},{6,7},{7,4},{8,9},{9,10},{10,1... | collective-permute-start | bytes 147464 | tf_op jit(solution)/shard_map/ppermute | solution.py:215
  16.9 4.1 %collective-permute-start.7 = (bf16[6,32,128]{2,1,0:T(8,128)(2,1)S(1)}, bf16[6,32,128]{2,1,0:T(8,128)(2,1)S(1)}, u32[]{:S(2)}, u32[]{:S(2)}) collective-permute-start(bf16[6,32,128]{2,1,0:T(8,128)(2,1)S(1)} %get-tuple-element.19), channel_id=1, source_target_pairs={{0,2},{1,3},{2,0},{3,1},{4,6},{5,7},{6,4},{7,5},{8,10},{9,11},{10,... | collective-permute-start | bytes 147464 | tf_op jit(solution)/shard_map/ppermute | solution.py:215
  20.5 1.8 %collective-permute-start.8 = (bf16[6,32,128]{2,1,0:T(8,128)(2,1)S(1)}, bf16[6,32,128]{2,1,0:T(8,128)(2,1)S(1)}, u32[]{:S(2)}, u32[]{:S(2)}) collective-permute-start(bf16[6,32,128]{2,1,0:T(8,128)(2,1)S(1)} %get-tuple-element.20), channel_id=1, source_target_pairs={{0,3},{1,0},{2,1},{3,2},{4,7},{5,4},{6,5},{7,6},{8,11},{9,8},{10,9... | collective-permute-start | bytes 147464 | tf_op jit(solution)/shard_map/ppermute | solution.py:215
  22.2 7.2 %collective-permute-start.11 = (bf16[24,32,128]{2,1,0:T(8,128)(2,1)S(1)}, bf16[24,32,128]{2,1,0:T(8,128)(2,1)S(1)}, u32[]{:S(2)}, u32[]{:S(2)}) collective-permute-start(bf16[24,32,128]{2,1,0:T(8,128)(2,1)S(1)} %constant_dynamic-update-slice_fusion.4.refs_4_), channel_id=1, source_target_pairs={{0,12},{1,13},{2,14},{3,15},{4,0},{5,1},{6,2},{7,3},{8,4},{9,5},{1... | collective-permute-start | bytes 589832 | tf_op jit(solution)/shard_map/ppermute | solution.py:211
  22.7 19.4 %collective-permute-start.10 = (bf16[24,32,128]{2,1,0:T(8,128)(2,1)S(1)}, bf16[24,32,128]{2,1,0:T(8,128)(2,1)S(1)}, u32[]{:S(2)}, u32[]{:S(2)}) collective-permute-start(bf16[24,32,128]{2,1,0:T(8,128)(2,1)S(1)} %constant_dynamic-update-slice_fusion.4.refs_4_), channel_id=1, source_target_pairs={{0,8},{1,9},{2,10},{3,11},{4,12},{5,13},{6,14},{7,15},{8,0},{9,1},... | collective-permute-start | bytes 589832 | tf_op jit(solution)/shard_map/ppermute | solution.py:211
  24.4 17.7 %collective-permute-start.9 = (bf16[24,32,128]{2,1,0:T(8,128)(2,1)S(1)}, bf16[24,32,128]{2,1,0:T(8,128)(2,1)S(1)}, u32[]{:S(2)}, u32[]{:S(2)}) collective-permute-start(bf16[24,32,128]{2,1,0:T(8,128)(2,1)S(1)} %constant_dynamic-update-slice_fusion.4.refs_4_), channel_id=1, source_target_pairs={{0,4},{1,5},{2,6},{3,7},{4,8},{5,9},{6,10},{7,11},{8,12},{9,13},{1... | collective-permute-start | bytes 589832 | tf_op jit(solution)/shard_map/ppermute | solution.py:211
  24.6 17.6 %collective-permute-start.5 = (bf16[24,32,128]{2,1,0:T(8,128)(2,1)S(1)}, bf16[24,32,128]{2,1,0:T(8,128)(2,1)S(1)}, u32[]{:S(2)}, u32[]{:S(2)}) collective-permute-start(bf16[24,32,128]{2,1,0:T(8,128)(2,1)S(1)} %constant_dynamic-update-slice_fusion.refs_0_), channel_id=1, source_target_pairs={{0,3},{1,0},{2,1},{3,2},{4,7},{5,4},{6,5},{7,6},{8,11},{9,8},{10,9... | collective-permute-start | bytes 589832 | tf_op jit(solution)/shard_map/ppermute | solution.py:215
  25.8 16.4 %collective-permute-start.4 = (bf16[24,32,128]{2,1,0:T(8,128)(2,1)S(1)}, bf16[24,32,128]{2,1,0:T(8,128)(2,1)S(1)}, u32[]{:S(2)}, u32[]{:S(2)}) collective-permute-start(bf16[24,32,128]{2,1,0:T(8,128)(2,1)S(1)} %constant_dynamic-update-slice_fusion.refs_0_), channel_id=1, source_target_pairs={{0,2},{1,3},{2,0},{3,1},{4,6},{5,7},{6,4},{7,5},{8,10},{9,11},{10,... | collective-permute-start | bytes 589832 | tf_op jit(solution)/shard_map/ppermute | solution.py:215
  29.4 12.8 %collective-permute-start.3 = (bf16[24,32,128]{2,1,0:T(8,128)(2,1)S(1)}, bf16[24,32,128]{2,1,0:T(8,128)(2,1)S(1)}, u32[]{:S(2)}, u32[]{:S(2)}) collective-permute-start(bf16[24,32,128]{2,1,0:T(8,128)(2,1)S(1)} %constant_dynamic-update-slice_fusion.refs_0_), channel_id=1, source_target_pairs={{0,1},{1,2},{2,3},{3,0},{4,5},{5,6},{6,7},{7,4},{8,9},{9,10},{10,1... | collective-permute-start | bytes 589832 | tf_op jit(solution)/shard_map/ppermute | solution.py:215
  42.2 2.2 %copy-start = (bf16[1,128,128,128]{3,2,1,0:T(8,128)(2,1)S(1)}, bf16[1,128,128,128]{3,2,1,0:T(8,128)(2,1)}, u32[]{:S(2)}) copy-start(bf16[1,128,128,128]{3,2,1,0:T(8,128)(2,1)} %param.11) | copy-start | bytes 12582916
  44.4 0.7 %copy-start.5 = (f32[128]{0:T(128)S(1)}, f32[128]{0:T(128)}, u32[]{:S(2)}) copy-start(f32[128]{0:T(128)} %param.19) | copy-start | bytes 1540

commit v2 on v1

v2 whole, which is shorter than its diff:
```python
import functools
import math

import jax
import jax.numpy as jnp
from jax import lax
from jax.experimental import pallas as pl
from jax.experimental.pallas import tpu as pltpu
from jax.sharding import PartitionSpec as P

LANES = 128
VMEM_BYTES = 60 * 1024 * 1024


def project_kernel(side, x_ref, gain_ref, offset_ref, wl_ref, bl_ref, wr_ref, br_ref, left_ref, right_ref):
    width, chans = wl_ref.shape
    residues = x_ref.shape[1]
    tile = residues // side
    pack = LANES // width
    rows = tile // pack
    x = x_ref[0].astype(jnp.float32)
    center = x - jnp.mean(x, axis=-1, keepdims=True)
    variance = jnp.mean(center * center, axis=-1, keepdims=True)
    normed = (center * lax.rsqrt(variance + 1e-05) * gain_ref[...] + offset_ref[...]).astype(
        jnp.bfloat16
    )
    nt = (((1,), (1,)), ((), ()))
    wl = wl_ref[...]
    total = jnp.concatenate([bl_ref[...]] * pack, axis=1)
    for h in range(pack):
        placed = jnp.concatenate(
            [wl if k == h else jnp.zeros_like(wl) for k in range(pack)], axis=0
        )
        picked = jnp.concatenate(
            [normed[a * tile + h * rows : a * tile + (h + 1) * rows] for a in range(side)], axis=0
        )
        total = total + lax.dot_general(picked, placed, nt, preferred_element_type=jnp.float32)
    left = total.astype(jnp.bfloat16)
    bias = jnp.broadcast_to(br_ref[...], (tile, width)).T
    right = lax.dot_general(wr_ref[...], normed, nt, preferred_element_type=jnp.float32)
    for a in range(side):
        left_ref[a, 0] = left[a * rows : (a + 1) * rows]
        right_ref[a, 0] = (right[:, a * tile : (a + 1) * tile] + bias).astype(jnp.bfloat16)


def project(side, x, gain, offset, wl, bl, wr, br):
    seqs, residues, chans = x.shape
    width = wl.shape[1]
    tile = residues // side
    rows = tile * width // LANES
    whole = lambda *shape: pl.BlockSpec(shape, lambda s: (0,) * len(shape))
    return pl.pallas_call(
        functools.partial(project_kernel, side),
        grid=(seqs,),
        in_specs=[
            pl.BlockSpec((1, residues, chans), lambda s: (s, 0, 0)),
            whole(1, chans),
            whole(1, chans),
            whole(width, chans),
            whole(1, width),
            whole(width, chans),
            whole(1, width),
        ],
        out_specs=[
            pl.BlockSpec((side, 1, rows, LANES), lambda s: (0, s, 0, 0)),
            pl.BlockSpec((side, 1, width, tile), lambda s: (0, s, 0, 0)),
        ],
        out_shape=[
            jax.ShapeDtypeStruct((side, seqs, rows, LANES), jnp.bfloat16),
            jax.ShapeDtypeStruct((side, seqs, width, tile), jnp.bfloat16),
        ],
        compiler_params=pltpu.CompilerParams(vmem_limit_bytes=VMEM_BYTES),
        name="project",
    )(x, gain[None], offset[None], wl.T, bl[None], wr.T, br[None])


def update_kernel(side, seqs, seq_total, *refs):
    left_ref, right_ref, wt_ref, bias_ref, pair_ref = refs[:5]
    out_ref, left_wide, right_wide, right_flat, outer = refs[5:]
    _, rows, lanes = left_ref.shape
    _, width, tile = right_ref.shape
    depth = right_flat.shape[0]
    pack, group = pair_ref.shape[0], pair_ref.shape[1]
    step = pl.program_id(0)

    @pl.when(step == 0)
    def _():
        left_wide[: seq_total * rows] = (
            left_ref[...].astype(jnp.float32).reshape(seq_total * rows, lanes)
        )
        for a in range(side):
            for b in range(side):
                at, to = (a * side + b) * seqs, (b * side + a) * seqs
                right_wide[to * width : (to + seqs) * width] = (
                    right_ref[at : at + seqs].astype(jnp.float32).reshape(seqs * width, tile)
                )
        if depth > seq_total:
            left_wide[seq_total * rows :] = jnp.zeros(
                ((depth - seq_total) * rows, lanes), jnp.float32
            )
            right_wide[seq_total * width :] = jnp.zeros(
                ((depth - seq_total) * width, tile), jnp.float32
            )
        for e in range(width):
            right_flat[:, e * tile : (e + 1) * tile] = right_wide[
                pl.ds(e, depth, stride=width), :
            ].astype(jnp.bfloat16)

    for q in range(group):
        x = left_wide[pl.ds(step * group + q, depth, stride=rows), :]
        left = x.T.astype(jnp.bfloat16)
        for n in range(width // 2):
            both = jnp.dot(
                left, right_flat[:, 2 * n * tile : (2 * n + 2) * tile], preferred_element_type=jnp.float32
            ).astype(jnp.bfloat16)
            for k in range(2):
                e = 2 * n + k
                for h in range(pack):
                    outer[
                        q * (pack // 2) + h // 2,
                        e * width : (e + 1) * width,
                        (h % 2) * tile : (h % 2 + 1) * tile,
                    ] = both[h * width : (h + 1) * width, k * tile : (k + 1) * tile]
    for q in range(group):
        for g in range(pack // 2):
            update = jnp.dot(
                wt_ref[...], outer[q * (pack // 2) + g], preferred_element_type=jnp.float32
            )
            for k in range(2):
                h = 2 * g + k
                part = update[:, k * tile : (k + 1) * tile].T * (1.0 / seq_total) + bias_ref[...]
                out_ref[h, q] = (pair_ref[h, q].astype(jnp.float32) + part).astype(jnp.bfloat16)


def tile_update(side, seqs, left, right, pair, wt, bias):
    seq_total, rows, lanes = left.shape
    _, width, tile = right.shape
    depth = -(-seq_total // LANES) * LANES
    chans = wt.shape[0]
    pack = tile // rows
    group = 4
    whole = lambda shape: pl.BlockSpec(shape, lambda g: (0,) * len(shape))
    pair_spec = pl.BlockSpec((pack, group, tile, chans), lambda g: (0, g, 0, 0))
    out = pl.pallas_call(
        functools.partial(update_kernel, side, seqs, seq_total),
        grid=(rows // group,),
        in_specs=[whole(left.shape), whole(right.shape), whole(wt.shape), whole((1, chans)), pair_spec],
        out_specs=pair_spec,
        out_shape=jax.ShapeDtypeStruct((pack, rows, tile, chans), jnp.bfloat16),
        scratch_shapes=[
            pltpu.VMEM((depth * rows, lanes), jnp.float32),
            pltpu.VMEM((depth * width, tile), jnp.float32),
            pltpu.VMEM((depth, width * tile), jnp.bfloat16),
            pltpu.VMEM((group * pack // 2, width * width, 2 * tile), jnp.bfloat16),
        ],
        compiler_params=pltpu.CompilerParams(vmem_limit_bytes=VMEM_BYTES),
        name="tile_update",
    )(left, right, wt, bias[None], pair.reshape(pack, rows, tile, chans))
    return out.reshape(1, tile, tile, chans)


def local(
    alignment_features,
    pairwise_features,
    standardize_scaling,
    standardize_additive,
    first_factor_matrix,
    first_factor_intercept,
    second_factor_matrix,
    second_factor_intercept,
    final_matrix,
    final_intercept,
):
    devices = lax.axis_size("row")
    side = math.isqrt(devices)
    seqs = alignment_features.shape[0]
    width = first_factor_matrix.shape[1]
    left, right = project(
        side,
        alignment_features,
        standardize_scaling,
        standardize_additive,
        first_factor_matrix,
        first_factor_intercept,
        second_factor_matrix,
        second_factor_intercept,
    )
    same_a = [[a * side + b for b in range(side)] for a in range(side)]
    same_b = [[a * side + b for a in range(side)] for b in range(side)]

    def spread(x, groups):
        x = lax.all_to_all(x, "row", 0, 0, axis_index_groups=groups, tiled=True)
        return x.reshape((side * seqs,) + x.shape[2:])

    def collect(x, groups):
        return lax.all_gather(x, "row", axis_index_groups=groups, tiled=True)

    right = collect(spread(right, same_a), same_b)
    left = collect(spread(left, same_b), same_a)
    wt = final_matrix.reshape(width, width, -1).transpose(2, 1, 0).reshape(-1, width * width)
    return tile_update(side, seqs, left, right, pairwise_features, wt, final_intercept)


def solution(mesh):
    placed = (
        P(("grp", "row"), None, None),
        P(("grp", "row"), None, None, None),
        P(),
        P(),
        P(),
        P(),
        P(),
        P(),
        P(),
        P(),
    )
    return jax.shard_map(
        local,
        mesh=mesh,
        in_specs=placed,
        out_specs=P(("grp", "row"), None, None, None),
        check_vma=False,
    )
```

time: 64.8 us -> 71.2 us (1.099)
  blocking collectives: 0 us -> 29.2 us
  waiting for transfers between devices: 16.9 us -> 3.43 us
  local copies, waits for them, and re-layouts: 9.9 us -> 1.9 us
  starting transfers between devices: 14 us -> 9.67 us
  Pallas kernels: 23.4 us -> 26.5 us
    all_gather x0 -> x2, blocking collectives: none -> 29.2 us  [collect(): return lax.all_gather(x, 'row', axis_index_groups=groups, tiled=True)]
    ppermute x12 -> x0, waiting for transfers between devices: 16.9 us -> none  [the longest x6 13.2 us: along_a(): return lax.ppermute(x, 'row', perm)]
    ppermute x12 -> x0, starting transfers between devices: 14 us -> none  [the longest x6 9.29 us: along_a(): return lax.ppermute(x, 'row', perm)]
    all_to_all x0 -> x2, starting transfers between devices: none -> 9.67 us  [spread(): x = lax.all_to_all(x, 'row', 0, 0, axis_index_groups=groups, tiled=True)]
    unnamed x18 -> x0, local copies, waits for them, and re-layouts: 6.37 us -> none
    all_to_all x0 -> x2, waiting for transfers between devices: none -> 3.43 us  [spread(): x = lax.all_to_all(x, 'row', 0, 0, axis_index_groups=groups, tiled=True)]
    pallas_call x1, Pallas kernels: 4.01 us -> 5.67 us  [project(): pl.pallas_call(functools.partial(project_kernel, side), grid=(seqs,), in_...]
    another operation x4 -> x0, local copies, waits for them, and re-layouts: 1.57 us -> none  [the longest x2 0.83 us: project(): jnp.tile(wl, (1, pack))]
  transfers between devices with their start and end apart: 12 -> 2, of which waited for: 5 -> 1; matrix products, arithmetic and copies ran while one was open for 2% -> 3% of each run, Pallas kernels for 0% -> 0%
where the time goes in v2:
time: 71.2 us; the launch traced here: 70.7 us
  blocking collectives  29.2 us (41%)
  Pallas kernels  26.5 us (37%)
  starting transfers between devices  9.67 us (14%)
  waiting for transfers between devices  3.43 us (5%)
  local copies, waits for them, and re-layouts  1.9 us (3%)
    all_gather x2, blocking collectives, collect(): return lax.all_gather(x, 'row', axis_index_groups=groups, tiled=True)  29.2 us
    pallas_call x1, Pallas kernels, tile_update(): pl.pallas_call(functools.partial(update_kernel, side, seqs, seq_total), g...  20.8 us
    all_to_all x2, starting transfers between devices, spread(): x = lax.all_to_all(x, 'row', 0, 0, axis_index_groups=groups, tiled=True)  9.67 us
    pallas_call x1, Pallas kernels, project(): pl.pallas_call(functools.partial(project_kernel, side), grid=(seqs,), in_...  5.67 us
    all_to_all x2, waiting for transfers between devices, spread(): x = lax.all_to_all(x, 'row', 0, 0, axis_index_groups=groups, tiled=True)  3.43 us
  transfers between devices with their start and end apart: 2, of which 1 were waited for; matrix products, arithmetic and copies ran while one was open for 3% of the time, Pallas kernels for 0%

profile of v2, /device:TPU:0, one launch (start us, length us, event | category | flops | bytes accessed | tf_op | source)
XLA Modules:
  0.0 70.7 jit_solution(7876703314677022587)
XLA Ops:
  0.0 5.7 %project.1 = (bf16[4,6,32,128]{3,2,1,0:T(8,128)(2,1)}, bf16[4,6,32,128]{3,2,1,0:T(8,128)(2,1)}) custom-call(bf16[6,512,256]{2,1,0:T(8,128)(2,1)} %x_ref.1, f32[1,256]{1,0:T(1,128)} %bitcast.22, f32[1,256]{1,0:T(1,128)} %bitcast.23, bf16[32,256]{1,0:T(8,128)(2,1)} %bitcast.20, f32[1,32]{1,0:T(1,128)} %bitcast.24, bf16[32,256]{1,0:T(8,128)(2,1)} %bitcast.21, ...), custom_call_target="tpu_custom_call" | custom-call | tf_op jit(solution)/shard_map/project/pallas_call | solution.py:52
  5.7 4.2 %all-to-all-start.1 = ((bf16[4,6,32,128]{3,2,1,0:T(8,128)(2,1)}), bf16[4,6,32,128]{3,2,1,0:T(8,128)(2,1)S(1)}, u32[]{:S(2)}, u32[]{:S(2)}) async-start(bf16[4,6,32,128]{3,2,1,0:T(8,128)(2,1)} %get-tuple-element.8), calls=%async_computation.1 | async-start | bytes 393216 | tf_op jit(solution)/shard_map/all_to_all | solution.py:192
  9.9 1.1 %copy.15 = bf16[128,32,32]{0,2,1:T(8,128)(2,1)S(1)} copy(bf16[128,32,32]{0,1,2:T(8,128)(2,1)} %bitcast.19) | data formatting | bytes 524288 | tf_op jit(solution)/shard_map/transpose | solution.py:200
  11.0 0.8 %copy.16.refs_2_ = bf16[128,1024]{1,0:T(8,128)(2,1)} copy(bf16[128,1024]{0,1:T(8,128)(2,1)S(1)} %bitcast.16) | data formatting | bytes 524288 | tf_op jit(solution)/shard_map/reshape | solution.py:200
  11.8 3.4 %all-to-all-done.1 = bf16[4,6,32,128]{3,2,1,0:T(8,128)(2,1)S(1)} async-done(((bf16[4,6,32,128]{3,2,1,0:T(8,128)(2,1)}), bf16[4,6,32,128]{3,2,1,0:T(8,128)(2,1)S(1)}, u32[]{:S(2)}, u32[]{:S(2)}) %all-to-all-start.1) | async-done | bytes 196640 | tf_op jit(solution)/shard_map/all_to_all | solution.py:192
  15.3 5.4 %all-to-all-start = ((bf16[4,6,32,128]{3,2,1,0:T(8,128)(2,1)}), bf16[4,6,32,128]{3,2,1,0:T(8,128)(2,1)S(1)}, u32[]{:S(2)}, u32[]{:S(2)}) async-start(bf16[4,6,32,128]{3,2,1,0:T(8,128)(2,1)} %get-tuple-element.7), calls=%async_computation | async-start | bytes 393216 | tf_op jit(solution)/shard_map/all_to_all | solution.py:192
  20.7 21.2 %all_gather.7.refs_1_ = bf16[96,32,128]{2,1,0:T(8,128)(2,1)} all-gather(bf16[24,32,128]{2,1,0:T(8,128)(2,1)S(1)} %bitcast.17), channel_id=1, replica_groups={{0,4,8,12},{1,5,9,13},{2,6,10,14},{3,7,11,15},{16,20,24,28},{17,21,25,2..., dimensions={0}, use_global_device_ids=true | all-gather | bytes 983040 | tf_op jit(solution)/shard_map/all_gather | solution.py:196
  41.8 0.0 all-to-all-done
  41.8 8.1 %all_gather.6.refs_0_ = bf16[96,32,128]{2,1,0:T(8,128)(2,1)} all-gather(bf16[24,32,128]{2,1,0:T(8,128)(2,1)S(1)} %bitcast.18), channel_id=1, replica_groups={{0,1,2,3},{4,5,6,7},{8,9,10,11},{12,13,14,15},{16,17,18,19},{20,21,22,2..., dimensions={0}, use_global_device_ids=true | all-gather | bytes 983040 | tf_op jit(solution)/shard_map/all_gather | solution.py:196
  49.9 20.8 %tile_update.1 = bf16[4,32,128,128]{3,2,1,0:T(8,128)(2,1)} custom-call(bf16[96,32,128]{2,1,0:T(8,128)(2,1)} %all_gather.6.refs_0_, bf16[96,32,128]{2,1,0:T(8,128)(2,1)} %all_gather.7.refs_1_, bf16[128,1024]{1,0:T(8,128)(2,1)} %copy.16.refs_2_, f32[1,128]{1,0:T(1,128)} %bitcast.26, bf16[4,32,128,128]{3,2,1,0:T(8,128)(2,1)} %bitcast.15), custom_call_target="tpu_custom_call" | custom-call | tf_op jit(solution)/shard_map/tile_update/pallas_call | solution.py:144
Async XLA Ops:
  5.7 9.6 %all-to-all-start.1 = ((bf16[4,6,32,128]{3,2,1,0:T(8,128)(2,1)}), bf16[4,6,32,128]{3,2,1,0:T(8,128)(2,1)S(1)}, u32[]{:S(2)}, u32[]{:S(2)}) async-start(bf16[4,6,32,128]{3,2,1,0:T(8,128)(2,1)} %get-tuple-element.8), calls=%async_computation.1 | async-start | bytes 393216 | tf_op jit(solution)/shard_map/all_to_all | solution.py:192
  15.3 26.6 %all-to-all-start = ((bf16[4,6,32,128]{3,2,1,0:T(8,128)(2,1)}), bf16[4,6,32,128]{3,2,1,0:T(8,128)(2,1)S(1)}, u32[]{:S(2)}, u32[]{:S(2)}) async-start(bf16[4,6,32,128]{3,2,1,0:T(8,128)(2,1)} %get-tuple-element.7), calls=%async_computation | async-start | bytes 393216 | tf_op jit(solution)/shard_map/all_to_all | solution.py:192

commit v3 on v2

--- a/solution.py
+++ b/solution.py
@@ -75,24 +75,29 @@
 
 
 def update_kernel(side, seqs, seq_total, *refs):
-    left_ref, right_ref, wt_ref, bias_ref, pair_ref = refs[:5]
-    out_ref, left_wide, right_wide, right_flat, outer = refs[5:]
-    _, rows, lanes = left_ref.shape
-    _, width, tile = right_ref.shape
+    place_ref, left_refs = refs[0], refs[1 : 1 + side]
+    right_ref, wt_ref, bias_ref, pair_ref, out_ref = refs[1 + side : 6 + side]
+    left_wide, right_wide, right_flat, left_rows, outer = refs[6 + side :]
+    _, rows, lanes = left_refs[0].shape
+    _, _, width, tile = right_ref.shape
     depth = right_flat.shape[0]
     pack, group = pair_ref.shape[0], pair_ref.shape[1]
     step = pl.program_id(0)
 
     @pl.when(step == 0)
     def _():
-        left_wide[: seq_total * rows] = (
-            left_ref[...].astype(jnp.float32).reshape(seq_total * rows, lanes)
-        )
-        for a in range(side):
-            for b in range(side):
-                at, to = (a * side + b) * seqs, (b * side + a) * seqs
+        part = side * seqs
+        for d in range(side):
+            left_wide[d * part * rows : (d + 1) * part * rows] = (
+                left_refs[d][...].astype(jnp.float32).reshape(part * rows, lanes)
+            )
+            b = lax.rem(place_ref[0] + side - d, side)
+            for a in range(side):
+                to = (d * side + a) * seqs
                 right_wide[to * width : (to + seqs) * width] = (
-                    right_ref[at : at + seqs].astype(jnp.float32).reshape(seqs * width, tile)
+                    right_ref[0, pl.ds((a * side + b) * seqs, seqs)]
+                    .astype(jnp.float32)
+                    .reshape(seqs * width, tile)
                 )
         if depth > seq_total:
             left_wide[seq_total * rows :] = jnp.zeros(
@@ -108,19 +113,19 @@
 
     for q in range(group):
         x = left_wide[pl.ds(step * group + q, depth, stride=rows), :]
-        left = x.T.astype(jnp.bfloat16)
-        for n in range(width // 2):
-            both = jnp.dot(
-                left, right_flat[:, 2 * n * tile : (2 * n + 2) * tile], preferred_element_type=jnp.float32
-            ).astype(jnp.bfloat16)
-            for k in range(2):
-                e = 2 * n + k
-                for h in range(pack):
-                    outer[
-                        q * (pack // 2) + h // 2,
-                        e * width : (e + 1) * width,
-                        (h % 2) * tile : (h % 2 + 1) * tile,
-                    ] = both[h * width : (h + 1) * width, k * tile : (k + 1) * tile]
+        left_rows[q * lanes : (q + 1) * lanes] = x.T.astype(jnp.bfloat16)
+    for n in range(width // 2):
+        both = jnp.dot(
+            left_rows[...],
+            right_flat[:, 2 * n * tile : (2 * n + 2) * tile],
+            preferred_element_type=jnp.float32,
+        ).astype(jnp.bfloat16)
+        for k in range(2):
+            e = 2 * n + k
+            for h in range(group * pack):
+                outer[
+                    h // 2, e * width : (e + 1) * width, (h % 2) * tile : (h % 2 + 1) * tile
+                ] = both[h * width : (h + 1) * width, k * tile : (k + 1) * tile]
     for q in range(group):
         for g in range(pack // 2):
             update = jnp.dot(
@@ -132,30 +137,40 @@
                 out_ref[h, q] = (pair_ref[h, q].astype(jnp.float32) + part).astype(jnp.bfloat16)
 
 
-def tile_update(side, seqs, left, right, pair, wt, bias):
-    seq_total, rows, lanes = left.shape
-    _, width, tile = right.shape
+def tile_update(side, seqs, place, left, right, pair, wt, bias):
+    part, rows, lanes = left[0].shape
+    _, seq_total, width, tile = right.shape
     depth = -(-seq_total // LANES) * LANES
     chans = wt.shape[0]
     pack = tile // rows
     group = 4
-    whole = lambda shape: pl.BlockSpec(shape, lambda g: (0,) * len(shape))
-    pair_spec = pl.BlockSpec((pack, group, tile, chans), lambda g: (0, g, 0, 0))
+    whole = lambda shape: pl.BlockSpec(shape, lambda g, place: (0,) * len(shape))
+    pair_spec = pl.BlockSpec((pack, group, tile, chans), lambda g, place: (0, g, 0, 0))
     out = pl.pallas_call(
         functools.partial(update_kernel, side, seqs, seq_total),
-        grid=(rows // group,),
-        in_specs=[whole(left.shape), whole(right.shape), whole(wt.shape), whole((1, chans)), pair_spec],
-        out_specs=pair_spec,
+        grid_spec=pltpu.PrefetchScalarGridSpec(
+            num_scalar_prefetch=1,
+            grid=(rows // group,),
+            in_specs=[whole(x.shape) for x in left]
+            + [
+                pl.BlockSpec((1, seq_total, width, tile), lambda g, place: (place[0], 0, 0, 0)),
+                whole(wt.shape),
+                whole((1, chans)),
+                pair_spec,
+            ],
+            out_specs=pair_spec,
+            scratch_shapes=[
+                pltpu.VMEM((depth * rows, lanes), jnp.float32),
+                pltpu.VMEM((depth * width, tile), jnp.float32),
+                pltpu.VMEM((depth, width * tile), jnp.bfloat16),
+                pltpu.VMEM((group * lanes, depth), jnp.bfloat16),
+                pltpu.VMEM((group * pack // 2, width * width, 2 * tile), jnp.bfloat16),
+            ],
+        ),
         out_shape=jax.ShapeDtypeStruct((pack, rows, tile, chans), jnp.bfloat16),
-        scratch_shapes=[
-            pltpu.VMEM((depth * rows, lanes), jnp.float32),
-            pltpu.VMEM((depth * width, tile), jnp.float32),
-            pltpu.VMEM((depth, width * tile), jnp.bfloat16),
-            pltpu.VMEM((group * pack // 2, width * width, 2 * tile), jnp.bfloat16),
-        ],
         compiler_params=pltpu.CompilerParams(vmem_limit_bytes=VMEM_BYTES),
         name="tile_update",
-    )(left, right, wt, bias[None], pair.reshape(pack, rows, tile, chans))
+    )(place, *left, right, wt, bias[None], pair.reshape(pack, rows, tile, chans))
     return out.reshape(1, tile, tile, chans)
 
 
@@ -185,20 +200,23 @@
         second_factor_matrix,
         second_factor_intercept,
     )
-    same_a = [[a * side + b for b in range(side)] for a in range(side)]
     same_b = [[a * side + b for a in range(side)] for b in range(side)]
 
     def spread(x, groups):
         x = lax.all_to_all(x, "row", 0, 0, axis_index_groups=groups, tiled=True)
         return x.reshape((side * seqs,) + x.shape[2:])
 
-    def collect(x, groups):
-        return lax.all_gather(x, "row", axis_index_groups=groups, tiled=True)
-
-    right = collect(spread(right, same_a), same_b)
-    left = collect(spread(left, same_b), same_a)
+    right = lax.all_gather(right, "row", axis=1, tiled=True)
+    left = spread(left, same_b)
+    pieces = [left] + [
+        lax.ppermute(
+            left, "row", [(i, i // side * side + (i % side + d) % side) for i in range(devices)]
+        )
+        for d in range(1, side)
+    ]
+    place = (lax.axis_index("row") % side).reshape(1).astype(jnp.int32)
     wt = final_matrix.reshape(width, width, -1).transpose(2, 1, 0).reshape(-1, width * width)
-    return tile_update(side, seqs, left, right, pairwise_features, wt, final_intercept)
+    return tile_update(side, seqs, place, pieces, right, pairwise_features, wt, final_intercept)
 
 
 def solution(mesh):

time: 71.2 us -> 89.8 us (1.26)
  waiting for transfers between devices: 3.43 us -> 31.1 us
  blocking collectives: 29.2 us -> 13.9 us
  between operations: 0.01 us -> 13.4 us
  starting transfers between devices: 9.67 us -> 1.75 us
  Pallas kernels: 26.5 us -> 27.4 us
    all_gather x2 -> x0, blocking collectives: 29.2 us -> none  [collect(): return lax.all_gather(x, 'row', axis_index_groups=groups, tiled=True)]
    all_gather x0 -> x1, waiting for transfers between devices: none -> 23.2 us  [local(): right = lax.all_gather(right, 'row', axis=1, tiled=True)]
    all_to_all x0 -> x1, blocking collectives: none -> 13.9 us  [spread(): x = lax.all_to_all(x, 'row', 0, 0, axis_index_groups=groups, tiled=True)]
    all_to_all x2 -> x0, starting transfers between devices: 9.67 us -> none  [spread(): x = lax.all_to_all(x, 'row', 0, 0, axis_index_groups=groups, tiled=True)]
    ppermute x0 -> x3, waiting for transfers between devices: none -> 7.82 us  [local(): lax.ppermute(left, 'row', [(i, i // side * side + (i % side + d) % side)...]
    all_to_all x2 -> x0, waiting for transfers between devices: 3.43 us -> none  [spread(): x = lax.all_to_all(x, 'row', 0, 0, axis_index_groups=groups, tiled=True)]
    ppermute x0 -> x3, starting transfers between devices: none -> 1.75 us  [local(): lax.ppermute(left, 'row', [(i, i // side * side + (i % side + d) % side)...]
    pallas_call x1, Pallas kernels: 20.8 us -> 21.7 us  [tile_update(): pl.pallas_call(functools.partial(update_kernel, side, seqs, seq_total), g...]
  transfers between devices with their start and end apart: 2 -> 4, of which waited for: 1 -> 3; matrix products, arithmetic and copies ran while one was open for 3% -> 2% of each run, Pallas kernels for 0% -> 0%
where the time goes in v3:
time: 89.8 us; the launch traced here: 89.5 us
  waiting for transfers between devices  31.1 us (35%)
  Pallas kernels  27.4 us (31%)
  blocking collectives  13.9 us (15%)
  between operations  13.4 us (15%)
  local copies, waits for them, and re-layouts  1.92 us (2%)
  starting transfers between devices  1.75 us (2%)
    all_gather x1, waiting for transfers between devices, local(): right = lax.all_gather(right, 'row', axis=1, tiled=True)  23.2 us
    pallas_call x1, Pallas kernels, tile_update(): pl.pallas_call(functools.partial(update_kernel, side, seqs, seq_total), g...  21.7 us
    all_to_all x1, blocking collectives, spread(): x = lax.all_to_all(x, 'row', 0, 0, axis_index_groups=groups, tiled=True)  13.9 us
    ppermute x3, waiting for transfers between devices, local(): lax.ppermute(left, 'row', [(i, i // side * side + (i % side + d) % side)...  7.82 us
    pallas_call x1, Pallas kernels, project(): pl.pallas_call(functools.partial(project_kernel, side), grid=(seqs,), in_...  5.69 us
  transfers between devices with their start and end apart: 4, of which 3 were waited for; matrix products, arithmetic and copies ran while one was open for 2% of the time, Pallas kernels for 0%

profile of v3, /device:TPU:0, one launch (start us, length us, event | category | flops | bytes accessed | tf_op | source)
XLA Modules:
  0.0 89.5 jit_solution(10357326417287792827)
XLA Ops:
  6.5 0.0 all-gather.2.cloned.1.call-start
  6.5 5.7 %project.1 = (bf16[4,6,32,128]{3,2,1,0:T(8,128)(2,1)}, bf16[4,6,32,128]{3,2,1,0:T(8,128)(2,1)}) custom-call(bf16[6,512,256]{2,1,0:T(8,128)(2,1)} %x_ref.1, f32[1,256]{1,0:T(1,128)} %bitcast.24, f32[1,256]{1,0:T(1,128)} %bitcast.25, bf16[32,256]{1,0:T(8,128)(2,1)} %bitcast.22, f32[1,32]{1,0:T(1,128)} %bitcast.26, bf16[32,256]{1,0:T(8,128)(2,1)} %bitcast.23, ...), custom_call_target="tpu_custom_call" | custom-call | tf_op jit(solution)/shard_map/project/pallas_call | solution.py:52
  12.2 0.0 all-gather.2.cloned.1.call-update
  12.3 13.9 %all_to_all.5 = bf16[4,6,32,128]{3,2,1,0:T(8,128)(2,1)S(1)} all-to-all(bf16[4,6,32,128]{3,2,1,0:T(8,128)(2,1)} %get-tuple-element.7), channel_id=1, replica_groups={{0,4,8,12},{1,5,9,13},{2,6,10,14},{3,7,11,15},{16,20,24,28},{17,21,25,2..., dimensions={0} | all-to-all | bytes 393216 | tf_op jit(solution)/shard_map/all_to_all | solution.py:206
  26.2 0.0 copy-start
  26.2 0.0 collective-permute-start.2
  26.2 1.5 %collective-permute-start.1 = (bf16[24,32,128]{2,1,0:T(8,128)(2,1)S(1)}, bf16[24,32,128]{2,1,0:T(8,128)(2,1)S(1)}, u32[]{:S(2)}, u32[]{:S(2)}) collective-permute-start(bf16[24,32,128]{2,1,0:T(8,128)(2,1)S(1)} %bitcast.18), channel_id=1, source_target_pairs={{0,2},{1,3},{2,0},{3,1},{4,6},{5,7},{6,4},{7,5},{8,10},{9,11},{10,... | collective-permute-start | bytes 589832 | tf_op jit(solution)/shard_map/ppermute | solution.py:212
  27.7 0.2 collective-permute-start
  27.9 1.1 %copy.13 = bf16[128,32,32]{0,2,1:T(8,128)(2,1)S(1)} copy(bf16[128,32,32]{0,1,2:T(8,128)(2,1)} %bitcast.21) | data formatting | bytes 524288 | tf_op jit(solution)/shard_map/transpose | solution.py:218
  29.0 0.8 copy.14.refs_6_
  29.8 0.6 collective-permute-done.2.refs_4_
  30.4 0.0 copy-start.1
  30.4 7.2 %collective-permute-done.1.refs_3_ = bf16[24,32,128]{2,1,0:T(8,128)(2,1)S(1)} collective-permute-done((bf16[24,32,128]{2,1,0:T(8,128)(2,1)S(1)}, bf16[24,32,128]{2,1,0:T(8,128)(2,1)S(1)}, u32[]{:S(2)}, u32[]{:S(2)}) %collective-permute-start.1) | collective-permute-done | bytes 196640 | tf_op jit(solution)/shard_map/ppermute | solution.py:212
  37.6 0.0 copy-start.2
  37.6 0.0 collective-permute-done.refs_2_
  37.7 0.0 copy-start.3
  37.7 23.2 %all-gather.2.cloned.1.call-done.refs_5_ = bf16[4,96,32,128]{3,2,1,0:T(8,128)(2,1)} async-done(((bf16[4,6,32,128]{3,2,1,0:T(8,128)(2,1)}), bf16[4,96,32,128]{3,2,1,0:T(8,128)(2,1)}) %all-gather.2.cloned.1.call-update) | async-done | bytes 3145744 | tf_op jit(solution)/shard_map/all_gather | solution.py:209
  60.9 0.0 copy-done
  60.9 0.0 copy-done.1
  60.9 0.0 copy-done.2
  60.9 0.0 copy-done.3
  60.9 21.7 %tile_update.1 = bf16[4,32,128,128]{3,2,1,0:T(8,128)(2,1)} custom-call(s32[1]{0:T(128)} %bitcast.refs_0_, bf16[24,32,128]{2,1,0:T(8,128)(2,1)} %bitcast.20, bf16[24,32,128]{2,1,0:T(8,128)(2,1)} %copy-done.3, bf16[24,32,128]{2,1,0:T(8,128)(2,1)} %copy-done.2, bf16[24,32,128]{2,1,0:T(8,128)(2,1)} %copy-done.1, ...), custom_call_target="tpu_custom_call" | custom-call | tf_op jit(solution)/shard_map/tile_update/pallas_call | solution.py:149
Async XLA Ops:
  6.5 54.3 %all-gather.2.cloned.1.call-start = ((), (), s32[]{:S(2)}) async-start(), calls=%async_computation.1 | async-start | bytes 3342336 | tf_op jit(solution)/shard_map/all_gather | solution.py:209
  26.2 34.7 %copy-start = (bf16[4,6,32,128]{3,2,1,0:T(8,128)(2,1)}, bf16[4,6,32,128]{3,2,1,0:T(8,128)(2,1)S(1)}, u32[]{:S(2)}) copy-start(bf16[4,6,32,128]{3,2,1,0:T(8,128)(2,1)S(1)} %all_to_all.5) | copy-start | bytes 589828
  26.2 4.2 %collective-permute-start.2 = (bf16[24,32,128]{2,1,0:T(8,128)(2,1)S(1)}, bf16[24,32,128]{2,1,0:T(8,128)(2,1)S(1)}, u32[]{:S(2)}, u32[]{:S(2)}) collective-permute-start(bf16[24,32,128]{2,1,0:T(8,128)(2,1)S(1)} %bitcast.17), channel_id=1, source_target_pairs={{0,3},{1,0},{2,1},{3,2},{4,7},{5,4},{6,5},{7,6},{8,11},{9,8},{10,9... | collective-permute-start | bytes 589832 | tf_op jit(solution)/shard_map/ppermute | solution.py:212
  26.2 11.4 %collective-permute-start.1 = (bf16[24,32,128]{2,1,0:T(8,128)(2,1)S(1)}, bf16[24,32,128]{2,1,0:T(8,128)(2,1)S(1)}, u32[]{:S(2)}, u32[]{:S(2)}) collective-permute-start(bf16[24,32,128]{2,1,0:T(8,128)(2,1)S(1)} %bitcast.18), channel_id=1, source_target_pairs={{0,2},{1,3},{2,0},{3,1},{4,6},{5,7},{6,4},{7,5},{8,10},{9,11},{10,... | collective-permute-start | bytes 589832 | tf_op jit(solution)/shard_map/ppermute | solution.py:212
  27.7 10.0 %collective-permute-start = (bf16[24,32,128]{2,1,0:T(8,128)(2,1)S(1)}, bf16[24,32,128]{2,1,0:T(8,128)(2,1)S(1)}, u32[]{:S(2)}, u32[]{:S(2)}) collective-permute-start(bf16[24,32,128]{2,1,0:T(8,128)(2,1)S(1)} %bitcast.19), channel_id=1, source_target_pairs={{0,1},{1,2},{2,3},{3,0},{4,5},{5,6},{6,7},{7,4},{8,9},{9,10},{10,1... | collective-permute-start | bytes 589832 | tf_op jit(solution)/shard_map/ppermute | solution.py:212
  30.4 30.5 %copy-start.1 = (bf16[24,32,128]{2,1,0:T(8,128)(2,1)}, bf16[24,32,128]{2,1,0:T(8,128)(2,1)S(1)}, u32[]{:S(2)}) copy-start(bf16[24,32,128]{2,1,0:T(8,128)(2,1)S(1)} %collective-permute-done.2.refs_4_) | copy-start | bytes 589828
  37.6 23.3 %copy-start.2 = (bf16[24,32,128]{2,1,0:T(8,128)(2,1)}, bf16[24,32,128]{2,1,0:T(8,128)(2,1)S(1)}, u32[]{:S(2)}) copy-start(bf16[24,32,128]{2,1,0:T(8,128)(2,1)S(1)} %collective-permute-done.1.refs_3_) | copy-start | bytes 589828
  37.7 23.2 %copy-start.3 = (bf16[24,32,128]{2,1,0:T(8,128)(2,1)}, bf16[24,32,128]{2,1,0:T(8,128)(2,1)S(1)}, u32[]{:S(2)}) copy-start(bf16[24,32,128]{2,1,0:T(8,128)(2,1)S(1)} %collective-permute-done.refs_2_) | copy-start | bytes 589828
Sparse Core Ops, SparseCore 0:
  12.4 48.4 all-gather.1

commit v4 on v1

v4 whole, which is shorter than its diff:
```python
import functools
import math

import jax
import jax.numpy as jnp
from jax import lax
from jax.experimental import pallas as pl
from jax.experimental.pallas import tpu as pltpu
from jax.sharding import PartitionSpec as P

LANES = 128
PARTS = 2
MIB = 1024 * 1024


def project_kernel(side, place_ref, x_ref, gain_ref, offset_ref, wl_ref, bl_ref, wr_ref, br_ref, *rest):
    left_out, right_out, normed_ref = rest[:side], rest[side : 2 * side], rest[2 * side]
    width, chans = wl_ref.shape
    tile = x_ref.shape[1] // side
    pack = LANES // width
    rows = tile // pack
    x = x_ref[0].astype(jnp.float32)
    center = x - jnp.mean(x, axis=-1, keepdims=True)
    variance = jnp.mean(center * center, axis=-1, keepdims=True)
    normed_ref[...] = (
        center * lax.rsqrt(variance + 1e-05) * gain_ref[...] + offset_ref[...]
    ).astype(jnp.bfloat16)
    nt = (((1,), (1,)), ((), ()))
    blocks = []
    for d in range(side):
        a = place_ref[0] ^ d
        blocks.append(normed_ref[pl.ds(pl.multiple_of(a * tile, tile), tile), :])
    wl = wl_ref[...]
    total = jnp.concatenate([bl_ref[...]] * pack, axis=1)
    for h in range(pack):
        placed = jnp.concatenate(
            [wl if k == h else jnp.zeros_like(wl) for k in range(pack)], axis=0
        )
        picked = jnp.concatenate([block[h * rows : (h + 1) * rows] for block in blocks], axis=0)
        total = total + lax.dot_general(picked, placed, nt, preferred_element_type=jnp.float32)
    left = total.astype(jnp.bfloat16)
    bias = jnp.broadcast_to(br_ref[...], (tile, width)).T
    for d in range(side):
        left_out[d][0] = left[d * rows : (d + 1) * rows]
        b = place_ref[1] ^ d
        block = normed_ref[pl.ds(pl.multiple_of(b * tile, tile), tile), :]
        right = lax.dot_general(wr_ref[...], block, nt, preferred_element_type=jnp.float32) + bias
        right_out[d][:, 0] = right.astype(jnp.bfloat16).reshape(PARTS, width // PARTS, tile)


def project(side, place, x, gain, offset, wl, bl, wr, br):
    seqs, residues, chans = x.shape
    width = wl.shape[1]
    tile = residues // side
    rows = tile * width // LANES
    some = width // PARTS
    whole = lambda *shape: pl.BlockSpec(shape, lambda s, place: (0,) * len(shape))
    out = pl.pallas_call(
        functools.partial(project_kernel, side),
        grid_spec=pltpu.PrefetchScalarGridSpec(
            num_scalar_prefetch=1,
            grid=(seqs,),
            in_specs=[
                pl.BlockSpec((1, residues, chans), lambda s, place: (s, 0, 0)),
                whole(1, chans),
                whole(1, chans),
                whole(width, chans),
                whole(1, width),
                whole(width, chans),
                whole(1, width),
            ],
            out_specs=[pl.BlockSpec((1, rows, LANES), lambda s, place: (s, 0, 0))] * side
            + [pl.BlockSpec((PARTS, 1, some, tile), lambda s, place: (0, s, 0, 0))] * side,
            scratch_shapes=[pltpu.VMEM((residues, chans), jnp.bfloat16)],
        ),
        out_shape=[jax.ShapeDtypeStruct((seqs, rows, LANES), jnp.bfloat16)] * side
        + [jax.ShapeDtypeStruct((PARTS, seqs, some, tile), jnp.bfloat16)] * side,
        compiler_params=pltpu.CompilerParams(vmem_limit_bytes=60 * MIB),
        name="project",
    )(place, x, gain[None], offset[None], wl.T, bl[None], wr.T, br[None])
    return out[:side], out[side:]


def update_kernel(side, seqs, order, lefts, first, last, *refs):
    left_refs, refs = refs[:lefts], refs[lefts:]
    right_refs, refs = refs[:side], refs[side:]
    wt_ref, refs = refs[0], refs[1:]
    if not first:
        before_ref, refs = refs[0], refs[1:]
    if last:
        bias_ref, pair_ref, refs = refs[0], refs[1], refs[2:]
    out_ref, left_wide, right_wide, right_flat, outer = refs
    _, rows, lanes = left_refs[0].shape
    _, some, tile = right_refs[0].shape
    depth = right_flat.shape[0]
    pack = tile // rows
    width = lanes // pack
    halves = pack // 2
    group = outer.shape[0] // halves
    seq_total = side * side * seqs
    step = pl.program_id(0)

    @pl.when(step == 0)
    def _():
        at = 0
        for ref in left_refs:
            count = ref.shape[0] * rows
            left_wide[at : at + count] = ref[...].astype(jnp.float32).reshape(count, lanes)
            at += count
        for dz in range(side):
            for k, dy in enumerate(order):
                to = (k * side + dz) * seqs
                right_wide[to * some : (to + seqs) * some] = (
                    right_refs[dz][dy * seqs : (dy + 1) * seqs]
                    .astype(jnp.float32)
                    .reshape(seqs * some, tile)
                )
        if depth > seq_total:
            left_wide[seq_total * rows :] = jnp.zeros(
                ((depth - seq_total) * rows, lanes), jnp.float32
            )
            right_wide[seq_total * some :] = jnp.zeros(
                ((depth - seq_total) * some, tile), jnp.float32
            )
        for e in range(some):
            right_flat[:, e * tile : (e + 1) * tile] = right_wide[
                pl.ds(e, depth, stride=some), :
            ].astype(jnp.bfloat16)

    for q in range(group):
        x = left_wide[pl.ds(step * group + q, depth, stride=rows), :]
        left = x.T.astype(jnp.bfloat16)
        for n in range(some // 2):
            both = jnp.dot(
                left, right_flat[:, 2 * n * tile : (2 * n + 2) * tile], preferred_element_type=jnp.float32
            ).astype(jnp.bfloat16)
            for k in range(2):
                e = 2 * n + k
                for h in range(pack):
                    outer[
                        q * halves + h // 2,
                        e * width : (e + 1) * width,
                        (h % 2) * tile : (h % 2 + 1) * tile,
                    ] = both[h * width : (h + 1) * width, k * tile : (k + 1) * tile]
    for q in range(group):
        for g in range(halves):
            update = jnp.dot(wt_ref[...], outer[q * halves + g], preferred_element_type=jnp.float32)
            if not first:
                update = update + before_ref[q, g]
            if not last:
                out_ref[q, g] = update
                continue
            for k in range(2):
                h = 2 * g + k
                share = update[:, k * tile : (k + 1) * tile].T * (1.0 / seq_total) + bias_ref[...]
                out_ref[h, q] = (pair_ref[h, q].astype(jnp.float32) + share).astype(jnp.bfloat16)


def update_part(side, seqs, order, part, left, right, wt, before, bias, pair):
    _, rows, lanes = left[0].shape
    _, some, tile = right[0].shape
    chans = wt.shape[0]
    pack = tile // rows
    width = lanes // pack
    halves = pack // 2
    depth = -(-side * side * seqs // LANES) * LANES
    group = 4
    first, last = part == 0, part == PARTS - 1
    whole = lambda shape: pl.BlockSpec(shape, lambda g: (0,) * len(shape))
    sum_spec = pl.BlockSpec((group, halves, chans, 2 * tile), lambda g: (g, 0, 0, 0))
    pair_spec = pl.BlockSpec((pack, group, tile, chans), lambda g: (0, g, 0, 0))
    operands = list(left) + list(right) + [wt]
    specs = [whole(x.shape) for x in operands[:-1]]
    specs.append(pl.BlockSpec((chans, some * width), lambda g: (0, part)))
    if not first:
        operands.append(before)
        specs.append(sum_spec)
    if last:
        operands += [bias[None], pair.reshape(pack, rows, tile, chans)]
        specs += [whole((1, chans)), pair_spec]
        out_shape, out_spec = jax.ShapeDtypeStruct((pack, rows, tile, chans), jnp.bfloat16), pair_spec
    else:
        out_shape = jax.ShapeDtypeStruct((rows, halves, chans, 2 * tile), jnp.float32)
        out_spec = sum_spec
    return pl.pallas_call(
        functools.partial(update_kernel, side, seqs, order, len(left), first, last),
        grid=(rows // group,),
        in_specs=specs,
        out_specs=out_spec,
        out_shape=out_shape,
        scratch_shapes=[
            pltpu.VMEM((depth * rows, lanes), jnp.float32),
            pltpu.VMEM((depth * some, tile), jnp.float32),
            pltpu.VMEM((depth, some * tile), jnp.bfloat16),
            pltpu.VMEM((group * halves, some * width, 2 * tile), jnp.bfloat16),
        ],
        compiler_params=pltpu.CompilerParams(vmem_limit_bytes=48 * MIB),
        cost_estimate=pl.CostEstimate(
            flops=2 * tile * tile * some * width * (side * side * seqs + chans),
            bytes_accessed=16 * MIB,
            transcendentals=0,
        ),
        name="update_%d" % part,
    )(*operands)


def local(
    alignment_features,
    pairwise_features,
    standardize_scaling,
    standardize_additive,
    first_factor_matrix,
    first_factor_intercept,
    second_factor_matrix,
    second_factor_intercept,
    final_matrix,
    final_intercept,
):
    devices = lax.axis_size("row")
    side = math.isqrt(devices)
    me = lax.axis_index("row")
    place = jnp.stack([me // side, me % side]).astype(jnp.int32)
    seqs, residues, _ = alignment_features.shape
    tile = residues // side
    width = first_factor_matrix.shape[1]
    left, right = project(
        side,
        place,
        alignment_features,
        standardize_scaling,
        standardize_additive,
        first_factor_matrix,
        first_factor_intercept,
        second_factor_matrix,
        second_factor_intercept,
    )

    def swap(x, da, db):
        return lax.ppermute(x, "row", [(i, i ^ (da * side + db)) for i in range(devices)])

    right = [right[0]] + [swap(right[d], 0, d) for d in range(1, side)]
    left = jnp.concatenate([left[0]] + [swap(left[d], d, 0) for d in range(1, side)])
    parts = []
    for part in range(PARTS):
        mine = jnp.concatenate([x[part] for x in right])
        parts.append([mine] + [swap(mine, d, 0) for d in range(1, side)])
    order = [0]
    lefts = [left]
    step = side // 2
    while step > 0:
        left = jnp.concatenate(lefts) if len(lefts) > 1 else lefts[0]
        lefts = [left, swap(left, 0, step)]
        order += [o ^ step for o in order]
        step //= 2
    wt = final_matrix.reshape(width, width, -1).transpose(2, 1, 0).reshape(-1, width * width)
    total = None
    for part in range(PARTS):
        total = update_part(
            side, seqs, order, part, lefts, parts[part], wt, total, final_intercept, pairwise_features
        )
    return total.reshape(1, tile, tile, -1)


def solution(mesh):
    placed = (
        P(("grp", "row"), None, None),
        P(("grp", "row"), None, None, None),
        P(),
        P(),
        P(),
        P(),
        P(),
        P(),
        P(),
        P(),
    )
    return jax.shard_map(
        local,
        mesh=mesh,
        in_specs=placed,
        out_specs=P(("grp", "row"), None, None, None),
        check_vma=False,
    )
```

time: 64.8 us -> 66 us (1.019)
  local copies, waits for them, and re-layouts: 9.9 us -> 2.85 us
  Pallas kernels: 23.4 us -> 30 us
  starting transfers between devices: 14 us -> 18.2 us
  waiting for transfers between devices: 16.9 us -> 12.7 us
  other arithmetic: 0.08 us -> 1.47 us
    unnamed x18 -> x8, local copies, waits for them, and re-layouts: 6.37 us -> 0.85 us
    pallas_call x1 -> x2, Pallas kernels: 19.4 us -> 23.6 us  [update_part(): pl.pallas_call(functools.partial(update_kernel, side, seqs, order, len(le...]
    ppermute x12 -> x14, waiting for transfers between devices: 16.9 us -> 12.7 us  [swap(): lax.ppermute(x, 'row', [(i, i ^ da * side + db) for i in range(devices)])]
    ppermute x12 -> x14, starting transfers between devices: 14 us -> 18.2 us  [swap(): lax.ppermute(x, 'row', [(i, i ^ da * side + db) for i in range(devices)])]
    pallas_call x1, Pallas kernels: 4.01 us -> 6.41 us  [project(): pl.pallas_call(functools.partial(project_kernel, side), grid_spec=pltpu.P...]
    another operation x4 -> x0, local copies, waits for them, and re-layouts: 1.57 us -> none  [the longest x2 0.83 us: project(): jnp.tile(wl, (1, pack))]
    concatenate x0 -> x3, other arithmetic: none -> 0.86 us  [the longest x1 0.82 us: local(): jnp.concatenate([left[0]] + [swap(left[d], d, 0) for d in range(1, side)])]
    squeeze x0 -> x4, local copies, waits for them, and re-layouts: none -> 0.77 us  [local(): mine = jnp.concatenate([x[part] for x in right])]
  transfers between devices with their start and end apart: 12 -> 14, of which waited for: 5 -> 3; matrix products, arithmetic and copies ran while one was open for 2% -> 6% of each run, Pallas kernels for 0% -> 16%
where the time goes in v4:
time: 66 us; the launch traced here: 65.3 us
  Pallas kernels  30 us (45%)
  starting transfers between devices  18.2 us (28%)
  waiting for transfers between devices  12.7 us (19%)
  local copies, waits for them, and re-layouts  2.85 us (4%)
  other arithmetic  1.47 us (2%)
    pallas_call x2, Pallas kernels, update_part(): pl.pallas_call(functools.partial(update_kernel, side, seqs, order, len(le...  23.6 us
    ppermute x14, starting transfers between devices, swap(): lax.ppermute(x, 'row', [(i, i ^ da * side + db) for i in range(devices)])  18.2 us
    ppermute x14, waiting for transfers between devices, swap(): lax.ppermute(x, 'row', [(i, i ^ da * side + db) for i in range(devices)])  12.7 us
    pallas_call x1, Pallas kernels, project(): pl.pallas_call(functools.partial(project_kernel, side), grid_spec=pltpu.P...  6.41 us
  transfers between devices with their start and end apart: 14, of which 3 were waited for; matrix products, arithmetic and copies ran while one was open for 6% of the time, Pallas kernels for 16%

profile of v4, /device:TPU:0, one launch (start us, length us, event | category | flops | bytes accessed | tf_op | source)
XLA Modules:
  0.0 65.3 jit_solution(6121159145316204650)
XLA Ops:
  0.0 0.6 pad_add_fusion.place_ref
  0.6 6.4 %project.1 = (bf16[6,32,128]{2,1,0:T(8,128)(2,1)}, bf16[6,32,128]{2,1,0:T(8,128)(2,1)}, bf16[6,32,128]{2,1,0:T(8,128)(2,1)}, bf16[6,32,128]{2,1,0:T(8,128)(2,1)}...) custom-call(s32[2]{0:T(128)} %pad_add_fusion.place_ref, ...), custom_call_target="tpu_custom_call" | custom-call | tf_op jit(solution)/shard_map/project/pallas_call | solution.py:58
  7.0 3.1 %collective-permute-start = (bf16[6,32,128]{2,1,0:T(8,128)(2,1)}, bf16[6,32,128]{2,1,0:T(8,128)(2,1)S(1)}, u32[]{:S(2)}, u32[]{:S(2)}) collective-permute-start(bf16[6,32,128]{2,1,0:T(8,128)(2,1)} %get-tuple-element.14), channel_id=1, source_target_pairs={{0,4},{1,5},{2,6},{3,7},{4,0},{5,1},{6,2},{7,3},{8,12},{9,13},{10,... | collective-permute-start | bytes 147464 | tf_op jit(solution)/shard_map/ppermute | solution.py:239
  10.1 2.6 %collective-permute-start.1 = (bf16[6,32,128]{2,1,0:T(8,128)(2,1)}, bf16[6,32,128]{2,1,0:T(8,128)(2,1)S(1)}, u32[]{:S(2)}, u32[]{:S(2)}) collective-permute-start(bf16[6,32,128]{2,1,0:T(8,128)(2,1)} %get-tuple-element.15), channel_id=1, source_target_pairs={{0,8},{1,9},{2,10},{3,11},{4,12},{5,13},{6,14},{7,15},{8,0},{9,1},... | collective-permute-start | bytes 147464 | tf_op jit(solution)/shard_map/ppermute | solution.py:239
  12.7 0.0 collective-permute-start.2
  12.7 0.0 collective-permute-start.5
  12.7 1.7 %collective-permute-start.6 = (bf16[2,6,16,128]{3,2,1,0:T(8,128)(2,1)}, bf16[2,6,16,128]{3,2,1,0:T(8,128)(2,1)S(1)}, u32[]{:S(2)}, u32[]{:S(2)}) collective-permute-start(bf16[2,6,16,128]{3,2,1,0:T(8,128)(2,1)} %get-tuple-element.19), channel_id=1, source_target_pairs={{0,2},{1,3},{2,0},{3,1},{4,6},{5,7},{6,4},{7,5},{8,10},{9,11},{10,... | collective-permute-start | bytes 147464 | tf_op jit(solution)/shard_map/ppermute | solution.py:239
  14.4 0.8 %slice_bitcast_fusion.6 = (bf16[6,16,128]{2,1,0:T(8,128)(2,1)S(1)}, bf16[6,16,128]{2,1,0:T(8,128)(2,1)S(1)}) fusion(bf16[2,6,16,128]{3,2,1,0:T(8,128)(2,1)} %get-tuple-element.17), kind=kLoop, calls=%fused_computation.9 | loop fusion | bytes 98304 | tf_op jit(solution)/shard_map/squeeze | solution.py:245
  15.2 0.8 %constant_dynamic-update-slice_fusion.4 = bf16[48,32,128]{2,1,0:T(8,128)(2,1)S(1)} fusion(bf16[6,32,128]{2,1,0:T(8,128)(2,1)} %get-tuple-element.13), kind=kLoop, calls=%fused_computation.15 | loop fusion | bytes 98304
  16.0 1.1 %copy.14 = bf16[128,32,32]{0,2,1:T(8,128)(2,1)S(1)} copy(bf16[128,32,32]{0,1,2:T(8,128)(2,1)} %bitcast.34) | data formatting | bytes 524288 | tf_op jit(solution)/shard_map/transpose | solution.py:255
  17.1 0.1 copy.16.refs_6_
  17.2 0.0 collective-permute-done
  17.2 0.2 collective-permute-start.7
  17.4 0.0 collective-permute-done.1
  17.4 1.4 %collective-permute-done.2 = bf16[6,32,128]{2,1,0:T(8,128)(2,1)S(1)} collective-permute-done((bf16[6,32,128]{2,1,0:T(8,128)(2,1)}, bf16[6,32,128]{2,1,0:T(8,128)(2,1)S(1)}, u32[]{:S(2)}, u32[]{:S(2)}) %collective-permute-start.2) | collective-permute-done | bytes 49184 | tf_op jit(solution)/shard_map/ppermute | solution.py:239
  18.8 0.8 %pad_maximum_fusion = bf16[24,32,128]{2,1,0:T(8,128)(2,1)S(1)} fusion(bf16[6,32,128]{2,1,0:T(8,128)(2,1)S(1)} %collective-permute-done.2, bf16[6,32,128]{2,1,0:T(8,128)(2,1)S(1)} %collective-permute-done.1, bf16[6,32,128]{2,1,0:T(8,128)(2,1)S(1)} %collective-permute-done, bf16[6,32,128]{2,1,0:T(8,128)(2,1)} %get-tuple-element.13), kind=kLoop, calls=%fused_computation | loop fusion | flops 294912 | bytes 393216 | tf_op jit(solution)/shard_map/concatenate | solution.py:242
  19.6 1.6 %collective-permute-start.3 = (bf16[24,32,128]{2,1,0:T(8,128)(2,1)S(1)}, bf16[24,32,128]{2,1,0:T(8,128)(2,1)S(1)}, u32[]{:S(2)}, u32[]{:S(2)}) collective-permute-start(bf16[24,32,128]{2,1,0:T(8,128)(2,1)S(1)} %pad_maximum_fusion), channel_id=1, source_target_pairs={{0,2},{1,3},{2,0},{3,1},{4,6},{5,7},{6,4},{7,5},{8,10},{9,11},{10,... | collective-permute-start | bytes 589832 | tf_op jit(solution)/shard_map/ppermute | solution.py:239
  21.2 0.0 collective-permute-done.5
  21.3 0.0 collective-permute-done.6
  21.3 4.5 %collective-permute-done.3 = bf16[24,32,128]{2,1,0:T(8,128)(2,1)S(1)} collective-permute-done((bf16[24,32,128]{2,1,0:T(8,128)(2,1)S(1)}, bf16[24,32,128]{2,1,0:T(8,128)(2,1)S(1)}, u32[]{:S(2)}, u32[]{:S(2)}) %collective-permute-start.3) | collective-permute-done | bytes 196640 | tf_op jit(solution)/shard_map/ppermute | solution.py:239
  25.8 0.1 collective-permute-start.4
  25.9 0.0 collective-permute-done.7
  25.9 3.7 %collective-permute-start.13 = (bf16[24,16,128]{2,1,0:T(8,128)(2,1)S(1)}, bf16[24,16,128]{2,1,0:T(8,128)(2,1)S(1)}, u32[]{:S(2)}, u32[]{:S(2)}) collective-permute-start(bf16[24,16,128]{2,1,0:T(8,128)(2,1)S(1)} %pad_maximum_fusion.2.refs_2_), channel_id=1, source_target_pairs={{0,12},{1,13},{2,14},{3,15},{4,8},{5,9},{6,10},{7,11},{8,4},{9,5},... | collective-permute-start | bytes 294920 | tf_op jit(solution)/shard_map/ppermute | solution.py:239
  29.6 0.0 collective-permute-start.12
  29.6 0.8 %collective-permute-start.11 = (bf16[24,16,128]{2,1,0:T(8,128)(2,1)S(1)}, bf16[24,16,128]{2,1,0:T(8,128)(2,1)S(1)}, u32[]{:S(2)}, u32[]{:S(2)}) collective-permute-start(bf16[24,16,128]{2,1,0:T(8,128)(2,1)S(1)} %pad_maximum_fusion.2.refs_2_), channel_id=1, source_target_pairs={{0,4},{1,5},{2,6},{3,7},{4,0},{5,1},{6,2},{7,3},{8,12},{9,13},{10,... | collective-permute-start | bytes 294920 | tf_op jit(solution)/shard_map/ppermute | solution.py:239
  30.4 0.0 copy-start
  30.4 0.0 copy-start.1
  30.4 3.7 %collective-permute-start.10 = (bf16[24,16,128]{2,1,0:T(8,128)(2,1)S(1)}, bf16[24,16,128]{2,1,0:T(8,128)(2,1)S(1)}, u32[]{:S(2)}, u32[]{:S(2)}) collective-permute-start(bf16[24,16,128]{2,1,0:T(8,128)(2,1)S(1)} %pad_maximum_fusion.1.refs_2_), channel_id=1, source_target_pairs={{0,12},{1,13},{2,14},{3,15},{4,8},{5,9},{6,10},{7,11},{8,4},{9,5},... | collective-permute-start | bytes 294920 | tf_op jit(solution)/shard_map/ppermute | solution.py:239
  34.1 0.0 collective-permute-done.13.refs_5_
  34.1 0.8 %collective-permute-start.9 = (bf16[24,16,128]{2,1,0:T(8,128)(2,1)S(1)}, bf16[24,16,128]{2,1,0:T(8,128)(2,1)S(1)}, u32[]{:S(2)}, u32[]{:S(2)}) collective-permute-start(bf16[24,16,128]{2,1,0:T(8,128)(2,1)S(1)} %pad_maximum_fusion.1.refs_2_), channel_id=1, source_target_pairs={{0,8},{1,9},{2,10},{3,11},{4,12},{5,13},{6,14},{7,15},{8,0},{9,1},... | collective-permute-start | bytes 294920 | tf_op jit(solution)/shard_map/ppermute | solution.py:239
  34.9 6.8 %collective-permute-done.12.refs_4_ = bf16[24,16,128]{2,1,0:T(8,128)(2,1)S(1)} collective-permute-done((bf16[24,16,128]{2,1,0:T(8,128)(2,1)S(1)}, bf16[24,16,128]{2,1,0:T(8,128)(2,1)S(1)}, u32[]{:S(2)}, u32[]{:S(2)}) %collective-permute-start.12) | collective-permute-done | bytes 98336 | tf_op jit(solution)/shard_map/ppermute | solution.py:239
  41.7 0.0 collective-permute-start.8
  41.7 0.0 collective-permute-done.11.refs_3_
  41.7 0.0 collective-permute-done.4.refs_1_
  41.7 10.5 %update_0.1.refs_7_ = f32[32,2,128,256]{3,2,1,0:T(8,128)} custom-call(bf16[48,32,128]{2,1,0:T(8,128)(2,1)S(1)} %constant_dynamic-update-slice_fusion.refs_0_, bf16[48,32,128]{2,1,0:T(8,128)(2,1)S(1)} %collective-permute-done.4.refs_1_, bf16[24,16,128]{2,1,0:T(8,128)(2,1)S(1)} %pad_maximum_fusion.2.refs_2_, ...), custom_call_target="tpu_custom_call" | custom-call | flops 3758096384 | bytes 16777216 | tf_op jit(solution)/shard_map/update_0/pallas_call | solution.py:185
  52.2 0.0 collective-permute-done.10.refs_5_
  52.2 0.0 collective-permute-done.9.refs_4_
  52.2 0.0 collective-permute-done.8.refs_3_
  52.2 0.0 copy-done
  52.2 0.0 copy-done.1
  52.2 13.1 %update_1.1 = bf16[4,32,128,128]{3,2,1,0:T(8,128)(2,1)} custom-call(bf16[48,32,128]{2,1,0:T(8,128)(2,1)S(1)} %constant_dynamic-update-slice_fusion.refs_0_, bf16[48,32,128]{2,1,0:T(8,128)(2,1)S(1)} %collective-permute-done.4.refs_1_, bf16[24,16,128]{2,1,0:T(8,128)(2,1)S(1)} %pad_maximum_fusion.1.refs_2_, ...), custom_call_target="tpu_custom_call" | custom-call | flops 3758096384 | bytes 16777216 | tf_op jit(solution)/shard_map/update_1/pallas_call | solution.py:185
  (9 shorter events, 0.1 us)
Async XLA Ops:
  7.0 10.2 %collective-permute-start = (bf16[6,32,128]{2,1,0:T(8,128)(2,1)}, bf16[6,32,128]{2,1,0:T(8,128)(2,1)S(1)}, u32[]{:S(2)}, u32[]{:S(2)}) collective-permute-start(bf16[6,32,128]{2,1,0:T(8,128)(2,1)} %get-tuple-element.14), channel_id=1, source_target_pairs={{0,4},{1,5},{2,6},{3,7},{4,0},{5,1},{6,2},{7,3},{8,12},{9,13},{10,... | collective-permute-start | bytes 147464 | tf_op jit(solution)/shard_map/ppermute | solution.py:239
  10.1 7.3 %collective-permute-start.1 = (bf16[6,32,128]{2,1,0:T(8,128)(2,1)}, bf16[6,32,128]{2,1,0:T(8,128)(2,1)S(1)}, u32[]{:S(2)}, u32[]{:S(2)}) collective-permute-start(bf16[6,32,128]{2,1,0:T(8,128)(2,1)} %get-tuple-element.15), channel_id=1, source_target_pairs={{0,8},{1,9},{2,10},{3,11},{4,12},{5,13},{6,14},{7,15},{8,0},{9,1},... | collective-permute-start | bytes 147464 | tf_op jit(solution)/shard_map/ppermute | solution.py:239
  12.7 6.1 %collective-permute-start.2 = (bf16[6,32,128]{2,1,0:T(8,128)(2,1)}, bf16[6,32,128]{2,1,0:T(8,128)(2,1)S(1)}, u32[]{:S(2)}, u32[]{:S(2)}) collective-permute-start(bf16[6,32,128]{2,1,0:T(8,128)(2,1)} %get-tuple-element.16), channel_id=1, source_target_pairs={{0,12},{1,13},{2,14},{3,15},{4,8},{5,9},{6,10},{7,11},{8,4},{9,5},... | collective-permute-start | bytes 147464 | tf_op jit(solution)/shard_map/ppermute | solution.py:239
  12.7 8.5 %collective-permute-start.5 = (bf16[2,6,16,128]{3,2,1,0:T(8,128)(2,1)}, bf16[2,6,16,128]{3,2,1,0:T(8,128)(2,1)S(1)}, u32[]{:S(2)}, u32[]{:S(2)}) collective-permute-start(bf16[2,6,16,128]{3,2,1,0:T(8,128)(2,1)} %get-tuple-element.18), channel_id=1, source_target_pairs={{0,1},{1,0},{2,3},{3,2},{4,5},{5,4},{6,7},{7,6},{8,9},{9,8},{10,11... | collective-permute-start | bytes 147464 | tf_op jit(solution)/shard_map/ppermute | solution.py:239
  12.7 8.6 %collective-permute-start.6 = (bf16[2,6,16,128]{3,2,1,0:T(8,128)(2,1)}, bf16[2,6,16,128]{3,2,1,0:T(8,128)(2,1)S(1)}, u32[]{:S(2)}, u32[]{:S(2)}) collective-permute-start(bf16[2,6,16,128]{3,2,1,0:T(8,128)(2,1)} %get-tuple-element.19), channel_id=1, source_target_pairs={{0,2},{1,3},{2,0},{3,1},{4,6},{5,7},{6,4},{7,5},{8,10},{9,11},{10,... | collective-permute-start | bytes 147464 | tf_op jit(solution)/shard_map/ppermute | solution.py:239
  17.2 8.6 %collective-permute-start.7 = (bf16[2,6,16,128]{3,2,1,0:T(8,128)(2,1)}, bf16[2,6,16,128]{3,2,1,0:T(8,128)(2,1)S(1)}, u32[]{:S(2)}, u32[]{:S(2)}) collective-permute-start(bf16[2,6,16,128]{3,2,1,0:T(8,128)(2,1)} %get-tuple-element.20), channel_id=1, source_target_pairs={{0,3},{1,2},{2,1},{3,0},{4,7},{5,6},{6,5},{7,4},{8,11},{9,10},{10,... | collective-permute-start | bytes 147464 | tf_op jit(solution)/shard_map/ppermute | solution.py:239
  19.6 6.1 %collective-permute-start.3 = (bf16[24,32,128]{2,1,0:T(8,128)(2,1)S(1)}, bf16[24,32,128]{2,1,0:T(8,128)(2,1)S(1)}, u32[]{:S(2)}, u32[]{:S(2)}) collective-permute-start(bf16[24,32,128]{2,1,0:T(8,128)(2,1)S(1)} %pad_maximum_fusion), channel_id=1, source_target_pairs={{0,2},{1,3},{2,0},{3,1},{4,6},{5,7},{6,4},{7,5},{8,10},{9,11},{10,... | collective-permute-start | bytes 589832 | tf_op jit(solution)/shard_map/ppermute | solution.py:239
  25.8 15.9 %collective-permute-start.4 = (bf16[48,32,128]{2,1,0:T(8,128)(2,1)S(1)}, bf16[48,32,128]{2,1,0:T(8,128)(2,1)S(1)}, u32[]{:S(2)}, u32[]{:S(2)}) collective-permute-start(bf16[48,32,128]{2,1,0:T(8,128)(2,1)S(1)} %constant_dynamic-update-slice_fusion.refs_0_), channel_id=1, source_target_pairs={{0,1},{1,0},{2,3},{3,2},{4,5},{5,4},{6,7},{7,6},{8,9},{9,8},{10,11... | collective-permute-start | bytes 1179656 | tf_op jit(solution)/shard_map/ppermute | solution.py:239
  25.9 8.2 %collective-permute-start.13 = (bf16[24,16,128]{2,1,0:T(8,128)(2,1)S(1)}, bf16[24,16,128]{2,1,0:T(8,128)(2,1)S(1)}, u32[]{:S(2)}, u32[]{:S(2)}) collective-permute-start(bf16[24,16,128]{2,1,0:T(8,128)(2,1)S(1)} %pad_maximum_fusion.2.refs_2_), channel_id=1, source_target_pairs={{0,12},{1,13},{2,14},{3,15},{4,8},{5,9},{6,10},{7,11},{8,4},{9,5},... | collective-permute-start | bytes 294920 | tf_op jit(solution)/shard_map/ppermute | solution.py:239
  29.6 12.1 %collective-permute-start.12 = (bf16[24,16,128]{2,1,0:T(8,128)(2,1)S(1)}, bf16[24,16,128]{2,1,0:T(8,128)(2,1)S(1)}, u32[]{:S(2)}, u32[]{:S(2)}) collective-permute-start(bf16[24,16,128]{2,1,0:T(8,128)(2,1)S(1)} %pad_maximum_fusion.2.refs_2_), channel_id=1, source_target_pairs={{0,8},{1,9},{2,10},{3,11},{4,12},{5,13},{6,14},{7,15},{8,0},{9,1},... | collective-permute-start | bytes 294920 | tf_op jit(solution)/shard_map/ppermute | solution.py:239
  29.6 12.1 %collective-permute-start.11 = (bf16[24,16,128]{2,1,0:T(8,128)(2,1)S(1)}, bf16[24,16,128]{2,1,0:T(8,128)(2,1)S(1)}, u32[]{:S(2)}, u32[]{:S(2)}) collective-permute-start(bf16[24,16,128]{2,1,0:T(8,128)(2,1)S(1)} %pad_maximum_fusion.2.refs_2_), channel_id=1, source_target_pairs={{0,4},{1,5},{2,6},{3,7},{4,0},{5,1},{6,2},{7,3},{8,12},{9,13},{10,... | collective-permute-start | bytes 294920 | tf_op jit(solution)/shard_map/ppermute | solution.py:239
  30.4 21.8 %copy-start = (bf16[1,128,128,128]{3,2,1,0:T(8,128)(2,1)S(1)}, bf16[1,128,128,128]{3,2,1,0:T(8,128)(2,1)}, u32[]{:S(2)}) copy-start(bf16[1,128,128,128]{3,2,1,0:T(8,128)(2,1)} %param.11) | copy-start | bytes 12582916
  30.4 21.8 %copy-start.1 = (f32[128]{0:T(128)S(1)}, f32[128]{0:T(128)}, u32[]{:S(2)}) copy-start(f32[128]{0:T(128)} %param.19) | copy-start | bytes 1540
  30.4 21.8 %collective-permute-start.10 = (bf16[24,16,128]{2,1,0:T(8,128)(2,1)S(1)}, bf16[24,16,128]{2,1,0:T(8,128)(2,1)S(1)}, u32[]{:S(2)}, u32[]{:S(2)}) collective-permute-start(bf16[24,16,128]{2,1,0:T(8,128)(2,1)S(1)} %pad_maximum_fusion.1.refs_2_), channel_id=1, source_target_pairs={{0,12},{1,13},{2,14},{3,15},{4,8},{5,9},{6,10},{7,11},{8,4},{9,5},... | collective-permute-start | bytes 294920 | tf_op jit(solution)/shard_map/ppermute | solution.py:239
  34.1 18.1 %collective-permute-start.9 = (bf16[24,16,128]{2,1,0:T(8,128)(2,1)S(1)}, bf16[24,16,128]{2,1,0:T(8,128)(2,1)S(1)}, u32[]{:S(2)}, u32[]{:S(2)}) collective-permute-start(bf16[24,16,128]{2,1,0:T(8,128)(2,1)S(1)} %pad_maximum_fusion.1.refs_2_), channel_id=1, source_target_pairs={{0,8},{1,9},{2,10},{3,11},{4,12},{5,13},{6,14},{7,15},{8,0},{9,1},... | collective-permute-start | bytes 294920 | tf_op jit(solution)/shard_map/ppermute | solution.py:239
  41.7 10.5 %collective-permute-start.8 = (bf16[24,16,128]{2,1,0:T(8,128)(2,1)S(1)}, bf16[24,16,128]{2,1,0:T(8,128)(2,1)S(1)}, u32[]{:S(2)}, u32[]{:S(2)}) collective-permute-start(bf16[24,16,128]{2,1,0:T(8,128)(2,1)S(1)} %pad_maximum_fusion.1.refs_2_), channel_id=1, source_target_pairs={{0,4},{1,5},{2,6},{3,7},{4,0},{5,1},{6,2},{7,3},{8,12},{9,13},{10,... | collective-permute-start | bytes 294920 | tf_op jit(solution)/shard_map/ppermute | solution.py:239

commit v5 on v4

--- a/solution.py
+++ b/solution.py
@@ -9,75 +9,91 @@
 from jax.sharding import PartitionSpec as P
 
 LANES = 128
-PARTS = 2
+PARTS = 1
 MIB = 1024 * 1024
 
 
-def project_kernel(side, place_ref, x_ref, gain_ref, offset_ref, wl_ref, bl_ref, wr_ref, br_ref, *rest):
-    left_out, right_out, normed_ref = rest[:side], rest[side : 2 * side], rest[2 * side]
-    width, chans = wl_ref.shape
-    tile = x_ref.shape[1] // side
+def project_kernel(side, *refs):
+    sources, refs = refs[:7], refs[7:]
+    left_out, right_out, refs = refs[:side], refs[side : 2 * side], refs[2 * side :]
+    buffers, normed_ref, sems, x_sems = refs[:7], refs[7], refs[8], refs[9]
+    x_ref, gain_ref, offset_ref, wl_ref, bl_ref, wr_ref, br_ref = buffers
+    seqs, residues, chans = x_ref.shape
+    width = wl_ref.shape[0]
+    tile = residues // side
     pack = LANES // width
     rows = tile // pack
-    x = x_ref[0].astype(jnp.float32)
-    center = x - jnp.mean(x, axis=-1, keepdims=True)
-    variance = jnp.mean(center * center, axis=-1, keepdims=True)
-    normed_ref[...] = (
-        center * lax.rsqrt(variance + 1e-05) * gain_ref[...] + offset_ref[...]
-    ).astype(jnp.bfloat16)
+    x_copies = [
+        pltpu.make_async_copy(sources[0].at[s], x_ref.at[s], x_sems.at[s]) for s in range(seqs)
+    ]
+    copies = [
+        pltpu.make_async_copy(sources[k], buffers[k], sems.at[k]) for k in range(1, len(buffers))
+    ]
+    for copy in x_copies[:1] + copies + x_copies[1:]:
+        copy.start()
+    for copy in copies:
+        copy.wait()
+    me = lax.axis_index("row")
+    place_a, place_b = me // side, lax.rem(me, side)
     nt = (((1,), (1,)), ((), ()))
-    blocks = []
-    for d in range(side):
-        a = place_ref[0] ^ d
-        blocks.append(normed_ref[pl.ds(pl.multiple_of(a * tile, tile), tile), :])
     wl = wl_ref[...]
-    total = jnp.concatenate([bl_ref[...]] * pack, axis=1)
-    for h in range(pack):
-        placed = jnp.concatenate(
-            [wl if k == h else jnp.zeros_like(wl) for k in range(pack)], axis=0
-        )
-        picked = jnp.concatenate([block[h * rows : (h + 1) * rows] for block in blocks], axis=0)
-        total = total + lax.dot_general(picked, placed, nt, preferred_element_type=jnp.float32)
-    left = total.astype(jnp.bfloat16)
-    bias = jnp.broadcast_to(br_ref[...], (tile, width)).T
-    for d in range(side):
-        left_out[d][0] = left[d * rows : (d + 1) * rows]
-        b = place_ref[1] ^ d
-        block = normed_ref[pl.ds(pl.multiple_of(b * tile, tile), tile), :]
-        right = lax.dot_general(wr_ref[...], block, nt, preferred_element_type=jnp.float32) + bias
-        right_out[d][:, 0] = right.astype(jnp.bfloat16).reshape(PARTS, width // PARTS, tile)
-
-
-def project(side, place, x, gain, offset, wl, bl, wr, br):
+    placed = [
+        jnp.concatenate([wl if k == h else jnp.zeros_like(wl) for k in range(pack)], axis=0)
+        for h in range(pack)
+    ]
+    left_bias = jnp.concatenate([bl_ref[...]] * pack, axis=1)
+    right_bias = jnp.broadcast_to(br_ref[...], (tile, width)).T
+    for s in range(seqs):
+        x_copies[s].wait()
+        normed = normed_ref.at[s % 2]
+        x = x_ref[s].astype(jnp.float32)
+        center = x - jnp.mean(x, axis=-1, keepdims=True)
+        variance = jnp.mean(center * center, axis=-1, keepdims=True)
+        normed[...] = (
+            center * lax.rsqrt(variance + 1e-05) * gain_ref[...] + offset_ref[...]
+        ).astype(jnp.bfloat16)
+        blocks = []
+        for d in range(side):
+            b = place_b ^ d
+            block = normed[pl.ds(pl.multiple_of(b * tile, tile), tile), :]
+            right = lax.dot_general(wr_ref[...], block, nt, preferred_element_type=jnp.float32)
+            right_out[d][:, s] = (
+                (right + right_bias).astype(jnp.bfloat16).reshape(PARTS, width // PARTS, tile)
+            )
+            a = place_a ^ d
+            blocks.append(normed[pl.ds(pl.multiple_of(a * tile, tile), tile), :])
+        total = left_bias
+        for h in range(pack):
+            picked = jnp.concatenate([block[h * rows : (h + 1) * rows] for block in blocks], axis=0)
+            total = total + lax.dot_general(
+                picked, placed[h], nt, preferred_element_type=jnp.float32
+            )
+        left = total.astype(jnp.bfloat16)
+        for d in range(side):
+            left_out[d][s] = left[d * rows : (d + 1) * rows]
+
+
+def project(side, x, gain, offset, wl, bl, wr, br):
     seqs, residues, chans = x.shape
     width = wl.shape[1]
     tile = residues // side
     rows = tile * width // LANES
-    some = width // PARTS
-    whole = lambda *shape: pl.BlockSpec(shape, lambda s, place: (0,) * len(shape))
+    operands = (x, gain[None], offset[None], wl.T, bl[None], wr.T, br[None])
     out = pl.pallas_call(
         functools.partial(project_kernel, side),
-        grid_spec=pltpu.PrefetchScalarGridSpec(
-            num_scalar_prefetch=1,
-            grid=(seqs,),
-            in_specs=[
-                pl.BlockSpec((1, residues, chans), lambda s, place: (s, 0, 0)),
-                whole(1, chans),
-                whole(1, chans),
-                whole(width, chans),
-                whole(1, width),
-                whole(width, chans),
-                whole(1, width),
-            ],
-            out_specs=[pl.BlockSpec((1, rows, LANES), lambda s, place: (s, 0, 0))] * side
-            + [pl.BlockSpec((PARTS, 1, some, tile), lambda s, place: (0, s, 0, 0))] * side,
-            scratch_shapes=[pltpu.VMEM((residues, chans), jnp.bfloat16)],
-        ),
+        in_specs=[pl.BlockSpec(memory_space=pltpu.HBM)] * len(operands),
+        out_specs=[pl.BlockSpec(memory_space=pltpu.VMEM)] * (2 * side),
         out_shape=[jax.ShapeDtypeStruct((seqs, rows, LANES), jnp.bfloat16)] * side
-        + [jax.ShapeDtypeStruct((PARTS, seqs, some, tile), jnp.bfloat16)] * side,
-        compiler_params=pltpu.CompilerParams(vmem_limit_bytes=60 * MIB),
+        + [jax.ShapeDtypeStruct((PARTS, seqs, width // PARTS, tile), jnp.bfloat16)] * side,
+        scratch_shapes=[pltpu.VMEM(o.shape, o.dtype) for o in operands]
+        + [
+            pltpu.VMEM((2, residues, chans), jnp.bfloat16),
+            pltpu.SemaphoreType.DMA((len(operands),)),
+            pltpu.SemaphoreType.DMA((seqs,)),
+        ],
+        compiler_params=pltpu.CompilerParams(vmem_limit_bytes=32 * MIB),
         name="project",
-    )(place, x, gain[None], offset[None], wl.T, bl[None], wr.T, br[None])
+    )(*operands)
     return out[:side], out[side:]
 
 
@@ -218,14 +234,11 @@
 ):
     devices = lax.axis_size("row")
     side = math.isqrt(devices)
-    me = lax.axis_index("row")
-    place = jnp.stack([me // side, me % side]).astype(jnp.int32)
     seqs, residues, _ = alignment_features.shape
     tile = residues // side
     width = first_factor_matrix.shape[1]
     left, right = project(
         side,
-        place,
         alignment_features,
         standardize_scaling,
         standardize_additive,
@@ -239,16 +252,21 @@
         return lax.ppermute(x, "row", [(i, i ^ (da * side + db)) for i in range(devices)])
 
     right = [right[0]] + [swap(right[d], 0, d) for d in range(1, side)]
+    *left, right[1] = lax.optimization_barrier((*left, right[1]))
     left = jnp.concatenate([left[0]] + [swap(left[d], d, 0) for d in range(1, side)])
     parts = []
     for part in range(PARTS):
         mine = jnp.concatenate([x[part] for x in right])
+        if part > 0:
+            mine, left = lax.optimization_barrier((mine, left))
         parts.append([mine] + [swap(mine, d, 0) for d in range(1, side)])
     order = [0]
     lefts = [left]
     step = side // 2
     while step > 0:
         left = jnp.concatenate(lefts) if len(lefts) > 1 else lefts[0]
+        if len(lefts) > 1:
+            left, parts[0][1] = lax.optimization_barrier((left, parts[0][1]))
         lefts = [left, swap(left, 0, step)]
         order += [o ^ step for o in order]
         step //= 2

time: 66 us -> 69.6 us (1.055)
  waiting for transfers between devices: 12.7 us -> 25.9 us
  Pallas kernels: 30 us -> 23 us
  starting transfers between devices: 18.2 us -> 11.3 us
  local copies, waits for them, and re-layouts: 2.85 us -> 8.98 us
  other arithmetic: 1.47 us -> 0.05 us
    ppermute x14 -> x11, waiting for transfers between devices: 12.7 us -> 25.9 us  [swap(): lax.ppermute(x, 'row', [(i, i ^ da * side + db) for i in range(devices)])]
    ppermute x14 -> x11, starting transfers between devices: 18.2 us -> 11.3 us  [swap(): lax.ppermute(x, 'row', [(i, i ^ da * side + db) for i in range(devices)])]
    unnamed x8 -> x22, local copies, waits for them, and re-layouts: 0.85 us -> 7.75 us
    pallas_call x2 -> x1, Pallas kernels: 23.6 us -> 19.4 us  [update_part(): pl.pallas_call(functools.partial(update_kernel, side, seqs, order, len(le...]
    pallas_call x1, Pallas kernels: 6.41 us -> 3.57 us  [project(): pl.pallas_call(functools.partial(project_kernel, side), in_specs=[pl.Bloc...]
    concatenate x1, other arithmetic: 0.82 us -> 0.03 us  [local(): jnp.concatenate([left[0]] + [swap(left[d], d, 0) for d in range(1, side)])]
    squeeze x4 -> x0, local copies, waits for them, and re-layouts: 0.77 us -> none  [local(): mine = jnp.concatenate([x[part] for x in right])]
  transfers between devices with their start and end apart: 14 -> 11, of which waited for: 3 -> 5; matrix products, arithmetic and copies ran while one was open for 6% -> 2% of each run, Pallas kernels for 16% -> 0%
where the time goes in v5:
time: 69.6 us; the launch traced here: 69.2 us
  waiting for transfers between devices  25.9 us (37%)
  Pallas kernels  23 us (33%)
  starting transfers between devices  11.3 us (16%)
  local copies, waits for them, and re-layouts  8.98 us (13%)
    ppermute x11, waiting for transfers between devices, swap(): lax.ppermute(x, 'row', [(i, i ^ da * side + db) for i in range(devices)])  25.9 us
    pallas_call x1, Pallas kernels, update_part(): pl.pallas_call(functools.partial(update_kernel, side, seqs, order, len(le...  19.4 us
    ppermute x11, starting transfers between devices, swap(): lax.ppermute(x, 'row', [(i, i ^ da * side + db) for i in range(devices)])  11.3 us
    unnamed x22, local copies, waits for them, and re-layouts  7.75 us
    pallas_call x1, Pallas kernels, project(): pl.pallas_call(functools.partial(project_kernel, side), in_specs=[pl.Bloc...  3.57 us
  transfers between devices with their start and end apart: 11, of which 5 were waited for; matrix products, arithmetic and copies ran while one was open for 2% of the time, Pallas kernels for 0%

profile of v5, /device:TPU:0, one launch (start us, length us, event | category | flops | bytes accessed | tf_op | source)
XLA Modules:
  0.0 69.2 jit_solution(1716369598903206605)
XLA Ops:
  0.0 0.0 copy-start.8
  0.0 0.0 copy-start
  0.0 1.4 %copy-done = bf16[6,512,256]{2,1,0:T(8,128)(2,1)S(1)} copy-done((bf16[6,512,256]{2,1,0:T(8,128)(2,1)S(1)}, bf16[6,512,256]{2,1,0:T(8,128)(2,1)}, u32[]{:S(2)}) %copy-start) | copy-done | bytes 1572888
  1.4 0.0 copy-start.1
  1.4 0.7 %copy-done.1 = bf16[256,32]{0,1:T(8,128)(2,1)S(1)} copy-done((bf16[256,32]{0,1:T(8,128)(2,1)S(1)}, bf16[256,32]{0,1:T(8,128)(2,1)}, u32[]{:S(2)}) %copy-start.1) | copy-done | bytes 16408
  2.1 0.0 copy-start.2
  2.1 0.7 %copy-done.2 = bf16[256,32]{0,1:T(8,128)(2,1)S(1)} copy-done((bf16[256,32]{0,1:T(8,128)(2,1)S(1)}, bf16[256,32]{0,1:T(8,128)(2,1)}, u32[]{:S(2)}) %copy-start.2) | copy-done | bytes 16408
  2.9 0.0 copy-start.3
  2.9 0.7 copy-done.3
  3.5 0.0 copy-start.4
  3.5 0.7 copy-done.4
  4.2 0.0 copy-start.5
  4.2 0.7 copy-done.5
  4.9 0.0 copy-start.6
  4.9 0.7 copy-done.6
  5.5 3.6 %project.1 = (bf16[6,32,128]{2,1,0:T(8,128)(2,1)S(1)}, bf16[6,32,128]{2,1,0:T(8,128)(2,1)S(1)}, bf16[6,32,128]{2,1,0:T(8,128)(2,1)S(1)}, bf16[6,32,128]{2,1,0:T(...) custom-call(bf16[6,512,256]{2,1,0:T(8,128)(2,1)S(1)} %copy-done, ...), custom_call_target="tpu_custom_call" | custom-call | tf_op jit(solution)/shard_map/project/pallas_call | solution.py:82
  9.1 0.5 collective-permute-start
  9.6 2.6 %collective-permute-start.5 = (bf16[1,6,32,128]{3,2,1,0:T(8,128)(2,1)S(1)}, bf16[1,6,32,128]{3,2,1,0:T(8,128)(2,1)S(1)}, u32[]{:S(2)}, u32[]{:S(2)}) collective-permute-start(bf16[1,6,32,128]{3,2,1,0:T(8,128)(2,1)S(1)} %get-tuple-element.31), channel_id=1, source_target_pairs={{0,2},{1,3},{2,0},{3,1},{4,6},{5,7},{6,4},{7,5},{8,10},{9,11},{10,... | collective-permute-start | bytes 147464 | tf_op jit(solution)/shard_map/ppermute | solution.py:252
  12.2 0.1 collective-permute-start.6
  12.3 0.0 collective-permute-done
  12.3 1.8 %collective-permute-start.1 = (bf16[6,32,128]{2,1,0:T(8,128)(2,1)S(1)}, bf16[6,32,128]{2,1,0:T(8,128)(2,1)S(1)}, u32[]{:S(2)}, u32[]{:S(2)}) collective-permute-start(bf16[6,32,128]{2,1,0:T(8,128)(2,1)S(1)} %get-tuple-element.26), channel_id=1, source_target_pairs={{0,4},{1,5},{2,6},{3,7},{4,0},{5,1},{6,2},{7,3},{8,12},{9,13},{10,... | collective-permute-start | bytes 147464 | tf_op jit(solution)/shard_map/ppermute | solution.py:252
  14.1 2.6 %collective-permute-start.2 = (bf16[6,32,128]{2,1,0:T(8,128)(2,1)S(1)}, bf16[6,32,128]{2,1,0:T(8,128)(2,1)S(1)}, u32[]{:S(2)}, u32[]{:S(2)}) collective-permute-start(bf16[6,32,128]{2,1,0:T(8,128)(2,1)S(1)} %get-tuple-element.27), channel_id=1, source_target_pairs={{0,8},{1,9},{2,10},{3,11},{4,12},{5,13},{6,14},{7,15},{8,0},{9,1},... | collective-permute-start | bytes 147464 | tf_op jit(solution)/shard_map/ppermute | solution.py:252
  16.7 0.0 collective-permute-start.3
  16.7 0.0 collective-permute-done.5
  16.7 0.0 collective-permute-done.6
  16.7 1.0 %collective-permute-start.7 = (bf16[24,32,128]{2,1,0:T(8,128)(2,1)S(1)}, bf16[24,32,128]{2,1,0:T(8,128)(2,1)S(1)}, u32[]{:S(2)}, u32[]{:S(2)}) collective-permute-start(bf16[24,32,128]{2,1,0:T(8,128)(2,1)S(1)} %pad_maximum_fusion.1.refs_2_), channel_id=1, source_target_pairs={{0,4},{1,5},{2,6},{3,7},{4,0},{5,1},{6,2},{7,3},{8,12},{9,13},{10,... | collective-permute-start | bytes 589832 | tf_op jit(solution)/shard_map/ppermute | solution.py:252
  17.7 0.0 collective-permute-done.1
  17.7 2.5 %collective-permute-done.2 = bf16[6,32,128]{2,1,0:T(8,128)(2,1)S(1)} collective-permute-done((bf16[6,32,128]{2,1,0:T(8,128)(2,1)S(1)}, bf16[6,32,128]{2,1,0:T(8,128)(2,1)S(1)}, u32[]{:S(2)}, u32[]{:S(2)}) %collective-permute-start.2) | collective-permute-done | bytes 49184 | tf_op jit(solution)/shard_map/ppermute | solution.py:252
  20.2 2.9 %collective-permute-done.3 = bf16[6,32,128]{2,1,0:T(8,128)(2,1)S(1)} collective-permute-done((bf16[6,32,128]{2,1,0:T(8,128)(2,1)S(1)}, bf16[6,32,128]{2,1,0:T(8,128)(2,1)S(1)}, u32[]{:S(2)}, u32[]{:S(2)}) %collective-permute-start.3) | collective-permute-done | bytes 49184 | tf_op jit(solution)/shard_map/ppermute | solution.py:252
  23.1 1.6 %collective-permute-start.4 = (bf16[24,32,128]{2,1,0:T(8,128)(2,1)S(1)}, bf16[24,32,128]{2,1,0:T(8,128)(2,1)S(1)}, u32[]{:S(2)}, u32[]{:S(2)}) collective-permute-start(bf16[24,32,128]{2,1,0:T(8,128)(2,1)S(1)} %pad_maximum_fusion), channel_id=1, source_target_pairs={{0,2},{1,3},{2,0},{3,1},{4,6},{5,7},{6,4},{7,5},{8,10},{9,11},{10,... | collective-permute-start | bytes 589832 | tf_op jit(solution)/shard_map/ppermute | solution.py:252
  24.8 4.1 %collective-permute-done.4 = bf16[24,32,128]{2,1,0:T(8,128)(2,1)S(1)} collective-permute-done((bf16[24,32,128]{2,1,0:T(8,128)(2,1)S(1)}, bf16[24,32,128]{2,1,0:T(8,128)(2,1)S(1)}, u32[]{:S(2)}, u32[]{:S(2)}) %collective-permute-start.4) | collective-permute-done | bytes 196640 | tf_op jit(solution)/shard_map/ppermute | solution.py:252
  28.9 0.0 collective-permute-done.7.refs_3_
  28.9 0.1 collective-permute-start.8
  29.0 1.1 %collective-permute-start.10 = (bf16[24,32,128]{2,1,0:T(8,128)(2,1)S(1)}, bf16[24,32,128]{2,1,0:T(8,128)(2,1)S(1)}, u32[]{:S(2)}, u32[]{:S(2)}) collective-permute-start(bf16[24,32,128]{2,1,0:T(8,128)(2,1)S(1)} %pad_maximum_fusion.1.refs_2_), channel_id=1, source_target_pairs={{0,12},{1,13},{2,14},{3,15},{4,8},{5,9},{6,10},{7,11},{8,4},{9,5},... | collective-permute-start | bytes 589832 | tf_op jit(solution)/shard_map/ppermute | solution.py:252
  30.1 0.0 collective-permute-start.9
  30.1 1.1 %copy.13 = bf16[128,32,32]{0,2,1:T(8,128)(2,1)S(1)} copy(bf16[128,32,32]{0,1,2:T(8,128)(2,1)} %bitcast.27) | data formatting | bytes 524288 | tf_op jit(solution)/shard_map/transpose | solution.py:273
  31.1 0.1 copy.14.refs_6_
  31.3 7.4 %collective-permute-done.10.refs_5_ = bf16[24,32,128]{2,1,0:T(8,128)(2,1)S(1)} collective-permute-done((bf16[24,32,128]{2,1,0:T(8,128)(2,1)S(1)}, bf16[24,32,128]{2,1,0:T(8,128)(2,1)S(1)}, u32[]{:S(2)}, u32[]{:S(2)}) %collective-permute-start.10) | collective-permute-done | bytes 196640 | tf_op jit(solution)/shard_map/ppermute | solution.py:252
  38.7 9.0 %collective-permute-done.9.refs_4_ = bf16[24,32,128]{2,1,0:T(8,128)(2,1)S(1)} collective-permute-done((bf16[24,32,128]{2,1,0:T(8,128)(2,1)S(1)}, bf16[24,32,128]{2,1,0:T(8,128)(2,1)S(1)}, u32[]{:S(2)}, u32[]{:S(2)}) %collective-permute-start.9) | collective-permute-done | bytes 196640 | tf_op jit(solution)/shard_map/ppermute | solution.py:252
  47.6 0.0 collective-permute-done.8.refs_1_
  47.6 0.0 copy-done.8
  47.6 0.0 copy-start.7
  47.6 2.2 %copy-done.7 = bf16[1,128,128,128]{3,2,1,0:T(8,128)(2,1)S(1)} copy-done((bf16[1,128,128,128]{3,2,1,0:T(8,128)(2,1)S(1)}, bf16[1,128,128,128]{3,2,1,0:T(8,128)(2,1)}, u32[]{:S(2)}) %copy-start.7) | copy-done | bytes 4194328
  49.8 19.4 %update_0.1 = bf16[4,32,128,128]{3,2,1,0:T(8,128)(2,1)} custom-call(bf16[48,32,128]{2,1,0:T(8,128)(2,1)S(1)} %constant_dynamic-update-slice_fusion.refs_0_, bf16[48,32,128]{2,1,0:T(8,128)(2,1)S(1)} %collective-permute-done.8.refs_1_, bf16[24,32,128]{2,1,0:T(8,128)(2,1)S(1)} %pad_maximum_fusion.1.refs_2_, ...), custom_call_target="tpu_custom_call" | custom-call | flops 7516192768 | bytes 16777216 | tf_op jit(solution)/shard_map/update_0/pallas_call | solution.py:201
  (7 shorter events, 0.1 us)
Async XLA Ops:
  0.0 47.6 %copy-start.8 = (f32[128]{0:T(128)S(1)}, f32[128]{0:T(128)}, u32[]{:S(2)}) copy-start(f32[128]{0:T(128)} %param.19) | copy-start | bytes 1540
  0.0 1.4 %copy-start = (bf16[6,512,256]{2,1,0:T(8,128)(2,1)S(1)}, bf16[6,512,256]{2,1,0:T(8,128)(2,1)}, u32[]{:S(2)}) copy-start(bf16[6,512,256]{2,1,0:T(8,128)(2,1)} %refs_0_.1) | copy-start | bytes 4718596
  1.4 0.7 %copy-start.1 = (bf16[256,32]{0,1:T(8,128)(2,1)S(1)}, bf16[256,32]{0,1:T(8,128)(2,1)}, u32[]{:S(2)}) copy-start(bf16[256,32]{0,1:T(8,128)(2,1)} %param.14) | copy-start | bytes 49156
  2.1 0.7 %copy-start.2 = (bf16[256,32]{0,1:T(8,128)(2,1)S(1)}, bf16[256,32]{0,1:T(8,128)(2,1)}, u32[]{:S(2)}) copy-start(bf16[256,32]{0,1:T(8,128)(2,1)} %param.16) | copy-start | bytes 49156
  2.9 0.7 copy-start.3
  3.5 0.7 copy-start.4
  4.2 0.7 copy-start.5
  4.9 0.7 copy-start.6
  9.1 3.2 %collective-permute-start = (bf16[1,6,32,128]{3,2,1,0:T(8,128)(2,1)S(1)}, bf16[1,6,32,128]{3,2,1,0:T(8,128)(2,1)S(1)}, u32[]{:S(2)}, u32[]{:S(2)}) collective-permute-start(bf16[1,6,32,128]{3,2,1,0:T(8,128)(2,1)S(1)} %get-tuple-element.24), channel_id=1, source_target_pairs={{0,1},{1,0},{2,3},{3,2},{4,5},{5,4},{6,7},{7,6},{8,9},{9,8},{10,11... | collective-permute-start | bytes 147464 | tf_op jit(solution)/shard_map/ppermute | solution.py:252
  9.6 7.1 %collective-permute-start.5 = (bf16[1,6,32,128]{3,2,1,0:T(8,128)(2,1)S(1)}, bf16[1,6,32,128]{3,2,1,0:T(8,128)(2,1)S(1)}, u32[]{:S(2)}, u32[]{:S(2)}) collective-permute-start(bf16[1,6,32,128]{3,2,1,0:T(8,128)(2,1)S(1)} %get-tuple-element.31), channel_id=1, source_target_pairs={{0,2},{1,3},{2,0},{3,1},{4,6},{5,7},{6,4},{7,5},{8,10},{9,11},{10,... | collective-permute-start | bytes 147464 | tf_op jit(solution)/shard_map/ppermute | solution.py:252
  12.2 4.5 %collective-permute-start.6 = (bf16[1,6,32,128]{3,2,1,0:T(8,128)(2,1)S(1)}, bf16[1,6,32,128]{3,2,1,0:T(8,128)(2,1)S(1)}, u32[]{:S(2)}, u32[]{:S(2)}) collective-permute-start(bf16[1,6,32,128]{3,2,1,0:T(8,128)(2,1)S(1)} %get-tuple-element.32), channel_id=1, source_target_pairs={{0,3},{1,2},{2,1},{3,0},{4,7},{5,6},{6,5},{7,4},{8,11},{9,10},{10,... | collective-permute-start | bytes 147464 | tf_op jit(solution)/shard_map/ppermute | solution.py:252
  12.3 5.4 %collective-permute-start.1 = (bf16[6,32,128]{2,1,0:T(8,128)(2,1)S(1)}, bf16[6,32,128]{2,1,0:T(8,128)(2,1)S(1)}, u32[]{:S(2)}, u32[]{:S(2)}) collective-permute-start(bf16[6,32,128]{2,1,0:T(8,128)(2,1)S(1)} %get-tuple-element.26), channel_id=1, source_target_pairs={{0,4},{1,5},{2,6},{3,7},{4,0},{5,1},{6,2},{7,3},{8,12},{9,13},{10,... | collective-permute-start | bytes 147464 | tf_op jit(solution)/shard_map/ppermute | solution.py:252
  14.1 6.1 %collective-permute-start.2 = (bf16[6,32,128]{2,1,0:T(8,128)(2,1)S(1)}, bf16[6,32,128]{2,1,0:T(8,128)(2,1)S(1)}, u32[]{:S(2)}, u32[]{:S(2)}) collective-permute-start(bf16[6,32,128]{2,1,0:T(8,128)(2,1)S(1)} %get-tuple-element.27), channel_id=1, source_target_pairs={{0,8},{1,9},{2,10},{3,11},{4,12},{5,13},{6,14},{7,15},{8,0},{9,1},... | collective-permute-start | bytes 147464 | tf_op jit(solution)/shard_map/ppermute | solution.py:252
  16.7 6.4 %collective-permute-start.3 = (bf16[6,32,128]{2,1,0:T(8,128)(2,1)S(1)}, bf16[6,32,128]{2,1,0:T(8,128)(2,1)S(1)}, u32[]{:S(2)}, u32[]{:S(2)}) collective-permute-start(bf16[6,32,128]{2,1,0:T(8,128)(2,1)S(1)} %get-tuple-element.28), channel_id=1, source_target_pairs={{0,12},{1,13},{2,14},{3,15},{4,8},{5,9},{6,10},{7,11},{8,4},{9,5},... | collective-permute-start | bytes 147464 | tf_op jit(solution)/shard_map/ppermute | solution.py:252
  16.7 12.2 %collective-permute-start.7 = (bf16[24,32,128]{2,1,0:T(8,128)(2,1)S(1)}, bf16[24,32,128]{2,1,0:T(8,128)(2,1)S(1)}, u32[]{:S(2)}, u32[]{:S(2)}) collective-permute-start(bf16[24,32,128]{2,1,0:T(8,128)(2,1)S(1)} %pad_maximum_fusion.1.refs_2_), channel_id=1, source_target_pairs={{0,4},{1,5},{2,6},{3,7},{4,0},{5,1},{6,2},{7,3},{8,12},{9,13},{10,... | collective-permute-start | bytes 589832 | tf_op jit(solution)/shard_map/ppermute | solution.py:252
  23.1 5.7 %collective-permute-start.4 = (bf16[24,32,128]{2,1,0:T(8,128)(2,1)S(1)}, bf16[24,32,128]{2,1,0:T(8,128)(2,1)S(1)}, u32[]{:S(2)}, u32[]{:S(2)}) collective-permute-start(bf16[24,32,128]{2,1,0:T(8,128)(2,1)S(1)} %pad_maximum_fusion), channel_id=1, source_target_pairs={{0,2},{1,3},{2,0},{3,1},{4,6},{5,7},{6,4},{7,5},{8,10},{9,11},{10,... | collective-permute-start | bytes 589832 | tf_op jit(solution)/shard_map/ppermute | solution.py:252
  28.9 18.7 %collective-permute-start.8 = (bf16[48,32,128]{2,1,0:T(8,128)(2,1)S(1)}, bf16[48,32,128]{2,1,0:T(8,128)(2,1)S(1)}, u32[]{:S(2)}, u32[]{:S(2)}) collective-permute-start(bf16[48,32,128]{2,1,0:T(8,128)(2,1)S(1)} %constant_dynamic-update-slice_fusion.refs_0_), channel_id=1, source_target_pairs={{0,1},{1,0},{2,3},{3,2},{4,5},{5,4},{6,7},{7,6},{8,9},{9,8},{10,11... | collective-permute-start | bytes 1179656 | tf_op jit(solution)/shard_map/ppermute | solution.py:252
  29.0 9.7 %collective-permute-start.10 = (bf16[24,32,128]{2,1,0:T(8,128)(2,1)S(1)}, bf16[24,32,128]{2,1,0:T(8,128)(2,1)S(1)}, u32[]{:S(2)}, u32[]{:S(2)}) collective-permute-start(bf16[24,32,128]{2,1,0:T(8,128)(2,1)S(1)} %pad_maximum_fusion.1.refs_2_), channel_id=1, source_target_pairs={{0,12},{1,13},{2,14},{3,15},{4,8},{5,9},{6,10},{7,11},{8,4},{9,5},... | collective-permute-start | bytes 589832 | tf_op jit(solution)/shard_map/ppermute | solution.py:252
  30.1 17.6 %collective-permute-start.9 = (bf16[24,32,128]{2,1,0:T(8,128)(2,1)S(1)}, bf16[24,32,128]{2,1,0:T(8,128)(2,1)S(1)}, u32[]{:S(2)}, u32[]{:S(2)}) collective-permute-start(bf16[24,32,128]{2,1,0:T(8,128)(2,1)S(1)} %pad_maximum_fusion.1.refs_2_), channel_id=1, source_target_pairs={{0,8},{1,9},{2,10},{3,11},{4,12},{5,13},{6,14},{7,15},{8,0},{9,1},... | collective-permute-start | bytes 589832 | tf_op jit(solution)/shard_map/ppermute | solution.py:252
  47.6 2.2 %copy-start.7 = (bf16[1,128,128,128]{3,2,1,0:T(8,128)(2,1)S(1)}, bf16[1,128,128,128]{3,2,1,0:T(8,128)(2,1)}, u32[]{:S(2)}) copy-start(bf16[1,128,128,128]{3,2,1,0:T(8,128)(2,1)} %param.11) | copy-start | bytes 12582916

commit v6 on v5

--- a/solution.py
+++ b/solution.py
@@ -9,8 +9,12 @@
 from jax.sharding import PartitionSpec as P
 
 LANES = 128
-PARTS = 1
+PARTS = 2
 MIB = 1024 * 1024
+
+
+def in_hbm(x):
+    return pltpu.with_memory_space_constraint(x, pltpu.HBM)
 
 
 def project_kernel(side, *refs):
@@ -78,7 +82,7 @@
     width = wl.shape[1]
     tile = residues // side
     rows = tile * width // LANES
-    operands = (x, gain[None], offset[None], wl.T, bl[None], wr.T, br[None])
+    operands = [in_hbm(o) for o in (x, gain[None], offset[None], wl.T, bl[None], wr.T, br[None])]
     out = pl.pallas_call(
         functools.partial(project_kernel, side),
         in_specs=[pl.BlockSpec(memory_space=pltpu.HBM)] * len(operands),
@@ -180,7 +184,7 @@
     width = lanes // pack
     halves = pack // 2
     depth = -(-side * side * seqs // LANES) * LANES
-    group = 4
+    group = 8
     first, last = part == 0, part == PARTS - 1
     whole = lambda shape: pl.BlockSpec(shape, lambda g: (0,) * len(shape))
     sum_spec = pl.BlockSpec((group, halves, chans, 2 * tile), lambda g: (g, 0, 0, 0))
@@ -192,7 +196,7 @@
         operands.append(before)
         specs.append(sum_spec)
     if last:
-        operands += [bias[None], pair.reshape(pack, rows, tile, chans)]
+        operands += [in_hbm(bias[None]), in_hbm(pair.reshape(pack, rows, tile, chans))]
         specs += [whole((1, chans)), pair_spec]
         out_shape, out_spec = jax.ShapeDtypeStruct((pack, rows, tile, chans), jnp.bfloat16), pair_spec
     else:
@@ -257,8 +261,6 @@
     parts = []
     for part in range(PARTS):
         mine = jnp.concatenate([x[part] for x in right])
-        if part > 0:
-            mine, left = lax.optimization_barrier((mine, left))
         parts.append([mine] + [swap(mine, d, 0) for d in range(1, side)])
     order = [0]
     lefts = [left]
@@ -266,7 +268,7 @@
     while step > 0:
         left = jnp.concatenate(lefts) if len(lefts) > 1 else lefts[0]
         if len(lefts) > 1:
-            left, parts[0][1] = lax.optimization_barrier((left, parts[0][1]))
+            left, *parts[0] = lax.optimization_barrier((left, *parts[0]))
         lefts = [left, swap(left, 0, step)]
         order += [o ^ step for o in order]
         step //= 2

time: 69.6 us -> 60.9 us (0.88)
  waiting for transfers between devices: 25.9 us -> 13.6 us
  starting transfers between devices: 11.3 us -> 19.4 us
  local copies, waits for them, and re-layouts: 8.98 us -> 1.28 us
  Pallas kernels: 23 us -> 26.3 us
    ppermute x11 -> x14, waiting for transfers between devices: 25.9 us -> 13.6 us  [swap(): lax.ppermute(x, 'row', [(i, i ^ da * side + db) for i in range(devices)])]
    ppermute x11 -> x14, starting transfers between devices: 11.3 us -> 19.4 us  [swap(): lax.ppermute(x, 'row', [(i, i ^ da * side + db) for i in range(devices)])]
    unnamed x22 -> x4, local copies, waits for them, and re-layouts: 7.75 us -> 0.04 us
    pallas_call x1 -> x2, Pallas kernels: 19.4 us -> 21.8 us  [update_part(): pl.pallas_call(functools.partial(update_kernel, side, seqs, order, len(le...]
    pallas_call x1, Pallas kernels: 3.57 us -> 4.52 us  [project(): pl.pallas_call(functools.partial(project_kernel, side), in_specs=[pl.Bloc...]
  transfers between devices with their start and end apart: 11 -> 14, of which waited for: 5 -> 5; matrix products, arithmetic and copies ran while one was open for 2% -> 2% of each run, Pallas kernels for 0% -> 16%
where the time goes in v6:
time: 60.9 us; the launch traced here: 60.7 us
  Pallas kernels  26.3 us (43%)
  starting transfers between devices  19.4 us (32%)
  waiting for transfers between devices  13.6 us (22%)
  local copies, waits for them, and re-layouts  1.28 us (2%)
    pallas_call x2, Pallas kernels, update_part(): pl.pallas_call(functools.partial(update_kernel, side, seqs, order, len(le...  21.8 us
    ppermute x14, starting transfers between devices, swap(): lax.ppermute(x, 'row', [(i, i ^ da * side + db) for i in range(devices)])  19.4 us
    ppermute x14, waiting for transfers between devices, swap(): lax.ppermute(x, 'row', [(i, i ^ da * side + db) for i in range(devices)])  13.6 us
    pallas_call x1, Pallas kernels, project(): pl.pallas_call(functools.partial(project_kernel, side), in_specs=[pl.Bloc...  4.52 us
  transfers between devices with their start and end apart: 14, of which 5 were waited for; matrix products, arithmetic and copies ran while one was open for 2% of the time, Pallas kernels for 16%

profile of v6, /device:TPU:0, one launch (start us, length us, event | category | flops | bytes accessed | tf_op | source)
XLA Modules:
  0.0 60.7 jit_solution(4109608790710458525)
XLA Ops:
  0.0 4.5 %project.1 = (bf16[6,32,128]{2,1,0:T(8,128)(2,1)S(1)}, bf16[6,32,128]{2,1,0:T(8,128)(2,1)S(1)}, bf16[6,32,128]{2,1,0:T(8,128)(2,1)S(1)}, bf16[6,32,128]{2,1,0:T(...) custom-call(bf16[6,512,256]{2,1,0:T(8,128)(2,1)} %refs_0_.1, ...), custom_call_target="tpu_custom_call" | custom-call | tf_op jit(solution)/shard_map/project/pallas_call | solution.py:86
  4.5 0.5 collective-permute-start
  5.0 2.6 %collective-permute-start.5 = (bf16[2,6,16,128]{3,2,1,0:T(8,128)(2,1)S(1)}, bf16[2,6,16,128]{3,2,1,0:T(8,128)(2,1)S(1)}, u32[]{:S(2)}, u32[]{:S(2)}) collective-permute-start(bf16[2,6,16,128]{3,2,1,0:T(8,128)(2,1)S(1)} %get-tuple-element.34), channel_id=1, source_target_pairs={{0,2},{1,3},{2,0},{3,1},{4,6},{5,7},{6,4},{7,5},{8,10},{9,11},{10,... | collective-permute-start | bytes 147464 | tf_op jit(solution)/shard_map/ppermute | solution.py:256
  7.6 0.1 collective-permute-start.6
  7.7 0.0 collective-permute-done
  7.7 2.2 %collective-permute-done.5 = bf16[2,6,16,128]{3,2,1,0:T(8,128)(2,1)S(1)} collective-permute-done((bf16[2,6,16,128]{3,2,1,0:T(8,128)(2,1)S(1)}, bf16[2,6,16,128]{3,2,1,0:T(8,128)(2,1)S(1)}, u32[]{:S(2)}, u32[]{:S(2)}) %collective-permute-start.5) | collective-permute-done | bytes 49184 | tf_op jit(solution)/shard_map/ppermute | solution.py:256
  10.0 1.4 %collective-permute-done.6 = bf16[2,6,16,128]{3,2,1,0:T(8,128)(2,1)S(1)} collective-permute-done((bf16[2,6,16,128]{3,2,1,0:T(8,128)(2,1)S(1)}, bf16[2,6,16,128]{3,2,1,0:T(8,128)(2,1)S(1)}, u32[]{:S(2)}, u32[]{:S(2)}) %collective-permute-start.6) | collective-permute-done | bytes 49184 | tf_op jit(solution)/shard_map/ppermute | solution.py:256
  11.4 3.7 %collective-permute-start.9 = (bf16[24,16,128]{2,1,0:T(8,128)(2,1)S(1)}, bf16[24,16,128]{2,1,0:T(8,128)(2,1)S(1)}, u32[]{:S(2)}, u32[]{:S(2)}) collective-permute-start(bf16[24,16,128]{2,1,0:T(8,128)(2,1)S(1)} %pad_maximum_fusion.1.refs_2_), channel_id=1, source_target_pairs={{0,12},{1,13},{2,14},{3,15},{4,8},{5,9},{6,10},{7,11},{8,4},{9,5},... | collective-permute-start | bytes 294920 | tf_op jit(solution)/shard_map/ppermute | solution.py:256
  15.0 0.0 collective-permute-start.8
  15.0 0.8 %collective-permute-start.1 = (bf16[6,32,128]{2,1,0:T(8,128)(2,1)S(1)}, bf16[6,32,128]{2,1,0:T(8,128)(2,1)S(1)}, u32[]{:S(2)}, u32[]{:S(2)}) collective-permute-start(bf16[6,32,128]{2,1,0:T(8,128)(2,1)S(1)} %get-tuple-element.29), channel_id=1, source_target_pairs={{0,4},{1,5},{2,6},{3,7},{4,0},{5,1},{6,2},{7,3},{8,12},{9,13},{10,... | collective-permute-start | bytes 147464 | tf_op jit(solution)/shard_map/ppermute | solution.py:256
  15.8 2.1 %collective-permute-start.2 = (bf16[6,32,128]{2,1,0:T(8,128)(2,1)S(1)}, bf16[6,32,128]{2,1,0:T(8,128)(2,1)S(1)}, u32[]{:S(2)}, u32[]{:S(2)}) collective-permute-start(bf16[6,32,128]{2,1,0:T(8,128)(2,1)S(1)} %get-tuple-element.30), channel_id=1, source_target_pairs={{0,8},{1,9},{2,10},{3,11},{4,12},{5,13},{6,14},{7,15},{8,0},{9,1},... | collective-permute-start | bytes 147464 | tf_op jit(solution)/shard_map/ppermute | solution.py:256
  18.0 1.5 %collective-permute-start.3 = (bf16[6,32,128]{2,1,0:T(8,128)(2,1)S(1)}, bf16[6,32,128]{2,1,0:T(8,128)(2,1)S(1)}, u32[]{:S(2)}, u32[]{:S(2)}) collective-permute-start(bf16[6,32,128]{2,1,0:T(8,128)(2,1)S(1)} %get-tuple-element.31), channel_id=1, source_target_pairs={{0,12},{1,13},{2,14},{3,15},{4,8},{5,9},{6,10},{7,11},{8,4},{9,5},... | collective-permute-start | bytes 147464 | tf_op jit(solution)/shard_map/ppermute | solution.py:256
  19.4 2.0 %collective-permute-done.1 = bf16[6,32,128]{2,1,0:T(8,128)(2,1)S(1)} collective-permute-done((bf16[6,32,128]{2,1,0:T(8,128)(2,1)S(1)}, bf16[6,32,128]{2,1,0:T(8,128)(2,1)S(1)}, u32[]{:S(2)}, u32[]{:S(2)}) %collective-permute-start.1) | collective-permute-done | bytes 49184 | tf_op jit(solution)/shard_map/ppermute | solution.py:256
  21.4 2.5 %collective-permute-start.7 = (bf16[24,16,128]{2,1,0:T(8,128)(2,1)S(1)}, bf16[24,16,128]{2,1,0:T(8,128)(2,1)S(1)}, u32[]{:S(2)}, u32[]{:S(2)}) collective-permute-start(bf16[24,16,128]{2,1,0:T(8,128)(2,1)S(1)} %pad_maximum_fusion.1.refs_2_), channel_id=1, source_target_pairs={{0,4},{1,5},{2,6},{3,7},{4,0},{5,1},{6,2},{7,3},{8,12},{9,13},{10,... | collective-permute-start | bytes 294920 | tf_op jit(solution)/shard_map/ppermute | solution.py:256
  23.9 3.5 %collective-permute-done.2 = bf16[6,32,128]{2,1,0:T(8,128)(2,1)S(1)} collective-permute-done((bf16[6,32,128]{2,1,0:T(8,128)(2,1)S(1)}, bf16[6,32,128]{2,1,0:T(8,128)(2,1)S(1)}, u32[]{:S(2)}, u32[]{:S(2)}) %collective-permute-start.2) | collective-permute-done | bytes 49184 | tf_op jit(solution)/shard_map/ppermute | solution.py:256
  27.3 0.0 collective-permute-done.3
  27.4 1.1 %collective-permute-start.4 = (bf16[24,32,128]{2,1,0:T(8,128)(2,1)S(1)}, bf16[24,32,128]{2,1,0:T(8,128)(2,1)S(1)}, u32[]{:S(2)}, u32[]{:S(2)}) collective-permute-start(bf16[24,32,128]{2,1,0:T(8,128)(2,1)S(1)} %pad_maximum_fusion), channel_id=1, source_target_pairs={{0,2},{1,3},{2,0},{3,1},{4,6},{5,7},{6,4},{7,5},{8,10},{9,11},{10,... | collective-permute-start | bytes 589832 | tf_op jit(solution)/shard_map/ppermute | solution.py:256
  28.6 4.5 %collective-permute-done.4 = bf16[24,32,128]{2,1,0:T(8,128)(2,1)S(1)} collective-permute-done((bf16[24,32,128]{2,1,0:T(8,128)(2,1)S(1)}, bf16[24,32,128]{2,1,0:T(8,128)(2,1)S(1)}, u32[]{:S(2)}, u32[]{:S(2)}) %collective-permute-start.4) | collective-permute-done | bytes 196640 | tf_op jit(solution)/shard_map/ppermute | solution.py:256
  33.1 0.0 collective-permute-done.9.refs_5_
  33.2 0.0 collective-permute-done.8.refs_4_
  33.2 0.0 collective-permute-done.7.refs_3_
  33.2 0.1 collective-permute-start.10
  33.3 1.1 %copy.14 = bf16[128,32,32]{0,2,1:T(8,128)(2,1)S(1)} copy(bf16[128,32,32]{0,1,2:T(8,128)(2,1)} %bitcast.31) | data formatting | bytes 524288 | tf_op jit(solution)/shard_map/transpose | solution.py:275
  34.3 0.1 copy.16.refs_6_
  34.5 2.5 %collective-permute-start.13 = (bf16[24,16,128]{2,1,0:T(8,128)(2,1)S(1)}, bf16[24,16,128]{2,1,0:T(8,128)(2,1)S(1)}, u32[]{:S(2)}, u32[]{:S(2)}) collective-permute-start(bf16[24,16,128]{2,1,0:T(8,128)(2,1)S(1)} %pad_maximum_fusion.2.refs_2_), channel_id=1, source_target_pairs={{0,12},{1,13},{2,14},{3,15},{4,8},{5,9},{6,10},{7,11},{8,4},{9,5},... | collective-permute-start | bytes 294920 | tf_op jit(solution)/shard_map/ppermute | solution.py:256
  37.0 0.5 collective-permute-start.12
  37.5 1.4 %collective-permute-start.11 = (bf16[24,16,128]{2,1,0:T(8,128)(2,1)S(1)}, bf16[24,16,128]{2,1,0:T(8,128)(2,1)S(1)}, u32[]{:S(2)}, u32[]{:S(2)}) collective-permute-start(bf16[24,16,128]{2,1,0:T(8,128)(2,1)S(1)} %pad_maximum_fusion.2.refs_2_), channel_id=1, source_target_pairs={{0,4},{1,5},{2,6},{3,7},{4,0},{5,1},{6,2},{7,3},{8,12},{9,13},{10,... | collective-permute-start | bytes 294920 | tf_op jit(solution)/shard_map/ppermute | solution.py:256
  38.9 0.0 collective-permute-done.10.refs_1_
  38.9 9.8 %update_0.1.refs_7_ = f32[32,2,128,256]{3,2,1,0:T(8,128)} custom-call(bf16[48,32,128]{2,1,0:T(8,128)(2,1)S(1)} %constant_dynamic-update-slice_fusion.refs_0_, bf16[48,32,128]{2,1,0:T(8,128)(2,1)S(1)} %collective-permute-done.10.refs_1_, bf16[24,16,128]{2,1,0:T(8,128)(2,1)S(1)} %pad_maximum_fusion.1.refs_2_, ...), custom_call_target="tpu_custom_call" | custom-call | flops 3758096384 | bytes 16777216 | tf_op jit(solution)/shard_map/update_0/pallas_call | solution.py:205
  48.7 0.0 collective-permute-done.13.refs_5_
  48.7 0.0 collective-permute-done.12.refs_4_
  48.8 0.0 collective-permute-done.11.refs_3_
  48.8 12.0 %update_1.1 = bf16[4,32,128,128]{3,2,1,0:T(8,128)(2,1)} custom-call(bf16[48,32,128]{2,1,0:T(8,128)(2,1)S(1)} %constant_dynamic-update-slice_fusion.refs_0_, bf16[48,32,128]{2,1,0:T(8,128)(2,1)S(1)} %collective-permute-done.10.refs_1_, bf16[24,16,128]{2,1,0:T(8,128)(2,1)S(1)} %pad_maximum_fusion.2.refs_2_, ...), custom_call_target="tpu_custom_call" | custom-call | flops 3758096384 | bytes 16777216 | tf_op jit(solution)/shard_map/update_1/pallas_call | solution.py:205
  (12 shorter events, 0.1 us)
Async XLA Ops:
  4.5 3.2 %collective-permute-start = (bf16[2,6,16,128]{3,2,1,0:T(8,128)(2,1)S(1)}, bf16[2,6,16,128]{3,2,1,0:T(8,128)(2,1)S(1)}, u32[]{:S(2)}, u32[]{:S(2)}) collective-permute-start(bf16[2,6,16,128]{3,2,1,0:T(8,128)(2,1)S(1)} %get-tuple-element.27), channel_id=1, source_target_pairs={{0,1},{1,0},{2,3},{3,2},{4,5},{5,4},{6,7},{7,6},{8,9},{9,8},{10,11... | collective-permute-start | bytes 147464 | tf_op jit(solution)/shard_map/ppermute | solution.py:256
  5.0 4.9 %collective-permute-start.5 = (bf16[2,6,16,128]{3,2,1,0:T(8,128)(2,1)S(1)}, bf16[2,6,16,128]{3,2,1,0:T(8,128)(2,1)S(1)}, u32[]{:S(2)}, u32[]{:S(2)}) collective-permute-start(bf16[2,6,16,128]{3,2,1,0:T(8,128)(2,1)S(1)} %get-tuple-element.34), channel_id=1, source_target_pairs={{0,2},{1,3},{2,0},{3,1},{4,6},{5,7},{6,4},{7,5},{8,10},{9,11},{10,... | collective-permute-start | bytes 147464 | tf_op jit(solution)/shard_map/ppermute | solution.py:256
  7.6 3.7 %collective-permute-start.6 = (bf16[2,6,16,128]{3,2,1,0:T(8,128)(2,1)S(1)}, bf16[2,6,16,128]{3,2,1,0:T(8,128)(2,1)S(1)}, u32[]{:S(2)}, u32[]{:S(2)}) collective-permute-start(bf16[2,6,16,128]{3,2,1,0:T(8,128)(2,1)S(1)} %get-tuple-element.35), channel_id=1, source_target_pairs={{0,3},{1,2},{2,1},{3,0},{4,7},{5,6},{6,5},{7,4},{8,11},{9,10},{10,... | collective-permute-start | bytes 147464 | tf_op jit(solution)/shard_map/ppermute | solution.py:256
  11.4 21.8 %collective-permute-start.9 = (bf16[24,16,128]{2,1,0:T(8,128)(2,1)S(1)}, bf16[24,16,128]{2,1,0:T(8,128)(2,1)S(1)}, u32[]{:S(2)}, u32[]{:S(2)}) collective-permute-start(bf16[24,16,128]{2,1,0:T(8,128)(2,1)S(1)} %pad_maximum_fusion.1.refs_2_), channel_id=1, source_target_pairs={{0,12},{1,13},{2,14},{3,15},{4,8},{5,9},{6,10},{7,11},{8,4},{9,5},... | collective-permute-start | bytes 294920 | tf_op jit(solution)/shard_map/ppermute | solution.py:256
  15.0 18.1 %collective-permute-start.8 = (bf16[24,16,128]{2,1,0:T(8,128)(2,1)S(1)}, bf16[24,16,128]{2,1,0:T(8,128)(2,1)S(1)}, u32[]{:S(2)}, u32[]{:S(2)}) collective-permute-start(bf16[24,16,128]{2,1,0:T(8,128)(2,1)S(1)} %pad_maximum_fusion.1.refs_2_), channel_id=1, source_target_pairs={{0,8},{1,9},{2,10},{3,11},{4,12},{5,13},{6,14},{7,15},{8,0},{9,1},... | collective-permute-start | bytes 294920 | tf_op jit(solution)/shard_map/ppermute | solution.py:256
  15.0 6.4 %collective-permute-start.1 = (bf16[6,32,128]{2,1,0:T(8,128)(2,1)S(1)}, bf16[6,32,128]{2,1,0:T(8,128)(2,1)S(1)}, u32[]{:S(2)}, u32[]{:S(2)}) collective-permute-start(bf16[6,32,128]{2,1,0:T(8,128)(2,1)S(1)} %get-tuple-element.29), channel_id=1, source_target_pairs={{0,4},{1,5},{2,6},{3,7},{4,0},{5,1},{6,2},{7,3},{8,12},{9,13},{10,... | collective-permute-start | bytes 147464 | tf_op jit(solution)/shard_map/ppermute | solution.py:256
  15.8 11.5 %collective-permute-start.2 = (bf16[6,32,128]{2,1,0:T(8,128)(2,1)S(1)}, bf16[6,32,128]{2,1,0:T(8,128)(2,1)S(1)}, u32[]{:S(2)}, u32[]{:S(2)}) collective-permute-start(bf16[6,32,128]{2,1,0:T(8,128)(2,1)S(1)} %get-tuple-element.30), channel_id=1, source_target_pairs={{0,8},{1,9},{2,10},{3,11},{4,12},{5,13},{6,14},{7,15},{8,0},{9,1},... | collective-permute-start | bytes 147464 | tf_op jit(solution)/shard_map/ppermute | solution.py:256
  18.0 9.4 %collective-permute-start.3 = (bf16[6,32,128]{2,1,0:T(8,128)(2,1)S(1)}, bf16[6,32,128]{2,1,0:T(8,128)(2,1)S(1)}, u32[]{:S(2)}, u32[]{:S(2)}) collective-permute-start(bf16[6,32,128]{2,1,0:T(8,128)(2,1)S(1)} %get-tuple-element.31), channel_id=1, source_target_pairs={{0,12},{1,13},{2,14},{3,15},{4,8},{5,9},{6,10},{7,11},{8,4},{9,5},... | collective-permute-start | bytes 147464 | tf_op jit(solution)/shard_map/ppermute | solution.py:256
  21.4 11.8 %collective-permute-start.7 = (bf16[24,16,128]{2,1,0:T(8,128)(2,1)S(1)}, bf16[24,16,128]{2,1,0:T(8,128)(2,1)S(1)}, u32[]{:S(2)}, u32[]{:S(2)}) collective-permute-start(bf16[24,16,128]{2,1,0:T(8,128)(2,1)S(1)} %pad_maximum_fusion.1.refs_2_), channel_id=1, source_target_pairs={{0,4},{1,5},{2,6},{3,7},{4,0},{5,1},{6,2},{7,3},{8,12},{9,13},{10,... | collective-permute-start | bytes 294920 | tf_op jit(solution)/shard_map/ppermute | solution.py:256
  27.4 5.7 %collective-permute-start.4 = (bf16[24,32,128]{2,1,0:T(8,128)(2,1)S(1)}, bf16[24,32,128]{2,1,0:T(8,128)(2,1)S(1)}, u32[]{:S(2)}, u32[]{:S(2)}) collective-permute-start(bf16[24,32,128]{2,1,0:T(8,128)(2,1)S(1)} %pad_maximum_fusion), channel_id=1, source_target_pairs={{0,2},{1,3},{2,0},{3,1},{4,6},{5,7},{6,4},{7,5},{8,10},{9,11},{10,... | collective-permute-start | bytes 589832 | tf_op jit(solution)/shard_map/ppermute | solution.py:256
  33.2 5.8 %collective-permute-start.10 = (bf16[48,32,128]{2,1,0:T(8,128)(2,1)S(1)}, bf16[48,32,128]{2,1,0:T(8,128)(2,1)S(1)}, u32[]{:S(2)}, u32[]{:S(2)}) collective-permute-start(bf16[48,32,128]{2,1,0:T(8,128)(2,1)S(1)} %constant_dynamic-update-slice_fusion.refs_0_), channel_id=1, source_target_pairs={{0,1},{1,0},{2,3},{3,2},{4,5},{5,4},{6,7},{7,6},{8,9},{9,8},{10,11... | collective-permute-start | bytes 1179656 | tf_op jit(solution)/shard_map/ppermute | solution.py:256
  34.5 14.3 %collective-permute-start.13 = (bf16[24,16,128]{2,1,0:T(8,128)(2,1)S(1)}, bf16[24,16,128]{2,1,0:T(8,128)(2,1)S(1)}, u32[]{:S(2)}, u32[]{:S(2)}) collective-permute-start(bf16[24,16,128]{2,1,0:T(8,128)(2,1)S(1)} %pad_maximum_fusion.2.refs_2_), channel_id=1, source_target_pairs={{0,12},{1,13},{2,14},{3,15},{4,8},{5,9},{6,10},{7,11},{8,4},{9,5},... | collective-permute-start | bytes 294920 | tf_op jit(solution)/shard_map/ppermute | solution.py:256
  37.0 11.7 %collective-permute-start.12 = (bf16[24,16,128]{2,1,0:T(8,128)(2,1)S(1)}, bf16[24,16,128]{2,1,0:T(8,128)(2,1)S(1)}, u32[]{:S(2)}, u32[]{:S(2)}) collective-permute-start(bf16[24,16,128]{2,1,0:T(8,128)(2,1)S(1)} %pad_maximum_fusion.2.refs_2_), channel_id=1, source_target_pairs={{0,8},{1,9},{2,10},{3,11},{4,12},{5,13},{6,14},{7,15},{8,0},{9,1},... | collective-permute-start | bytes 294920 | tf_op jit(solution)/shard_map/ppermute | solution.py:256
  37.5 11.2 %collective-permute-start.11 = (bf16[24,16,128]{2,1,0:T(8,128)(2,1)S(1)}, bf16[24,16,128]{2,1,0:T(8,128)(2,1)S(1)}, u32[]{:S(2)}, u32[]{:S(2)}) collective-permute-start(bf16[24,16,128]{2,1,0:T(8,128)(2,1)S(1)} %pad_maximum_fusion.2.refs_2_), channel_id=1, source_target_pairs={{0,4},{1,5},{2,6},{3,7},{4,0},{5,1},{6,2},{7,3},{8,12},{9,13},{10,... | collective-permute-start | bytes 294920 | tf_op jit(solution)/shard_map/ppermute | solution.py:256

commit v7 on v6

--- a/solution.py
+++ b/solution.py
@@ -19,7 +19,7 @@
 
 def project_kernel(side, *refs):
     sources, refs = refs[:7], refs[7:]
-    left_out, right_out, refs = refs[:side], refs[side : 2 * side], refs[2 * side :]
+    left_out, right_out, refs = refs[:side], refs[side : side + PARTS], refs[side + PARTS :]
     buffers, normed_ref, sems, x_sems = refs[:7], refs[7], refs[8], refs[9]
     x_ref, gain_ref, offset_ref, wl_ref, bl_ref, wr_ref, br_ref = buffers
     seqs, residues, chans = x_ref.shape
@@ -27,6 +27,7 @@
     tile = residues // side
     pack = LANES // width
     rows = tile // pack
+    some = width // PARTS
     x_copies = [
         pltpu.make_async_copy(sources[0].at[s], x_ref.at[s], x_sems.at[s]) for s in range(seqs)
     ]
@@ -37,8 +38,7 @@
         copy.start()
     for copy in copies:
         copy.wait()
-    me = lax.axis_index("row")
-    place_a, place_b = me // side, lax.rem(me, side)
+    place_a = lax.axis_index("row") // side
     nt = (((1,), (1,)), ((), ()))
     wl = wl_ref[...]
     placed = [
@@ -56,14 +56,14 @@
         normed[...] = (
             center * lax.rsqrt(variance + 1e-05) * gain_ref[...] + offset_ref[...]
         ).astype(jnp.bfloat16)
+        right = lax.dot_general(wr_ref[...], normed[...], nt, preferred_element_type=jnp.float32)
+        for b in range(side):
+            block = (right[:, b * tile : (b + 1) * tile] + right_bias).astype(jnp.bfloat16)
+            for part in range(PARTS):
+                for a in range(side):
+                    right_out[part][a * side + b, s] = block[part * some : (part + 1) * some]
         blocks = []
         for d in range(side):
-            b = place_b ^ d
-            block = normed[pl.ds(pl.multiple_of(b * tile, tile), tile), :]
-            right = lax.dot_general(wr_ref[...], block, nt, preferred_element_type=jnp.float32)
-            right_out[d][:, s] = (
-                (right + right_bias).astype(jnp.bfloat16).reshape(PARTS, width // PARTS, tile)
-            )
             a = place_a ^ d
             blocks.append(normed[pl.ds(pl.multiple_of(a * tile, tile), tile), :])
         total = left_bias
@@ -86,9 +86,9 @@
     out = pl.pallas_call(
         functools.partial(project_kernel, side),
         in_specs=[pl.BlockSpec(memory_space=pltpu.HBM)] * len(operands),
-        out_specs=[pl.BlockSpec(memory_space=pltpu.VMEM)] * (2 * side),
+        out_specs=[pl.BlockSpec(memory_space=pltpu.VMEM)] * (side + PARTS),
         out_shape=[jax.ShapeDtypeStruct((seqs, rows, LANES), jnp.bfloat16)] * side
-        + [jax.ShapeDtypeStruct((PARTS, seqs, width // PARTS, tile), jnp.bfloat16)] * side,
+        + [jax.ShapeDtypeStruct((side * side, seqs, width // PARTS, tile), jnp.bfloat16)] * PARTS,
         scratch_shapes=[pltpu.VMEM(o.shape, o.dtype) for o in operands]
         + [
             pltpu.VMEM((2, residues, chans), jnp.bfloat16),
@@ -103,15 +103,14 @@
 
 def update_kernel(side, seqs, order, lefts, first, last, *refs):
     left_refs, refs = refs[:lefts], refs[lefts:]
-    right_refs, refs = refs[:side], refs[side:]
-    wt_ref, refs = refs[0], refs[1:]
+    right_ref, wt_ref, refs = refs[0], refs[1], refs[2:]
     if not first:
         before_ref, refs = refs[0], refs[1:]
     if last:
         bias_ref, pair_ref, refs = refs[0], refs[1], refs[2:]
     out_ref, left_wide, right_wide, right_flat, outer = refs
     _, rows, lanes = left_refs[0].shape
-    _, some, tile = right_refs[0].shape
+    _, _, some, tile = right_ref.shape
     depth = right_flat.shape[0]
     pack = tile // rows
     width = lanes // pack
@@ -122,19 +121,20 @@
 
     @pl.when(step == 0)
     def _():
-        at = 0
-        for ref in left_refs:
-            count = ref.shape[0] * rows
-            left_wide[at : at + count] = ref[...].astype(jnp.float32).reshape(count, lanes)
-            at += count
-        for dz in range(side):
-            for k, dy in enumerate(order):
-                to = (k * side + dz) * seqs
-                right_wide[to * some : (to + seqs) * some] = (
-                    right_refs[dz][dy * seqs : (dy + 1) * seqs]
-                    .astype(jnp.float32)
-                    .reshape(seqs * some, tile)
-                )
+        me = lax.axis_index("row")
+        place_a, place_b = me // side, lax.rem(me, side)
+        for k, db in enumerate(order):
+            ref = left_refs[k * lefts // side]
+            start = (k * side * seqs) % ref.shape[0]
+            for dz in range(side):
+                piece = ref[start + dz * seqs : start + (dz + 1) * seqs]
+                to = ((place_a ^ dz) * side + (place_b ^ db)) * (seqs * rows)
+                left_wide[pl.ds(pl.multiple_of(to, seqs * rows), seqs * rows)] = piece.astype(
+                    jnp.float32
+                ).reshape(seqs * rows, lanes)
+        right_wide[: seq_total * some] = (
+            right_ref[...].astype(jnp.float32).reshape(seq_total * some, tile)
+        )
         if depth > seq_total:
             left_wide[seq_total * rows :] = jnp.zeros(
                 ((depth - seq_total) * rows, lanes), jnp.float32
@@ -178,7 +178,7 @@
 
 def update_part(side, seqs, order, part, left, right, wt, before, bias, pair):
     _, rows, lanes = left[0].shape
-    _, some, tile = right[0].shape
+    _, _, some, tile = right.shape
     chans = wt.shape[0]
     pack = tile // rows
     width = lanes // pack
@@ -189,7 +189,7 @@
     whole = lambda shape: pl.BlockSpec(shape, lambda g: (0,) * len(shape))
     sum_spec = pl.BlockSpec((group, halves, chans, 2 * tile), lambda g: (g, 0, 0, 0))
     pair_spec = pl.BlockSpec((pack, group, tile, chans), lambda g: (0, g, 0, 0))
-    operands = list(left) + list(right) + [wt]
+    operands = list(left) + [right, wt]
     specs = [whole(x.shape) for x in operands[:-1]]
     specs.append(pl.BlockSpec((chans, some * width), lambda g: (0, part)))
     if not first:
@@ -255,20 +255,18 @@
     def swap(x, da, db):
         return lax.ppermute(x, "row", [(i, i ^ (da * side + db)) for i in range(devices)])
 
-    right = [right[0]] + [swap(right[d], 0, d) for d in range(1, side)]
-    *left, right[1] = lax.optimization_barrier((*left, right[1]))
     left = jnp.concatenate([left[0]] + [swap(left[d], d, 0) for d in range(1, side)])
     parts = []
     for part in range(PARTS):
-        mine = jnp.concatenate([x[part] for x in right])
-        parts.append([mine] + [swap(mine, d, 0) for d in range(1, side)])
+        mine = right[part]
+        if part > 0:
+            mine, left = lax.optimization_barrier((mine, left))
+        parts.append(lax.all_to_all(mine, "row", 0, 0, tiled=True))
     order = [0]
     lefts = [left]
     step = side // 2
     while step > 0:
         left = jnp.concatenate(lefts) if len(lefts) > 1 else lefts[0]
-        if len(lefts) > 1:
-            left, *parts[0] = lax.optimization_barrier((left, *parts[0]))
         lefts = [left, swap(left, 0, step)]
         order += [o ^ step for o in order]
         step //= 2

time: 60.9 us -> 63.8 us (1.048)
  waiting for transfers between devices: 13.6 us -> 18.2 us
  starting transfers between devices: 19.4 us -> 17.6 us
  local copies, waits for them, and re-layouts: 1.28 us -> 0.29 us
  Pallas kernels: 26.3 us -> 27.2 us
    ppermute x14 -> x5, starting transfers between devices: 19.4 us -> 6.05 us  [swap(): lax.ppermute(x, 'row', [(i, i ^ da * side + db) for i in range(devices)])]
    all_to_all x0 -> x2, starting transfers between devices: none -> 11.6 us  [local(): parts.append(lax.all_to_all(mine, 'row', 0, 0, tiled=True))]
    ppermute x14 -> x5, waiting for transfers between devices: 13.6 us -> 16.1 us  [swap(): lax.ppermute(x, 'row', [(i, i ^ da * side + db) for i in range(devices)])]
    all_to_all x0 -> x2, waiting for transfers between devices: none -> 2.1 us  [local(): parts.append(lax.all_to_all(mine, 'row', 0, 0, tiled=True))]
    transpose x1, local copies, waits for them, and re-layouts: 1.06 us -> 0.11 us  [local(): final_matrix.reshape(width, width, -1).transpose(2, 1, 0)]
    pallas_call x1, Pallas kernels: 4.52 us -> 5.43 us  [project(): pl.pallas_call(functools.partial(project_kernel, side), in_specs=[pl.Bloc...]
  transfers between devices with their start and end apart: 14 -> 7, of which waited for: 5 -> 4; matrix products, arithmetic and copies ran while one was open for 2% -> 1% of each run, Pallas kernels for 16% -> 15%
where the time goes in v7:
time: 63.8 us; the launch traced here: 63.4 us
  Pallas kernels  27.2 us (43%)
  waiting for transfers between devices  18.2 us (29%)
  starting transfers between devices  17.6 us (28%)
    pallas_call x2, Pallas kernels, update_part(): pl.pallas_call(functools.partial(update_kernel, side, seqs, order, len(le...  21.7 us
    ppermute x5, waiting for transfers between devices, swap(): lax.ppermute(x, 'row', [(i, i ^ da * side + db) for i in range(devices)])  16.1 us
    all_to_all x2, starting transfers between devices, local(): parts.append(lax.all_to_all(mine, 'row', 0, 0, tiled=True))  11.6 us
    ppermute x5, starting transfers between devices, swap(): lax.ppermute(x, 'row', [(i, i ^ da * side + db) for i in range(devices)])  6.05 us
    pallas_call x1, Pallas kernels, project(): pl.pallas_call(functools.partial(project_kernel, side), in_specs=[pl.Bloc...  5.43 us
    all_to_all x2, waiting for transfers between devices, local(): parts.append(lax.all_to_all(mine, 'row', 0, 0, tiled=True))  2.1 us
  transfers between devices with their start and end apart: 7, of which 4 were waited for; matrix products, arithmetic and copies ran while one was open for 1% of the time, Pallas kernels for 15%

profile of v7, /device:TPU:0, one launch (start us, length us, event | category | flops | bytes accessed | tf_op | source)
XLA Modules:
  0.0 63.4 jit_solution(16707994741836262933)
XLA Ops:
  0.0 0.0 copy-start
  0.0 5.4 %project.1 = (bf16[6,32,128]{2,1,0:T(8,128)(2,1)S(1)}, bf16[6,32,128]{2,1,0:T(8,128)(2,1)S(1)}, bf16[6,32,128]{2,1,0:T(8,128)(2,1)S(1)}, bf16[6,32,128]{2,1,0:T(...) custom-call(bf16[6,512,256]{2,1,0:T(8,128)(2,1)} %refs_0_.1, f32[1,256]{1,0:T(1,128)} %bitcast.18, ...), custom_call_target="tpu_custom_call" | custom-call | tf_op jit(solution)/shard_map/project/pallas_call | solution.py:86
  5.4 7.4 %all-to-all-start.1 = ((bf16[16,6,16,128]{3,2,1,0:T(8,128)(2,1)}), bf16[16,6,16,128]{3,2,1,0:T(8,128)(2,1)S(1)}, u32[]{:S(2)}, u32[]{:S(2)}) async-start(bf16[16,6,16,128]{3,2,1,0:T(8,128)(2,1)} %get-tuple-element.20), calls=%async_computation.1 | async-start | bytes 786432 | tf_op jit(solution)/shard_map/all_to_all | solution.py:264
  12.8 1.9 %collective-permute-start = (bf16[6,32,128]{2,1,0:T(8,128)(2,1)S(1)}, bf16[6,32,128]{2,1,0:T(8,128)(2,1)S(1)}, u32[]{:S(2)}, u32[]{:S(2)}) collective-permute-start(bf16[6,32,128]{2,1,0:T(8,128)(2,1)S(1)} %get-tuple-element.15), channel_id=1, source_target_pairs={{0,4},{1,5},{2,6},{3,7},{4,0},{5,1},{6,2},{7,3},{8,12},{9,13},{10,... | collective-permute-start | bytes 147464 | tf_op jit(solution)/shard_map/ppermute | solution.py:256
  14.8 2.4 %collective-permute-start.1 = (bf16[6,32,128]{2,1,0:T(8,128)(2,1)S(1)}, bf16[6,32,128]{2,1,0:T(8,128)(2,1)S(1)}, u32[]{:S(2)}, u32[]{:S(2)}) collective-permute-start(bf16[6,32,128]{2,1,0:T(8,128)(2,1)S(1)} %get-tuple-element.16), channel_id=1, source_target_pairs={{0,8},{1,9},{2,10},{3,11},{4,12},{5,13},{6,14},{7,15},{8,0},{9,1},... | collective-permute-start | bytes 147464 | tf_op jit(solution)/shard_map/ppermute | solution.py:256
  17.1 0.2 collective-permute-start.2
  17.3 5.1 %collective-permute-done = bf16[6,32,128]{2,1,0:T(8,128)(2,1)S(1)} collective-permute-done((bf16[6,32,128]{2,1,0:T(8,128)(2,1)S(1)}, bf16[6,32,128]{2,1,0:T(8,128)(2,1)S(1)}, u32[]{:S(2)}, u32[]{:S(2)}) %collective-permute-start) | collective-permute-done | bytes 49184 | tf_op jit(solution)/shard_map/ppermute | solution.py:256
  22.4 6.5 %collective-permute-done.1 = bf16[6,32,128]{2,1,0:T(8,128)(2,1)S(1)} collective-permute-done((bf16[6,32,128]{2,1,0:T(8,128)(2,1)S(1)}, bf16[6,32,128]{2,1,0:T(8,128)(2,1)S(1)}, u32[]{:S(2)}, u32[]{:S(2)}) %collective-permute-start.1) | collective-permute-done | bytes 49184 | tf_op jit(solution)/shard_map/ppermute | solution.py:256
  28.9 0.0 collective-permute-done.2
  29.0 1.5 %collective-permute-start.3 = (bf16[24,32,128]{2,1,0:T(8,128)(2,1)S(1)}, bf16[24,32,128]{2,1,0:T(8,128)(2,1)S(1)}, u32[]{:S(2)}, u32[]{:S(2)}) collective-permute-start(bf16[24,32,128]{2,1,0:T(8,128)(2,1)S(1)} %pad_maximum_fusion), channel_id=1, source_target_pairs={{0,2},{1,3},{2,0},{3,1},{4,6},{5,7},{6,4},{7,5},{8,10},{9,11},{10,... | collective-permute-start | bytes 589832 | tf_op jit(solution)/shard_map/ppermute | solution.py:256
  30.5 4.5 %collective-permute-done.3 = bf16[24,32,128]{2,1,0:T(8,128)(2,1)S(1)} collective-permute-done((bf16[24,32,128]{2,1,0:T(8,128)(2,1)S(1)}, bf16[24,32,128]{2,1,0:T(8,128)(2,1)S(1)}, u32[]{:S(2)}, u32[]{:S(2)}) %collective-permute-start.3) | collective-permute-done | bytes 196640 | tf_op jit(solution)/shard_map/ppermute | solution.py:256
  35.0 0.1 collective-permute-start.4
  35.1 0.0 all-to-all-done.1.refs_2_
  35.1 4.2 %all-to-all-start = ((bf16[16,6,16,128]{3,2,1,0:T(8,128)(2,1)}), bf16[16,6,16,128]{3,2,1,0:T(8,128)(2,1)S(1)}, u32[]{:S(2)}, u32[]{:S(2)}) async-start(bf16[16,6,16,128]{3,2,1,0:T(8,128)(2,1)} %get-tuple-element.19), calls=%async_computation | async-start | bytes 786432 | tf_op jit(solution)/shard_map/all_to_all | solution.py:264
  39.3 0.0 copy-done
  39.3 0.1 copy.14
  39.4 0.1 copy.16.refs_3_
  39.6 0.0 collective-permute-done.4.refs_1_
  39.6 9.8 %update_0.1.refs_4_ = f32[32,2,128,256]{3,2,1,0:T(8,128)} custom-call(bf16[48,32,128]{2,1,0:T(8,128)(2,1)S(1)} %constant_dynamic-update-slice_fusion.refs_0_, bf16[48,32,128]{2,1,0:T(8,128)(2,1)S(1)} %collective-permute-done.4.refs_1_, bf16[16,6,16,128]{3,2,1,0:T(8,128)(2,1)S(1)} %all-to-all-done.1.refs_2_, bf16[128,1024]{1,0:T(8,128)(2,1)S(1)} %copy.16.refs_3_), custom_call_target="tpu_custom_call" | custom-call | flops 3758096384 | bytes 16777216 | tf_op jit(solution)/shard_map/update_0/pallas_call | solution.py:205
  49.4 2.1 %all-to-all-done.refs_2_ = bf16[16,6,16,128]{3,2,1,0:T(8,128)(2,1)S(1)} async-done(((bf16[16,6,16,128]{3,2,1,0:T(8,128)(2,1)}), bf16[16,6,16,128]{3,2,1,0:T(8,128)(2,1)S(1)}, u32[]{:S(2)}, u32[]{:S(2)}) %all-to-all-start) | async-done | bytes 393248 | tf_op jit(solution)/shard_map/all_to_all | solution.py:264
  51.5 11.9 %update_1.1 = bf16[4,32,128,128]{3,2,1,0:T(8,128)(2,1)} custom-call(bf16[48,32,128]{2,1,0:T(8,128)(2,1)S(1)} %constant_dynamic-update-slice_fusion.refs_0_, bf16[48,32,128]{2,1,0:T(8,128)(2,1)S(1)} %collective-permute-done.4.refs_1_, bf16[16,6,16,128]{3,2,1,0:T(8,128)(2,1)S(1)} %all-to-all-done.refs_2_, bf16[128,1024]{1,0:T(8,128)(2,1)S(1)} %copy.16.refs_3_, ...), custom_call_target="tpu_custom_call" | custom-call | flops 3758096384 | bytes 16777216 | tf_op jit(solution)/shard_map/update_1/pallas_call | solution.py:205
  (3 shorter events, 0.1 us)
Async XLA Ops:
  0.0 39.3 %copy-start = (bf16[1024,128]{1,0:T(8,128)(2,1)S(1)}, bf16[1024,128]{1,0:T(8,128)(2,1)}, u32[]{:S(2)}) copy-start(bf16[1024,128]{1,0:T(8,128)(2,1)} %param.18) | copy-start | bytes 786436
  5.4 29.7 %all-to-all-start.1 = ((bf16[16,6,16,128]{3,2,1,0:T(8,128)(2,1)}), bf16[16,6,16,128]{3,2,1,0:T(8,128)(2,1)S(1)}, u32[]{:S(2)}, u32[]{:S(2)}) async-start(bf16[16,6,16,128]{3,2,1,0:T(8,128)(2,1)} %get-tuple-element.20), calls=%async_computation.1 | async-start | bytes 786432 | tf_op jit(solution)/shard_map/all_to_all | solution.py:264
  12.8 9.6 %collective-permute-start = (bf16[6,32,128]{2,1,0:T(8,128)(2,1)S(1)}, bf16[6,32,128]{2,1,0:T(8,128)(2,1)S(1)}, u32[]{:S(2)}, u32[]{:S(2)}) collective-permute-start(bf16[6,32,128]{2,1,0:T(8,128)(2,1)S(1)} %get-tuple-element.15), channel_id=1, source_target_pairs={{0,4},{1,5},{2,6},{3,7},{4,0},{5,1},{6,2},{7,3},{8,12},{9,13},{10,... | collective-permute-start | bytes 147464 | tf_op jit(solution)/shard_map/ppermute | solution.py:256
  14.8 14.2 %collective-permute-start.1 = (bf16[6,32,128]{2,1,0:T(8,128)(2,1)S(1)}, bf16[6,32,128]{2,1,0:T(8,128)(2,1)S(1)}, u32[]{:S(2)}, u32[]{:S(2)}) collective-permute-start(bf16[6,32,128]{2,1,0:T(8,128)(2,1)S(1)} %get-tuple-element.16), channel_id=1, source_target_pairs={{0,8},{1,9},{2,10},{3,11},{4,12},{5,13},{6,14},{7,15},{8,0},{9,1},... | collective-permute-start | bytes 147464 | tf_op jit(solution)/shard_map/ppermute | solution.py:256
  17.1 11.8 %collective-permute-start.2 = (bf16[6,32,128]{2,1,0:T(8,128)(2,1)S(1)}, bf16[6,32,128]{2,1,0:T(8,128)(2,1)S(1)}, u32[]{:S(2)}, u32[]{:S(2)}) collective-permute-start(bf16[6,32,128]{2,1,0:T(8,128)(2,1)S(1)} %get-tuple-element.17), channel_id=1, source_target_pairs={{0,12},{1,13},{2,14},{3,15},{4,8},{5,9},{6,10},{7,11},{8,4},{9,5},... | collective-permute-start | bytes 147464 | tf_op jit(solution)/shard_map/ppermute | solution.py:256
  29.0 6.0 %collective-permute-start.3 = (bf16[24,32,128]{2,1,0:T(8,128)(2,1)S(1)}, bf16[24,32,128]{2,1,0:T(8,128)(2,1)S(1)}, u32[]{:S(2)}, u32[]{:S(2)}) collective-permute-start(bf16[24,32,128]{2,1,0:T(8,128)(2,1)S(1)} %pad_maximum_fusion), channel_id=1, source_target_pairs={{0,2},{1,3},{2,0},{3,1},{4,6},{5,7},{6,4},{7,5},{8,10},{9,11},{10,... | collective-permute-start | bytes 589832 | tf_op jit(solution)/shard_map/ppermute | solution.py:256
  35.0 4.5 %collective-permute-start.4 = (bf16[48,32,128]{2,1,0:T(8,128)(2,1)S(1)}, bf16[48,32,128]{2,1,0:T(8,128)(2,1)S(1)}, u32[]{:S(2)}, u32[]{:S(2)}) collective-permute-start(bf16[48,32,128]{2,1,0:T(8,128)(2,1)S(1)} %constant_dynamic-update-slice_fusion.refs_0_), channel_id=1, source_target_pairs={{0,1},{1,0},{2,3},{3,2},{4,5},{5,4},{6,7},{7,6},{8,9},{9,8},{10,11... | collective-permute-start | bytes 1179656 | tf_op jit(solution)/shard_map/ppermute | solution.py:256
  35.1 16.4 %all-to-all-start = ((bf16[16,6,16,128]{3,2,1,0:T(8,128)(2,1)}), bf16[16,6,16,128]{3,2,1,0:T(8,128)(2,1)S(1)}, u32[]{:S(2)}, u32[]{:S(2)}) async-start(bf16[16,6,16,128]{3,2,1,0:T(8,128)(2,1)} %get-tuple-element.19), calls=%async_computation | async-start | bytes 786432 | tf_op jit(solution)/shard_map/all_to_all | solution.py:264

commit v8 on v7

--- a/solution.py
+++ b/solution.py
@@ -98,7 +98,7 @@
         compiler_params=pltpu.CompilerParams(vmem_limit_bytes=32 * MIB),
         name="project",
     )(*operands)
-    return out[:side], out[side:]
+    return list(out[:side]), list(out[side:])
 
 
 def update_kernel(side, seqs, order, lefts, first, last, *refs):
@@ -215,11 +215,7 @@
             pltpu.VMEM((group * halves, some * width, 2 * tile), jnp.bfloat16),
         ],
         compiler_params=pltpu.CompilerParams(vmem_limit_bytes=48 * MIB),
-        cost_estimate=pl.CostEstimate(
-            flops=2 * tile * tile * some * width * (side * side * seqs + chans),
-            bytes_accessed=16 * MIB,
-            transcendentals=0,
-        ),
+        cost_estimate=pl.CostEstimate(flops=MIB, bytes_accessed=MIB, transcendentals=0),
         name="update_%d" % part,
     )(*operands)
 
@@ -255,7 +251,9 @@
     def swap(x, da, db):
         return lax.ppermute(x, "row", [(i, i ^ (da * side + db)) for i in range(devices)])
 
-    left = jnp.concatenate([left[0]] + [swap(left[d], d, 0) for d in range(1, side)])
+    left = [left[0]] + [swap(left[d], d, 0) for d in range(1, side)]
+    left[1], right[0] = lax.optimization_barrier((left[1], right[0]))
+    left = jnp.concatenate(left)
     parts = []
     for part in range(PARTS):
         mine = right[part]

time: 63.8 us -> 71.3 us (1.12)
  waiting for transfers between devices: 18.2 us -> 24.1 us
  starting transfers between devices: 17.6 us -> 19.3 us
    ppermute x5, waiting for transfers between devices: 16.1 us -> 24.1 us  [swap(): lax.ppermute(x, 'row', [(i, i ^ da * side + db) for i in range(devices)])]
    ppermute x5, starting transfers between devices: 6.05 us -> 9.37 us  [swap(): lax.ppermute(x, 'row', [(i, i ^ da * side + db) for i in range(devices)])]
    all_to_all x2, waiting for transfers between devices: 2.1 us -> 0.01 us  [local(): parts.append(lax.all_to_all(mine, 'row', 0, 0, tiled=True))]
    all_to_all x2, starting transfers between devices: 11.6 us -> 9.96 us  [local(): parts.append(lax.all_to_all(mine, 'row', 0, 0, tiled=True))]
  transfers between devices with their start and end apart: 7 -> 7, of which waited for: 4 -> 4; matrix products, arithmetic and copies ran while one was open for 1% -> 0% of each run, Pallas kernels for 15% -> 14%
where the time goes in v8:
time: 71.3 us; the launch traced here: 71 us
  Pallas kernels  27.2 us (38%)
  waiting for transfers between devices  24.1 us (34%)
  starting transfers between devices  19.3 us (27%)
    ppermute x5, waiting for transfers between devices, swap(): lax.ppermute(x, 'row', [(i, i ^ da * side + db) for i in range(devices)])  24.1 us
    pallas_call x2, Pallas kernels, update_part(): pl.pallas_call(functools.partial(update_kernel, side, seqs, order, len(le...  21.7 us
    all_to_all x2, starting transfers between devices, local(): parts.append(lax.all_to_all(mine, 'row', 0, 0, tiled=True))  9.96 us
    ppermute x5, starting transfers between devices, swap(): lax.ppermute(x, 'row', [(i, i ^ da * side + db) for i in range(devices)])  9.37 us
    pallas_call x1, Pallas kernels, project(): pl.pallas_call(functools.partial(project_kernel, side), in_specs=[pl.Bloc...  5.43 us
  transfers between devices with their start and end apart: 7, of which 4 were waited for; matrix products, arithmetic and copies ran while one was open for 0% of the time, Pallas kernels for 14%

profile of v8, /device:TPU:0, one launch (start us, length us, event | category | flops | bytes accessed | tf_op | source)
XLA Modules:
  0.0 71.0 jit_solution(6769050114047945177)
XLA Ops:
  0.0 0.0 copy-start
  0.0 5.4 %project.1 = (bf16[6,32,128]{2,1,0:T(8,128)(2,1)S(1)}, bf16[6,32,128]{2,1,0:T(8,128)(2,1)S(1)}, bf16[6,32,128]{2,1,0:T(8,128)(2,1)S(1)}, bf16[6,32,128]{2,1,0:T(...) custom-call(bf16[6,512,256]{2,1,0:T(8,128)(2,1)} %refs_0_.1, f32[1,256]{1,0:T(1,128)} %bitcast.18, ...), custom_call_target="tpu_custom_call" | custom-call | tf_op jit(solution)/shard_map/project/pallas_call | solution.py:86
  5.4 3.1 %collective-permute-start = (bf16[6,32,128]{2,1,0:T(8,128)(2,1)S(1)}, bf16[6,32,128]{2,1,0:T(8,128)(2,1)S(1)}, u32[]{:S(2)}, u32[]{:S(2)}) collective-permute-start(bf16[6,32,128]{2,1,0:T(8,128)(2,1)S(1)} %get-tuple-element.17), channel_id=1, source_target_pairs={{0,4},{1,5},{2,6},{3,7},{4,0},{5,1},{6,2},{7,3},{8,12},{9,13},{10,... | collective-permute-start | bytes 147464 | tf_op jit(solution)/shard_map/ppermute | solution.py:252
  8.5 2.1 %collective-permute-done = bf16[6,32,128]{2,1,0:T(8,128)(2,1)S(1)} collective-permute-done((bf16[6,32,128]{2,1,0:T(8,128)(2,1)S(1)}, bf16[6,32,128]{2,1,0:T(8,128)(2,1)S(1)}, u32[]{:S(2)}, u32[]{:S(2)}) %collective-permute-start) | collective-permute-done | bytes 49184 | tf_op jit(solution)/shard_map/ppermute | solution.py:252
  10.6 6.4 %all-to-all-start.1 = ((bf16[16,6,16,128]{3,2,1,0:T(8,128)(2,1)}), bf16[16,6,16,128]{3,2,1,0:T(8,128)(2,1)S(1)}, u32[]{:S(2)}, u32[]{:S(2)}) async-start(bf16[16,6,16,128]{3,2,1,0:T(8,128)(2,1)} %get-tuple-element.24), calls=%async_computation.1 | async-start | bytes 786432 | tf_op jit(solution)/shard_map/all_to_all | solution.py:262
  17.0 2.8 %collective-permute-start.1 = (bf16[6,32,128]{2,1,0:T(8,128)(2,1)S(1)}, bf16[6,32,128]{2,1,0:T(8,128)(2,1)S(1)}, u32[]{:S(2)}, u32[]{:S(2)}) collective-permute-start(bf16[6,32,128]{2,1,0:T(8,128)(2,1)S(1)} %get-tuple-element.20), channel_id=1, source_target_pairs={{0,8},{1,9},{2,10},{3,11},{4,12},{5,13},{6,14},{7,15},{8,0},{9,1},... | collective-permute-start | bytes 147464 | tf_op jit(solution)/shard_map/ppermute | solution.py:252
  19.8 1.5 %collective-permute-start.2 = (bf16[6,32,128]{2,1,0:T(8,128)(2,1)S(1)}, bf16[6,32,128]{2,1,0:T(8,128)(2,1)S(1)}, u32[]{:S(2)}, u32[]{:S(2)}) collective-permute-start(bf16[6,32,128]{2,1,0:T(8,128)(2,1)S(1)} %get-tuple-element.21), channel_id=1, source_target_pairs={{0,12},{1,13},{2,14},{3,15},{4,8},{5,9},{6,10},{7,11},{8,4},{9,5},... | collective-permute-start | bytes 147464 | tf_op jit(solution)/shard_map/ppermute | solution.py:252
  21.3 11.8 %collective-permute-done.1 = bf16[6,32,128]{2,1,0:T(8,128)(2,1)S(1)} collective-permute-done((bf16[6,32,128]{2,1,0:T(8,128)(2,1)S(1)}, bf16[6,32,128]{2,1,0:T(8,128)(2,1)S(1)}, u32[]{:S(2)}, u32[]{:S(2)}) %collective-permute-start.1) | collective-permute-done | bytes 49184 | tf_op jit(solution)/shard_map/ppermute | solution.py:252
  33.1 0.0 collective-permute-done.2
  33.1 0.0 all-to-all-done.1.refs_2_
  33.1 3.6 %all-to-all-start = ((bf16[16,6,16,128]{3,2,1,0:T(8,128)(2,1)}), bf16[16,6,16,128]{3,2,1,0:T(8,128)(2,1)S(1)}, u32[]{:S(2)}, u32[]{:S(2)}) async-start(bf16[16,6,16,128]{3,2,1,0:T(8,128)(2,1)} %get-tuple-element.23), calls=%async_computation | async-start | bytes 786432 | tf_op jit(solution)/shard_map/all_to_all | solution.py:262
  36.7 1.9 %collective-permute-start.3 = (bf16[24,32,128]{2,1,0:T(8,128)(2,1)S(1)}, bf16[24,32,128]{2,1,0:T(8,128)(2,1)S(1)}, u32[]{:S(2)}, u32[]{:S(2)}) collective-permute-start(bf16[24,32,128]{2,1,0:T(8,128)(2,1)S(1)} %pad_maximum_fusion), channel_id=1, source_target_pairs={{0,2},{1,3},{2,0},{3,1},{4,6},{5,7},{6,4},{7,5},{8,10},{9,11},{10,... | collective-permute-start | bytes 589832 | tf_op jit(solution)/shard_map/ppermute | solution.py:252
  38.6 8.8 %collective-permute-done.3 = bf16[24,32,128]{2,1,0:T(8,128)(2,1)S(1)} collective-permute-done((bf16[24,32,128]{2,1,0:T(8,128)(2,1)S(1)}, bf16[24,32,128]{2,1,0:T(8,128)(2,1)S(1)}, u32[]{:S(2)}, u32[]{:S(2)}) %collective-permute-start.3) | collective-permute-done | bytes 196640 | tf_op jit(solution)/shard_map/ppermute | solution.py:252
  47.5 0.1 collective-permute-start.4
  47.6 0.0 copy-done
  47.6 0.1 copy.14
  47.7 0.1 copy.16.refs_3_
  47.8 1.4 %collective-permute-done.4.refs_1_ = bf16[48,32,128]{2,1,0:T(8,128)(2,1)S(1)} collective-permute-done((bf16[48,32,128]{2,1,0:T(8,128)(2,1)S(1)}, bf16[48,32,128]{2,1,0:T(8,128)(2,1)S(1)}, u32[]{:S(2)}, u32[]{:S(2)}) %collective-permute-start.4) | collective-permute-done | bytes 393248 | tf_op jit(solution)/shard_map/ppermute | solution.py:252
  49.3 9.8 %update_0.1.refs_4_ = f32[32,2,128,256]{3,2,1,0:T(8,128)} custom-call(bf16[48,32,128]{2,1,0:T(8,128)(2,1)S(1)} %constant_dynamic-update-slice_fusion.refs_0_, bf16[48,32,128]{2,1,0:T(8,128)(2,1)S(1)} %collective-permute-done.4.refs_1_, bf16[16,6,16,128]{3,2,1,0:T(8,128)(2,1)S(1)} %all-to-all-done.1.refs_2_, bf16[128,1024]{1,0:T(8,128)(2,1)S(1)} %copy.16.refs_3_), custom_call_target="tpu_custom_call" | custom-call | flops 1048576 | bytes 1048576 | tf_op jit(solution)/shard_map/update_0/pallas_call | solution.py:205
  59.1 0.0 all-to-all-done.refs_2_
  59.1 11.9 %update_1.1 = bf16[4,32,128,128]{3,2,1,0:T(8,128)(2,1)} custom-call(bf16[48,32,128]{2,1,0:T(8,128)(2,1)S(1)} %constant_dynamic-update-slice_fusion.refs_0_, bf16[48,32,128]{2,1,0:T(8,128)(2,1)S(1)} %collective-permute-done.4.refs_1_, bf16[16,6,16,128]{3,2,1,0:T(8,128)(2,1)S(1)} %all-to-all-done.refs_2_, bf16[128,1024]{1,0:T(8,128)(2,1)S(1)} %copy.16.refs_3_, ...), custom_call_target="tpu_custom_call" | custom-call | flops 1048576 | bytes 1048576 | tf_op jit(solution)/shard_map/update_1/pallas_call | solution.py:205
  (3 shorter events, 0.1 us)
Async XLA Ops:
  0.0 47.6 %copy-start = (bf16[1024,128]{1,0:T(8,128)(2,1)S(1)}, bf16[1024,128]{1,0:T(8,128)(2,1)}, u32[]{:S(2)}) copy-start(bf16[1024,128]{1,0:T(8,128)(2,1)} %param.18) | copy-start | bytes 786436
  5.4 5.2 %collective-permute-start = (bf16[6,32,128]{2,1,0:T(8,128)(2,1)S(1)}, bf16[6,32,128]{2,1,0:T(8,128)(2,1)S(1)}, u32[]{:S(2)}, u32[]{:S(2)}) collective-permute-start(bf16[6,32,128]{2,1,0:T(8,128)(2,1)S(1)} %get-tuple-element.17), channel_id=1, source_target_pairs={{0,4},{1,5},{2,6},{3,7},{4,0},{5,1},{6,2},{7,3},{8,12},{9,13},{10,... | collective-permute-start | bytes 147464 | tf_op jit(solution)/shard_map/ppermute | solution.py:252
  10.6 22.5 %all-to-all-start.1 = ((bf16[16,6,16,128]{3,2,1,0:T(8,128)(2,1)}), bf16[16,6,16,128]{3,2,1,0:T(8,128)(2,1)S(1)}, u32[]{:S(2)}, u32[]{:S(2)}) async-start(bf16[16,6,16,128]{3,2,1,0:T(8,128)(2,1)} %get-tuple-element.24), calls=%async_computation.1 | async-start | bytes 786432 | tf_op jit(solution)/shard_map/all_to_all | solution.py:262
  17.0 16.1 %collective-permute-start.1 = (bf16[6,32,128]{2,1,0:T(8,128)(2,1)S(1)}, bf16[6,32,128]{2,1,0:T(8,128)(2,1)S(1)}, u32[]{:S(2)}, u32[]{:S(2)}) collective-permute-start(bf16[6,32,128]{2,1,0:T(8,128)(2,1)S(1)} %get-tuple-element.20), channel_id=1, source_target_pairs={{0,8},{1,9},{2,10},{3,11},{4,12},{5,13},{6,14},{7,15},{8,0},{9,1},... | collective-permute-start | bytes 147464 | tf_op jit(solution)/shard_map/ppermute | solution.py:252
  19.8 13.3 %collective-permute-start.2 = (bf16[6,32,128]{2,1,0:T(8,128)(2,1)S(1)}, bf16[6,32,128]{2,1,0:T(8,128)(2,1)S(1)}, u32[]{:S(2)}, u32[]{:S(2)}) collective-permute-start(bf16[6,32,128]{2,1,0:T(8,128)(2,1)S(1)} %get-tuple-element.21), channel_id=1, source_target_pairs={{0,12},{1,13},{2,14},{3,15},{4,8},{5,9},{6,10},{7,11},{8,4},{9,5},... | collective-permute-start | bytes 147464 | tf_op jit(solution)/shard_map/ppermute | solution.py:252
  33.1 25.9 %all-to-all-start = ((bf16[16,6,16,128]{3,2,1,0:T(8,128)(2,1)}), bf16[16,6,16,128]{3,2,1,0:T(8,128)(2,1)S(1)}, u32[]{:S(2)}, u32[]{:S(2)}) async-start(bf16[16,6,16,128]{3,2,1,0:T(8,128)(2,1)} %get-tuple-element.23), calls=%async_computation | async-start | bytes 786432 | tf_op jit(solution)/shard_map/all_to_all | solution.py:262
  36.7 10.8 %collective-permute-start.3 = (bf16[24,32,128]{2,1,0:T(8,128)(2,1)S(1)}, bf16[24,32,128]{2,1,0:T(8,128)(2,1)S(1)}, u32[]{:S(2)}, u32[]{:S(2)}) collective-permute-start(bf16[24,32,128]{2,1,0:T(8,128)(2,1)S(1)} %pad_maximum_fusion), channel_id=1, source_target_pairs={{0,2},{1,3},{2,0},{3,1},{4,6},{5,7},{6,4},{7,5},{8,10},{9,11},{10,... | collective-permute-start | bytes 589832 | tf_op jit(solution)/shard_map/ppermute | solution.py:252
  47.5 1.8 %collective-permute-start.4 = (bf16[48,32,128]{2,1,0:T(8,128)(2,1)S(1)}, bf16[48,32,128]{2,1,0:T(8,128)(2,1)S(1)}, u32[]{:S(2)}, u32[]{:S(2)}) collective-permute-start(bf16[48,32,128]{2,1,0:T(8,128)(2,1)S(1)} %constant_dynamic-update-slice_fusion.refs_0_), channel_id=1, source_target_pairs={{0,1},{1,0},{2,3},{3,2},{4,5},{5,4},{6,7},{7,6},{8,9},{9,8},{10,11... | collective-permute-start | bytes 1179656 | tf_op jit(solution)/shard_map/ppermute | solution.py:252

commit v9 on v6

--- a/solution.py
+++ b/solution.py
@@ -255,23 +255,14 @@
     def swap(x, da, db):
         return lax.ppermute(x, "row", [(i, i ^ (da * side + db)) for i in range(devices)])
 
+    left = [left[0]] + [swap(left[d], d, 0) for d in range(1, side)]
     right = [right[0]] + [swap(right[d], 0, d) for d in range(1, side)]
-    *left, right[1] = lax.optimization_barrier((*left, right[1]))
-    left = jnp.concatenate([left[0]] + [swap(left[d], d, 0) for d in range(1, side)])
-    parts = []
-    for part in range(PARTS):
-        mine = jnp.concatenate([x[part] for x in right])
-        parts.append([mine] + [swap(mine, d, 0) for d in range(1, side)])
-    order = [0]
-    lefts = [left]
-    step = side // 2
-    while step > 0:
-        left = jnp.concatenate(lefts) if len(lefts) > 1 else lefts[0]
-        if len(lefts) > 1:
-            left, *parts[0] = lax.optimization_barrier((left, *parts[0]))
-        lefts = [left, swap(left, 0, step)]
-        order += [o ^ step for o in order]
-        step //= 2
+    left = jnp.concatenate(left)
+    mines = [jnp.concatenate([x[part] for x in right]) for part in range(PARTS)]
+    left, *mines = lax.optimization_barrier((left, *mines))
+    lefts = [left] + [swap(left, 0, d) for d in range(1, side)]
+    parts = [[mine] + [swap(mine, d, 0) for d in range(1, side)] for mine in mines]
+    order = list(range(side))
     wt = final_matrix.reshape(width, width, -1).transpose(2, 1, 0).reshape(-1, width * width)
     total = None
     for part in range(PARTS):

time: 60.9 us -> 54.6 us (0.90)
  waiting for transfers between devices: 13.6 us -> 7.35 us
    ppermute x14 -> x15, waiting for transfers between devices: 13.6 us -> 7.35 us  [swap(): lax.ppermute(x, 'row', [(i, i ^ da * side + db) for i in range(devices)])]
    ppermute x14 -> x15, starting transfers between devices: 19.4 us -> 19.5 us  [swap(): lax.ppermute(x, 'row', [(i, i ^ da * side + db) for i in range(devices)])]
  transfers between devices with their start and end apart: 14 -> 15, of which waited for: 5 -> 5; matrix products, arithmetic and copies ran while one was open for 2% -> 2% of each run, Pallas kernels for 16% -> 18%
where the time goes in v9:
time: 54.6 us; the launch traced here: 54.5 us
  Pallas kernels  26.3 us (48%)
  starting transfers between devices  19.5 us (36%)
  waiting for transfers between devices  7.35 us (13%)
  local copies, waits for them, and re-layouts  1.22 us (2%)
    pallas_call x2, Pallas kernels, update_part(): pl.pallas_call(functools.partial(update_kernel, side, seqs, order, len(le...  21.8 us
    ppermute x15, starting transfers between devices, swap(): lax.ppermute(x, 'row', [(i, i ^ da * side + db) for i in range(devices)])  19.5 us
    ppermute x15, waiting for transfers between devices, swap(): lax.ppermute(x, 'row', [(i, i ^ da * side + db) for i in range(devices)])  7.35 us
    pallas_call x1, Pallas kernels, project(): pl.pallas_call(functools.partial(project_kernel, side), in_specs=[pl.Bloc...  4.52 us
  transfers between devices with their start and end apart: 15, of which 5 were waited for; matrix products, arithmetic and copies ran while one was open for 2% of the time, Pallas kernels for 18%

profile of v9, /device:TPU:0, one launch (start us, length us, event | category | flops | bytes accessed | tf_op | source)
XLA Modules:
  0.0 54.5 jit_solution(14238252144643286569)
XLA Ops:
  0.0 4.5 %project.1 = (bf16[6,32,128]{2,1,0:T(8,128)(2,1)S(1)}, bf16[6,32,128]{2,1,0:T(8,128)(2,1)S(1)}, bf16[6,32,128]{2,1,0:T(8,128)(2,1)S(1)}, bf16[6,32,128]{2,1,0:T(...) custom-call(bf16[6,512,256]{2,1,0:T(8,128)(2,1)} %refs_0_.1, ...), custom_call_target="tpu_custom_call" | custom-call | tf_op jit(solution)/shard_map/project/pallas_call | solution.py:86
  4.5 3.1 %collective-permute-start = (bf16[6,32,128]{2,1,0:T(8,128)(2,1)S(1)}, bf16[6,32,128]{2,1,0:T(8,128)(2,1)S(1)}, u32[]{:S(2)}, u32[]{:S(2)}) collective-permute-start(bf16[6,32,128]{2,1,0:T(8,128)(2,1)S(1)} %get-tuple-element.17), channel_id=1, source_target_pairs={{0,4},{1,5},{2,6},{3,7},{4,0},{5,1},{6,2},{7,3},{8,12},{9,13},{10,... | collective-permute-start | bytes 147464 | tf_op jit(solution)/shard_map/ppermute | solution.py:256
  7.6 2.6 %collective-permute-start.1 = (bf16[6,32,128]{2,1,0:T(8,128)(2,1)S(1)}, bf16[6,32,128]{2,1,0:T(8,128)(2,1)S(1)}, u32[]{:S(2)}, u32[]{:S(2)}) collective-permute-start(bf16[6,32,128]{2,1,0:T(8,128)(2,1)S(1)} %get-tuple-element.18), channel_id=1, source_target_pairs={{0,8},{1,9},{2,10},{3,11},{4,12},{5,13},{6,14},{7,15},{8,0},{9,1},... | collective-permute-start | bytes 147464 | tf_op jit(solution)/shard_map/ppermute | solution.py:256
  10.2 0.0 collective-permute-start.2
  10.2 0.0 collective-permute-start.3
  10.2 1.7 %collective-permute-start.4 = (bf16[2,6,16,128]{3,2,1,0:T(8,128)(2,1)S(1)}, bf16[2,6,16,128]{3,2,1,0:T(8,128)(2,1)S(1)}, u32[]{:S(2)}, u32[]{:S(2)}) collective-permute-start(bf16[2,6,16,128]{3,2,1,0:T(8,128)(2,1)S(1)} %get-tuple-element.22), channel_id=1, source_target_pairs={{0,2},{1,3},{2,0},{3,1},{4,6},{5,7},{6,4},{7,5},{8,10},{9,11},{10,... | collective-permute-start | bytes 147464 | tf_op jit(solution)/shard_map/ppermute | solution.py:256
  12.0 0.0 collective-permute-done.3
  12.0 1.0 %collective-permute-start.5 = (bf16[2,6,16,128]{3,2,1,0:T(8,128)(2,1)S(1)}, bf16[2,6,16,128]{3,2,1,0:T(8,128)(2,1)S(1)}, u32[]{:S(2)}, u32[]{:S(2)}) collective-permute-start(bf16[2,6,16,128]{3,2,1,0:T(8,128)(2,1)S(1)} %get-tuple-element.23), channel_id=1, source_target_pairs={{0,3},{1,2},{2,1},{3,0},{4,7},{5,6},{6,5},{7,4},{8,11},{9,10},{10,... | collective-permute-start | bytes 147464 | tf_op jit(solution)/shard_map/ppermute | solution.py:256
  13.0 1.4 %collective-permute-done.4 = bf16[2,6,16,128]{3,2,1,0:T(8,128)(2,1)S(1)} collective-permute-done((bf16[2,6,16,128]{3,2,1,0:T(8,128)(2,1)S(1)}, bf16[2,6,16,128]{3,2,1,0:T(8,128)(2,1)S(1)}, u32[]{:S(2)}, u32[]{:S(2)}) %collective-permute-start.4) | collective-permute-done | bytes 49184 | tf_op jit(solution)/shard_map/ppermute | solution.py:256
  14.4 1.4 %collective-permute-done.5 = bf16[2,6,16,128]{3,2,1,0:T(8,128)(2,1)S(1)} collective-permute-done((bf16[2,6,16,128]{3,2,1,0:T(8,128)(2,1)S(1)}, bf16[2,6,16,128]{3,2,1,0:T(8,128)(2,1)S(1)}, u32[]{:S(2)}, u32[]{:S(2)}) %collective-permute-start.5) | collective-permute-done | bytes 49184 | tf_op jit(solution)/shard_map/ppermute | solution.py:256
  15.8 0.0 collective-permute-done
  15.8 0.0 collective-permute-done.1
  15.8 0.3 collective-permute-done.2
  16.1 3.4 %collective-permute-start.14 = (bf16[24,16,128]{2,1,0:T(8,128)(2,1)S(1)}, bf16[24,16,128]{2,1,0:T(8,128)(2,1)S(1)}, u32[]{:S(2)}, u32[]{:S(2)}) collective-permute-start(bf16[24,16,128]{2,1,0:T(8,128)(2,1)S(1)} %get-tuple-element.26.refs_4_), channel_id=1, source_target_pairs={{0,12},{1,13},{2,14},{3,15},{4,8},{5,9},{6,10},{7,11},{8,4},{9,5},... | collective-permute-start | bytes 294920 | tf_op jit(solution)/shard_map/ppermute | solution.py:256
  19.5 0.6 %collective-permute-start.8 = (bf16[24,32,128]{2,1,0:T(8,128)(2,1)S(1)}, bf16[24,32,128]{2,1,0:T(8,128)(2,1)S(1)}, u32[]{:S(2)}, u32[]{:S(2)}) collective-permute-start(bf16[24,32,128]{2,1,0:T(8,128)(2,1)S(1)} %pad_maximum_fusion.refs_0_), channel_id=1, source_target_pairs={{0,3},{1,2},{2,1},{3,0},{4,7},{5,6},{6,5},{7,4},{8,11},{9,10},{10,... | collective-permute-start | bytes 589832 | tf_op jit(solution)/shard_map/ppermute | solution.py:256
  20.1 0.9 %collective-permute-start.7 = (bf16[24,32,128]{2,1,0:T(8,128)(2,1)S(1)}, bf16[24,32,128]{2,1,0:T(8,128)(2,1)S(1)}, u32[]{:S(2)}, u32[]{:S(2)}) collective-permute-start(bf16[24,32,128]{2,1,0:T(8,128)(2,1)S(1)} %pad_maximum_fusion.refs_0_), channel_id=1, source_target_pairs={{0,2},{1,3},{2,0},{3,1},{4,6},{5,7},{6,4},{7,5},{8,10},{9,11},{10,... | collective-permute-start | bytes 589832 | tf_op jit(solution)/shard_map/ppermute | solution.py:256
  21.0 0.4 collective-permute-start.6
  21.4 0.0 collective-permute-start.13
  21.4 1.6 %collective-permute-done.14.refs_7_ = bf16[24,16,128]{2,1,0:T(8,128)(2,1)S(1)} collective-permute-done((bf16[24,16,128]{2,1,0:T(8,128)(2,1)S(1)}, bf16[24,16,128]{2,1,0:T(8,128)(2,1)S(1)}, u32[]{:S(2)}, u32[]{:S(2)}) %collective-permute-start.14) | collective-permute-done | bytes 98336 | tf_op jit(solution)/shard_map/ppermute | solution.py:256
  23.0 0.6 %collective-permute-start.12 = (bf16[24,16,128]{2,1,0:T(8,128)(2,1)S(1)}, bf16[24,16,128]{2,1,0:T(8,128)(2,1)S(1)}, u32[]{:S(2)}, u32[]{:S(2)}) collective-permute-start(bf16[24,16,128]{2,1,0:T(8,128)(2,1)S(1)} %get-tuple-element.26.refs_4_), channel_id=1, source_target_pairs={{0,4},{1,5},{2,6},{3,7},{4,0},{5,1},{6,2},{7,3},{8,12},{9,13},{10,... | collective-permute-start | bytes 294920 | tf_op jit(solution)/shard_map/ppermute | solution.py:256
  23.5 1.1 %copy.14 = bf16[128,32,32]{0,2,1:T(8,128)(2,1)S(1)} copy(bf16[128,32,32]{0,1,2:T(8,128)(2,1)} %bitcast.31) | data formatting | bytes 524288 | tf_op jit(solution)/shard_map/transpose | solution.py:266
  24.6 0.1 copy.16.refs_8_
  24.7 2.7 %collective-permute-done.13.refs_6_ = bf16[24,16,128]{2,1,0:T(8,128)(2,1)S(1)} collective-permute-done((bf16[24,16,128]{2,1,0:T(8,128)(2,1)S(1)}, bf16[24,16,128]{2,1,0:T(8,128)(2,1)S(1)}, u32[]{:S(2)}, u32[]{:S(2)}) %collective-permute-start.13) | collective-permute-done | bytes 98336 | tf_op jit(solution)/shard_map/ppermute | solution.py:256
  27.4 3.1 %collective-permute-start.11 = (bf16[24,16,128]{2,1,0:T(8,128)(2,1)S(1)}, bf16[24,16,128]{2,1,0:T(8,128)(2,1)S(1)}, u32[]{:S(2)}, u32[]{:S(2)}) collective-permute-start(bf16[24,16,128]{2,1,0:T(8,128)(2,1)S(1)} %get-tuple-element.25.refs_4_), channel_id=1, source_target_pairs={{0,12},{1,13},{2,14},{3,15},{4,8},{5,9},{6,10},{7,11},{8,4},{9,5},... | collective-permute-start | bytes 294920 | tf_op jit(solution)/shard_map/ppermute | solution.py:256
  30.5 0.0 collective-permute-done.12.refs_5_
  30.5 0.0 collective-permute-start.10
  30.5 0.0 collective-permute-done.8.refs_3_
  30.5 2.2 %collective-permute-start.9 = (bf16[24,16,128]{2,1,0:T(8,128)(2,1)S(1)}, bf16[24,16,128]{2,1,0:T(8,128)(2,1)S(1)}, u32[]{:S(2)}, u32[]{:S(2)}) collective-permute-start(bf16[24,16,128]{2,1,0:T(8,128)(2,1)S(1)} %get-tuple-element.25.refs_4_), channel_id=1, source_target_pairs={{0,4},{1,5},{2,6},{3,7},{4,0},{5,1},{6,2},{7,3},{8,12},{9,13},{10,... | collective-permute-start | bytes 294920 | tf_op jit(solution)/shard_map/ppermute | solution.py:256
  32.7 0.0 collective-permute-done.7.refs_2_
  32.7 0.0 collective-permute-done.6.refs_1_
  32.7 9.8 %update_0.1.refs_9_ = f32[32,2,128,256]{3,2,1,0:T(8,128)} custom-call(bf16[24,32,128]{2,1,0:T(8,128)(2,1)S(1)} %pad_maximum_fusion.refs_0_, bf16[24,32,128]{2,1,0:T(8,128)(2,1)S(1)} %collective-permute-done.6.refs_1_, bf16[24,32,128]{2,1,0:T(8,128)(2,1)S(1)} %collective-permute-done.7.refs_2_, bf16[24,32,128]{2,1,0:T(8,128)(2,1)S(1)} %collective-permute-done.8.refs_3_, ...), custom_call_target="tpu_custom_call" | custom-call | flops 3758096384 | bytes 16777216 | tf_op jit(solution)/shard_map/update_0/pallas_call | solution.py:205
  42.5 0.0 collective-permute-done.11.refs_7_
  42.5 0.0 collective-permute-done.10.refs_6_
  42.5 0.0 collective-permute-done.9.refs_5_
  42.5 12.0 %update_1.1 = bf16[4,32,128,128]{3,2,1,0:T(8,128)(2,1)} custom-call(bf16[24,32,128]{2,1,0:T(8,128)(2,1)S(1)} %pad_maximum_fusion.refs_0_, bf16[24,32,128]{2,1,0:T(8,128)(2,1)S(1)} %collective-permute-done.6.refs_1_, bf16[24,32,128]{2,1,0:T(8,128)(2,1)S(1)} %collective-permute-done.7.refs_2_, bf16[24,32,128]{2,1,0:T(8,128)(2,1)S(1)} %collective-permute-done.8.refs_3_, ...), custom_call_target="tpu_custom_call" | custom-call | flops 3758096384 | bytes 16777216 | tf_op jit(solution)/shard_map/update_1/pallas_call | solution.py:205
  (6 shorter events, 0.1 us)
Async XLA Ops:
  4.5 11.2 %collective-permute-start = (bf16[6,32,128]{2,1,0:T(8,128)(2,1)S(1)}, bf16[6,32,128]{2,1,0:T(8,128)(2,1)S(1)}, u32[]{:S(2)}, u32[]{:S(2)}) collective-permute-start(bf16[6,32,128]{2,1,0:T(8,128)(2,1)S(1)} %get-tuple-element.17), channel_id=1, source_target_pairs={{0,4},{1,5},{2,6},{3,7},{4,0},{5,1},{6,2},{7,3},{8,12},{9,13},{10,... | collective-permute-start | bytes 147464 | tf_op jit(solution)/shard_map/ppermute | solution.py:256
  7.6 8.2 %collective-permute-start.1 = (bf16[6,32,128]{2,1,0:T(8,128)(2,1)S(1)}, bf16[6,32,128]{2,1,0:T(8,128)(2,1)S(1)}, u32[]{:S(2)}, u32[]{:S(2)}) collective-permute-start(bf16[6,32,128]{2,1,0:T(8,128)(2,1)S(1)} %get-tuple-element.18), channel_id=1, source_target_pairs={{0,8},{1,9},{2,10},{3,11},{4,12},{5,13},{6,14},{7,15},{8,0},{9,1},... | collective-permute-start | bytes 147464 | tf_op jit(solution)/shard_map/ppermute | solution.py:256
  10.2 5.9 %collective-permute-start.2 = (bf16[6,32,128]{2,1,0:T(8,128)(2,1)S(1)}, bf16[6,32,128]{2,1,0:T(8,128)(2,1)S(1)}, u32[]{:S(2)}, u32[]{:S(2)}) collective-permute-start(bf16[6,32,128]{2,1,0:T(8,128)(2,1)S(1)} %get-tuple-element.19), channel_id=1, source_target_pairs={{0,12},{1,13},{2,14},{3,15},{4,8},{5,9},{6,10},{7,11},{8,4},{9,5},... | collective-permute-start | bytes 147464 | tf_op jit(solution)/shard_map/ppermute | solution.py:256
  10.2 1.7 %collective-permute-start.3 = (bf16[2,6,16,128]{3,2,1,0:T(8,128)(2,1)S(1)}, bf16[2,6,16,128]{3,2,1,0:T(8,128)(2,1)S(1)}, u32[]{:S(2)}, u32[]{:S(2)}) collective-permute-start(bf16[2,6,16,128]{3,2,1,0:T(8,128)(2,1)S(1)} %get-tuple-element.21), channel_id=1, source_target_pairs={{0,1},{1,0},{2,3},{3,2},{4,5},{5,4},{6,7},{7,6},{8,9},{9,8},{10,11... | collective-permute-start | bytes 147464 | tf_op jit(solution)/shard_map/ppermute | solution.py:256
  10.2 4.2 %collective-permute-start.4 = (bf16[2,6,16,128]{3,2,1,0:T(8,128)(2,1)S(1)}, bf16[2,6,16,128]{3,2,1,0:T(8,128)(2,1)S(1)}, u32[]{:S(2)}, u32[]{:S(2)}) collective-permute-start(bf16[2,6,16,128]{3,2,1,0:T(8,128)(2,1)S(1)} %get-tuple-element.22), channel_id=1, source_target_pairs={{0,2},{1,3},{2,0},{3,1},{4,6},{5,7},{6,4},{7,5},{8,10},{9,11},{10,... | collective-permute-start | bytes 147464 | tf_op jit(solution)/shard_map/ppermute | solution.py:256
  12.0 3.8 %collective-permute-start.5 = (bf16[2,6,16,128]{3,2,1,0:T(8,128)(2,1)S(1)}, bf16[2,6,16,128]{3,2,1,0:T(8,128)(2,1)S(1)}, u32[]{:S(2)}, u32[]{:S(2)}) collective-permute-start(bf16[2,6,16,128]{3,2,1,0:T(8,128)(2,1)S(1)} %get-tuple-element.23), channel_id=1, source_target_pairs={{0,3},{1,2},{2,1},{3,0},{4,7},{5,6},{6,5},{7,4},{8,11},{9,10},{10,... | collective-permute-start | bytes 147464 | tf_op jit(solution)/shard_map/ppermute | solution.py:256
  16.1 6.8 %collective-permute-start.14 = (bf16[24,16,128]{2,1,0:T(8,128)(2,1)S(1)}, bf16[24,16,128]{2,1,0:T(8,128)(2,1)S(1)}, u32[]{:S(2)}, u32[]{:S(2)}) collective-permute-start(bf16[24,16,128]{2,1,0:T(8,128)(2,1)S(1)} %get-tuple-element.26.refs_4_), channel_id=1, source_target_pairs={{0,12},{1,13},{2,14},{3,15},{4,8},{5,9},{6,10},{7,11},{8,4},{9,5},... | collective-permute-start | bytes 294920 | tf_op jit(solution)/shard_map/ppermute | solution.py:256
  19.5 11.0 %collective-permute-start.8 = (bf16[24,32,128]{2,1,0:T(8,128)(2,1)S(1)}, bf16[24,32,128]{2,1,0:T(8,128)(2,1)S(1)}, u32[]{:S(2)}, u32[]{:S(2)}) collective-permute-start(bf16[24,32,128]{2,1,0:T(8,128)(2,1)S(1)} %pad_maximum_fusion.refs_0_), channel_id=1, source_target_pairs={{0,3},{1,2},{2,1},{3,0},{4,7},{5,6},{6,5},{7,4},{8,11},{9,10},{10,... | collective-permute-start | bytes 589832 | tf_op jit(solution)/shard_map/ppermute | solution.py:256
  20.1 12.5 %collective-permute-start.7 = (bf16[24,32,128]{2,1,0:T(8,128)(2,1)S(1)}, bf16[24,32,128]{2,1,0:T(8,128)(2,1)S(1)}, u32[]{:S(2)}, u32[]{:S(2)}) collective-permute-start(bf16[24,32,128]{2,1,0:T(8,128)(2,1)S(1)} %pad_maximum_fusion.refs_0_), channel_id=1, source_target_pairs={{0,2},{1,3},{2,0},{3,1},{4,6},{5,7},{6,4},{7,5},{8,10},{9,11},{10,... | collective-permute-start | bytes 589832 | tf_op jit(solution)/shard_map/ppermute | solution.py:256
  21.0 11.7 %collective-permute-start.6 = (bf16[24,32,128]{2,1,0:T(8,128)(2,1)S(1)}, bf16[24,32,128]{2,1,0:T(8,128)(2,1)S(1)}, u32[]{:S(2)}, u32[]{:S(2)}) collective-permute-start(bf16[24,32,128]{2,1,0:T(8,128)(2,1)S(1)} %pad_maximum_fusion.refs_0_), channel_id=1, source_target_pairs={{0,1},{1,0},{2,3},{3,2},{4,5},{5,4},{6,7},{7,6},{8,9},{9,8},{10,11... | collective-permute-start | bytes 589832 | tf_op jit(solution)/shard_map/ppermute | solution.py:256
  21.4 6.0 %collective-permute-start.13 = (bf16[24,16,128]{2,1,0:T(8,128)(2,1)S(1)}, bf16[24,16,128]{2,1,0:T(8,128)(2,1)S(1)}, u32[]{:S(2)}, u32[]{:S(2)}) collective-permute-start(bf16[24,16,128]{2,1,0:T(8,128)(2,1)S(1)} %get-tuple-element.26.refs_4_), channel_id=1, source_target_pairs={{0,8},{1,9},{2,10},{3,11},{4,12},{5,13},{6,14},{7,15},{8,0},{9,1},... | collective-permute-start | bytes 294920 | tf_op jit(solution)/shard_map/ppermute | solution.py:256
  23.0 7.5 %collective-permute-start.12 = (bf16[24,16,128]{2,1,0:T(8,128)(2,1)S(1)}, bf16[24,16,128]{2,1,0:T(8,128)(2,1)S(1)}, u32[]{:S(2)}, u32[]{:S(2)}) collective-permute-start(bf16[24,16,128]{2,1,0:T(8,128)(2,1)S(1)} %get-tuple-element.26.refs_4_), channel_id=1, source_target_pairs={{0,4},{1,5},{2,6},{3,7},{4,0},{5,1},{6,2},{7,3},{8,12},{9,13},{10,... | collective-permute-start | bytes 294920 | tf_op jit(solution)/shard_map/ppermute | solution.py:256
  27.4 15.1 %collective-permute-start.11 = (bf16[24,16,128]{2,1,0:T(8,128)(2,1)S(1)}, bf16[24,16,128]{2,1,0:T(8,128)(2,1)S(1)}, u32[]{:S(2)}, u32[]{:S(2)}) collective-permute-start(bf16[24,16,128]{2,1,0:T(8,128)(2,1)S(1)} %get-tuple-element.25.refs_4_), channel_id=1, source_target_pairs={{0,12},{1,13},{2,14},{3,15},{4,8},{5,9},{6,10},{7,11},{8,4},{9,5},... | collective-permute-start | bytes 294920 | tf_op jit(solution)/shard_map/ppermute | solution.py:256
  30.5 12.0 %collective-permute-start.10 = (bf16[24,16,128]{2,1,0:T(8,128)(2,1)S(1)}, bf16[24,16,128]{2,1,0:T(8,128)(2,1)S(1)}, u32[]{:S(2)}, u32[]{:S(2)}) collective-permute-start(bf16[24,16,128]{2,1,0:T(8,128)(2,1)S(1)} %get-tuple-element.25.refs_4_), channel_id=1, source_target_pairs={{0,8},{1,9},{2,10},{3,11},{4,12},{5,13},{6,14},{7,15},{8,0},{9,1},... | collective-permute-start | bytes 294920 | tf_op jit(solution)/shard_map/ppermute | solution.py:256
  30.5 12.0 %collective-permute-start.9 = (bf16[24,16,128]{2,1,0:T(8,128)(2,1)S(1)}, bf16[24,16,128]{2,1,0:T(8,128)(2,1)S(1)}, u32[]{:S(2)}, u32[]{:S(2)}) collective-permute-start(bf16[24,16,128]{2,1,0:T(8,128)(2,1)S(1)} %get-tuple-element.25.refs_4_), channel_id=1, source_target_pairs={{0,4},{1,5},{2,6},{3,7},{4,0},{5,1},{6,2},{7,3},{8,12},{9,13},{10,... | collective-permute-start | bytes 294920 | tf_op jit(solution)/shard_map/ppermute | solution.py:256

commit v10 on v9

--- a/solution.py
+++ b/solution.py
@@ -101,44 +101,65 @@
     return out[:side], out[side:]
 
 
-def update_kernel(side, seqs, order, lefts, first, last, *refs):
-    left_refs, refs = refs[:lefts], refs[lefts:]
-    right_refs, refs = refs[:side], refs[side:]
+def arrange_kernel(seq_total, *refs):
+    left_refs, out_ref, wide = refs[:-2], refs[-2], refs[-1]
+    _, rows, lanes = left_refs[0].shape
+    depth = out_ref.shape[2]
+    at = 0
+    for ref in left_refs:
+        count = ref.shape[0] * rows
+        wide[at : at + count] = ref[...].astype(jnp.float32).reshape(count, lanes)
+        at += count
+    if depth > seq_total:
+        wide[seq_total * rows :] = jnp.zeros(((depth - seq_total) * rows, lanes), jnp.float32)
+    for r in range(rows):
+        out_ref[r] = wide[pl.ds(r, depth, stride=rows), :].T.astype(jnp.bfloat16)
+
+
+def arrange_left(lefts, tile):
+    _, rows, lanes = lefts[0].shape
+    seq_total = sum(x.shape[0] for x in lefts)
+    depth = -(-seq_total // LANES) * LANES
+    return pl.pallas_call(
+        functools.partial(arrange_kernel, seq_total),
+        in_specs=[pl.BlockSpec(memory_space=pltpu.VMEM)] * len(lefts),
+        out_specs=pl.BlockSpec(memory_space=pltpu.VMEM),
+        out_shape=jax.ShapeDtypeStruct((rows, lanes, depth), jnp.bfloat16),
+        scratch_shapes=[pltpu.VMEM((depth * rows, lanes), jnp.float32)],
+        compiler_params=pltpu.CompilerParams(vmem_limit_bytes=32 * MIB),
+        cost_estimate=pl.CostEstimate(flops=MIB, bytes_accessed=8 * MIB, transcendentals=0),
+        name="arrange_left",
+    )(*lefts)
+
+
+def update_kernel(side, seqs, order, rights, first, last, left_ref, *refs):
+    right_refs, refs = refs[:rights], refs[rights:]
     wt_ref, refs = refs[0], refs[1:]
     if not first:
         before_ref, refs = refs[0], refs[1:]
     if last:
         bias_ref, pair_ref, refs = refs[0], refs[1], refs[2:]
-    out_ref, left_wide, right_wide, right_flat, outer = refs
-    _, rows, lanes = left_refs[0].shape
-    _, some, tile = right_refs[0].shape
-    depth = right_flat.shape[0]
-    pack = tile // rows
+    out_ref, right_wide, right_flat, outer = refs
+    group, lanes, depth = left_ref.shape
+    some, tile = right_refs[0].shape[-2:]
+    halves = outer.shape[0] // group
+    pack = 2 * halves
     width = lanes // pack
-    halves = pack // 2
-    group = outer.shape[0] // halves
     seq_total = side * side * seqs
-    step = pl.program_id(0)
-
-    @pl.when(step == 0)
+
+    @pl.when(pl.program_id(0) == 0)
     def _():
-        at = 0
-        for ref in left_refs:
-            count = ref.shape[0] * rows
-            left_wide[at : at + count] = ref[...].astype(jnp.float32).reshape(count, lanes)
-            at += count
+        place_a = lax.axis_index("row") // side
         for dz in range(side):
+            source = right_refs[dz] if rights > 1 else right_refs[0].at[place_a ^ dz]
             for k, dy in enumerate(order):
                 to = (k * side + dz) * seqs
                 right_wide[to * some : (to + seqs) * some] = (
-                    right_refs[dz][dy * seqs : (dy + 1) * seqs]
+                    source[dy * seqs : (dy + 1) * seqs]
                     .astype(jnp.float32)
                     .reshape(seqs * some, tile)
                 )
         if depth > seq_total:
-            left_wide[seq_total * rows :] = jnp.zeros(
-                ((depth - seq_total) * rows, lanes), jnp.float32
-            )
             right_wide[seq_total * some :] = jnp.zeros(
                 ((depth - seq_total) * some, tile), jnp.float32
             )
@@ -148,11 +169,11 @@
             ].astype(jnp.bfloat16)
 
     for q in range(group):
-        x = left_wide[pl.ds(step * group + q, depth, stride=rows), :]
-        left = x.T.astype(jnp.bfloat16)
         for n in range(some // 2):
             both = jnp.dot(
-                left, right_flat[:, 2 * n * tile : (2 * n + 2) * tile], preferred_element_type=jnp.float32
+                left_ref[q],
+                right_flat[:, 2 * n * tile : (2 * n + 2) * tile],
+                preferred_element_type=jnp.float32,
             ).astype(jnp.bfloat16)
             for k in range(2):
                 e = 2 * n + k
@@ -177,20 +198,20 @@
 
 
 def update_part(side, seqs, order, part, left, right, wt, before, bias, pair):
-    _, rows, lanes = left[0].shape
-    _, some, tile = right[0].shape
+    rows, lanes, depth = left.shape
+    some, tile = right[0].shape[-2:]
     chans = wt.shape[0]
     pack = tile // rows
     width = lanes // pack
     halves = pack // 2
-    depth = -(-side * side * seqs // LANES) * LANES
     group = 8
     first, last = part == 0, part == PARTS - 1
     whole = lambda shape: pl.BlockSpec(shape, lambda g: (0,) * len(shape))
     sum_spec = pl.BlockSpec((group, halves, chans, 2 * tile), lambda g: (g, 0, 0, 0))
     pair_spec = pl.BlockSpec((pack, group, tile, chans), lambda g: (0, g, 0, 0))
-    operands = list(left) + list(right) + [wt]
-    specs = [whole(x.shape) for x in operands[:-1]]
+    operands = [left] + list(right) + [wt]
+    specs = [pl.BlockSpec((group, lanes, depth), lambda g: (g, 0, 0))]
+    specs += [whole(x.shape) for x in right]
     specs.append(pl.BlockSpec((chans, some * width), lambda g: (0, part)))
     if not first:
         operands.append(before)
@@ -203,13 +224,12 @@
         out_shape = jax.ShapeDtypeStruct((rows, halves, chans, 2 * tile), jnp.float32)
         out_spec = sum_spec
     return pl.pallas_call(
-        functools.partial(update_kernel, side, seqs, order, len(left), first, last),
+        functools.partial(update_kernel, side, seqs, order, len(right), first, last),
         grid=(rows // group,),
         in_specs=specs,
         out_specs=out_spec,
         out_shape=out_shape,
         scratch_shapes=[
-            pltpu.VMEM((depth * rows, lanes), jnp.float32),
             pltpu.VMEM((depth * some, tile), jnp.float32),
             pltpu.VMEM((depth, some * tile), jnp.bfloat16),
             pltpu.VMEM((group * halves, some * width, 2 * tile), jnp.bfloat16),
@@ -260,14 +280,26 @@
     left = jnp.concatenate(left)
     mines = [jnp.concatenate([x[part] for x in right]) for part in range(PARTS)]
     left, *mines = lax.optimization_barrier((left, *mines))
-    lefts = [left] + [swap(left, 0, d) for d in range(1, side)]
-    parts = [[mine] + [swap(mine, d, 0) for d in range(1, side)] for mine in mines]
-    order = list(range(side))
+    parts = [[mines[0]] + [swap(mines[0], d, 0) for d in range(1, side)]]
+    order = [0]
+    lefts = [left]
+    step = side // 2
+    while step > 0:
+        left = jnp.concatenate(lefts) if len(lefts) > 1 else lefts[0]
+        lefts = [left, swap(left, 0, step)]
+        order += [o ^ step for o in order]
+        step //= 2
+    columns = [[a * side + b for a in range(side)] for b in range(side)]
+    for mine in mines[1:]:
+        parts[0][1], mine = lax.optimization_barrier((parts[0][1], mine))
+        slots = jnp.broadcast_to(mine[None], (side,) + mine.shape)
+        parts.append([lax.all_to_all(slots, "row", 0, 0, axis_index_groups=columns, tiled=True)])
+    left = arrange_left(lefts, tile)
     wt = final_matrix.reshape(width, width, -1).transpose(2, 1, 0).reshape(-1, width * width)
     total = None
     for part in range(PARTS):
         total = update_part(
-            side, seqs, order, part, lefts, parts[part], wt, total, final_intercept, pairwise_features
+            side, seqs, order, part, left, parts[part], wt, total, final_intercept, pairwise_features
         )
     return total.reshape(1, tile, tile, -1)
 

time: 54.6 us -> 74.3 us (1.36)
  waiting for transfers between devices: 7.35 us -> 27.8 us
    ppermute x15 -> x11, waiting for transfers between devices: 7.35 us -> 27.8 us  [swap(): lax.ppermute(x, 'row', [(i, i ^ da * side + db) for i in range(devices)])]
    ppermute x15 -> x11, starting transfers between devices: 19.5 us -> 14.3 us  [swap(): lax.ppermute(x, 'row', [(i, i ^ da * side + db) for i in range(devices)])]
    all_to_all x0 -> x1, starting transfers between devices: none -> 4.58 us  [local(): lax.all_to_all(slots, 'row', 0, 0, axis_index_groups=columns, tiled=True)]
    transpose x1, local copies, waits for them, and re-layouts: 1.05 us -> 0.1 us  [local(): final_matrix.reshape(width, width, -1).transpose(2, 1, 0)]
    broadcast_in_dim x0 -> x1, local copies, waits for them, and re-layouts: none -> 0.8 us  [local(): slots = jnp.broadcast_to(mine[None], (side,) + mine.shape)]
    pallas_call x2 -> x3, Pallas kernels: 21.8 us -> 21.6 us  [the longest x2 20.3 us: update_part(): pl.pallas_call(functools.partial(update_kernel, side, seqs, order, len(ri...]
  transfers between devices with their start and end apart: 15 -> 12, of which waited for: 5 -> 7; matrix products, arithmetic and copies ran while one was open for 2% -> 1% of each run, Pallas kernels for 18% -> 14%
where the time goes in v10:
time: 74.3 us; the launch traced here: 74.1 us
  waiting for transfers between devices  27.8 us (37%)
  Pallas kernels  26.2 us (35%)
  starting transfers between devices  18.9 us (25%)
  local copies, waits for them, and re-layouts  1.11 us (1%)
    ppermute x11, waiting for transfers between devices, swap(): lax.ppermute(x, 'row', [(i, i ^ da * side + db) for i in range(devices)])  27.8 us
    pallas_call x2, Pallas kernels, update_part(): pl.pallas_call(functools.partial(update_kernel, side, seqs, order, len(ri...  20.3 us
    ppermute x11, starting transfers between devices, swap(): lax.ppermute(x, 'row', [(i, i ^ da * side + db) for i in range(devices)])  14.3 us
    all_to_all x1, starting transfers between devices, local(): lax.all_to_all(slots, 'row', 0, 0, axis_index_groups=columns, tiled=True)  4.58 us
    pallas_call x1, Pallas kernels, project(): pl.pallas_call(functools.partial(project_kernel, side), in_specs=[pl.Bloc...  4.57 us
  transfers between devices with their start and end apart: 12, of which 7 were waited for; matrix products, arithmetic and copies ran while one was open for 1% of the time, Pallas kernels for 14%

profile of v10, /device:TPU:0, one launch (start us, length us, event | category | flops | bytes accessed | tf_op | source)
XLA Modules:
  0.0 74.1 jit_solution(6191845168787211360)
XLA Ops:
  0.0 0.0 copy-start
  0.0 4.6 %project.1 = (bf16[6,32,128]{2,1,0:T(8,128)(2,1)S(1)}, bf16[6,32,128]{2,1,0:T(8,128)(2,1)S(1)}, bf16[6,32,128]{2,1,0:T(8,128)(2,1)S(1)}, bf16[6,32,128]{2,1,0:T(...) custom-call(bf16[6,512,256]{2,1,0:T(8,128)(2,1)} %refs_0_.1, ...), custom_call_target="tpu_custom_call" | custom-call | tf_op jit(solution)/shard_map/project/pallas_call | solution.py:86
  4.6 3.1 %collective-permute-start = (bf16[6,32,128]{2,1,0:T(8,128)(2,1)S(1)}, bf16[6,32,128]{2,1,0:T(8,128)(2,1)S(1)}, u32[]{:S(2)}, u32[]{:S(2)}) collective-permute-start(bf16[6,32,128]{2,1,0:T(8,128)(2,1)S(1)} %get-tuple-element.19), channel_id=1, source_target_pairs={{0,4},{1,5},{2,6},{3,7},{4,0},{5,1},{6,2},{7,3},{8,12},{9,13},{10,... | collective-permute-start | bytes 147464 | tf_op jit(solution)/shard_map/ppermute | solution.py:276
  7.7 2.6 %collective-permute-start.1 = (bf16[6,32,128]{2,1,0:T(8,128)(2,1)S(1)}, bf16[6,32,128]{2,1,0:T(8,128)(2,1)S(1)}, u32[]{:S(2)}, u32[]{:S(2)}) collective-permute-start(bf16[6,32,128]{2,1,0:T(8,128)(2,1)S(1)} %get-tuple-element.20), channel_id=1, source_target_pairs={{0,8},{1,9},{2,10},{3,11},{4,12},{5,13},{6,14},{7,15},{8,0},{9,1},... | collective-permute-start | bytes 147464 | tf_op jit(solution)/shard_map/ppermute | solution.py:276
  10.3 0.0 collective-permute-start.2
  10.3 0.0 collective-permute-start.3
  10.3 1.7 %collective-permute-start.4 = (bf16[2,6,16,128]{3,2,1,0:T(8,128)(2,1)S(1)}, bf16[2,6,16,128]{3,2,1,0:T(8,128)(2,1)S(1)}, u32[]{:S(2)}, u32[]{:S(2)}) collective-permute-start(bf16[2,6,16,128]{3,2,1,0:T(8,128)(2,1)S(1)} %get-tuple-element.24), channel_id=1, source_target_pairs={{0,2},{1,3},{2,0},{3,1},{4,6},{5,7},{6,4},{7,5},{8,10},{9,11},{10,... | collective-permute-start | bytes 147464 | tf_op jit(solution)/shard_map/ppermute | solution.py:276
  12.0 0.0 collective-permute-done.3
  12.0 1.0 %collective-permute-start.5 = (bf16[2,6,16,128]{3,2,1,0:T(8,128)(2,1)S(1)}, bf16[2,6,16,128]{3,2,1,0:T(8,128)(2,1)S(1)}, u32[]{:S(2)}, u32[]{:S(2)}) collective-permute-start(bf16[2,6,16,128]{3,2,1,0:T(8,128)(2,1)S(1)} %get-tuple-element.25), channel_id=1, source_target_pairs={{0,3},{1,2},{2,1},{3,0},{4,7},{5,6},{6,5},{7,4},{8,11},{9,10},{10,... | collective-permute-start | bytes 147464 | tf_op jit(solution)/shard_map/ppermute | solution.py:276
  13.0 1.4 %collective-permute-done.4 = bf16[2,6,16,128]{3,2,1,0:T(8,128)(2,1)S(1)} collective-permute-done((bf16[2,6,16,128]{3,2,1,0:T(8,128)(2,1)S(1)}, bf16[2,6,16,128]{3,2,1,0:T(8,128)(2,1)S(1)}, u32[]{:S(2)}, u32[]{:S(2)}) %collective-permute-start.4) | collective-permute-done | bytes 49184 | tf_op jit(solution)/shard_map/ppermute | solution.py:276
  14.4 1.4 %collective-permute-done.5 = bf16[2,6,16,128]{3,2,1,0:T(8,128)(2,1)S(1)} collective-permute-done((bf16[2,6,16,128]{3,2,1,0:T(8,128)(2,1)S(1)}, bf16[2,6,16,128]{3,2,1,0:T(8,128)(2,1)S(1)}, u32[]{:S(2)}, u32[]{:S(2)}) %collective-permute-start.5) | collective-permute-done | bytes 49184 | tf_op jit(solution)/shard_map/ppermute | solution.py:276
  15.8 0.0 collective-permute-done
  15.8 0.0 collective-permute-done.1
  15.8 0.3 collective-permute-done.2
  16.2 1.6 %collective-permute-start.6 = (bf16[24,32,128]{2,1,0:T(8,128)(2,1)S(1)}, bf16[24,32,128]{2,1,0:T(8,128)(2,1)S(1)}, u32[]{:S(2)}, u32[]{:S(2)}) collective-permute-start(bf16[24,32,128]{2,1,0:T(8,128)(2,1)S(1)} %pad_maximum_fusion), channel_id=1, source_target_pairs={{0,2},{1,3},{2,0},{3,1},{4,6},{5,7},{6,4},{7,5},{8,10},{9,11},{10,... | collective-permute-start | bytes 589832 | tf_op jit(solution)/shard_map/ppermute | solution.py:276
  17.8 5.4 %collective-permute-done.6 = bf16[24,32,128]{2,1,0:T(8,128)(2,1)S(1)} collective-permute-done((bf16[24,32,128]{2,1,0:T(8,128)(2,1)S(1)}, bf16[24,32,128]{2,1,0:T(8,128)(2,1)S(1)}, u32[]{:S(2)}, u32[]{:S(2)}) %collective-permute-start.6) | collective-permute-done | bytes 196640 | tf_op jit(solution)/shard_map/ppermute | solution.py:276
  23.2 0.1 collective-permute-start.7
  23.3 0.4 collective-permute-start.8
  23.8 4.8 %collective-permute-done.8.refs_1_ = bf16[24,16,128]{2,1,0:T(8,128)(2,1)S(1)} collective-permute-done((bf16[24,16,128]{2,1,0:T(8,128)(2,1)S(1)}, bf16[24,16,128]{2,1,0:T(8,128)(2,1)S(1)}, u32[]{:S(2)}, u32[]{:S(2)}) %collective-permute-start.8) | collective-permute-done | bytes 98336 | tf_op jit(solution)/shard_map/ppermute | solution.py:276
  28.5 0.8 %broadcast_in_dim.25 = bf16[4,24,16,128]{3,2,1,0:T(8,128)(2,1)} broadcast(bf16[24,16,128]{2,1,0:T(8,128)(2,1)S(1)} %get-tuple-element.29), dimensions={1,2,3} | broadcast | bytes 491520 | tf_op jit(solution)/shard_map/broadcast_in_dim | solution.py:295
  29.3 4.6 %all-to-all-start = ((bf16[4,24,16,128]{3,2,1,0:T(8,128)(2,1)}), bf16[4,24,16,128]{3,2,1,0:T(8,128)(2,1)S(1)}, u32[]{:S(2)}, u32[]{:S(2)}) async-start(bf16[4,24,16,128]{3,2,1,0:T(8,128)(2,1)} %broadcast_in_dim.25), calls=%async_computation | async-start | bytes 786432 | tf_op jit(solution)/shard_map/all_to_all | solution.py:296
  33.9 3.8 %collective-permute-start.10 = (bf16[24,16,128]{2,1,0:T(8,128)(2,1)S(1)}, bf16[24,16,128]{2,1,0:T(8,128)(2,1)S(1)}, u32[]{:S(2)}, u32[]{:S(2)}) collective-permute-start(bf16[24,16,128]{2,1,0:T(8,128)(2,1)S(1)} %get-tuple-element.27.refs_0_), channel_id=1, source_target_pairs={{0,12},{1,13},{2,14},{3,15},{4,8},{5,9},{6,10},{7,11},{8,4},{9,5},... | collective-permute-start | bytes 294920 | tf_op jit(solution)/shard_map/ppermute | solution.py:276
  37.7 0.0 collective-permute-start.9
  37.7 0.0 copy-done
  37.7 0.1 copy.14
  37.8 0.1 copy.16.refs_4_.refs_1_
  38.0 0.0 collective-permute-done.7.refs_1_
  38.0 1.3 %arrange_left.1.left_ref = bf16[32,128,128]{2,1,0:T(8,128)(2,1)S(1)} custom-call(bf16[48,32,128]{2,1,0:T(8,128)(2,1)S(1)} %constant_dynamic-update-slice_fusion.refs_0_, bf16[48,32,128]{2,1,0:T(8,128)(2,1)S(1)} %collective-permute-done.7.refs_1_), custom_call_target="tpu_custom_call" | custom-call | flops 1048576 | bytes 8388608 | tf_op jit(solution)/shard_map/arrange_left/pallas_call | solution.py:123
  39.3 8.1 %collective-permute-done.10.refs_3_ = bf16[24,16,128]{2,1,0:T(8,128)(2,1)S(1)} collective-permute-done((bf16[24,16,128]{2,1,0:T(8,128)(2,1)S(1)}, bf16[24,16,128]{2,1,0:T(8,128)(2,1)S(1)}, u32[]{:S(2)}, u32[]{:S(2)}) %collective-permute-start.10) | collective-permute-done | bytes 98336 | tf_op jit(solution)/shard_map/ppermute | solution.py:276
  47.4 6.4 %collective-permute-done.9.refs_2_ = bf16[24,16,128]{2,1,0:T(8,128)(2,1)S(1)} collective-permute-done((bf16[24,16,128]{2,1,0:T(8,128)(2,1)S(1)}, bf16[24,16,128]{2,1,0:T(8,128)(2,1)S(1)}, u32[]{:S(2)}, u32[]{:S(2)}) %collective-permute-start.9) | collective-permute-done | bytes 98336 | tf_op jit(solution)/shard_map/ppermute | solution.py:276
  53.8 9.0 %update_0.1.refs_2_ = f32[32,2,128,256]{3,2,1,0:T(8,128)} custom-call(bf16[32,128,128]{2,1,0:T(8,128)(2,1)S(1)} %arrange_left.1.left_ref, bf16[24,16,128]{2,1,0:T(8,128)(2,1)S(1)} %get-tuple-element.27.refs_0_, bf16[24,16,128]{2,1,0:T(8,128)(2,1)S(1)} %collective-permute-done.8.refs_1_, bf16[24,16,128]{2,1,0:T(8,128)(2,1)S(1)} %collective-permute-done.9.refs_2_, ...), custom_call_target="tpu_custom_call" | custom-call | flops 3758096384 | bytes 16777216 | tf_op jit(solution)/shard_map/update_0/pallas_call | solution.py:226
  62.8 0.0 all-to-all-done.refs_0_
  62.8 11.3 %update_1.1 = bf16[4,32,128,128]{3,2,1,0:T(8,128)(2,1)} custom-call(bf16[32,128,128]{2,1,0:T(8,128)(2,1)S(1)} %arrange_left.1.left_ref, bf16[4,24,16,128]{3,2,1,0:T(8,128)(2,1)S(1)} %all-to-all-done.refs_0_, bf16[128,1024]{1,0:T(8,128)(2,1)S(1)} %copy.16.refs_4_.refs_1_, f32[32,2,128,256]{3,2,1,0:T(8,128)} %update_0.1.refs_2_, f32[1,128]{1,0:T(1,128)} %bitcast.38, ...), custom_call_target="tpu_custom_call" | custom-call | flops 3758096384 | bytes 16777216 | tf_op jit(solution)/shard_map/update_1/pallas_call | solution.py:226
  (8 shorter events, 0.1 us)
Async XLA Ops:
  0.0 37.7 %copy-start = (bf16[1024,128]{1,0:T(8,128)(2,1)S(1)}, bf16[1024,128]{1,0:T(8,128)(2,1)}, u32[]{:S(2)}) copy-start(bf16[1024,128]{1,0:T(8,128)(2,1)} %param.18) | copy-start | bytes 786436
  4.6 11.2 %collective-permute-start = (bf16[6,32,128]{2,1,0:T(8,128)(2,1)S(1)}, bf16[6,32,128]{2,1,0:T(8,128)(2,1)S(1)}, u32[]{:S(2)}, u32[]{:S(2)}) collective-permute-start(bf16[6,32,128]{2,1,0:T(8,128)(2,1)S(1)} %get-tuple-element.19), channel_id=1, source_target_pairs={{0,4},{1,5},{2,6},{3,7},{4,0},{5,1},{6,2},{7,3},{8,12},{9,13},{10,... | collective-permute-start | bytes 147464 | tf_op jit(solution)/shard_map/ppermute | solution.py:276
  7.7 8.2 %collective-permute-start.1 = (bf16[6,32,128]{2,1,0:T(8,128)(2,1)S(1)}, bf16[6,32,128]{2,1,0:T(8,128)(2,1)S(1)}, u32[]{:S(2)}, u32[]{:S(2)}) collective-permute-start(bf16[6,32,128]{2,1,0:T(8,128)(2,1)S(1)} %get-tuple-element.20), channel_id=1, source_target_pairs={{0,8},{1,9},{2,10},{3,11},{4,12},{5,13},{6,14},{7,15},{8,0},{9,1},... | collective-permute-start | bytes 147464 | tf_op jit(solution)/shard_map/ppermute | solution.py:276
  10.3 5.9 %collective-permute-start.2 = (bf16[6,32,128]{2,1,0:T(8,128)(2,1)S(1)}, bf16[6,32,128]{2,1,0:T(8,128)(2,1)S(1)}, u32[]{:S(2)}, u32[]{:S(2)}) collective-permute-start(bf16[6,32,128]{2,1,0:T(8,128)(2,1)S(1)} %get-tuple-element.21), channel_id=1, source_target_pairs={{0,12},{1,13},{2,14},{3,15},{4,8},{5,9},{6,10},{7,11},{8,4},{9,5},... | collective-permute-start | bytes 147464 | tf_op jit(solution)/shard_map/ppermute | solution.py:276
  10.3 1.7 %collective-permute-start.3 = (bf16[2,6,16,128]{3,2,1,0:T(8,128)(2,1)S(1)}, bf16[2,6,16,128]{3,2,1,0:T(8,128)(2,1)S(1)}, u32[]{:S(2)}, u32[]{:S(2)}) collective-permute-start(bf16[2,6,16,128]{3,2,1,0:T(8,128)(2,1)S(1)} %get-tuple-element.23), channel_id=1, source_target_pairs={{0,1},{1,0},{2,3},{3,2},{4,5},{5,4},{6,7},{7,6},{8,9},{9,8},{10,11... | collective-permute-start | bytes 147464 | tf_op jit(solution)/shard_map/ppermute | solution.py:276
  10.3 4.2 %collective-permute-start.4 = (bf16[2,6,16,128]{3,2,1,0:T(8,128)(2,1)S(1)}, bf16[2,6,16,128]{3,2,1,0:T(8,128)(2,1)S(1)}, u32[]{:S(2)}, u32[]{:S(2)}) collective-permute-start(bf16[2,6,16,128]{3,2,1,0:T(8,128)(2,1)S(1)} %get-tuple-element.24), channel_id=1, source_target_pairs={{0,2},{1,3},{2,0},{3,1},{4,6},{5,7},{6,4},{7,5},{8,10},{9,11},{10,... | collective-permute-start | bytes 147464 | tf_op jit(solution)/shard_map/ppermute | solution.py:276
  12.0 3.8 %collective-permute-start.5 = (bf16[2,6,16,128]{3,2,1,0:T(8,128)(2,1)S(1)}, bf16[2,6,16,128]{3,2,1,0:T(8,128)(2,1)S(1)}, u32[]{:S(2)}, u32[]{:S(2)}) collective-permute-start(bf16[2,6,16,128]{3,2,1,0:T(8,128)(2,1)S(1)} %get-tuple-element.25), channel_id=1, source_target_pairs={{0,3},{1,2},{2,1},{3,0},{4,7},{5,6},{6,5},{7,4},{8,11},{9,10},{10,... | collective-permute-start | bytes 147464 | tf_op jit(solution)/shard_map/ppermute | solution.py:276
  16.2 7.0 %collective-permute-start.6 = (bf16[24,32,128]{2,1,0:T(8,128)(2,1)S(1)}, bf16[24,32,128]{2,1,0:T(8,128)(2,1)S(1)}, u32[]{:S(2)}, u32[]{:S(2)}) collective-permute-start(bf16[24,32,128]{2,1,0:T(8,128)(2,1)S(1)} %pad_maximum_fusion), channel_id=1, source_target_pairs={{0,2},{1,3},{2,0},{3,1},{4,6},{5,7},{6,4},{7,5},{8,10},{9,11},{10,... | collective-permute-start | bytes 589832 | tf_op jit(solution)/shard_map/ppermute | solution.py:276
  23.2 14.8 %collective-permute-start.7 = (bf16[48,32,128]{2,1,0:T(8,128)(2,1)S(1)}, bf16[48,32,128]{2,1,0:T(8,128)(2,1)S(1)}, u32[]{:S(2)}, u32[]{:S(2)}) collective-permute-start(bf16[48,32,128]{2,1,0:T(8,128)(2,1)S(1)} %constant_dynamic-update-slice_fusion.refs_0_), channel_id=1, source_target_pairs={{0,1},{1,0},{2,3},{3,2},{4,5},{5,4},{6,7},{7,6},{8,9},{9,8},{10,11... | collective-permute-start | bytes 1179656 | tf_op jit(solution)/shard_map/ppermute | solution.py:276
  23.3 5.2 %collective-permute-start.8 = (bf16[24,16,128]{2,1,0:T(8,128)(2,1)S(1)}, bf16[24,16,128]{2,1,0:T(8,128)(2,1)S(1)}, u32[]{:S(2)}, u32[]{:S(2)}) collective-permute-start(bf16[24,16,128]{2,1,0:T(8,128)(2,1)S(1)} %get-tuple-element.27.refs_0_), channel_id=1, source_target_pairs={{0,4},{1,5},{2,6},{3,7},{4,0},{5,1},{6,2},{7,3},{8,12},{9,13},{10,... | collective-permute-start | bytes 294920 | tf_op jit(solution)/shard_map/ppermute | solution.py:276
  29.3 33.5 %all-to-all-start = ((bf16[4,24,16,128]{3,2,1,0:T(8,128)(2,1)}), bf16[4,24,16,128]{3,2,1,0:T(8,128)(2,1)S(1)}, u32[]{:S(2)}, u32[]{:S(2)}) async-start(bf16[4,24,16,128]{3,2,1,0:T(8,128)(2,1)} %broadcast_in_dim.25), calls=%async_computation | async-start | bytes 786432 | tf_op jit(solution)/shard_map/all_to_all | solution.py:296
  33.9 13.5 %collective-permute-start.10 = (bf16[24,16,128]{2,1,0:T(8,128)(2,1)S(1)}, bf16[24,16,128]{2,1,0:T(8,128)(2,1)S(1)}, u32[]{:S(2)}, u32[]{:S(2)}) collective-permute-start(bf16[24,16,128]{2,1,0:T(8,128)(2,1)S(1)} %get-tuple-element.27.refs_0_), channel_id=1, source_target_pairs={{0,12},{1,13},{2,14},{3,15},{4,8},{5,9},{6,10},{7,11},{8,4},{9,5},... | collective-permute-start | bytes 294920 | tf_op jit(solution)/shard_map/ppermute | solution.py:276
  37.7 16.1 %collective-permute-start.9 = (bf16[24,16,128]{2,1,0:T(8,128)(2,1)S(1)}, bf16[24,16,128]{2,1,0:T(8,128)(2,1)S(1)}, u32[]{:S(2)}, u32[]{:S(2)}) collective-permute-start(bf16[24,16,128]{2,1,0:T(8,128)(2,1)S(1)} %get-tuple-element.27.refs_0_), channel_id=1, source_target_pairs={{0,8},{1,9},{2,10},{3,11},{4,12},{5,13},{6,14},{7,15},{8,0},{9,1},... | collective-permute-start | bytes 294920 | tf_op jit(solution)/shard_map/ppermute | solution.py:276

commit v11 on v10

--- a/solution.py
+++ b/solution.py
@@ -132,30 +132,29 @@
     )(*lefts)
 
 
-def update_kernel(side, seqs, order, rights, first, last, left_ref, *refs):
-    right_refs, refs = refs[:rights], refs[rights:]
+def update_kernel(side, seqs, group, first, last, left_ref, *refs):
+    right_refs, refs = refs[:side], refs[side:]
     wt_ref, refs = refs[0], refs[1:]
     if not first:
         before_ref, refs = refs[0], refs[1:]
     if last:
         bias_ref, pair_ref, refs = refs[0], refs[1], refs[2:]
     out_ref, right_wide, right_flat, outer = refs
-    group, lanes, depth = left_ref.shape
-    some, tile = right_refs[0].shape[-2:]
+    rows, lanes, depth = left_ref.shape
+    _, some, tile = right_refs[0].shape
     halves = outer.shape[0] // group
     pack = 2 * halves
     width = lanes // pack
     seq_total = side * side * seqs
+    at = pl.program_id(0) * group
 
     @pl.when(pl.program_id(0) == 0)
     def _():
-        place_a = lax.axis_index("row") // side
         for dz in range(side):
-            source = right_refs[dz] if rights > 1 else right_refs[0].at[place_a ^ dz]
-            for k, dy in enumerate(order):
-                to = (k * side + dz) * seqs
+            for dy in range(side):
+                to = (dy * side + dz) * seqs
                 right_wide[to * some : (to + seqs) * some] = (
-                    source[dy * seqs : (dy + 1) * seqs]
+                    right_refs[dz][dy * seqs : (dy + 1) * seqs]
                     .astype(jnp.float32)
                     .reshape(seqs * some, tile)
                 )
@@ -168,10 +167,10 @@
                 pl.ds(e, depth, stride=some), :
             ].astype(jnp.bfloat16)
 
-    for q in range(group):
+    def outer_products(q):
         for n in range(some // 2):
             both = jnp.dot(
-                left_ref[q],
+                left_ref[at + q],
                 right_flat[:, 2 * n * tile : (2 * n + 2) * tile],
                 preferred_element_type=jnp.float32,
             ).astype(jnp.bfloat16)
@@ -183,21 +182,29 @@
                         e * width : (e + 1) * width,
                         (h % 2) * tile : (h % 2 + 1) * tile,
                     ] = both[h * width : (h + 1) * width, k * tile : (k + 1) * tile]
-    for q in range(group):
+
+    def project_back(q):
         for g in range(halves):
             update = jnp.dot(wt_ref[...], outer[q * halves + g], preferred_element_type=jnp.float32)
             if not first:
-                update = update + before_ref[q, g]
+                update = update + before_ref[at + q, g]
             if not last:
-                out_ref[q, g] = update
+                out_ref[at + q, g] = update
                 continue
             for k in range(2):
                 h = 2 * g + k
                 share = update[:, k * tile : (k + 1) * tile].T * (1.0 / seq_total) + bias_ref[...]
-                out_ref[h, q] = (pair_ref[h, q].astype(jnp.float32) + share).astype(jnp.bfloat16)
-
-
-def update_part(side, seqs, order, part, left, right, wt, before, bias, pair):
+                old = pair_ref[h, at + q].astype(jnp.float32)
+                out_ref[h, q] = (old + share).astype(jnp.bfloat16)
+
+    for q in range(group + 1):
+        if q < group:
+            outer_products(q)
+        if q > 0:
+            project_back(q - 1)
+
+
+def update_part(side, seqs, part, left, right, wt, before, bias, pair):
     rows, lanes, depth = left.shape
     some, tile = right[0].shape[-2:]
     chans = wt.shape[0]
@@ -206,27 +213,20 @@
     halves = pack // 2
     group = 8
     first, last = part == 0, part == PARTS - 1
-    whole = lambda shape: pl.BlockSpec(shape, lambda g: (0,) * len(shape))
-    sum_spec = pl.BlockSpec((group, halves, chans, 2 * tile), lambda g: (g, 0, 0, 0))
-    pair_spec = pl.BlockSpec((pack, group, tile, chans), lambda g: (0, g, 0, 0))
-    operands = [left] + list(right) + [wt]
-    specs = [pl.BlockSpec((group, lanes, depth), lambda g: (g, 0, 0))]
-    specs += [whole(x.shape) for x in right]
-    specs.append(pl.BlockSpec((chans, some * width), lambda g: (0, part)))
+    in_vmem = pl.BlockSpec(memory_space=pltpu.VMEM)
+    operands = [left] + list(right) + [wt[:, part * some * width : (part + 1) * some * width]]
     if not first:
         operands.append(before)
-        specs.append(sum_spec)
     if last:
-        operands += [in_hbm(bias[None]), in_hbm(pair.reshape(pack, rows, tile, chans))]
-        specs += [whole((1, chans)), pair_spec]
-        out_shape, out_spec = jax.ShapeDtypeStruct((pack, rows, tile, chans), jnp.bfloat16), pair_spec
+        operands += [bias[None], pair.reshape(pack, rows, tile, chans)]
+        out_shape = jax.ShapeDtypeStruct((pack, rows, tile, chans), jnp.bfloat16)
+        out_spec = pl.BlockSpec((pack, group, tile, chans), lambda g: (0, g, 0, 0))
     else:
-        out_shape = jax.ShapeDtypeStruct((rows, halves, chans, 2 * tile), jnp.float32)
-        out_spec = sum_spec
+        out_shape, out_spec = pltpu.VMEM((rows, halves, chans, 2 * tile), jnp.float32), in_vmem
     return pl.pallas_call(
-        functools.partial(update_kernel, side, seqs, order, len(right), first, last),
+        functools.partial(update_kernel, side, seqs, group, first, last),
         grid=(rows // group,),
-        in_specs=specs,
+        in_specs=[in_vmem] * len(operands),
         out_specs=out_spec,
         out_shape=out_shape,
         scratch_shapes=[
@@ -234,7 +234,7 @@
             pltpu.VMEM((depth, some * tile), jnp.bfloat16),
             pltpu.VMEM((group * halves, some * width, 2 * tile), jnp.bfloat16),
         ],
-        compiler_params=pltpu.CompilerParams(vmem_limit_bytes=48 * MIB),
+        compiler_params=pltpu.CompilerParams(vmem_limit_bytes=24 * MIB),
         cost_estimate=pl.CostEstimate(
             flops=2 * tile * tile * some * width * (side * side * seqs + chans),
             bytes_accessed=16 * MIB,
@@ -280,26 +280,14 @@
     left = jnp.concatenate(left)
     mines = [jnp.concatenate([x[part] for x in right]) for part in range(PARTS)]
     left, *mines = lax.optimization_barrier((left, *mines))
-    parts = [[mines[0]] + [swap(mines[0], d, 0) for d in range(1, side)]]
-    order = [0]
-    lefts = [left]
-    step = side // 2
-    while step > 0:
-        left = jnp.concatenate(lefts) if len(lefts) > 1 else lefts[0]
-        lefts = [left, swap(left, 0, step)]
-        order += [o ^ step for o in order]
-        step //= 2
-    columns = [[a * side + b for a in range(side)] for b in range(side)]
-    for mine in mines[1:]:
-        parts[0][1], mine = lax.optimization_barrier((parts[0][1], mine))
-        slots = jnp.broadcast_to(mine[None], (side,) + mine.shape)
-        parts.append([lax.all_to_all(slots, "row", 0, 0, axis_index_groups=columns, tiled=True)])
+    lefts = [left] + [swap(left, 0, d) for d in range(1, side)]
+    parts = [[mine] + [swap(mine, d, 0) for d in range(1, side)] for mine in mines]
     left = arrange_left(lefts, tile)
     wt = final_matrix.reshape(width, width, -1).transpose(2, 1, 0).reshape(-1, width * width)
     total = None
     for part in range(PARTS):
         total = update_part(
-            side, seqs, order, part, left, parts[part], wt, total, final_intercept, pairwise_features
+            side, seqs, part, left, parts[part], wt, total, final_intercept, pairwise_features
         )
     return total.reshape(1, tile, tile, -1)
 

time: 74.3 us -> 52.6 us (0.71)
  waiting for transfers between devices: 27.8 us -> 8.66 us
  Pallas kernels: 26.2 us -> 23.1 us
    ppermute x11 -> x15, waiting for transfers between devices: 27.8 us -> 8.66 us  [swap(): lax.ppermute(x, 'row', [(i, i ^ da * side + db) for i in range(devices)])]
    ppermute x11 -> x15, starting transfers between devices: 14.3 us -> 19.2 us  [swap(): lax.ppermute(x, 'row', [(i, i ^ da * side + db) for i in range(devices)])]
    all_to_all x1 -> x0, starting transfers between devices: 4.58 us -> none  [local(): lax.all_to_all(slots, 'row', 0, 0, axis_index_groups=columns, tiled=True)]
    pallas_call x2, Pallas kernels: 20.3 us -> 17.2 us  [update_part(): pl.pallas_call(functools.partial(update_kernel, side, seqs, group, first,...]
    transpose x1, local copies, waits for them, and re-layouts: 0.1 us -> 1.05 us  [local(): final_matrix.reshape(width, width, -1).transpose(2, 1, 0)]
    broadcast_in_dim x1 -> x0, local copies, waits for them, and re-layouts: 0.8 us -> none  [local(): slots = jnp.broadcast_to(mine[None], (side,) + mine.shape)]
  transfers between devices with their start and end apart: 12 -> 15, of which waited for: 7 -> 4; matrix products, arithmetic and copies ran while one was open for 1% -> 3% of each run, Pallas kernels for 14% -> 17%
where the time goes in v11:
time: 52.6 us; the launch traced here: 52.4 us
  Pallas kernels  23.1 us (44%)
  starting transfers between devices  19.2 us (37%)
  waiting for transfers between devices  8.66 us (16%)
  local copies, waits for them, and re-layouts  1.33 us (3%)
    ppermute x15, starting transfers between devices, swap(): lax.ppermute(x, 'row', [(i, i ^ da * side + db) for i in range(devices)])  19.2 us
    pallas_call x2, Pallas kernels, update_part(): pl.pallas_call(functools.partial(update_kernel, side, seqs, group, first,...  17.2 us
    ppermute x15, waiting for transfers between devices, swap(): lax.ppermute(x, 'row', [(i, i ^ da * side + db) for i in range(devices)])  8.66 us
    pallas_call x1, Pallas kernels, project(): pl.pallas_call(functools.partial(project_kernel, side), in_specs=[pl.Bloc...  4.52 us
    pallas_call x1, Pallas kernels, arrange_left(): pl.pallas_call(functools.partial(arrange_kernel, seq_total), in_specs=[pl...  1.33 us
    transpose x1, local copies, waits for them, and re-layouts, local(): final_matrix.reshape(width, width, -1).transpose(2, 1, 0)  1.05 us
  transfers between devices with their start and end apart: 15, of which 4 were waited for; matrix products, arithmetic and copies ran while one was open for 3% of the time, Pallas kernels for 17%

profile of v11, /device:TPU:0, one launch (start us, length us, event | category | flops | bytes accessed | tf_op | source)
XLA Modules:
  0.0 52.4 jit_solution(7812341355862934370)
XLA Ops:
  0.0 4.5 %project.1 = (bf16[6,32,128]{2,1,0:T(8,128)(2,1)S(1)}, bf16[6,32,128]{2,1,0:T(8,128)(2,1)S(1)}, bf16[6,32,128]{2,1,0:T(8,128)(2,1)S(1)}, bf16[6,32,128]{2,1,0:T(...) custom-call(bf16[6,512,256]{2,1,0:T(8,128)(2,1)} %refs_0_.1, ...), custom_call_target="tpu_custom_call" | custom-call | tf_op jit(solution)/shard_map/project/pallas_call | solution.py:86
  4.5 3.1 %collective-permute-start = (bf16[6,32,128]{2,1,0:T(8,128)(2,1)S(1)}, bf16[6,32,128]{2,1,0:T(8,128)(2,1)S(1)}, u32[]{:S(2)}, u32[]{:S(2)}) collective-permute-start(bf16[6,32,128]{2,1,0:T(8,128)(2,1)S(1)} %get-tuple-element.17), channel_id=1, source_target_pairs={{0,4},{1,5},{2,6},{3,7},{4,0},{5,1},{6,2},{7,3},{8,12},{9,13},{10,... | collective-permute-start | bytes 147464 | tf_op jit(solution)/shard_map/ppermute | solution.py:276
  7.6 2.6 %collective-permute-start.1 = (bf16[6,32,128]{2,1,0:T(8,128)(2,1)S(1)}, bf16[6,32,128]{2,1,0:T(8,128)(2,1)S(1)}, u32[]{:S(2)}, u32[]{:S(2)}) collective-permute-start(bf16[6,32,128]{2,1,0:T(8,128)(2,1)S(1)} %get-tuple-element.18), channel_id=1, source_target_pairs={{0,8},{1,9},{2,10},{3,11},{4,12},{5,13},{6,14},{7,15},{8,0},{9,1},... | collective-permute-start | bytes 147464 | tf_op jit(solution)/shard_map/ppermute | solution.py:276
  10.2 0.0 collective-permute-start.2
  10.2 0.0 collective-permute-start.3
  10.2 1.7 %collective-permute-start.4 = (bf16[2,6,16,128]{3,2,1,0:T(8,128)(2,1)S(1)}, bf16[2,6,16,128]{3,2,1,0:T(8,128)(2,1)S(1)}, u32[]{:S(2)}, u32[]{:S(2)}) collective-permute-start(bf16[2,6,16,128]{3,2,1,0:T(8,128)(2,1)S(1)} %get-tuple-element.22), channel_id=1, source_target_pairs={{0,2},{1,3},{2,0},{3,1},{4,6},{5,7},{6,4},{7,5},{8,10},{9,11},{10,... | collective-permute-start | bytes 147464 | tf_op jit(solution)/shard_map/ppermute | solution.py:276
  12.0 0.0 collective-permute-done.3
  12.0 1.0 %collective-permute-start.5 = (bf16[2,6,16,128]{3,2,1,0:T(8,128)(2,1)S(1)}, bf16[2,6,16,128]{3,2,1,0:T(8,128)(2,1)S(1)}, u32[]{:S(2)}, u32[]{:S(2)}) collective-permute-start(bf16[2,6,16,128]{3,2,1,0:T(8,128)(2,1)S(1)} %get-tuple-element.23), channel_id=1, source_target_pairs={{0,3},{1,2},{2,1},{3,0},{4,7},{5,6},{6,5},{7,4},{8,11},{9,10},{10,... | collective-permute-start | bytes 147464 | tf_op jit(solution)/shard_map/ppermute | solution.py:276
  13.0 1.4 %collective-permute-done.4 = bf16[2,6,16,128]{3,2,1,0:T(8,128)(2,1)S(1)} collective-permute-done((bf16[2,6,16,128]{3,2,1,0:T(8,128)(2,1)S(1)}, bf16[2,6,16,128]{3,2,1,0:T(8,128)(2,1)S(1)}, u32[]{:S(2)}, u32[]{:S(2)}) %collective-permute-start.4) | collective-permute-done | bytes 49184 | tf_op jit(solution)/shard_map/ppermute | solution.py:276
  14.4 1.4 %collective-permute-done.5 = bf16[2,6,16,128]{3,2,1,0:T(8,128)(2,1)S(1)} collective-permute-done((bf16[2,6,16,128]{3,2,1,0:T(8,128)(2,1)S(1)}, bf16[2,6,16,128]{3,2,1,0:T(8,128)(2,1)S(1)}, u32[]{:S(2)}, u32[]{:S(2)}) %collective-permute-start.5) | collective-permute-done | bytes 49184 | tf_op jit(solution)/shard_map/ppermute | solution.py:276
  15.8 0.0 collective-permute-done
  15.8 0.0 collective-permute-done.1
  15.8 0.3 collective-permute-done.2
  16.1 1.0 %collective-permute-start.8 = (bf16[24,32,128]{2,1,0:T(8,128)(2,1)S(1)}, bf16[24,32,128]{2,1,0:T(8,128)(2,1)S(1)}, u32[]{:S(2)}, u32[]{:S(2)}) collective-permute-start(bf16[24,32,128]{2,1,0:T(8,128)(2,1)S(1)} %pad_maximum_fusion.refs_0_), channel_id=1, source_target_pairs={{0,3},{1,2},{2,1},{3,0},{4,7},{5,6},{6,5},{7,4},{8,11},{9,10},{10,... | collective-permute-start | bytes 589832 | tf_op jit(solution)/shard_map/ppermute | solution.py:276
  17.1 1.1 %copy.14 = bf16[128,32,32]{0,2,1:T(8,128)(2,1)S(1)} copy(bf16[128,32,32]{0,1,2:T(8,128)(2,1)} %bitcast.32) | data formatting | bytes 524288 | tf_op jit(solution)/shard_map/transpose | solution.py:286
  18.2 3.4 %collective-permute-start.14 = (bf16[24,16,128]{2,1,0:T(8,128)(2,1)S(1)}, bf16[24,16,128]{2,1,0:T(8,128)(2,1)S(1)}, u32[]{:S(2)}, u32[]{:S(2)}) collective-permute-start(bf16[24,16,128]{2,1,0:T(8,128)(2,1)S(1)} %get-tuple-element.26.refs_0_), channel_id=1, source_target_pairs={{0,12},{1,13},{2,14},{3,15},{4,8},{5,9},{6,10},{7,11},{8,4},{9,5},... | collective-permute-start | bytes 294920 | tf_op jit(solution)/shard_map/ppermute | solution.py:276
  21.5 0.0 collective-permute-start.13
  21.5 1.1 %collective-permute-start.12 = (bf16[24,16,128]{2,1,0:T(8,128)(2,1)S(1)}, bf16[24,16,128]{2,1,0:T(8,128)(2,1)S(1)}, u32[]{:S(2)}, u32[]{:S(2)}) collective-permute-start(bf16[24,16,128]{2,1,0:T(8,128)(2,1)S(1)} %get-tuple-element.26.refs_0_), channel_id=1, source_target_pairs={{0,4},{1,5},{2,6},{3,7},{4,0},{5,1},{6,2},{7,3},{8,12},{9,13},{10,... | collective-permute-start | bytes 294920 | tf_op jit(solution)/shard_map/ppermute | solution.py:276
  22.6 0.9 %collective-permute-start.7 = (bf16[24,32,128]{2,1,0:T(8,128)(2,1)S(1)}, bf16[24,32,128]{2,1,0:T(8,128)(2,1)S(1)}, u32[]{:S(2)}, u32[]{:S(2)}) collective-permute-start(bf16[24,32,128]{2,1,0:T(8,128)(2,1)S(1)} %pad_maximum_fusion.refs_0_), channel_id=1, source_target_pairs={{0,2},{1,3},{2,0},{3,1},{4,6},{5,7},{6,4},{7,5},{8,10},{9,11},{10,... | collective-permute-start | bytes 589832 | tf_op jit(solution)/shard_map/ppermute | solution.py:276
  23.5 0.0 collective-permute-done.8.refs_3_
  23.5 0.0 collective-permute-start.6
  23.5 0.1 copy.18.refs_4_
  23.6 0.1 copy.17.refs_4_
  23.8 5.5 %collective-permute-done.7.refs_2_ = bf16[24,32,128]{2,1,0:T(8,128)(2,1)S(1)} collective-permute-done((bf16[24,32,128]{2,1,0:T(8,128)(2,1)S(1)}, bf16[24,32,128]{2,1,0:T(8,128)(2,1)S(1)}, u32[]{:S(2)}, u32[]{:S(2)}) %collective-permute-start.7) | collective-permute-done | bytes 196640 | tf_op jit(solution)/shard_map/ppermute | solution.py:276
  29.3 2.9 %collective-permute-start.11 = (bf16[24,16,128]{2,1,0:T(8,128)(2,1)S(1)}, bf16[24,16,128]{2,1,0:T(8,128)(2,1)S(1)}, u32[]{:S(2)}, u32[]{:S(2)}) collective-permute-start(bf16[24,16,128]{2,1,0:T(8,128)(2,1)S(1)} %get-tuple-element.25.refs_0_), channel_id=1, source_target_pairs={{0,12},{1,13},{2,14},{3,15},{4,8},{5,9},{6,10},{7,11},{8,4},{9,5},... | collective-permute-start | bytes 294920 | tf_op jit(solution)/shard_map/ppermute | solution.py:276
  32.2 0.0 collective-permute-done.6.refs_1_
  32.3 0.0 collective-permute-start.10
  32.3 1.3 %arrange_left.1.left_ref = bf16[32,128,128]{2,1,0:T(8,128)(2,1)S(1)} custom-call(bf16[24,32,128]{2,1,0:T(8,128)(2,1)S(1)} %pad_maximum_fusion.refs_0_, bf16[24,32,128]{2,1,0:T(8,128)(2,1)S(1)} %collective-permute-done.6.refs_1_, bf16[24,32,128]{2,1,0:T(8,128)(2,1)S(1)} %collective-permute-done.7.refs_2_, bf16[24,32,128]{2,1,0:T(8,128)(2,1)S(1)} %collective-permute-done.8.refs_3_), custom_call_target="tpu_custom_call" | custom-call | flops 1048576 | bytes 8388608 | tf_op jit(solution)/shard_map/arrange_left/pallas_call | solution.py:123
  33.6 0.0 copy-start
  33.6 0.0 copy-start.1
  33.6 0.0 collective-permute-done.14.refs_3_
  33.6 1.5 %collective-permute-start.9 = (bf16[24,16,128]{2,1,0:T(8,128)(2,1)S(1)}, bf16[24,16,128]{2,1,0:T(8,128)(2,1)S(1)}, u32[]{:S(2)}, u32[]{:S(2)}) collective-permute-start(bf16[24,16,128]{2,1,0:T(8,128)(2,1)S(1)} %get-tuple-element.25.refs_0_), channel_id=1, source_target_pairs={{0,4},{1,5},{2,6},{3,7},{4,0},{5,1},{6,2},{7,3},{8,12},{9,13},{10,... | collective-permute-start | bytes 294920 | tf_op jit(solution)/shard_map/ppermute | solution.py:276
  35.1 0.0 collective-permute-done.13.refs_2_
  35.1 0.0 collective-permute-done.12.refs_1_
  35.1 7.8 %update_0.1.refs_5_ = f32[32,2,128,256]{3,2,1,0:T(8,128)S(1)} custom-call(bf16[32,128,128]{2,1,0:T(8,128)(2,1)S(1)} %arrange_left.1.left_ref, bf16[24,16,128]{2,1,0:T(8,128)(2,1)S(1)} %get-tuple-element.26.refs_0_, bf16[24,16,128]{2,1,0:T(8,128)(2,1)S(1)} %collective-permute-done.12.refs_1_, bf16[24,16,128]{2,1,0:T(8,128)(2,1)S(1)} %collective-permute-done.13.refs_2_, ...), custom_call_target="tpu_custom_call" | custom-call | flops 3758096384 | bytes 16777216 | tf_op jit(solution)/shard_map/update_0/pallas_call | solution.py:226
  42.9 0.0 collective-permute-done.11.refs_3_
  43.0 0.0 collective-permute-done.10.refs_2_
  43.0 0.0 collective-permute-done.9.refs_1_
  43.0 0.0 copy-done
  43.0 0.0 copy-done.1
  43.0 9.4 %update_1.1 = bf16[4,32,128,128]{3,2,1,0:T(8,128)(2,1)} custom-call(bf16[32,128,128]{2,1,0:T(8,128)(2,1)S(1)} %arrange_left.1.left_ref, bf16[24,16,128]{2,1,0:T(8,128)(2,1)S(1)} %get-tuple-element.25.refs_0_, bf16[24,16,128]{2,1,0:T(8,128)(2,1)S(1)} %collective-permute-done.9.refs_1_, bf16[24,16,128]{2,1,0:T(8,128)(2,1)S(1)} %collective-permute-done.10.refs_2_, ...), custom_call_target="tpu_custom_call" | custom-call | flops 3758096384 | bytes 16777216 | tf_op jit(solution)/shard_map/update_1/pallas_call | solution.py:226
  (7 shorter events, 0.1 us)
Async XLA Ops:
  4.5 11.2 %collective-permute-start = (bf16[6,32,128]{2,1,0:T(8,128)(2,1)S(1)}, bf16[6,32,128]{2,1,0:T(8,128)(2,1)S(1)}, u32[]{:S(2)}, u32[]{:S(2)}) collective-permute-start(bf16[6,32,128]{2,1,0:T(8,128)(2,1)S(1)} %get-tuple-element.17), channel_id=1, source_target_pairs={{0,4},{1,5},{2,6},{3,7},{4,0},{5,1},{6,2},{7,3},{8,12},{9,13},{10,... | collective-permute-start | bytes 147464 | tf_op jit(solution)/shard_map/ppermute | solution.py:276
  7.6 8.2 %collective-permute-start.1 = (bf16[6,32,128]{2,1,0:T(8,128)(2,1)S(1)}, bf16[6,32,128]{2,1,0:T(8,128)(2,1)S(1)}, u32[]{:S(2)}, u32[]{:S(2)}) collective-permute-start(bf16[6,32,128]{2,1,0:T(8,128)(2,1)S(1)} %get-tuple-element.18), channel_id=1, source_target_pairs={{0,8},{1,9},{2,10},{3,11},{4,12},{5,13},{6,14},{7,15},{8,0},{9,1},... | collective-permute-start | bytes 147464 | tf_op jit(solution)/shard_map/ppermute | solution.py:276
  10.2 5.9 %collective-permute-start.2 = (bf16[6,32,128]{2,1,0:T(8,128)(2,1)S(1)}, bf16[6,32,128]{2,1,0:T(8,128)(2,1)S(1)}, u32[]{:S(2)}, u32[]{:S(2)}) collective-permute-start(bf16[6,32,128]{2,1,0:T(8,128)(2,1)S(1)} %get-tuple-element.19), channel_id=1, source_target_pairs={{0,12},{1,13},{2,14},{3,15},{4,8},{5,9},{6,10},{7,11},{8,4},{9,5},... | collective-permute-start | bytes 147464 | tf_op jit(solution)/shard_map/ppermute | solution.py:276
  10.2 1.7 %collective-permute-start.3 = (bf16[2,6,16,128]{3,2,1,0:T(8,128)(2,1)S(1)}, bf16[2,6,16,128]{3,2,1,0:T(8,128)(2,1)S(1)}, u32[]{:S(2)}, u32[]{:S(2)}) collective-permute-start(bf16[2,6,16,128]{3,2,1,0:T(8,128)(2,1)S(1)} %get-tuple-element.21), channel_id=1, source_target_pairs={{0,1},{1,0},{2,3},{3,2},{4,5},{5,4},{6,7},{7,6},{8,9},{9,8},{10,11... | collective-permute-start | bytes 147464 | tf_op jit(solution)/shard_map/ppermute | solution.py:276
  10.2 4.2 %collective-permute-start.4 = (bf16[2,6,16,128]{3,2,1,0:T(8,128)(2,1)S(1)}, bf16[2,6,16,128]{3,2,1,0:T(8,128)(2,1)S(1)}, u32[]{:S(2)}, u32[]{:S(2)}) collective-permute-start(bf16[2,6,16,128]{3,2,1,0:T(8,128)(2,1)S(1)} %get-tuple-element.22), channel_id=1, source_target_pairs={{0,2},{1,3},{2,0},{3,1},{4,6},{5,7},{6,4},{7,5},{8,10},{9,11},{10,... | collective-permute-start | bytes 147464 | tf_op jit(solution)/shard_map/ppermute | solution.py:276
  12.0 3.8 %collective-permute-start.5 = (bf16[2,6,16,128]{3,2,1,0:T(8,128)(2,1)S(1)}, bf16[2,6,16,128]{3,2,1,0:T(8,128)(2,1)S(1)}, u32[]{:S(2)}, u32[]{:S(2)}) collective-permute-start(bf16[2,6,16,128]{3,2,1,0:T(8,128)(2,1)S(1)} %get-tuple-element.23), channel_id=1, source_target_pairs={{0,3},{1,2},{2,1},{3,0},{4,7},{5,6},{6,5},{7,4},{8,11},{9,10},{10,... | collective-permute-start | bytes 147464 | tf_op jit(solution)/shard_map/ppermute | solution.py:276
  16.1 7.4 %collective-permute-start.8 = (bf16[24,32,128]{2,1,0:T(8,128)(2,1)S(1)}, bf16[24,32,128]{2,1,0:T(8,128)(2,1)S(1)}, u32[]{:S(2)}, u32[]{:S(2)}) collective-permute-start(bf16[24,32,128]{2,1,0:T(8,128)(2,1)S(1)} %pad_maximum_fusion.refs_0_), channel_id=1, source_target_pairs={{0,3},{1,2},{2,1},{3,0},{4,7},{5,6},{6,5},{7,4},{8,11},{9,10},{10,... | collective-permute-start | bytes 589832 | tf_op jit(solution)/shard_map/ppermute | solution.py:276
  18.2 15.4 %collective-permute-start.14 = (bf16[24,16,128]{2,1,0:T(8,128)(2,1)S(1)}, bf16[24,16,128]{2,1,0:T(8,128)(2,1)S(1)}, u32[]{:S(2)}, u32[]{:S(2)}) collective-permute-start(bf16[24,16,128]{2,1,0:T(8,128)(2,1)S(1)} %get-tuple-element.26.refs_0_), channel_id=1, source_target_pairs={{0,12},{1,13},{2,14},{3,15},{4,8},{5,9},{6,10},{7,11},{8,4},{9,5},... | collective-permute-start | bytes 294920 | tf_op jit(solution)/shard_map/ppermute | solution.py:276
  21.5 13.6 %collective-permute-start.13 = (bf16[24,16,128]{2,1,0:T(8,128)(2,1)S(1)}, bf16[24,16,128]{2,1,0:T(8,128)(2,1)S(1)}, u32[]{:S(2)}, u32[]{:S(2)}) collective-permute-start(bf16[24,16,128]{2,1,0:T(8,128)(2,1)S(1)} %get-tuple-element.26.refs_0_), channel_id=1, source_target_pairs={{0,8},{1,9},{2,10},{3,11},{4,12},{5,13},{6,14},{7,15},{8,0},{9,1},... | collective-permute-start | bytes 294920 | tf_op jit(solution)/shard_map/ppermute | solution.py:276
  21.5 13.6 %collective-permute-start.12 = (bf16[24,16,128]{2,1,0:T(8,128)(2,1)S(1)}, bf16[24,16,128]{2,1,0:T(8,128)(2,1)S(1)}, u32[]{:S(2)}, u32[]{:S(2)}) collective-permute-start(bf16[24,16,128]{2,1,0:T(8,128)(2,1)S(1)} %get-tuple-element.26.refs_0_), channel_id=1, source_target_pairs={{0,4},{1,5},{2,6},{3,7},{4,0},{5,1},{6,2},{7,3},{8,12},{9,13},{10,... | collective-permute-start | bytes 294920 | tf_op jit(solution)/shard_map/ppermute | solution.py:276
  22.6 6.7 %collective-permute-start.7 = (bf16[24,32,128]{2,1,0:T(8,128)(2,1)S(1)}, bf16[24,32,128]{2,1,0:T(8,128)(2,1)S(1)}, u32[]{:S(2)}, u32[]{:S(2)}) collective-permute-start(bf16[24,32,128]{2,1,0:T(8,128)(2,1)S(1)} %pad_maximum_fusion.refs_0_), channel_id=1, source_target_pairs={{0,2},{1,3},{2,0},{3,1},{4,6},{5,7},{6,4},{7,5},{8,10},{9,11},{10,... | collective-permute-start | bytes 589832 | tf_op jit(solution)/shard_map/ppermute | solution.py:276
  23.5 8.8 %collective-permute-start.6 = (bf16[24,32,128]{2,1,0:T(8,128)(2,1)S(1)}, bf16[24,32,128]{2,1,0:T(8,128)(2,1)S(1)}, u32[]{:S(2)}, u32[]{:S(2)}) collective-permute-start(bf16[24,32,128]{2,1,0:T(8,128)(2,1)S(1)} %pad_maximum_fusion.refs_0_), channel_id=1, source_target_pairs={{0,1},{1,0},{2,3},{3,2},{4,5},{5,4},{6,7},{7,6},{8,9},{9,8},{10,11... | collective-permute-start | bytes 589832 | tf_op jit(solution)/shard_map/ppermute | solution.py:276
  29.3 13.6 %collective-permute-start.11 = (bf16[24,16,128]{2,1,0:T(8,128)(2,1)S(1)}, bf16[24,16,128]{2,1,0:T(8,128)(2,1)S(1)}, u32[]{:S(2)}, u32[]{:S(2)}) collective-permute-start(bf16[24,16,128]{2,1,0:T(8,128)(2,1)S(1)} %get-tuple-element.25.refs_0_), channel_id=1, source_target_pairs={{0,12},{1,13},{2,14},{3,15},{4,8},{5,9},{6,10},{7,11},{8,4},{9,5},... | collective-permute-start | bytes 294920 | tf_op jit(solution)/shard_map/ppermute | solution.py:276
  32.3 10.7 %collective-permute-start.10 = (bf16[24,16,128]{2,1,0:T(8,128)(2,1)S(1)}, bf16[24,16,128]{2,1,0:T(8,128)(2,1)S(1)}, u32[]{:S(2)}, u32[]{:S(2)}) collective-permute-start(bf16[24,16,128]{2,1,0:T(8,128)(2,1)S(1)} %get-tuple-element.25.refs_0_), channel_id=1, source_target_pairs={{0,8},{1,9},{2,10},{3,11},{4,12},{5,13},{6,14},{7,15},{8,0},{9,1},... | collective-permute-start | bytes 294920 | tf_op jit(solution)/shard_map/ppermute | solution.py:276
  33.6 9.4 %copy-start = (bf16[1,128,128,128]{3,2,1,0:T(8,128)(2,1)S(1)}, bf16[1,128,128,128]{3,2,1,0:T(8,128)(2,1)}, u32[]{:S(2)}) copy-start(bf16[1,128,128,128]{3,2,1,0:T(8,128)(2,1)} %param.11) | copy-start | bytes 12582916
  33.6 9.4 %copy-start.1 = (f32[128]{0:T(128)S(1)}, f32[128]{0:T(128)}, u32[]{:S(2)}) copy-start(f32[128]{0:T(128)} %param.19) | copy-start | bytes 1540
  33.6 9.3 %collective-permute-start.9 = (bf16[24,16,128]{2,1,0:T(8,128)(2,1)S(1)}, bf16[24,16,128]{2,1,0:T(8,128)(2,1)S(1)}, u32[]{:S(2)}, u32[]{:S(2)}) collective-permute-start(bf16[24,16,128]{2,1,0:T(8,128)(2,1)S(1)} %get-tuple-element.25.refs_0_), channel_id=1, source_target_pairs={{0,4},{1,5},{2,6},{3,7},{4,0},{5,1},{6,2},{7,3},{8,12},{9,13},{10,... | collective-permute-start | bytes 294920 | tf_op jit(solution)/shard_map/ppermute | solution.py:276

commit v12 on v11

--- a/solution.py
+++ b/solution.py
@@ -281,8 +281,19 @@
     mines = [jnp.concatenate([x[part] for x in right]) for part in range(PARTS)]
     left, *mines = lax.optimization_barrier((left, *mines))
     lefts = [left] + [swap(left, 0, d) for d in range(1, side)]
-    parts = [[mine] + [swap(mine, d, 0) for d in range(1, side)] for mine in mines]
+    near = swap(jnp.stack(mines), 1, 0)
+    parts = [[mines[0], near[0]] + [swap(mines[0], d, 0) for d in range(2, side)]]
+    for part in range(1, PARTS):
+        pieces = [mines[part], near[part]]
+        mask = 2
+        while mask < side:
+            got = swap(jnp.concatenate(pieces), mask, 0)
+            count = mines[part].shape[0]
+            pieces += [got[k * count : (k + 1) * count] for k in range(mask)]
+            mask *= 2
+        parts.append(pieces)
     left = arrange_left(lefts, tile)
+    near, final_matrix = lax.optimization_barrier((near, final_matrix))
     wt = final_matrix.reshape(width, width, -1).transpose(2, 1, 0).reshape(-1, width * width)
     total = None
     for part in range(PARTS):

time: 52.6 us -> 50 us (0.951)
  starting transfers between devices: 19.2 us -> 15.1 us
  waiting for transfers between devices: 8.66 us -> 9.96 us
    ppermute x15 -> x13, starting transfers between devices: 19.2 us -> 15.1 us  [swap(): lax.ppermute(x, 'row', [(i, i ^ da * side + db) for i in range(devices)])]
    ppermute x15 -> x13, waiting for transfers between devices: 8.66 us -> 9.96 us  [swap(): lax.ppermute(x, 'row', [(i, i ^ da * side + db) for i in range(devices)])]
  transfers between devices with their start and end apart: 15 -> 13, of which waited for: 4 -> 6; matrix products, arithmetic and copies ran while one was open for 3% -> 3% of each run, Pallas kernels for 17% -> 18%
where the time goes in v12:
time: 50 us; the launch traced here: 49.8 us
  Pallas kernels  23.1 us (46%)
  starting transfers between devices  15.1 us (30%)
  waiting for transfers between devices  9.96 us (20%)
  local copies, waits for them, and re-layouts  1.36 us (3%)
    pallas_call x2, Pallas kernels, update_part(): pl.pallas_call(functools.partial(update_kernel, side, seqs, group, first,...  17.2 us
    ppermute x13, starting transfers between devices, swap(): lax.ppermute(x, 'row', [(i, i ^ da * side + db) for i in range(devices)])  15.1 us
    ppermute x13, waiting for transfers between devices, swap(): lax.ppermute(x, 'row', [(i, i ^ da * side + db) for i in range(devices)])  9.96 us
    pallas_call x1, Pallas kernels, project(): pl.pallas_call(functools.partial(project_kernel, side), in_specs=[pl.Bloc...  4.52 us
    pallas_call x1, Pallas kernels, arrange_left(): pl.pallas_call(functools.partial(arrange_kernel, seq_total), in_specs=[pl...  1.33 us
    transpose x1, local copies, waits for them, and re-layouts, local(): final_matrix.reshape(width, width, -1).transpose(2, 1, 0)  1.05 us
  transfers between devices with their start and end apart: 13, of which 6 were waited for; matrix products, arithmetic and copies ran while one was open for 3% of the time, Pallas kernels for 18%

profile of v12, /device:TPU:0, one launch (start us, length us, event | category | flops | bytes accessed | tf_op | source)
XLA Modules:
  0.0 49.8 jit_solution(14542733175406845039)
XLA Ops:
  0.0 4.5 %project.1 = (bf16[6,32,128]{2,1,0:T(8,128)(2,1)S(1)}, bf16[6,32,128]{2,1,0:T(8,128)(2,1)S(1)}, bf16[6,32,128]{2,1,0:T(8,128)(2,1)S(1)}, bf16[6,32,128]{2,1,0:T(...) custom-call(bf16[6,512,256]{2,1,0:T(8,128)(2,1)} %refs_0_.1, ...), custom_call_target="tpu_custom_call" | custom-call | tf_op jit(solution)/shard_map/project/pallas_call | solution.py:86
  4.5 3.1 %collective-permute-start = (bf16[6,32,128]{2,1,0:T(8,128)(2,1)S(1)}, bf16[6,32,128]{2,1,0:T(8,128)(2,1)S(1)}, u32[]{:S(2)}, u32[]{:S(2)}) collective-permute-start(bf16[6,32,128]{2,1,0:T(8,128)(2,1)S(1)} %get-tuple-element.18), channel_id=1, source_target_pairs={{0,4},{1,5},{2,6},{3,7},{4,0},{5,1},{6,2},{7,3},{8,12},{9,13},{10,... | collective-permute-start | bytes 147464 | tf_op jit(solution)/shard_map/ppermute | solution.py:276
  7.6 2.6 %collective-permute-start.1 = (bf16[6,32,128]{2,1,0:T(8,128)(2,1)S(1)}, bf16[6,32,128]{2,1,0:T(8,128)(2,1)S(1)}, u32[]{:S(2)}, u32[]{:S(2)}) collective-permute-start(bf16[6,32,128]{2,1,0:T(8,128)(2,1)S(1)} %get-tuple-element.19), channel_id=1, source_target_pairs={{0,8},{1,9},{2,10},{3,11},{4,12},{5,13},{6,14},{7,15},{8,0},{9,1},... | collective-permute-start | bytes 147464 | tf_op jit(solution)/shard_map/ppermute | solution.py:276
  10.2 0.0 collective-permute-start.2
  10.2 0.0 collective-permute-start.3
  10.2 1.7 %collective-permute-start.4 = (bf16[2,6,16,128]{3,2,1,0:T(8,128)(2,1)S(1)}, bf16[2,6,16,128]{3,2,1,0:T(8,128)(2,1)S(1)}, u32[]{:S(2)}, u32[]{:S(2)}) collective-permute-start(bf16[2,6,16,128]{3,2,1,0:T(8,128)(2,1)S(1)} %get-tuple-element.23), channel_id=1, source_target_pairs={{0,2},{1,3},{2,0},{3,1},{4,6},{5,7},{6,4},{7,5},{8,10},{9,11},{10,... | collective-permute-start | bytes 147464 | tf_op jit(solution)/shard_map/ppermute | solution.py:276
  12.0 0.0 collective-permute-done.3
  12.0 1.0 %collective-permute-start.5 = (bf16[2,6,16,128]{3,2,1,0:T(8,128)(2,1)S(1)}, bf16[2,6,16,128]{3,2,1,0:T(8,128)(2,1)S(1)}, u32[]{:S(2)}, u32[]{:S(2)}) collective-permute-start(bf16[2,6,16,128]{3,2,1,0:T(8,128)(2,1)S(1)} %get-tuple-element.24), channel_id=1, source_target_pairs={{0,3},{1,2},{2,1},{3,0},{4,7},{5,6},{6,5},{7,4},{8,11},{9,10},{10,... | collective-permute-start | bytes 147464 | tf_op jit(solution)/shard_map/ppermute | solution.py:276
  13.0 1.4 %collective-permute-done.4 = bf16[2,6,16,128]{3,2,1,0:T(8,128)(2,1)S(1)} collective-permute-done((bf16[2,6,16,128]{3,2,1,0:T(8,128)(2,1)S(1)}, bf16[2,6,16,128]{3,2,1,0:T(8,128)(2,1)S(1)}, u32[]{:S(2)}, u32[]{:S(2)}) %collective-permute-start.4) | collective-permute-done | bytes 49184 | tf_op jit(solution)/shard_map/ppermute | solution.py:276
  14.4 1.4 %collective-permute-done.5 = bf16[2,6,16,128]{3,2,1,0:T(8,128)(2,1)S(1)} collective-permute-done((bf16[2,6,16,128]{3,2,1,0:T(8,128)(2,1)S(1)}, bf16[2,6,16,128]{3,2,1,0:T(8,128)(2,1)S(1)}, u32[]{:S(2)}, u32[]{:S(2)}) %collective-permute-start.5) | collective-permute-done | bytes 49184 | tf_op jit(solution)/shard_map/ppermute | solution.py:276
  15.8 0.0 collective-permute-done
  15.8 0.0 collective-permute-done.1
  15.8 0.3 collective-permute-done.2
  16.2 0.5 collective-permute-start.9
  16.6 3.0 %collective-permute-start.12 = (bf16[24,16,128]{2,1,0:T(8,128)(2,1)S(1)}, bf16[24,16,128]{2,1,0:T(8,128)(2,1)S(1)}, u32[]{:S(2)}, u32[]{:S(2)}) collective-permute-start(bf16[24,16,128]{2,1,0:T(8,128)(2,1)S(1)} %get-tuple-element.27.refs_0_), channel_id=1, source_target_pairs={{0,12},{1,13},{2,14},{3,15},{4,8},{5,9},{6,10},{7,11},{8,4},{9,5},... | collective-permute-start | bytes 294920 | tf_op jit(solution)/shard_map/ppermute | solution.py:276
  19.6 0.5 collective-permute-start.11
  20.1 0.3 collective-permute-start.8
  20.5 0.9 %collective-permute-start.7 = (bf16[24,32,128]{2,1,0:T(8,128)(2,1)S(1)}, bf16[24,32,128]{2,1,0:T(8,128)(2,1)S(1)}, u32[]{:S(2)}, u32[]{:S(2)}) collective-permute-start(bf16[24,32,128]{2,1,0:T(8,128)(2,1)S(1)} %pad_maximum_fusion.refs_0_), channel_id=1, source_target_pairs={{0,2},{1,3},{2,0},{3,1},{4,6},{5,7},{6,4},{7,5},{8,10},{9,11},{10,... | collective-permute-start | bytes 589832 | tf_op jit(solution)/shard_map/ppermute | solution.py:276
  21.3 5.5 %collective-permute-done.9 = bf16[2,24,16,128]{3,2,1,0:T(8,128)(2,1)S(1)} collective-permute-done((bf16[2,24,16,128]{3,2,1,0:T(8,128)(2,1)S(1)}, bf16[2,24,16,128]{3,2,1,0:T(8,128)(2,1)S(1)}, u32[]{:S(2)}, u32[]{:S(2)}) %collective-permute-start.9) | collective-permute-done | bytes 196640 | tf_op jit(solution)/shard_map/ppermute | solution.py:276
  26.8 0.0 collective-permute-start.6
  26.8 1.1 %copy.14 = bf16[128,32,32]{0,2,1:T(8,128)(2,1)S(1)} copy(bf16[128,32,32]{0,1,2:T(8,128)(2,1)} %bitcast.40) | data formatting | bytes 524288 | tf_op jit(solution)/shard_map/transpose | solution.py:297
  27.9 0.1 copy.18.refs_4_
  28.0 0.1 copy.17.refs_4_
  28.2 0.0 collective-permute-done.8.refs_3_
  28.2 1.6 %collective-permute-start.10 = (bf16[48,16,128]{2,1,0:T(8,128)(2,1)S(1)}, bf16[48,16,128]{2,1,0:T(8,128)(2,1)S(1)}, u32[]{:S(2)}, u32[]{:S(2)}) collective-permute-start(bf16[48,16,128]{2,1,0:T(8,128)(2,1)S(1)} %pad_maximum_fusion.2), channel_id=1, source_target_pairs={{0,8},{1,9},{2,10},{3,11},{4,12},{5,13},{6,14},{7,15},{8,0},{9,1},... | collective-permute-start | bytes 589832 | tf_op jit(solution)/shard_map/ppermute | solution.py:276
  29.8 1.3 %collective-permute-done.7.refs_2_ = bf16[24,32,128]{2,1,0:T(8,128)(2,1)S(1)} collective-permute-done((bf16[24,32,128]{2,1,0:T(8,128)(2,1)S(1)}, bf16[24,32,128]{2,1,0:T(8,128)(2,1)S(1)}, u32[]{:S(2)}, u32[]{:S(2)}) %collective-permute-start.7) | collective-permute-done | bytes 196640 | tf_op jit(solution)/shard_map/ppermute | solution.py:276
  31.0 0.0 collective-permute-done.6.refs_1_
  31.1 1.3 %arrange_left.1.left_ref = bf16[32,128,128]{2,1,0:T(8,128)(2,1)S(1)} custom-call(bf16[24,32,128]{2,1,0:T(8,128)(2,1)S(1)} %pad_maximum_fusion.refs_0_, bf16[24,32,128]{2,1,0:T(8,128)(2,1)S(1)} %collective-permute-done.6.refs_1_, bf16[24,32,128]{2,1,0:T(8,128)(2,1)S(1)} %collective-permute-done.7.refs_2_, bf16[24,32,128]{2,1,0:T(8,128)(2,1)S(1)} %collective-permute-done.8.refs_3_), custom_call_target="tpu_custom_call" | custom-call | flops 1048576 | bytes 8388608 | tf_op jit(solution)/shard_map/arrange_left/pallas_call | solution.py:123
  32.4 0.0 collective-permute-done.12.refs_3_
  32.4 0.0 collective-permute-done.11.refs_2_
  32.4 0.0 copy-start
  32.4 0.0 copy-start.1
  32.4 7.8 %update_0.1.refs_5_ = f32[32,2,128,256]{3,2,1,0:T(8,128)S(1)} custom-call(bf16[32,128,128]{2,1,0:T(8,128)(2,1)S(1)} %arrange_left.1.left_ref, bf16[24,16,128]{2,1,0:T(8,128)(2,1)S(1)} %get-tuple-element.27.refs_0_, bf16[24,16,128]{2,1,0:T(8,128)(2,1)S(1)} %get-tuple-element.31.refs_1_, bf16[24,16,128]{2,1,0:T(8,128)(2,1)S(1)} %collective-permute-done.11.refs_2_, ...), custom_call_target="tpu_custom_call" | custom-call | flops 3758096384 | bytes 16777216 | tf_op jit(solution)/shard_map/update_0/pallas_call | solution.py:226
  40.3 0.1 collective-permute-done.10
  40.4 0.0 copy-done
  40.4 0.0 copy-done.1
  40.4 9.4 %update_1.1 = bf16[4,32,128,128]{3,2,1,0:T(8,128)(2,1)} custom-call(bf16[32,128,128]{2,1,0:T(8,128)(2,1)S(1)} %arrange_left.1.left_ref, bf16[24,16,128]{2,1,0:T(8,128)(2,1)S(1)} %get-tuple-element.26.refs_0_, bf16[24,16,128]{2,1,0:T(8,128)(2,1)S(1)} %get-tuple-element.32.refs_1_, bf16[24,16,128]{2,1,0:T(8,128)(2,1)S(1)} %get-tuple-element.34.refs_2_, ...), custom_call_target="tpu_custom_call" | custom-call | flops 3758096384 | bytes 16777216 | tf_op jit(solution)/shard_map/update_1/pallas_call | solution.py:226
  (11 shorter events, 0.2 us)
Async XLA Ops:
  4.5 11.2 %collective-permute-start = (bf16[6,32,128]{2,1,0:T(8,128)(2,1)S(1)}, bf16[6,32,128]{2,1,0:T(8,128)(2,1)S(1)}, u32[]{:S(2)}, u32[]{:S(2)}) collective-permute-start(bf16[6,32,128]{2,1,0:T(8,128)(2,1)S(1)} %get-tuple-element.18), channel_id=1, source_target_pairs={{0,4},{1,5},{2,6},{3,7},{4,0},{5,1},{6,2},{7,3},{8,12},{9,13},{10,... | collective-permute-start | bytes 147464 | tf_op jit(solution)/shard_map/ppermute | solution.py:276
  7.6 8.2 %collective-permute-start.1 = (bf16[6,32,128]{2,1,0:T(8,128)(2,1)S(1)}, bf16[6,32,128]{2,1,0:T(8,128)(2,1)S(1)}, u32[]{:S(2)}, u32[]{:S(2)}) collective-permute-start(bf16[6,32,128]{2,1,0:T(8,128)(2,1)S(1)} %get-tuple-element.19), channel_id=1, source_target_pairs={{0,8},{1,9},{2,10},{3,11},{4,12},{5,13},{6,14},{7,15},{8,0},{9,1},... | collective-permute-start | bytes 147464 | tf_op jit(solution)/shard_map/ppermute | solution.py:276
  10.2 5.9 %collective-permute-start.2 = (bf16[6,32,128]{2,1,0:T(8,128)(2,1)S(1)}, bf16[6,32,128]{2,1,0:T(8,128)(2,1)S(1)}, u32[]{:S(2)}, u32[]{:S(2)}) collective-permute-start(bf16[6,32,128]{2,1,0:T(8,128)(2,1)S(1)} %get-tuple-element.20), channel_id=1, source_target_pairs={{0,12},{1,13},{2,14},{3,15},{4,8},{5,9},{6,10},{7,11},{8,4},{9,5},... | collective-permute-start | bytes 147464 | tf_op jit(solution)/shard_map/ppermute | solution.py:276
  10.2 1.7 %collective-permute-start.3 = (bf16[2,6,16,128]{3,2,1,0:T(8,128)(2,1)S(1)}, bf16[2,6,16,128]{3,2,1,0:T(8,128)(2,1)S(1)}, u32[]{:S(2)}, u32[]{:S(2)}) collective-permute-start(bf16[2,6,16,128]{3,2,1,0:T(8,128)(2,1)S(1)} %get-tuple-element.22), channel_id=1, source_target_pairs={{0,1},{1,0},{2,3},{3,2},{4,5},{5,4},{6,7},{7,6},{8,9},{9,8},{10,11... | collective-permute-start | bytes 147464 | tf_op jit(solution)/shard_map/ppermute | solution.py:276
  10.2 4.2 %collective-permute-start.4 = (bf16[2,6,16,128]{3,2,1,0:T(8,128)(2,1)S(1)}, bf16[2,6,16,128]{3,2,1,0:T(8,128)(2,1)S(1)}, u32[]{:S(2)}, u32[]{:S(2)}) collective-permute-start(bf16[2,6,16,128]{3,2,1,0:T(8,128)(2,1)S(1)} %get-tuple-element.23), channel_id=1, source_target_pairs={{0,2},{1,3},{2,0},{3,1},{4,6},{5,7},{6,4},{7,5},{8,10},{9,11},{10,... | collective-permute-start | bytes 147464 | tf_op jit(solution)/shard_map/ppermute | solution.py:276
  12.0 3.8 %collective-permute-start.5 = (bf16[2,6,16,128]{3,2,1,0:T(8,128)(2,1)S(1)}, bf16[2,6,16,128]{3,2,1,0:T(8,128)(2,1)S(1)}, u32[]{:S(2)}, u32[]{:S(2)}) collective-permute-start(bf16[2,6,16,128]{3,2,1,0:T(8,128)(2,1)S(1)} %get-tuple-element.24), channel_id=1, source_target_pairs={{0,3},{1,2},{2,1},{3,0},{4,7},{5,6},{6,5},{7,4},{8,11},{9,10},{10,... | collective-permute-start | bytes 147464 | tf_op jit(solution)/shard_map/ppermute | solution.py:276
  16.2 10.6 %collective-permute-start.9 = (bf16[2,24,16,128]{3,2,1,0:T(8,128)(2,1)S(1)}, bf16[2,24,16,128]{3,2,1,0:T(8,128)(2,1)S(1)}, u32[]{:S(2)}, u32[]{:S(2)}) collective-permute-start(bf16[2,24,16,128]{3,2,1,0:T(8,128)(2,1)S(1)} %pad_maximum_fusion.1), channel_id=1, source_target_pairs={{0,4},{1,5},{2,6},{3,7},{4,0},{5,1},{6,2},{7,3},{8,12},{9,13},{10,... | collective-permute-start | bytes 589832 | tf_op jit(solution)/shard_map/ppermute | solution.py:276
  16.6 15.8 %collective-permute-start.12 = (bf16[24,16,128]{2,1,0:T(8,128)(2,1)S(1)}, bf16[24,16,128]{2,1,0:T(8,128)(2,1)S(1)}, u32[]{:S(2)}, u32[]{:S(2)}) collective-permute-start(bf16[24,16,128]{2,1,0:T(8,128)(2,1)S(1)} %get-tuple-element.27.refs_0_), channel_id=1, source_target_pairs={{0,12},{1,13},{2,14},{3,15},{4,8},{5,9},{6,10},{7,11},{8,4},{9,5},... | collective-permute-start | bytes 294920 | tf_op jit(solution)/shard_map/ppermute | solution.py:276
  19.6 12.8 %collective-permute-start.11 = (bf16[24,16,128]{2,1,0:T(8,128)(2,1)S(1)}, bf16[24,16,128]{2,1,0:T(8,128)(2,1)S(1)}, u32[]{:S(2)}, u32[]{:S(2)}) collective-permute-start(bf16[24,16,128]{2,1,0:T(8,128)(2,1)S(1)} %get-tuple-element.27.refs_0_), channel_id=1, source_target_pairs={{0,8},{1,9},{2,10},{3,11},{4,12},{5,13},{6,14},{7,15},{8,0},{9,1},... | collective-permute-start | bytes 294920 | tf_op jit(solution)/shard_map/ppermute | solution.py:276
  20.1 8.1 %collective-permute-start.8 = (bf16[24,32,128]{2,1,0:T(8,128)(2,1)S(1)}, bf16[24,32,128]{2,1,0:T(8,128)(2,1)S(1)}, u32[]{:S(2)}, u32[]{:S(2)}) collective-permute-start(bf16[24,32,128]{2,1,0:T(8,128)(2,1)S(1)} %pad_maximum_fusion.refs_0_), channel_id=1, source_target_pairs={{0,3},{1,2},{2,1},{3,0},{4,7},{5,6},{6,5},{7,4},{8,11},{9,10},{10,... | collective-permute-start | bytes 589832 | tf_op jit(solution)/shard_map/ppermute | solution.py:276
  20.5 10.6 %collective-permute-start.7 = (bf16[24,32,128]{2,1,0:T(8,128)(2,1)S(1)}, bf16[24,32,128]{2,1,0:T(8,128)(2,1)S(1)}, u32[]{:S(2)}, u32[]{:S(2)}) collective-permute-start(bf16[24,32,128]{2,1,0:T(8,128)(2,1)S(1)} %pad_maximum_fusion.refs_0_), channel_id=1, source_target_pairs={{0,2},{1,3},{2,0},{3,1},{4,6},{5,7},{6,4},{7,5},{8,10},{9,11},{10,... | collective-permute-start | bytes 589832 | tf_op jit(solution)/shard_map/ppermute | solution.py:276
  26.8 4.3 %collective-permute-start.6 = (bf16[24,32,128]{2,1,0:T(8,128)(2,1)S(1)}, bf16[24,32,128]{2,1,0:T(8,128)(2,1)S(1)}, u32[]{:S(2)}, u32[]{:S(2)}) collective-permute-start(bf16[24,32,128]{2,1,0:T(8,128)(2,1)S(1)} %pad_maximum_fusion.refs_0_), channel_id=1, source_target_pairs={{0,1},{1,0},{2,3},{3,2},{4,5},{5,4},{6,7},{7,6},{8,9},{9,8},{10,11... | collective-permute-start | bytes 589832 | tf_op jit(solution)/shard_map/ppermute | solution.py:276
  28.2 12.2 %collective-permute-start.10 = (bf16[48,16,128]{2,1,0:T(8,128)(2,1)S(1)}, bf16[48,16,128]{2,1,0:T(8,128)(2,1)S(1)}, u32[]{:S(2)}, u32[]{:S(2)}) collective-permute-start(bf16[48,16,128]{2,1,0:T(8,128)(2,1)S(1)} %pad_maximum_fusion.2), channel_id=1, source_target_pairs={{0,8},{1,9},{2,10},{3,11},{4,12},{5,13},{6,14},{7,15},{8,0},{9,1},... | collective-permute-start | bytes 589832 | tf_op jit(solution)/shard_map/ppermute | solution.py:276
  32.4 8.0 %copy-start = (bf16[1,128,128,128]{3,2,1,0:T(8,128)(2,1)S(1)}, bf16[1,128,128,128]{3,2,1,0:T(8,128)(2,1)}, u32[]{:S(2)}) copy-start(bf16[1,128,128,128]{3,2,1,0:T(8,128)(2,1)} %param.11) | copy-start | bytes 12582916
  32.4 8.0 %copy-start.1 = (f32[128]{0:T(128)S(1)}, f32[128]{0:T(128)}, u32[]{:S(2)}) copy-start(f32[128]{0:T(128)} %param.19) | copy-start | bytes 1540

commit v13 on v12

--- a/solution.py
+++ b/solution.py
@@ -132,8 +132,8 @@
     )(*lefts)
 
 
-def update_kernel(side, seqs, group, first, last, left_ref, *refs):
-    right_refs, refs = refs[:side], refs[side:]
+def update_kernel(side, seqs, order, rights, group, first, last, left_ref, *refs):
+    right_refs, refs = refs[:rights], refs[rights:]
     wt_ref, refs = refs[0], refs[1:]
     if not first:
         before_ref, refs = refs[0], refs[1:]
@@ -150,14 +150,17 @@
 
     @pl.when(pl.program_id(0) == 0)
     def _():
-        for dz in range(side):
-            for dy in range(side):
-                to = (dy * side + dz) * seqs
-                right_wide[to * some : (to + seqs) * some] = (
-                    right_refs[dz][dy * seqs : (dy + 1) * seqs]
-                    .astype(jnp.float32)
-                    .reshape(seqs * some, tile)
-                )
+        dz = 0
+        for ref in right_refs:
+            for start in range(0, ref.shape[0], side * seqs):
+                for k, dy in enumerate(order):
+                    to = (k * side + dz) * seqs
+                    right_wide[to * some : (to + seqs) * some] = (
+                        ref[start + dy * seqs : start + (dy + 1) * seqs]
+                        .astype(jnp.float32)
+                        .reshape(seqs * some, tile)
+                    )
+                dz += 1
         if depth > seq_total:
             right_wide[seq_total * some :] = jnp.zeros(
                 ((depth - seq_total) * some, tile), jnp.float32
@@ -204,7 +207,7 @@
             project_back(q - 1)
 
 
-def update_part(side, seqs, part, left, right, wt, before, bias, pair):
+def update_part(side, seqs, order, part, left, right, wt, before, bias, pair):
     rows, lanes, depth = left.shape
     some, tile = right[0].shape[-2:]
     chans = wt.shape[0]
@@ -224,7 +227,7 @@
     else:
         out_shape, out_spec = pltpu.VMEM((rows, halves, chans, 2 * tile), jnp.float32), in_vmem
     return pl.pallas_call(
-        functools.partial(update_kernel, side, seqs, group, first, last),
+        functools.partial(update_kernel, side, seqs, order, len(right), group, first, last),
         grid=(rows // group,),
         in_specs=[in_vmem] * len(operands),
         out_specs=out_spec,
@@ -280,16 +283,20 @@
     left = jnp.concatenate(left)
     mines = [jnp.concatenate([x[part] for x in right]) for part in range(PARTS)]
     left, *mines = lax.optimization_barrier((left, *mines))
-    lefts = [left] + [swap(left, 0, d) for d in range(1, side)]
+    lefts = [left]
+    order = [0]
+    mask = side // 2
+    while mask > 0:
+        lefts += [swap(jnp.concatenate(lefts), 0, mask)]
+        order += [o ^ mask for o in order]
+        mask //= 2
     near = swap(jnp.stack(mines), 1, 0)
     parts = [[mines[0], near[0]] + [swap(mines[0], d, 0) for d in range(2, side)]]
     for part in range(1, PARTS):
         pieces = [mines[part], near[part]]
         mask = 2
         while mask < side:
-            got = swap(jnp.concatenate(pieces), mask, 0)
-            count = mines[part].shape[0]
-            pieces += [got[k * count : (k + 1) * count] for k in range(mask)]
+            pieces.append(swap(jnp.concatenate(pieces), mask, 0))
             mask *= 2
         parts.append(pieces)
     left = arrange_left(lefts, tile)
@@ -297,8 +304,10 @@
     wt = final_matrix.reshape(width, width, -1).transpose(2, 1, 0).reshape(-1, width * width)
     total = None
     for part in range(PARTS):
+        if part > 0:
+            total, *parts[part] = lax.optimization_barrier((total, *parts[part]))
         total = update_part(
-            side, seqs, part, left, parts[part], wt, total, final_intercept, pairwise_features
+            side, seqs, order, part, left, parts[part], wt, total, final_intercept, pairwise_features
         )
     return total.reshape(1, tile, tile, -1)
 

time: 50 us -> 52.4 us (1.048)
  waiting for transfers between devices: 9.96 us -> 13.8 us
  local copies, waits for them, and re-layouts: 1.36 us -> 0.39 us
    ppermute x13 -> x12, waiting for transfers between devices: 9.96 us -> 13.8 us  [swap(): lax.ppermute(x, 'row', [(i, i ^ da * side + db) for i in range(devices)])]
    transpose x1, local copies, waits for them, and re-layouts: 1.05 us -> 0.1 us  [local(): final_matrix.reshape(width, width, -1).transpose(2, 1, 0)]
    ppermute x13 -> x12, starting transfers between devices: 15.1 us -> 14.7 us  [swap(): lax.ppermute(x, 'row', [(i, i ^ da * side + db) for i in range(devices)])]
  transfers between devices with their start and end apart: 13 -> 12, of which waited for: 6 -> 6; matrix products, arithmetic and copies ran while one was open for 3% -> 1% of each run, Pallas kernels for 18% -> 17%
where the time goes in v13:
time: 52.4 us; the launch traced here: 52.3 us
  Pallas kernels  23.1 us (44%)
  starting transfers between devices  14.7 us (28%)
  waiting for transfers between devices  13.8 us (26%)
    pallas_call x2, Pallas kernels, update_part(): pl.pallas_call(functools.partial(update_kernel, side, seqs, order, len(ri...  17.2 us
    ppermute x12, starting transfers between devices, swap(): lax.ppermute(x, 'row', [(i, i ^ da * side + db) for i in range(devices)])  14.7 us
    ppermute x12, waiting for transfers between devices, swap(): lax.ppermute(x, 'row', [(i, i ^ da * side + db) for i in range(devices)])  13.8 us
    pallas_call x1, Pallas kernels, project(): pl.pallas_call(functools.partial(project_kernel, side), in_specs=[pl.Bloc...  4.57 us
    pallas_call x1, Pallas kernels, arrange_left(): pl.pallas_call(functools.partial(arrange_kernel, seq_total), in_specs=[pl...  1.33 us
  transfers between devices with their start and end apart: 12, of which 6 were waited for; matrix products, arithmetic and copies ran while one was open for 1% of the time, Pallas kernels for 17%

profile of v13, /device:TPU:0, one launch (start us, length us, event | category | flops | bytes accessed | tf_op | source)
XLA Modules:
  0.0 52.3 jit_solution(15598549148120444985)
XLA Ops:
  0.0 0.0 copy-start.2
  0.0 4.6 %project.1 = (bf16[6,32,128]{2,1,0:T(8,128)(2,1)S(1)}, bf16[6,32,128]{2,1,0:T(8,128)(2,1)S(1)}, bf16[6,32,128]{2,1,0:T(8,128)(2,1)S(1)}, bf16[6,32,128]{2,1,0:T(...) custom-call(bf16[6,512,256]{2,1,0:T(8,128)(2,1)} %refs_0_.1, ...), custom_call_target="tpu_custom_call" | custom-call | tf_op jit(solution)/shard_map/project/pallas_call | solution.py:86
  4.6 3.1 %collective-permute-start = (bf16[6,32,128]{2,1,0:T(8,128)(2,1)S(1)}, bf16[6,32,128]{2,1,0:T(8,128)(2,1)S(1)}, u32[]{:S(2)}, u32[]{:S(2)}) collective-permute-start(bf16[6,32,128]{2,1,0:T(8,128)(2,1)S(1)} %get-tuple-element.22), channel_id=1, source_target_pairs={{0,4},{1,5},{2,6},{3,7},{4,0},{5,1},{6,2},{7,3},{8,12},{9,13},{10,... | collective-permute-start | bytes 147464 | tf_op jit(solution)/shard_map/ppermute | solution.py:279
  7.7 2.6 %collective-permute-start.1 = (bf16[6,32,128]{2,1,0:T(8,128)(2,1)S(1)}, bf16[6,32,128]{2,1,0:T(8,128)(2,1)S(1)}, u32[]{:S(2)}, u32[]{:S(2)}) collective-permute-start(bf16[6,32,128]{2,1,0:T(8,128)(2,1)S(1)} %get-tuple-element.23), channel_id=1, source_target_pairs={{0,8},{1,9},{2,10},{3,11},{4,12},{5,13},{6,14},{7,15},{8,0},{9,1},... | collective-permute-start | bytes 147464 | tf_op jit(solution)/shard_map/ppermute | solution.py:279
  10.3 0.0 collective-permute-start.2
  10.3 0.0 collective-permute-start.3
  10.3 1.7 %collective-permute-start.4 = (bf16[2,6,16,128]{3,2,1,0:T(8,128)(2,1)S(1)}, bf16[2,6,16,128]{3,2,1,0:T(8,128)(2,1)S(1)}, u32[]{:S(2)}, u32[]{:S(2)}) collective-permute-start(bf16[2,6,16,128]{3,2,1,0:T(8,128)(2,1)S(1)} %get-tuple-element.27), channel_id=1, source_target_pairs={{0,2},{1,3},{2,0},{3,1},{4,6},{5,7},{6,4},{7,5},{8,10},{9,11},{10,... | collective-permute-start | bytes 147464 | tf_op jit(solution)/shard_map/ppermute | solution.py:279
  12.0 0.0 collective-permute-done.3
  12.0 1.0 %collective-permute-start.5 = (bf16[2,6,16,128]{3,2,1,0:T(8,128)(2,1)S(1)}, bf16[2,6,16,128]{3,2,1,0:T(8,128)(2,1)S(1)}, u32[]{:S(2)}, u32[]{:S(2)}) collective-permute-start(bf16[2,6,16,128]{3,2,1,0:T(8,128)(2,1)S(1)} %get-tuple-element.28), channel_id=1, source_target_pairs={{0,3},{1,2},{2,1},{3,0},{4,7},{5,6},{6,5},{7,4},{8,11},{9,10},{10,... | collective-permute-start | bytes 147464 | tf_op jit(solution)/shard_map/ppermute | solution.py:279
  13.0 1.4 %collective-permute-done.4 = bf16[2,6,16,128]{3,2,1,0:T(8,128)(2,1)S(1)} collective-permute-done((bf16[2,6,16,128]{3,2,1,0:T(8,128)(2,1)S(1)}, bf16[2,6,16,128]{3,2,1,0:T(8,128)(2,1)S(1)}, u32[]{:S(2)}, u32[]{:S(2)}) %collective-permute-start.4) | collective-permute-done | bytes 49184 | tf_op jit(solution)/shard_map/ppermute | solution.py:279
  14.4 1.4 %collective-permute-done.5 = bf16[2,6,16,128]{3,2,1,0:T(8,128)(2,1)S(1)} collective-permute-done((bf16[2,6,16,128]{3,2,1,0:T(8,128)(2,1)S(1)}, bf16[2,6,16,128]{3,2,1,0:T(8,128)(2,1)S(1)}, u32[]{:S(2)}, u32[]{:S(2)}) %collective-permute-start.5) | collective-permute-done | bytes 49184 | tf_op jit(solution)/shard_map/ppermute | solution.py:279
  15.8 0.0 collective-permute-done
  15.8 0.0 collective-permute-done.1
  15.8 0.3 collective-permute-done.2
  16.2 1.6 %collective-permute-start.6 = (bf16[24,32,128]{2,1,0:T(8,128)(2,1)S(1)}, bf16[24,32,128]{2,1,0:T(8,128)(2,1)S(1)}, u32[]{:S(2)}, u32[]{:S(2)}) collective-permute-start(bf16[24,32,128]{2,1,0:T(8,128)(2,1)S(1)} %pad_maximum_fusion.1.refs_0_), channel_id=1, source_target_pairs={{0,2},{1,3},{2,0},{3,1},{4,6},{5,7},{6,4},{7,5},{8,10},{9,11},{10,... | collective-permute-start | bytes 589832 | tf_op jit(solution)/shard_map/ppermute | solution.py:279
  17.8 0.1 collective-permute-start.8
  17.9 3.0 %collective-permute-start.10 = (bf16[24,16,128]{2,1,0:T(8,128)(2,1)S(1)}, bf16[24,16,128]{2,1,0:T(8,128)(2,1)S(1)}, u32[]{:S(2)}, u32[]{:S(2)}) collective-permute-start(bf16[24,16,128]{2,1,0:T(8,128)(2,1)S(1)} %get-tuple-element.30.refs_0_), channel_id=1, source_target_pairs={{0,12},{1,13},{2,14},{3,15},{4,8},{5,9},{6,10},{7,11},{8,4},{9,5},... | collective-permute-start | bytes 294920 | tf_op jit(solution)/shard_map/ppermute | solution.py:279
  20.9 0.5 collective-permute-start.9
  21.4 1.8 %collective-permute-done.6.refs_1_ = bf16[24,32,128]{2,1,0:T(8,128)(2,1)S(1)} collective-permute-done((bf16[24,32,128]{2,1,0:T(8,128)(2,1)S(1)}, bf16[24,32,128]{2,1,0:T(8,128)(2,1)S(1)}, u32[]{:S(2)}, u32[]{:S(2)}) %collective-permute-start.6) | collective-permute-done | bytes 196640 | tf_op jit(solution)/shard_map/ppermute | solution.py:279
  23.2 0.1 collective-permute-start.7
  23.3 3.9 %collective-permute-done.8 = bf16[2,24,16,128]{3,2,1,0:T(8,128)(2,1)S(1)} collective-permute-done((bf16[2,24,16,128]{3,2,1,0:T(8,128)(2,1)S(1)}, bf16[2,24,16,128]{3,2,1,0:T(8,128)(2,1)S(1)}, u32[]{:S(2)}, u32[]{:S(2)}) %collective-permute-start.8) | collective-permute-done | bytes 196640 | tf_op jit(solution)/shard_map/ppermute | solution.py:279
  27.3 1.1 %collective-permute-start.11 = (bf16[48,16,128]{2,1,0:T(8,128)(2,1)S(1)}, bf16[48,16,128]{2,1,0:T(8,128)(2,1)S(1)}, u32[]{:S(2)}, u32[]{:S(2)}) collective-permute-start(bf16[48,16,128]{2,1,0:T(8,128)(2,1)S(1)} %pad_maximum_fusion.3), channel_id=1, source_target_pairs={{0,8},{1,9},{2,10},{3,11},{4,12},{5,13},{6,14},{7,15},{8,0},{9,1},... | collective-permute-start | bytes 589832 | tf_op jit(solution)/shard_map/ppermute | solution.py:279
  28.3 0.0 copy-done.2
  28.3 0.1 copy.14
  28.5 0.1 copy.18.refs_3_
  28.6 0.1 copy.17.refs_4_
  28.7 0.0 collective-permute-done.7.refs_2_
  28.7 1.3 %arrange_left.1.left_ref = bf16[32,128,128]{2,1,0:T(8,128)(2,1)S(1)} custom-call(bf16[24,32,128]{2,1,0:T(8,128)(2,1)S(1)} %pad_maximum_fusion.1.refs_0_, bf16[24,32,128]{2,1,0:T(8,128)(2,1)S(1)} %collective-permute-done.6.refs_1_, bf16[48,32,128]{2,1,0:T(8,128)(2,1)S(1)} %collective-permute-done.7.refs_2_), custom_call_target="tpu_custom_call" | custom-call | flops 1048576 | bytes 8388608 | tf_op jit(solution)/shard_map/arrange_left/pallas_call | solution.py:123
  30.1 0.0 collective-permute-done.10.refs_3_
  30.1 5.0 %collective-permute-done.9.refs_2_ = bf16[24,16,128]{2,1,0:T(8,128)(2,1)S(1)} collective-permute-done((bf16[24,16,128]{2,1,0:T(8,128)(2,1)S(1)}, bf16[24,16,128]{2,1,0:T(8,128)(2,1)S(1)}, u32[]{:S(2)}, u32[]{:S(2)}) %collective-permute-start.9) | collective-permute-done | bytes 98336 | tf_op jit(solution)/shard_map/ppermute | solution.py:279
  35.0 0.0 copy-start
  35.0 0.0 copy-start.1
  35.0 7.8 %update_0.1.refs_4_ = f32[32,2,128,256]{3,2,1,0:T(8,128)S(1)} custom-call(bf16[32,128,128]{2,1,0:T(8,128)(2,1)S(1)} %arrange_left.1.left_ref, bf16[24,16,128]{2,1,0:T(8,128)(2,1)S(1)} %get-tuple-element.30.refs_0_, bf16[24,16,128]{2,1,0:T(8,128)(2,1)S(1)} %get-tuple-element.40.refs_1_, bf16[24,16,128]{2,1,0:T(8,128)(2,1)S(1)} %collective-permute-done.9.refs_2_, ...), custom_call_target="tpu_custom_call" | custom-call | flops 3758096384 | bytes 16777216 | tf_op jit(solution)/shard_map/update_0/pallas_call | solution.py:229
  42.8 0.0 collective-permute-done.11.refs_2_
  42.8 0.0 copy-done
  42.9 0.0 copy-done.1
  42.9 9.4 %update_1.1 = bf16[4,32,128,128]{3,2,1,0:T(8,128)(2,1)} custom-call(bf16[32,128,128]{2,1,0:T(8,128)(2,1)S(1)} %arrange_left.1.left_ref, bf16[24,16,128]{2,1,0:T(8,128)(2,1)S(1)} %get-tuple-element.33.refs_0_, bf16[24,16,128]{2,1,0:T(8,128)(2,1)S(1)} %get-tuple-element.34.refs_1_, bf16[48,16,128]{2,1,0:T(8,128)(2,1)S(1)} %collective-permute-done.11.refs_2_, ...), custom_call_target="tpu_custom_call" | custom-call | flops 3758096384 | bytes 16777216 | tf_op jit(solution)/shard_map/update_1/pallas_call | solution.py:229
  (11 shorter events, 0.2 us)
Async XLA Ops:
  0.0 28.3 %copy-start.2 = (bf16[1024,128]{1,0:T(8,128)(2,1)S(1)}, bf16[1024,128]{1,0:T(8,128)(2,1)}, u32[]{:S(2)}) copy-start(bf16[1024,128]{1,0:T(8,128)(2,1)} %param.18) | copy-start | bytes 786436
  4.6 11.2 %collective-permute-start = (bf16[6,32,128]{2,1,0:T(8,128)(2,1)S(1)}, bf16[6,32,128]{2,1,0:T(8,128)(2,1)S(1)}, u32[]{:S(2)}, u32[]{:S(2)}) collective-permute-start(bf16[6,32,128]{2,1,0:T(8,128)(2,1)S(1)} %get-tuple-element.22), channel_id=1, source_target_pairs={{0,4},{1,5},{2,6},{3,7},{4,0},{5,1},{6,2},{7,3},{8,12},{9,13},{10,... | collective-permute-start | bytes 147464 | tf_op jit(solution)/shard_map/ppermute | solution.py:279
  7.7 8.2 %collective-permute-start.1 = (bf16[6,32,128]{2,1,0:T(8,128)(2,1)S(1)}, bf16[6,32,128]{2,1,0:T(8,128)(2,1)S(1)}, u32[]{:S(2)}, u32[]{:S(2)}) collective-permute-start(bf16[6,32,128]{2,1,0:T(8,128)(2,1)S(1)} %get-tuple-element.23), channel_id=1, source_target_pairs={{0,8},{1,9},{2,10},{3,11},{4,12},{5,13},{6,14},{7,15},{8,0},{9,1},... | collective-permute-start | bytes 147464 | tf_op jit(solution)/shard_map/ppermute | solution.py:279
  10.3 5.9 %collective-permute-start.2 = (bf16[6,32,128]{2,1,0:T(8,128)(2,1)S(1)}, bf16[6,32,128]{2,1,0:T(8,128)(2,1)S(1)}, u32[]{:S(2)}, u32[]{:S(2)}) collective-permute-start(bf16[6,32,128]{2,1,0:T(8,128)(2,1)S(1)} %get-tuple-element.24), channel_id=1, source_target_pairs={{0,12},{1,13},{2,14},{3,15},{4,8},{5,9},{6,10},{7,11},{8,4},{9,5},... | collective-permute-start | bytes 147464 | tf_op jit(solution)/shard_map/ppermute | solution.py:279
  10.3 1.7 %collective-permute-start.3 = (bf16[2,6,16,128]{3,2,1,0:T(8,128)(2,1)S(1)}, bf16[2,6,16,128]{3,2,1,0:T(8,128)(2,1)S(1)}, u32[]{:S(2)}, u32[]{:S(2)}) collective-permute-start(bf16[2,6,16,128]{3,2,1,0:T(8,128)(2,1)S(1)} %get-tuple-element.26), channel_id=1, source_target_pairs={{0,1},{1,0},{2,3},{3,2},{4,5},{5,4},{6,7},{7,6},{8,9},{9,8},{10,11... | collective-permute-start | bytes 147464 | tf_op jit(solution)/shard_map/ppermute | solution.py:279
  10.3 4.2 %collective-permute-start.4 = (bf16[2,6,16,128]{3,2,1,0:T(8,128)(2,1)S(1)}, bf16[2,6,16,128]{3,2,1,0:T(8,128)(2,1)S(1)}, u32[]{:S(2)}, u32[]{:S(2)}) collective-permute-start(bf16[2,6,16,128]{3,2,1,0:T(8,128)(2,1)S(1)} %get-tuple-element.27), channel_id=1, source_target_pairs={{0,2},{1,3},{2,0},{3,1},{4,6},{5,7},{6,4},{7,5},{8,10},{9,11},{10,... | collective-permute-start | bytes 147464 | tf_op jit(solution)/shard_map/ppermute | solution.py:279
  12.0 3.8 %collective-permute-start.5 = (bf16[2,6,16,128]{3,2,1,0:T(8,128)(2,1)S(1)}, bf16[2,6,16,128]{3,2,1,0:T(8,128)(2,1)S(1)}, u32[]{:S(2)}, u32[]{:S(2)}) collective-permute-start(bf16[2,6,16,128]{3,2,1,0:T(8,128)(2,1)S(1)} %get-tuple-element.28), channel_id=1, source_target_pairs={{0,3},{1,2},{2,1},{3,0},{4,7},{5,6},{6,5},{7,4},{8,11},{9,10},{10,... | collective-permute-start | bytes 147464 | tf_op jit(solution)/shard_map/ppermute | solution.py:279
  16.2 7.0 %collective-permute-start.6 = (bf16[24,32,128]{2,1,0:T(8,128)(2,1)S(1)}, bf16[24,32,128]{2,1,0:T(8,128)(2,1)S(1)}, u32[]{:S(2)}, u32[]{:S(2)}) collective-permute-start(bf16[24,32,128]{2,1,0:T(8,128)(2,1)S(1)} %pad_maximum_fusion.1.refs_0_), channel_id=1, source_target_pairs={{0,2},{1,3},{2,0},{3,1},{4,6},{5,7},{6,4},{7,5},{8,10},{9,11},{10,... | collective-permute-start | bytes 589832 | tf_op jit(solution)/shard_map/ppermute | solution.py:279
  17.8 9.4 %collective-permute-start.8 = (bf16[2,24,16,128]{3,2,1,0:T(8,128)(2,1)S(1)}, bf16[2,24,16,128]{3,2,1,0:T(8,128)(2,1)S(1)}, u32[]{:S(2)}, u32[]{:S(2)}) collective-permute-start(bf16[2,24,16,128]{3,2,1,0:T(8,128)(2,1)S(1)} %pad_maximum_fusion.2), channel_id=1, source_target_pairs={{0,4},{1,5},{2,6},{3,7},{4,0},{5,1},{6,2},{7,3},{8,12},{9,13},{10,... | collective-permute-start | bytes 589832 | tf_op jit(solution)/shard_map/ppermute | solution.py:279
  17.9 12.2 %collective-permute-start.10 = (bf16[24,16,128]{2,1,0:T(8,128)(2,1)S(1)}, bf16[24,16,128]{2,1,0:T(8,128)(2,1)S(1)}, u32[]{:S(2)}, u32[]{:S(2)}) collective-permute-start(bf16[24,16,128]{2,1,0:T(8,128)(2,1)S(1)} %get-tuple-element.30.refs_0_), channel_id=1, source_target_pairs={{0,12},{1,13},{2,14},{3,15},{4,8},{5,9},{6,10},{7,11},{8,4},{9,5},... | collective-permute-start | bytes 294920 | tf_op jit(solution)/shard_map/ppermute | solution.py:279
  20.9 14.2 %collective-permute-start.9 = (bf16[24,16,128]{2,1,0:T(8,128)(2,1)S(1)}, bf16[24,16,128]{2,1,0:T(8,128)(2,1)S(1)}, u32[]{:S(2)}, u32[]{:S(2)}) collective-permute-start(bf16[24,16,128]{2,1,0:T(8,128)(2,1)S(1)} %get-tuple-element.30.refs_0_), channel_id=1, source_target_pairs={{0,8},{1,9},{2,10},{3,11},{4,12},{5,13},{6,14},{7,15},{8,0},{9,1},... | collective-permute-start | bytes 294920 | tf_op jit(solution)/shard_map/ppermute | solution.py:279
  23.2 5.5 %collective-permute-start.7 = (bf16[48,32,128]{2,1,0:T(8,128)(2,1)S(1)}, bf16[48,32,128]{2,1,0:T(8,128)(2,1)S(1)}, u32[]{:S(2)}, u32[]{:S(2)}) collective-permute-start(bf16[48,32,128]{2,1,0:T(8,128)(2,1)S(1)} %pad_maximum_fusion), channel_id=1, source_target_pairs={{0,1},{1,0},{2,3},{3,2},{4,5},{5,4},{6,7},{7,6},{8,9},{9,8},{10,11... | collective-permute-start | bytes 1179656 | tf_op jit(solution)/shard_map/ppermute | solution.py:279
  27.3 15.6 %collective-permute-start.11 = (bf16[48,16,128]{2,1,0:T(8,128)(2,1)S(1)}, bf16[48,16,128]{2,1,0:T(8,128)(2,1)S(1)}, u32[]{:S(2)}, u32[]{:S(2)}) collective-permute-start(bf16[48,16,128]{2,1,0:T(8,128)(2,1)S(1)} %pad_maximum_fusion.3), channel_id=1, source_target_pairs={{0,8},{1,9},{2,10},{3,11},{4,12},{5,13},{6,14},{7,15},{8,0},{9,1},... | collective-permute-start | bytes 589832 | tf_op jit(solution)/shard_map/ppermute | solution.py:279
  35.0 7.8 %copy-start = (bf16[1,128,128,128]{3,2,1,0:T(8,128)(2,1)S(1)}, bf16[1,128,128,128]{3,2,1,0:T(8,128)(2,1)}, u32[]{:S(2)}) copy-start(bf16[1,128,128,128]{3,2,1,0:T(8,128)(2,1)} %param.11) | copy-start | bytes 12582916
  35.0 7.8 %copy-start.1 = (f32[128]{0:T(128)S(1)}, f32[128]{0:T(128)}, u32[]{:S(2)}) copy-start(f32[128]{0:T(128)} %param.19) | copy-start | bytes 1540

commit v14 on v13

--- a/solution.py
+++ b/solution.py
@@ -278,11 +278,13 @@
     def swap(x, da, db):
         return lax.ppermute(x, "row", [(i, i ^ (da * side + db)) for i in range(devices)])
 
+    right = [right[0]] + [swap(right[d], 0, d) for d in range(1, side)]
+    *left, right[1] = lax.optimization_barrier((*left, right[1]))
     left = [left[0]] + [swap(left[d], d, 0) for d in range(1, side)]
-    right = [right[0]] + [swap(right[d], 0, d) for d in range(1, side)]
+    mines = [jnp.concatenate([x[part] for x in right]) for part in range(PARTS)]
     left = jnp.concatenate(left)
-    mines = [jnp.concatenate([x[part] for x in right]) for part in range(PARTS)]
-    left, *mines = lax.optimization_barrier((left, *mines))
+    near = swap(jnp.stack(mines), 1, 0)
+    parts = [[mines[0], near[0]] + [swap(mines[0], d, 0) for d in range(2, side)]]
     lefts = [left]
     order = [0]
     mask = side // 2
@@ -290,8 +292,7 @@
         lefts += [swap(jnp.concatenate(lefts), 0, mask)]
         order += [o ^ mask for o in order]
         mask //= 2
-    near = swap(jnp.stack(mines), 1, 0)
-    parts = [[mines[0], near[0]] + [swap(mines[0], d, 0) for d in range(2, side)]]
+    lefts[-1], mines[-1] = lax.optimization_barrier((lefts[-1], mines[-1]))
     for part in range(1, PARTS):
         pieces = [mines[part], near[part]]
         mask = 2

time: 52.4 us -> 47.9 us (0.914)
  waiting for transfers between devices: 13.8 us -> 10.7 us
  starting transfers between devices: 14.7 us -> 12.3 us
  local copies, waits for them, and re-layouts: 0.39 us -> 1.45 us
    ppermute x12, waiting for transfers between devices: 13.8 us -> 10.7 us  [swap(): lax.ppermute(x, 'row', [(i, i ^ da * side + db) for i in range(devices)])]
    ppermute x12, starting transfers between devices: 14.7 us -> 12.3 us  [swap(): lax.ppermute(x, 'row', [(i, i ^ da * side + db) for i in range(devices)])]
    transpose x1, local copies, waits for them, and re-layouts: 0.1 us -> 1.06 us  [local(): final_matrix.reshape(width, width, -1).transpose(2, 1, 0)]
  transfers between devices with their start and end apart: 12 -> 12, of which waited for: 6 -> 6; matrix products, arithmetic and copies ran while one was open for 1% -> 3% of each run, Pallas kernels for 17% -> 19%
where the time goes in v14:
time: 47.9 us; the launch traced here: 47.7 us
  Pallas kernels  23 us (48%)
  starting transfers between devices  12.3 us (26%)
  waiting for transfers between devices  10.7 us (22%)
  local copies, waits for them, and re-layouts  1.45 us (3%)
    pallas_call x2, Pallas kernels, update_part(): pl.pallas_call(functools.partial(update_kernel, side, seqs, order, len(ri...  17.2 us
    ppermute x12, starting transfers between devices, swap(): lax.ppermute(x, 'row', [(i, i ^ da * side + db) for i in range(devices)])  12.3 us
    ppermute x12, waiting for transfers between devices, swap(): lax.ppermute(x, 'row', [(i, i ^ da * side + db) for i in range(devices)])  10.7 us
    pallas_call x1, Pallas kernels, project(): pl.pallas_call(functools.partial(project_kernel, side), in_specs=[pl.Bloc...  4.52 us
    pallas_call x1, Pallas kernels, arrange_left(): pl.pallas_call(functools.partial(arrange_kernel, seq_total), in_specs=[pl...  1.33 us
    transpose x1, local copies, waits for them, and re-layouts, local(): final_matrix.reshape(width, width, -1).transpose(2, 1, 0)  1.06 us
  transfers between devices with their start and end apart: 12, of which 6 were waited for; matrix products, arithmetic and copies ran while one was open for 3% of the time, Pallas kernels for 19%

profile of v14, /device:TPU:0, one launch (start us, length us, event | category | flops | bytes accessed | tf_op | source)
XLA Modules:
  0.0 47.7 jit_solution(15456000196215599148)
XLA Ops:
  0.0 4.5 %project.1 = (bf16[6,32,128]{2,1,0:T(8,128)(2,1)S(1)}, bf16[6,32,128]{2,1,0:T(8,128)(2,1)S(1)}, bf16[6,32,128]{2,1,0:T(8,128)(2,1)S(1)}, bf16[6,32,128]{2,1,0:T(...) custom-call(bf16[6,512,256]{2,1,0:T(8,128)(2,1)} %refs_0_.1, ...), custom_call_target="tpu_custom_call" | custom-call | tf_op jit(solution)/shard_map/project/pallas_call | solution.py:86
  4.5 0.5 %collective-permute-start = (bf16[2,6,16,128]{3,2,1,0:T(8,128)(2,1)S(1)}, bf16[2,6,16,128]{3,2,1,0:T(8,128)(2,1)S(1)}, u32[]{:S(2)}, u32[]{:S(2)}) collective-permute-start(bf16[2,6,16,128]{3,2,1,0:T(8,128)(2,1)S(1)} %get-tuple-element.29), channel_id=1, source_target_pairs={{0,1},{1,0},{2,3},{3,2},{4,5},{5,4},{6,7},{7,6},{8,9},{9,8},{10,11... | collective-permute-start | bytes 147464 | tf_op jit(solution)/shard_map/ppermute | solution.py:279
  5.0 2.6 %collective-permute-start.6 = (bf16[2,6,16,128]{3,2,1,0:T(8,128)(2,1)S(1)}, bf16[2,6,16,128]{3,2,1,0:T(8,128)(2,1)S(1)}, u32[]{:S(2)}, u32[]{:S(2)}) collective-permute-start(bf16[2,6,16,128]{3,2,1,0:T(8,128)(2,1)S(1)} %get-tuple-element.36), channel_id=1, source_target_pairs={{0,2},{1,3},{2,0},{3,1},{4,6},{5,7},{6,4},{7,5},{8,10},{9,11},{10,... | collective-permute-start | bytes 147464 | tf_op jit(solution)/shard_map/ppermute | solution.py:279
  7.6 0.1 collective-permute-start.7
  7.7 0.0 collective-permute-done
  7.7 1.8 %collective-permute-start.1 = (bf16[6,32,128]{2,1,0:T(8,128)(2,1)S(1)}, bf16[6,32,128]{2,1,0:T(8,128)(2,1)S(1)}, u32[]{:S(2)}, u32[]{:S(2)}) collective-permute-start(bf16[6,32,128]{2,1,0:T(8,128)(2,1)S(1)} %get-tuple-element.31), channel_id=1, source_target_pairs={{0,4},{1,5},{2,6},{3,7},{4,0},{5,1},{6,2},{7,3},{8,12},{9,13},{10,... | collective-permute-start | bytes 147464 | tf_op jit(solution)/shard_map/ppermute | solution.py:279
  9.6 2.6 %collective-permute-start.2 = (bf16[6,32,128]{2,1,0:T(8,128)(2,1)S(1)}, bf16[6,32,128]{2,1,0:T(8,128)(2,1)S(1)}, u32[]{:S(2)}, u32[]{:S(2)}) collective-permute-start(bf16[6,32,128]{2,1,0:T(8,128)(2,1)S(1)} %get-tuple-element.32), channel_id=1, source_target_pairs={{0,8},{1,9},{2,10},{3,11},{4,12},{5,13},{6,14},{7,15},{8,0},{9,1},... | collective-permute-start | bytes 147464 | tf_op jit(solution)/shard_map/ppermute | solution.py:279
  12.2 0.0 collective-permute-start.3
  12.2 0.0 collective-permute-done.6
  12.2 0.0 collective-permute-done.7
  12.3 1.0 %collective-permute-start.8 = (bf16[2,24,16,128]{3,2,1,0:T(8,128)(2,1)S(1)}, bf16[2,24,16,128]{3,2,1,0:T(8,128)(2,1)S(1)}, u32[]{:S(2)}, u32[]{:S(2)}) collective-permute-start(bf16[2,24,16,128]{3,2,1,0:T(8,128)(2,1)S(1)} %pad_maximum_fusion), channel_id=1, source_target_pairs={{0,4},{1,5},{2,6},{3,7},{4,0},{5,1},{6,2},{7,3},{8,12},{9,13},{10,... | collective-permute-start | bytes 589832 | tf_op jit(solution)/shard_map/ppermute | solution.py:279
  13.3 0.0 collective-permute-done.1
  13.3 2.4 %collective-permute-done.2 = bf16[6,32,128]{2,1,0:T(8,128)(2,1)S(1)} collective-permute-done((bf16[6,32,128]{2,1,0:T(8,128)(2,1)S(1)}, bf16[6,32,128]{2,1,0:T(8,128)(2,1)S(1)}, u32[]{:S(2)}, u32[]{:S(2)}) %collective-permute-start.2) | collective-permute-done | bytes 49184 | tf_op jit(solution)/shard_map/ppermute | solution.py:279
  15.7 2.9 %collective-permute-done.3 = bf16[6,32,128]{2,1,0:T(8,128)(2,1)S(1)} collective-permute-done((bf16[6,32,128]{2,1,0:T(8,128)(2,1)S(1)}, bf16[6,32,128]{2,1,0:T(8,128)(2,1)S(1)}, u32[]{:S(2)}, u32[]{:S(2)}) %collective-permute-start.3) | collective-permute-done | bytes 49184 | tf_op jit(solution)/shard_map/ppermute | solution.py:279
  18.6 1.6 %collective-permute-start.4 = (bf16[24,32,128]{2,1,0:T(8,128)(2,1)S(1)}, bf16[24,32,128]{2,1,0:T(8,128)(2,1)S(1)}, u32[]{:S(2)}, u32[]{:S(2)}) collective-permute-start(bf16[24,32,128]{2,1,0:T(8,128)(2,1)S(1)} %get-tuple-element.62.refs_0_), channel_id=1, source_target_pairs={{0,2},{1,3},{2,0},{3,1},{4,6},{5,7},{6,4},{7,5},{8,10},{9,11},{10,... | collective-permute-start | bytes 589832 | tf_op jit(solution)/shard_map/ppermute | solution.py:279
  20.2 1.1 %collective-permute-start.10 = (bf16[24,16,128]{2,1,0:T(8,128)(2,1)S(1)}, bf16[24,16,128]{2,1,0:T(8,128)(2,1)S(1)}, u32[]{:S(2)}, u32[]{:S(2)}) collective-permute-start(bf16[24,16,128]{2,1,0:T(8,128)(2,1)S(1)} %get-tuple-element.50.refs_0_), channel_id=1, source_target_pairs={{0,12},{1,13},{2,14},{3,15},{4,8},{5,9},{6,10},{7,11},{8,4},{9,5},... | collective-permute-start | bytes 294920 | tf_op jit(solution)/shard_map/ppermute | solution.py:279
  21.3 0.0 collective-permute-start.9
  21.3 0.0 collective-permute-done.8
  21.3 1.1 %copy.14 = bf16[128,32,32]{0,2,1:T(8,128)(2,1)S(1)} copy(bf16[128,32,32]{0,1,2:T(8,128)(2,1)} %bitcast.40) | data formatting | bytes 524288 | tf_op jit(solution)/shard_map/transpose | solution.py:305
  22.3 2.0 %collective-permute-done.4.refs_1_ = bf16[24,32,128]{2,1,0:T(8,128)(2,1)S(1)} collective-permute-done((bf16[24,32,128]{2,1,0:T(8,128)(2,1)S(1)}, bf16[24,32,128]{2,1,0:T(8,128)(2,1)S(1)}, u32[]{:S(2)}, u32[]{:S(2)}) %collective-permute-start.4) | collective-permute-done | bytes 196640 | tf_op jit(solution)/shard_map/ppermute | solution.py:279
  24.4 0.1 collective-permute-start.5
  24.5 0.1 copy.18.refs_3_
  24.6 0.1 copy.17.refs_4_
  24.8 1.4 %collective-permute-done.5.refs_2_ = bf16[48,32,128]{2,1,0:T(8,128)(2,1)S(1)} collective-permute-done((bf16[48,32,128]{2,1,0:T(8,128)(2,1)S(1)}, bf16[48,32,128]{2,1,0:T(8,128)(2,1)S(1)}, u32[]{:S(2)}, u32[]{:S(2)}) %collective-permute-start.5) | collective-permute-done | bytes 393248 | tf_op jit(solution)/shard_map/ppermute | solution.py:279
  26.2 1.0 %collective-permute-start.11 = (bf16[48,16,128]{2,1,0:T(8,128)(2,1)S(1)}, bf16[48,16,128]{2,1,0:T(8,128)(2,1)S(1)}, u32[]{:S(2)}, u32[]{:S(2)}) collective-permute-start(bf16[48,16,128]{2,1,0:T(8,128)(2,1)S(1)} %pad_maximum_fusion.1), channel_id=1, source_target_pairs={{0,8},{1,9},{2,10},{3,11},{4,12},{5,13},{6,14},{7,15},{8,0},{9,1},... | collective-permute-start | bytes 589832 | tf_op jit(solution)/shard_map/ppermute | solution.py:279
  27.2 1.3 %arrange_left.1.left_ref = bf16[32,128,128]{2,1,0:T(8,128)(2,1)S(1)} custom-call(bf16[24,32,128]{2,1,0:T(8,128)(2,1)S(1)} %get-tuple-element.62.refs_0_, bf16[24,32,128]{2,1,0:T(8,128)(2,1)S(1)} %collective-permute-done.4.refs_1_, bf16[48,32,128]{2,1,0:T(8,128)(2,1)S(1)} %collective-permute-done.5.refs_2_), custom_call_target="tpu_custom_call" | custom-call | flops 1048576 | bytes 8388608 | tf_op jit(solution)/shard_map/arrange_left/pallas_call | solution.py:123
  28.5 0.0 collective-permute-done.10.refs_3_
  28.5 0.9 %collective-permute-done.9.refs_2_ = bf16[24,16,128]{2,1,0:T(8,128)(2,1)S(1)} collective-permute-done((bf16[24,16,128]{2,1,0:T(8,128)(2,1)S(1)}, bf16[24,16,128]{2,1,0:T(8,128)(2,1)S(1)}, u32[]{:S(2)}, u32[]{:S(2)}) %collective-permute-start.9) | collective-permute-done | bytes 98336 | tf_op jit(solution)/shard_map/ppermute | solution.py:279
  29.4 0.0 copy-start
  29.5 0.0 copy-start.1
  29.5 7.8 %update_0.1.refs_4_ = f32[32,2,128,256]{3,2,1,0:T(8,128)S(1)} custom-call(bf16[32,128,128]{2,1,0:T(8,128)(2,1)S(1)} %arrange_left.1.left_ref, bf16[24,16,128]{2,1,0:T(8,128)(2,1)S(1)} %get-tuple-element.50.refs_0_, bf16[24,16,128]{2,1,0:T(8,128)(2,1)S(1)} %get-tuple-element.48.refs_1_, bf16[24,16,128]{2,1,0:T(8,128)(2,1)S(1)} %collective-permute-done.9.refs_2_, ...), custom_call_target="tpu_custom_call" | custom-call | flops 3758096384 | bytes 16777216 | tf_op jit(solution)/shard_map/update_0/pallas_call | solution.py:229
  37.3 1.1 %collective-permute-done.11.refs_2_ = bf16[48,16,128]{2,1,0:T(8,128)(2,1)S(1)} collective-permute-done((bf16[48,16,128]{2,1,0:T(8,128)(2,1)S(1)}, bf16[48,16,128]{2,1,0:T(8,128)(2,1)S(1)}, u32[]{:S(2)}, u32[]{:S(2)}) %collective-permute-start.11) | collective-permute-done | bytes 196640 | tf_op jit(solution)/shard_map/ppermute | solution.py:279
  38.3 0.0 copy-done
  38.3 0.0 copy-done.1
  38.3 9.4 %update_1.1 = bf16[4,32,128,128]{3,2,1,0:T(8,128)(2,1)} custom-call(bf16[32,128,128]{2,1,0:T(8,128)(2,1)S(1)} %arrange_left.1.left_ref, bf16[24,16,128]{2,1,0:T(8,128)(2,1)S(1)} %get-tuple-element.41.refs_0_, bf16[24,16,128]{2,1,0:T(8,128)(2,1)S(1)} %get-tuple-element.42.refs_1_, bf16[48,16,128]{2,1,0:T(8,128)(2,1)S(1)} %collective-permute-done.11.refs_2_, ...), custom_call_target="tpu_custom_call" | custom-call | flops 3758096384 | bytes 16777216 | tf_op jit(solution)/shard_map/update_1/pallas_call | solution.py:229
  (15 shorter events, 0.2 us)
Async XLA Ops:
  4.5 3.2 %collective-permute-start = (bf16[2,6,16,128]{3,2,1,0:T(8,128)(2,1)S(1)}, bf16[2,6,16,128]{3,2,1,0:T(8,128)(2,1)S(1)}, u32[]{:S(2)}, u32[]{:S(2)}) collective-permute-start(bf16[2,6,16,128]{3,2,1,0:T(8,128)(2,1)S(1)} %get-tuple-element.29), channel_id=1, source_target_pairs={{0,1},{1,0},{2,3},{3,2},{4,5},{5,4},{6,7},{7,6},{8,9},{9,8},{10,11... | collective-permute-start | bytes 147464 | tf_op jit(solution)/shard_map/ppermute | solution.py:279
  5.0 7.1 %collective-permute-start.6 = (bf16[2,6,16,128]{3,2,1,0:T(8,128)(2,1)S(1)}, bf16[2,6,16,128]{3,2,1,0:T(8,128)(2,1)S(1)}, u32[]{:S(2)}, u32[]{:S(2)}) collective-permute-start(bf16[2,6,16,128]{3,2,1,0:T(8,128)(2,1)S(1)} %get-tuple-element.36), channel_id=1, source_target_pairs={{0,2},{1,3},{2,0},{3,1},{4,6},{5,7},{6,4},{7,5},{8,10},{9,11},{10,... | collective-permute-start | bytes 147464 | tf_op jit(solution)/shard_map/ppermute | solution.py:279
  7.6 4.6 %collective-permute-start.7 = (bf16[2,6,16,128]{3,2,1,0:T(8,128)(2,1)S(1)}, bf16[2,6,16,128]{3,2,1,0:T(8,128)(2,1)S(1)}, u32[]{:S(2)}, u32[]{:S(2)}) collective-permute-start(bf16[2,6,16,128]{3,2,1,0:T(8,128)(2,1)S(1)} %get-tuple-element.37), channel_id=1, source_target_pairs={{0,3},{1,2},{2,1},{3,0},{4,7},{5,6},{6,5},{7,4},{8,11},{9,10},{10,... | collective-permute-start | bytes 147464 | tf_op jit(solution)/shard_map/ppermute | solution.py:279
  7.7 5.5 %collective-permute-start.1 = (bf16[6,32,128]{2,1,0:T(8,128)(2,1)S(1)}, bf16[6,32,128]{2,1,0:T(8,128)(2,1)S(1)}, u32[]{:S(2)}, u32[]{:S(2)}) collective-permute-start(bf16[6,32,128]{2,1,0:T(8,128)(2,1)S(1)} %get-tuple-element.31), channel_id=1, source_target_pairs={{0,4},{1,5},{2,6},{3,7},{4,0},{5,1},{6,2},{7,3},{8,12},{9,13},{10,... | collective-permute-start | bytes 147464 | tf_op jit(solution)/shard_map/ppermute | solution.py:279
  9.6 6.1 %collective-permute-start.2 = (bf16[6,32,128]{2,1,0:T(8,128)(2,1)S(1)}, bf16[6,32,128]{2,1,0:T(8,128)(2,1)S(1)}, u32[]{:S(2)}, u32[]{:S(2)}) collective-permute-start(bf16[6,32,128]{2,1,0:T(8,128)(2,1)S(1)} %get-tuple-element.32), channel_id=1, source_target_pairs={{0,8},{1,9},{2,10},{3,11},{4,12},{5,13},{6,14},{7,15},{8,0},{9,1},... | collective-permute-start | bytes 147464 | tf_op jit(solution)/shard_map/ppermute | solution.py:279
  12.2 6.4 %collective-permute-start.3 = (bf16[6,32,128]{2,1,0:T(8,128)(2,1)S(1)}, bf16[6,32,128]{2,1,0:T(8,128)(2,1)S(1)}, u32[]{:S(2)}, u32[]{:S(2)}) collective-permute-start(bf16[6,32,128]{2,1,0:T(8,128)(2,1)S(1)} %get-tuple-element.33), channel_id=1, source_target_pairs={{0,12},{1,13},{2,14},{3,15},{4,8},{5,9},{6,10},{7,11},{8,4},{9,5},... | collective-permute-start | bytes 147464 | tf_op jit(solution)/shard_map/ppermute | solution.py:279
  12.3 9.0 %collective-permute-start.8 = (bf16[2,24,16,128]{3,2,1,0:T(8,128)(2,1)S(1)}, bf16[2,24,16,128]{3,2,1,0:T(8,128)(2,1)S(1)}, u32[]{:S(2)}, u32[]{:S(2)}) collective-permute-start(bf16[2,24,16,128]{3,2,1,0:T(8,128)(2,1)S(1)} %pad_maximum_fusion), channel_id=1, source_target_pairs={{0,4},{1,5},{2,6},{3,7},{4,0},{5,1},{6,2},{7,3},{8,12},{9,13},{10,... | collective-permute-start | bytes 589832 | tf_op jit(solution)/shard_map/ppermute | solution.py:279
  18.6 5.7 %collective-permute-start.4 = (bf16[24,32,128]{2,1,0:T(8,128)(2,1)S(1)}, bf16[24,32,128]{2,1,0:T(8,128)(2,1)S(1)}, u32[]{:S(2)}, u32[]{:S(2)}) collective-permute-start(bf16[24,32,128]{2,1,0:T(8,128)(2,1)S(1)} %get-tuple-element.62.refs_0_), channel_id=1, source_target_pairs={{0,2},{1,3},{2,0},{3,1},{4,6},{5,7},{6,4},{7,5},{8,10},{9,11},{10,... | collective-permute-start | bytes 589832 | tf_op jit(solution)/shard_map/ppermute | solution.py:279
  20.2 8.3 %collective-permute-start.10 = (bf16[24,16,128]{2,1,0:T(8,128)(2,1)S(1)}, bf16[24,16,128]{2,1,0:T(8,128)(2,1)S(1)}, u32[]{:S(2)}, u32[]{:S(2)}) collective-permute-start(bf16[24,16,128]{2,1,0:T(8,128)(2,1)S(1)} %get-tuple-element.50.refs_0_), channel_id=1, source_target_pairs={{0,12},{1,13},{2,14},{3,15},{4,8},{5,9},{6,10},{7,11},{8,4},{9,5},... | collective-permute-start | bytes 294920 | tf_op jit(solution)/shard_map/ppermute | solution.py:279
  21.3 8.2 %collective-permute-start.9 = (bf16[24,16,128]{2,1,0:T(8,128)(2,1)S(1)}, bf16[24,16,128]{2,1,0:T(8,128)(2,1)S(1)}, u32[]{:S(2)}, u32[]{:S(2)}) collective-permute-start(bf16[24,16,128]{2,1,0:T(8,128)(2,1)S(1)} %get-tuple-element.50.refs_0_), channel_id=1, source_target_pairs={{0,8},{1,9},{2,10},{3,11},{4,12},{5,13},{6,14},{7,15},{8,0},{9,1},... | collective-permute-start | bytes 294920 | tf_op jit(solution)/shard_map/ppermute | solution.py:279
  24.4 1.8 %collective-permute-start.5 = (bf16[48,32,128]{2,1,0:T(8,128)(2,1)S(1)}, bf16[48,32,128]{2,1,0:T(8,128)(2,1)S(1)}, u32[]{:S(2)}, u32[]{:S(2)}) collective-permute-start(bf16[48,32,128]{2,1,0:T(8,128)(2,1)S(1)} %constant_dynamic-update-slice_fusion.4), channel_id=1, source_target_pairs={{0,1},{1,0},{2,3},{3,2},{4,5},{5,4},{6,7},{7,6},{8,9},{9,8},{10,11... | collective-permute-start | bytes 1179656 | tf_op jit(solution)/shard_map/ppermute | solution.py:279
  26.2 12.1 %collective-permute-start.11 = (bf16[48,16,128]{2,1,0:T(8,128)(2,1)S(1)}, bf16[48,16,128]{2,1,0:T(8,128)(2,1)S(1)}, u32[]{:S(2)}, u32[]{:S(2)}) collective-permute-start(bf16[48,16,128]{2,1,0:T(8,128)(2,1)S(1)} %pad_maximum_fusion.1), channel_id=1, source_target_pairs={{0,8},{1,9},{2,10},{3,11},{4,12},{5,13},{6,14},{7,15},{8,0},{9,1},... | collective-permute-start | bytes 589832 | tf_op jit(solution)/shard_map/ppermute | solution.py:279
  29.4 8.9 %copy-start = (bf16[1,128,128,128]{3,2,1,0:T(8,128)(2,1)S(1)}, bf16[1,128,128,128]{3,2,1,0:T(8,128)(2,1)}, u32[]{:S(2)}) copy-start(bf16[1,128,128,128]{3,2,1,0:T(8,128)(2,1)} %param.11) | copy-start | bytes 12582916
  29.5 8.9 %copy-start.1 = (f32[128]{0:T(128)S(1)}, f32[128]{0:T(128)}, u32[]{:S(2)}) copy-start(f32[128]{0:T(128)} %param.19) | copy-start | bytes 1540

commit v15 on v14

--- a/solution.py
+++ b/solution.py
@@ -282,17 +282,18 @@
     *left, right[1] = lax.optimization_barrier((*left, right[1]))
     left = [left[0]] + [swap(left[d], d, 0) for d in range(1, side)]
     mines = [jnp.concatenate([x[part] for x in right]) for part in range(PARTS)]
-    left = jnp.concatenate(left)
-    near = swap(jnp.stack(mines), 1, 0)
-    parts = [[mines[0], near[0]] + [swap(mines[0], d, 0) for d in range(2, side)]]
-    lefts = [left]
+    stacked = jnp.stack(mines)
+    left[1], mines[0] = lax.optimization_barrier((left[1], mines[0]))
+    *left, stacked = lax.optimization_barrier((*left, stacked))
+    lefts = [jnp.concatenate(left)]
     order = [0]
     mask = side // 2
     while mask > 0:
         lefts += [swap(jnp.concatenate(lefts), 0, mask)]
         order += [o ^ mask for o in order]
         mask //= 2
-    lefts[-1], mines[-1] = lax.optimization_barrier((lefts[-1], mines[-1]))
+    near = swap(stacked, 1, 0)
+    parts = [[mines[0], near[0]] + [swap(mines[0], d, 0) for d in range(2, side)]]
     for part in range(1, PARTS):
         pieces = [mines[part], near[part]]
         mask = 2

time: 47.9 us -> 50.4 us (1.052)
  starting transfers between devices: 12.3 us -> 16.3 us
  local copies, waits for them, and re-layouts: 1.45 us -> 0.56 us
  waiting for transfers between devices: 10.7 us -> 10 us
    ppermute x12, starting transfers between devices: 12.3 us -> 16.3 us  [swap(): lax.ppermute(x, 'row', [(i, i ^ da * side + db) for i in range(devices)])]
    transpose x1, local copies, waits for them, and re-layouts: 1.06 us -> 0.11 us  [local(): final_matrix.reshape(width, width, -1).transpose(2, 1, 0)]
    ppermute x12, waiting for transfers between devices: 10.7 us -> 10 us  [swap(): lax.ppermute(x, 'row', [(i, i ^ da * side + db) for i in range(devices)])]
  transfers between devices with their start and end apart: 12 -> 12, of which waited for: 6 -> 3; matrix products, arithmetic and copies ran while one was open for 3% -> 1% of each run, Pallas kernels for 19% -> 18%
where the time goes in v15:
time: 50.4 us; the launch traced here: 50.3 us
  Pallas kernels  23.1 us (46%)
  starting transfers between devices  16.3 us (32%)
  waiting for transfers between devices  10 us (20%)
  local copies, waits for them, and re-layouts  0.56 us (1%)
    pallas_call x2, Pallas kernels, update_part(): pl.pallas_call(functools.partial(update_kernel, side, seqs, order, len(ri...  17.2 us
    ppermute x12, starting transfers between devices, swap(): lax.ppermute(x, 'row', [(i, i ^ da * side + db) for i in range(devices)])  16.3 us
    ppermute x12, waiting for transfers between devices, swap(): lax.ppermute(x, 'row', [(i, i ^ da * side + db) for i in range(devices)])  10 us
    pallas_call x1, Pallas kernels, project(): pl.pallas_call(functools.partial(project_kernel, side), in_specs=[pl.Bloc...  4.57 us
    pallas_call x1, Pallas kernels, arrange_left(): pl.pallas_call(functools.partial(arrange_kernel, seq_total), in_specs=[pl...  1.33 us
  transfers between devices with their start and end apart: 12, of which 3 were waited for; matrix products, arithmetic and copies ran while one was open for 1% of the time, Pallas kernels for 18%

profile of v15, /device:TPU:0, one launch (start us, length us, event | category | flops | bytes accessed | tf_op | source)
XLA Modules:
  0.0 50.3 jit_solution(14734534741209654885)
XLA Ops:
  0.0 0.0 copy-start.2
  0.0 4.6 %project.1 = (bf16[6,32,128]{2,1,0:T(8,128)(2,1)S(1)}, bf16[6,32,128]{2,1,0:T(8,128)(2,1)S(1)}, bf16[6,32,128]{2,1,0:T(8,128)(2,1)S(1)}, bf16[6,32,128]{2,1,0:T(...) custom-call(bf16[6,512,256]{2,1,0:T(8,128)(2,1)} %refs_0_.1, ...), custom_call_target="tpu_custom_call" | custom-call | tf_op jit(solution)/shard_map/project/pallas_call | solution.py:86
  4.6 0.5 %collective-permute-start = (bf16[2,6,16,128]{3,2,1,0:T(8,128)(2,1)S(1)}, bf16[2,6,16,128]{3,2,1,0:T(8,128)(2,1)S(1)}, u32[]{:S(2)}, u32[]{:S(2)}) collective-permute-start(bf16[2,6,16,128]{3,2,1,0:T(8,128)(2,1)S(1)} %get-tuple-element.34), channel_id=1, source_target_pairs={{0,1},{1,0},{2,3},{3,2},{4,5},{5,4},{6,7},{7,6},{8,9},{9,8},{10,11... | collective-permute-start | bytes 147464 | tf_op jit(solution)/shard_map/ppermute | solution.py:279
  5.1 2.6 %collective-permute-start.2 = (bf16[2,6,16,128]{3,2,1,0:T(8,128)(2,1)S(1)}, bf16[2,6,16,128]{3,2,1,0:T(8,128)(2,1)S(1)}, u32[]{:S(2)}, u32[]{:S(2)}) collective-permute-start(bf16[2,6,16,128]{3,2,1,0:T(8,128)(2,1)S(1)} %get-tuple-element.39), channel_id=1, source_target_pairs={{0,2},{1,3},{2,0},{3,1},{4,6},{5,7},{6,4},{7,5},{8,10},{9,11},{10,... | collective-permute-start | bytes 147464 | tf_op jit(solution)/shard_map/ppermute | solution.py:279
  7.7 0.1 collective-permute-start.3
  7.8 0.0 collective-permute-done
  7.8 1.8 %collective-permute-start.1 = (bf16[6,32,128]{2,1,0:T(8,128)(2,1)S(1)}, bf16[6,32,128]{2,1,0:T(8,128)(2,1)S(1)}, u32[]{:S(2)}, u32[]{:S(2)}) collective-permute-start(bf16[6,32,128]{2,1,0:T(8,128)(2,1)S(1)} %get-tuple-element.36), channel_id=1, source_target_pairs={{0,4},{1,5},{2,6},{3,7},{4,0},{5,1},{6,2},{7,3},{8,12},{9,13},{10,... | collective-permute-start | bytes 147464 | tf_op jit(solution)/shard_map/ppermute | solution.py:279
  9.6 2.6 %collective-permute-start.4 = (bf16[6,32,128]{2,1,0:T(8,128)(2,1)S(1)}, bf16[6,32,128]{2,1,0:T(8,128)(2,1)S(1)}, u32[]{:S(2)}, u32[]{:S(2)}) collective-permute-start(bf16[6,32,128]{2,1,0:T(8,128)(2,1)S(1)} %get-tuple-element.42), channel_id=1, source_target_pairs={{0,8},{1,9},{2,10},{3,11},{4,12},{5,13},{6,14},{7,15},{8,0},{9,1},... | collective-permute-start | bytes 147464 | tf_op jit(solution)/shard_map/ppermute | solution.py:279
  12.2 0.0 collective-permute-start.5
  12.2 0.0 collective-permute-done.2
  12.3 0.0 collective-permute-done.3
  12.4 0.0 collective-permute-done.1
  12.4 3.9 %collective-permute-start.10 = (bf16[24,16,128]{2,1,0:T(8,128)(2,1)S(1)}, bf16[24,16,128]{2,1,0:T(8,128)(2,1)S(1)}, u32[]{:S(2)}, u32[]{:S(2)}) collective-permute-start(bf16[24,16,128]{2,1,0:T(8,128)(2,1)S(1)} %get-tuple-element.48.refs_0_), channel_id=1, source_target_pairs={{0,12},{1,13},{2,14},{3,15},{4,8},{5,9},{6,10},{7,11},{8,4},{9,5},... | collective-permute-start | bytes 294920 | tf_op jit(solution)/shard_map/ppermute | solution.py:279
  16.3 0.0 collective-permute-start.9
  16.3 0.0 collective-permute-done.4
  16.3 2.4 %collective-permute-done.5 = bf16[6,32,128]{2,1,0:T(8,128)(2,1)S(1)} collective-permute-done((bf16[6,32,128]{2,1,0:T(8,128)(2,1)S(1)}, bf16[6,32,128]{2,1,0:T(8,128)(2,1)S(1)}, u32[]{:S(2)}, u32[]{:S(2)}) %collective-permute-start.5) | collective-permute-done | bytes 49184 | tf_op jit(solution)/shard_map/ppermute | solution.py:279
  18.7 3.0 %collective-permute-start.8 = (bf16[2,24,16,128]{3,2,1,0:T(8,128)(2,1)S(1)}, bf16[2,24,16,128]{3,2,1,0:T(8,128)(2,1)S(1)}, u32[]{:S(2)}, u32[]{:S(2)}) collective-permute-start(bf16[2,24,16,128]{3,2,1,0:T(8,128)(2,1)S(1)} %pad_maximum_fusion), channel_id=1, source_target_pairs={{0,4},{1,5},{2,6},{3,7},{4,0},{5,1},{6,2},{7,3},{8,12},{9,13},{10,... | collective-permute-start | bytes 589832 | tf_op jit(solution)/shard_map/ppermute | solution.py:279
  21.9 1.6 %collective-permute-start.6 = (bf16[24,32,128]{2,1,0:T(8,128)(2,1)S(1)}, bf16[24,32,128]{2,1,0:T(8,128)(2,1)S(1)}, u32[]{:S(2)}, u32[]{:S(2)}) collective-permute-start(bf16[24,32,128]{2,1,0:T(8,128)(2,1)S(1)} %get-tuple-element.64.refs_0_), channel_id=1, source_target_pairs={{0,2},{1,3},{2,0},{3,1},{4,6},{5,7},{6,4},{7,5},{8,10},{9,11},{10,... | collective-permute-start | bytes 589832 | tf_op jit(solution)/shard_map/ppermute | solution.py:279
  23.4 6.2 %collective-permute-done.8 = bf16[2,24,16,128]{3,2,1,0:T(8,128)(2,1)S(1)} collective-permute-done((bf16[2,24,16,128]{3,2,1,0:T(8,128)(2,1)S(1)}, bf16[2,24,16,128]{3,2,1,0:T(8,128)(2,1)S(1)}, u32[]{:S(2)}, u32[]{:S(2)}) %collective-permute-start.8) | collective-permute-done | bytes 196640 | tf_op jit(solution)/shard_map/ppermute | solution.py:279
  29.6 0.1 collective-permute-start.11
  29.7 0.0 copy-done.2
  29.7 0.1 copy.14
  29.8 0.0 collective-permute-done.6.refs_1_
  29.9 0.1 collective-permute-start.7
  30.0 0.1 copy.18.refs_3_
  30.1 0.1 copy.17.refs_4_
  30.2 1.4 %collective-permute-done.7.refs_2_ = bf16[48,32,128]{2,1,0:T(8,128)(2,1)S(1)} collective-permute-done((bf16[48,32,128]{2,1,0:T(8,128)(2,1)S(1)}, bf16[48,32,128]{2,1,0:T(8,128)(2,1)S(1)}, u32[]{:S(2)}, u32[]{:S(2)}) %collective-permute-start.7) | collective-permute-done | bytes 393248 | tf_op jit(solution)/shard_map/ppermute | solution.py:279
  31.7 1.3 %arrange_left.1.left_ref = bf16[32,128,128]{2,1,0:T(8,128)(2,1)S(1)} custom-call(bf16[24,32,128]{2,1,0:T(8,128)(2,1)S(1)} %get-tuple-element.64.refs_0_, bf16[24,32,128]{2,1,0:T(8,128)(2,1)S(1)} %collective-permute-done.6.refs_1_, bf16[48,32,128]{2,1,0:T(8,128)(2,1)S(1)} %collective-permute-done.7.refs_2_), custom_call_target="tpu_custom_call" | custom-call | flops 1048576 | bytes 8388608 | tf_op jit(solution)/shard_map/arrange_left/pallas_call | solution.py:123
  33.0 0.0 collective-permute-done.10.refs_3_
  33.0 0.0 collective-permute-done.9.refs_2_
  33.0 0.0 copy-start
  33.0 0.0 copy-start.1
  33.0 7.8 %update_0.1.refs_4_ = f32[32,2,128,256]{3,2,1,0:T(8,128)S(1)} custom-call(bf16[32,128,128]{2,1,0:T(8,128)(2,1)S(1)} %arrange_left.1.left_ref, bf16[24,16,128]{2,1,0:T(8,128)(2,1)S(1)} %get-tuple-element.48.refs_0_, bf16[24,16,128]{2,1,0:T(8,128)(2,1)S(1)} %get-tuple-element.58.refs_1_, bf16[24,16,128]{2,1,0:T(8,128)(2,1)S(1)} %collective-permute-done.9.refs_2_, ...), custom_call_target="tpu_custom_call" | custom-call | flops 3758096384 | bytes 16777216 | tf_op jit(solution)/shard_map/update_0/pallas_call | solution.py:229
  40.9 0.0 collective-permute-done.11.refs_2_
  40.9 0.0 copy-done
  40.9 0.0 copy-done.1
  40.9 9.4 %update_1.1 = bf16[4,32,128,128]{3,2,1,0:T(8,128)(2,1)} custom-call(bf16[32,128,128]{2,1,0:T(8,128)(2,1)S(1)} %arrange_left.1.left_ref, bf16[24,16,128]{2,1,0:T(8,128)(2,1)S(1)} %get-tuple-element.51.refs_0_, bf16[24,16,128]{2,1,0:T(8,128)(2,1)S(1)} %get-tuple-element.52.refs_1_, bf16[48,16,128]{2,1,0:T(8,128)(2,1)S(1)} %collective-permute-done.11.refs_2_, ...), custom_call_target="tpu_custom_call" | custom-call | flops 3758096384 | bytes 16777216 | tf_op jit(solution)/shard_map/update_1/pallas_call | solution.py:229
  (19 shorter events, 0.3 us)
Async XLA Ops:
  0.0 29.7 %copy-start.2 = (bf16[1024,128]{1,0:T(8,128)(2,1)S(1)}, bf16[1024,128]{1,0:T(8,128)(2,1)}, u32[]{:S(2)}) copy-start(bf16[1024,128]{1,0:T(8,128)(2,1)} %param.18) | copy-start | bytes 786436
  4.6 3.2 %collective-permute-start = (bf16[2,6,16,128]{3,2,1,0:T(8,128)(2,1)S(1)}, bf16[2,6,16,128]{3,2,1,0:T(8,128)(2,1)S(1)}, u32[]{:S(2)}, u32[]{:S(2)}) collective-permute-start(bf16[2,6,16,128]{3,2,1,0:T(8,128)(2,1)S(1)} %get-tuple-element.34), channel_id=1, source_target_pairs={{0,1},{1,0},{2,3},{3,2},{4,5},{5,4},{6,7},{7,6},{8,9},{9,8},{10,11... | collective-permute-start | bytes 147464 | tf_op jit(solution)/shard_map/ppermute | solution.py:279
  5.1 7.1 %collective-permute-start.2 = (bf16[2,6,16,128]{3,2,1,0:T(8,128)(2,1)S(1)}, bf16[2,6,16,128]{3,2,1,0:T(8,128)(2,1)S(1)}, u32[]{:S(2)}, u32[]{:S(2)}) collective-permute-start(bf16[2,6,16,128]{3,2,1,0:T(8,128)(2,1)S(1)} %get-tuple-element.39), channel_id=1, source_target_pairs={{0,2},{1,3},{2,0},{3,1},{4,6},{5,7},{6,4},{7,5},{8,10},{9,11},{10,... | collective-permute-start | bytes 147464 | tf_op jit(solution)/shard_map/ppermute | solution.py:279
  7.7 4.6 %collective-permute-start.3 = (bf16[2,6,16,128]{3,2,1,0:T(8,128)(2,1)S(1)}, bf16[2,6,16,128]{3,2,1,0:T(8,128)(2,1)S(1)}, u32[]{:S(2)}, u32[]{:S(2)}) collective-permute-start(bf16[2,6,16,128]{3,2,1,0:T(8,128)(2,1)S(1)} %get-tuple-element.40), channel_id=1, source_target_pairs={{0,3},{1,2},{2,1},{3,0},{4,7},{5,6},{6,5},{7,4},{8,11},{9,10},{10,... | collective-permute-start | bytes 147464 | tf_op jit(solution)/shard_map/ppermute | solution.py:279
  7.8 4.6 %collective-permute-start.1 = (bf16[6,32,128]{2,1,0:T(8,128)(2,1)S(1)}, bf16[6,32,128]{2,1,0:T(8,128)(2,1)S(1)}, u32[]{:S(2)}, u32[]{:S(2)}) collective-permute-start(bf16[6,32,128]{2,1,0:T(8,128)(2,1)S(1)} %get-tuple-element.36), channel_id=1, source_target_pairs={{0,4},{1,5},{2,6},{3,7},{4,0},{5,1},{6,2},{7,3},{8,12},{9,13},{10,... | collective-permute-start | bytes 147464 | tf_op jit(solution)/shard_map/ppermute | solution.py:279
  9.6 6.7 %collective-permute-start.4 = (bf16[6,32,128]{2,1,0:T(8,128)(2,1)S(1)}, bf16[6,32,128]{2,1,0:T(8,128)(2,1)S(1)}, u32[]{:S(2)}, u32[]{:S(2)}) collective-permute-start(bf16[6,32,128]{2,1,0:T(8,128)(2,1)S(1)} %get-tuple-element.42), channel_id=1, source_target_pairs={{0,8},{1,9},{2,10},{3,11},{4,12},{5,13},{6,14},{7,15},{8,0},{9,1},... | collective-permute-start | bytes 147464 | tf_op jit(solution)/shard_map/ppermute | solution.py:279
  12.2 6.5 %collective-permute-start.5 = (bf16[6,32,128]{2,1,0:T(8,128)(2,1)S(1)}, bf16[6,32,128]{2,1,0:T(8,128)(2,1)S(1)}, u32[]{:S(2)}, u32[]{:S(2)}) collective-permute-start(bf16[6,32,128]{2,1,0:T(8,128)(2,1)S(1)} %get-tuple-element.43), channel_id=1, source_target_pairs={{0,12},{1,13},{2,14},{3,15},{4,8},{5,9},{6,10},{7,11},{8,4},{9,5},... | collective-permute-start | bytes 147464 | tf_op jit(solution)/shard_map/ppermute | solution.py:279
  12.4 20.6 %collective-permute-start.10 = (bf16[24,16,128]{2,1,0:T(8,128)(2,1)S(1)}, bf16[24,16,128]{2,1,0:T(8,128)(2,1)S(1)}, u32[]{:S(2)}, u32[]{:S(2)}) collective-permute-start(bf16[24,16,128]{2,1,0:T(8,128)(2,1)S(1)} %get-tuple-element.48.refs_0_), channel_id=1, source_target_pairs={{0,12},{1,13},{2,14},{3,15},{4,8},{5,9},{6,10},{7,11},{8,4},{9,5},... | collective-permute-start | bytes 294920 | tf_op jit(solution)/shard_map/ppermute | solution.py:279
  16.3 16.7 %collective-permute-start.9 = (bf16[24,16,128]{2,1,0:T(8,128)(2,1)S(1)}, bf16[24,16,128]{2,1,0:T(8,128)(2,1)S(1)}, u32[]{:S(2)}, u32[]{:S(2)}) collective-permute-start(bf16[24,16,128]{2,1,0:T(8,128)(2,1)S(1)} %get-tuple-element.48.refs_0_), channel_id=1, source_target_pairs={{0,8},{1,9},{2,10},{3,11},{4,12},{5,13},{6,14},{7,15},{8,0},{9,1},... | collective-permute-start | bytes 294920 | tf_op jit(solution)/shard_map/ppermute | solution.py:279
  18.7 10.9 %collective-permute-start.8 = (bf16[2,24,16,128]{3,2,1,0:T(8,128)(2,1)S(1)}, bf16[2,24,16,128]{3,2,1,0:T(8,128)(2,1)S(1)}, u32[]{:S(2)}, u32[]{:S(2)}) collective-permute-start(bf16[2,24,16,128]{3,2,1,0:T(8,128)(2,1)S(1)} %pad_maximum_fusion), channel_id=1, source_target_pairs={{0,4},{1,5},{2,6},{3,7},{4,0},{5,1},{6,2},{7,3},{8,12},{9,13},{10,... | collective-permute-start | bytes 589832 | tf_op jit(solution)/shard_map/ppermute | solution.py:279
  21.9 8.0 %collective-permute-start.6 = (bf16[24,32,128]{2,1,0:T(8,128)(2,1)S(1)}, bf16[24,32,128]{2,1,0:T(8,128)(2,1)S(1)}, u32[]{:S(2)}, u32[]{:S(2)}) collective-permute-start(bf16[24,32,128]{2,1,0:T(8,128)(2,1)S(1)} %get-tuple-element.64.refs_0_), channel_id=1, source_target_pairs={{0,2},{1,3},{2,0},{3,1},{4,6},{5,7},{6,4},{7,5},{8,10},{9,11},{10,... | collective-permute-start | bytes 589832 | tf_op jit(solution)/shard_map/ppermute | solution.py:279
  29.6 11.2 %collective-permute-start.11 = (bf16[48,16,128]{2,1,0:T(8,128)(2,1)S(1)}, bf16[48,16,128]{2,1,0:T(8,128)(2,1)S(1)}, u32[]{:S(2)}, u32[]{:S(2)}) collective-permute-start(bf16[48,16,128]{2,1,0:T(8,128)(2,1)S(1)} %constant_dynamic-update-slice_fusion.9), channel_id=1, source_target_pairs={{0,8},{1,9},{2,10},{3,11},{4,12},{5,13},{6,14},{7,15},{8,0},{9,1},... | collective-permute-start | bytes 589832 | tf_op jit(solution)/shard_map/ppermute | solution.py:279
  29.9 1.8 %collective-permute-start.7 = (bf16[48,32,128]{2,1,0:T(8,128)(2,1)S(1)}, bf16[48,32,128]{2,1,0:T(8,128)(2,1)S(1)}, u32[]{:S(2)}, u32[]{:S(2)}) collective-permute-start(bf16[48,32,128]{2,1,0:T(8,128)(2,1)S(1)} %constant_dynamic-update-slice_fusion.4), channel_id=1, source_target_pairs={{0,1},{1,0},{2,3},{3,2},{4,5},{5,4},{6,7},{7,6},{8,9},{9,8},{10,11... | collective-permute-start | bytes 1179656 | tf_op jit(solution)/shard_map/ppermute | solution.py:279
  33.0 7.9 %copy-start = (bf16[1,128,128,128]{3,2,1,0:T(8,128)(2,1)S(1)}, bf16[1,128,128,128]{3,2,1,0:T(8,128)(2,1)}, u32[]{:S(2)}) copy-start(bf16[1,128,128,128]{3,2,1,0:T(8,128)(2,1)} %param.11) | copy-start | bytes 12582916
  33.0 7.9 %copy-start.1 = (f32[128]{0:T(128)S(1)}, f32[128]{0:T(128)}, u32[]{:S(2)}) copy-start(f32[128]{0:T(128)} %param.19) | copy-start | bytes 1540

commit v16 on v15

--- a/solution.py
+++ b/solution.py
@@ -294,6 +294,7 @@
         mask //= 2
     near = swap(stacked, 1, 0)
     parts = [[mines[0], near[0]] + [swap(mines[0], d, 0) for d in range(2, side)]]
+    lefts[-1], *mines[1:] = lax.optimization_barrier((lefts[-1], *mines[1:]))
     for part in range(1, PARTS):
         pieces = [mines[part], near[part]]
         mask = 2

time: 50.4 us -> 49.1 us (0.974)
  starting transfers between devices: 16.3 us -> 13.6 us
  local copies, waits for them, and re-layouts: 0.56 us -> 1.46 us
    ppermute x12, starting transfers between devices: 16.3 us -> 13.6 us  [swap(): lax.ppermute(x, 'row', [(i, i ^ da * side + db) for i in range(devices)])]
    transpose x1, local copies, waits for them, and re-layouts: 0.11 us -> 1.05 us  [local(): final_matrix.reshape(width, width, -1).transpose(2, 1, 0)]
    ppermute x12, waiting for transfers between devices: 10 us -> 10.5 us  [swap(): lax.ppermute(x, 'row', [(i, i ^ da * side + db) for i in range(devices)])]
  transfers between devices with their start and end apart: 12 -> 12, of which waited for: 3 -> 5; matrix products, arithmetic and copies ran while one was open for 1% -> 3% of each run, Pallas kernels for 18% -> 19%
where the time goes in v16:
time: 49.1 us; the launch traced here: 48.9 us
  Pallas kernels  23 us (47%)
  starting transfers between devices  13.6 us (28%)
  waiting for transfers between devices  10.5 us (21%)
  local copies, waits for them, and re-layouts  1.46 us (3%)
    pallas_call x2, Pallas kernels, update_part(): pl.pallas_call(functools.partial(update_kernel, side, seqs, order, len(ri...  17.2 us
    ppermute x12, starting transfers between devices, swap(): lax.ppermute(x, 'row', [(i, i ^ da * side + db) for i in range(devices)])  13.6 us
    ppermute x12, waiting for transfers between devices, swap(): lax.ppermute(x, 'row', [(i, i ^ da * side + db) for i in range(devices)])  10.5 us
    pallas_call x1, Pallas kernels, project(): pl.pallas_call(functools.partial(project_kernel, side), in_specs=[pl.Bloc...  4.52 us
    pallas_call x1, Pallas kernels, arrange_left(): pl.pallas_call(functools.partial(arrange_kernel, seq_total), in_specs=[pl...  1.33 us
    transpose x1, local copies, waits for them, and re-layouts, local(): final_matrix.reshape(width, width, -1).transpose(2, 1, 0)  1.05 us
  transfers between devices with their start and end apart: 12, of which 5 were waited for; matrix products, arithmetic and copies ran while one was open for 3% of the time, Pallas kernels for 19%

profile of v16, /device:TPU:0, one launch (start us, length us, event | category | flops | bytes accessed | tf_op | source)
XLA Modules:
  0.0 48.9 jit_solution(13052269277538030921)
XLA Ops:
  0.0 4.5 %project.1 = (bf16[6,32,128]{2,1,0:T(8,128)(2,1)S(1)}, bf16[6,32,128]{2,1,0:T(8,128)(2,1)S(1)}, bf16[6,32,128]{2,1,0:T(8,128)(2,1)S(1)}, bf16[6,32,128]{2,1,0:T(...) custom-call(bf16[6,512,256]{2,1,0:T(8,128)(2,1)} %refs_0_.1, ...), custom_call_target="tpu_custom_call" | custom-call | tf_op jit(solution)/shard_map/project/pallas_call | solution.py:86
  4.5 0.5 %collective-permute-start = (bf16[2,6,16,128]{3,2,1,0:T(8,128)(2,1)S(1)}, bf16[2,6,16,128]{3,2,1,0:T(8,128)(2,1)S(1)}, u32[]{:S(2)}, u32[]{:S(2)}) collective-permute-start(bf16[2,6,16,128]{3,2,1,0:T(8,128)(2,1)S(1)} %get-tuple-element.36), channel_id=1, source_target_pairs={{0,1},{1,0},{2,3},{3,2},{4,5},{5,4},{6,7},{7,6},{8,9},{9,8},{10,11... | collective-permute-start | bytes 147464 | tf_op jit(solution)/shard_map/ppermute | solution.py:279
  5.0 2.6 %collective-permute-start.2 = (bf16[2,6,16,128]{3,2,1,0:T(8,128)(2,1)S(1)}, bf16[2,6,16,128]{3,2,1,0:T(8,128)(2,1)S(1)}, u32[]{:S(2)}, u32[]{:S(2)}) collective-permute-start(bf16[2,6,16,128]{3,2,1,0:T(8,128)(2,1)S(1)} %get-tuple-element.41), channel_id=1, source_target_pairs={{0,2},{1,3},{2,0},{3,1},{4,6},{5,7},{6,4},{7,5},{8,10},{9,11},{10,... | collective-permute-start | bytes 147464 | tf_op jit(solution)/shard_map/ppermute | solution.py:279
  7.6 0.1 collective-permute-start.3
  7.7 0.0 collective-permute-done
  7.7 1.8 %collective-permute-start.1 = (bf16[6,32,128]{2,1,0:T(8,128)(2,1)S(1)}, bf16[6,32,128]{2,1,0:T(8,128)(2,1)S(1)}, u32[]{:S(2)}, u32[]{:S(2)}) collective-permute-start(bf16[6,32,128]{2,1,0:T(8,128)(2,1)S(1)} %get-tuple-element.38), channel_id=1, source_target_pairs={{0,4},{1,5},{2,6},{3,7},{4,0},{5,1},{6,2},{7,3},{8,12},{9,13},{10,... | collective-permute-start | bytes 147464 | tf_op jit(solution)/shard_map/ppermute | solution.py:279
  9.6 2.6 %collective-permute-start.4 = (bf16[6,32,128]{2,1,0:T(8,128)(2,1)S(1)}, bf16[6,32,128]{2,1,0:T(8,128)(2,1)S(1)}, u32[]{:S(2)}, u32[]{:S(2)}) collective-permute-start(bf16[6,32,128]{2,1,0:T(8,128)(2,1)S(1)} %get-tuple-element.44), channel_id=1, source_target_pairs={{0,8},{1,9},{2,10},{3,11},{4,12},{5,13},{6,14},{7,15},{8,0},{9,1},... | collective-permute-start | bytes 147464 | tf_op jit(solution)/shard_map/ppermute | solution.py:279
  12.2 0.0 collective-permute-start.5
  12.2 0.0 collective-permute-done.2
  12.2 0.0 collective-permute-done.3
  12.3 0.0 collective-permute-done.1
  12.3 3.3 %collective-permute-done.4 = bf16[6,32,128]{2,1,0:T(8,128)(2,1)S(1)} collective-permute-done((bf16[6,32,128]{2,1,0:T(8,128)(2,1)S(1)}, bf16[6,32,128]{2,1,0:T(8,128)(2,1)S(1)}, u32[]{:S(2)}, u32[]{:S(2)}) %collective-permute-start.4) | collective-permute-done | bytes 49184 | tf_op jit(solution)/shard_map/ppermute | solution.py:279
  15.7 2.4 %collective-permute-done.5 = bf16[6,32,128]{2,1,0:T(8,128)(2,1)S(1)} collective-permute-done((bf16[6,32,128]{2,1,0:T(8,128)(2,1)S(1)}, bf16[6,32,128]{2,1,0:T(8,128)(2,1)S(1)}, u32[]{:S(2)}, u32[]{:S(2)}) %collective-permute-start.5) | collective-permute-done | bytes 49184 | tf_op jit(solution)/shard_map/ppermute | solution.py:279
  18.1 0.0 collective-permute-start.8
  18.2 1.6 %collective-permute-start.6 = (bf16[24,32,128]{2,1,0:T(8,128)(2,1)S(1)}, bf16[24,32,128]{2,1,0:T(8,128)(2,1)S(1)}, u32[]{:S(2)}, u32[]{:S(2)}) collective-permute-start(bf16[24,32,128]{2,1,0:T(8,128)(2,1)S(1)} %get-tuple-element.68.refs_0_), channel_id=1, source_target_pairs={{0,2},{1,3},{2,0},{3,1},{4,6},{5,7},{6,4},{7,5},{8,10},{9,11},{10,... | collective-permute-start | bytes 589832 | tf_op jit(solution)/shard_map/ppermute | solution.py:279
  19.8 2.3 %collective-permute-start.10 = (bf16[24,16,128]{2,1,0:T(8,128)(2,1)S(1)}, bf16[24,16,128]{2,1,0:T(8,128)(2,1)S(1)}, u32[]{:S(2)}, u32[]{:S(2)}) collective-permute-start(bf16[24,16,128]{2,1,0:T(8,128)(2,1)S(1)} %get-tuple-element.51.refs_0_), channel_id=1, source_target_pairs={{0,12},{1,13},{2,14},{3,15},{4,8},{5,9},{6,10},{7,11},{8,4},{9,5},... | collective-permute-start | bytes 294920 | tf_op jit(solution)/shard_map/ppermute | solution.py:279
  22.1 1.2 %collective-permute-start.9 = (bf16[24,16,128]{2,1,0:T(8,128)(2,1)S(1)}, bf16[24,16,128]{2,1,0:T(8,128)(2,1)S(1)}, u32[]{:S(2)}, u32[]{:S(2)}) collective-permute-start(bf16[24,16,128]{2,1,0:T(8,128)(2,1)S(1)} %get-tuple-element.51.refs_0_), channel_id=1, source_target_pairs={{0,8},{1,9},{2,10},{3,11},{4,12},{5,13},{6,14},{7,15},{8,0},{9,1},... | collective-permute-start | bytes 294920 | tf_op jit(solution)/shard_map/ppermute | solution.py:279
  23.2 2.3 %collective-permute-done.8 = bf16[2,24,16,128]{3,2,1,0:T(8,128)(2,1)S(1)} collective-permute-done((bf16[2,24,16,128]{3,2,1,0:T(8,128)(2,1)S(1)}, bf16[2,24,16,128]{3,2,1,0:T(8,128)(2,1)S(1)}, u32[]{:S(2)}, u32[]{:S(2)}) %collective-permute-start.8) | collective-permute-done | bytes 196640 | tf_op jit(solution)/shard_map/ppermute | solution.py:279
  25.5 1.1 %copy.14 = bf16[128,32,32]{0,2,1:T(8,128)(2,1)S(1)} copy(bf16[128,32,32]{0,1,2:T(8,128)(2,1)} %bitcast.40) | data formatting | bytes 524288 | tf_op jit(solution)/shard_map/transpose | solution.py:307
  26.6 0.0 collective-permute-done.6.refs_1_
  26.6 0.1 collective-permute-start.7
  26.7 0.1 copy.18.refs_3_
  26.9 0.1 copy.17.refs_4_
  27.0 1.4 %collective-permute-done.7.refs_2_ = bf16[48,32,128]{2,1,0:T(8,128)(2,1)S(1)} collective-permute-done((bf16[48,32,128]{2,1,0:T(8,128)(2,1)S(1)}, bf16[48,32,128]{2,1,0:T(8,128)(2,1)S(1)}, u32[]{:S(2)}, u32[]{:S(2)}) %collective-permute-start.7) | collective-permute-done | bytes 393248 | tf_op jit(solution)/shard_map/ppermute | solution.py:279
  28.4 0.8 %collective-permute-start.11 = (bf16[48,16,128]{2,1,0:T(8,128)(2,1)S(1)}, bf16[48,16,128]{2,1,0:T(8,128)(2,1)S(1)}, u32[]{:S(2)}, u32[]{:S(2)}) collective-permute-start(bf16[48,16,128]{2,1,0:T(8,128)(2,1)S(1)} %pad_maximum_fusion.1), channel_id=1, source_target_pairs={{0,8},{1,9},{2,10},{3,11},{4,12},{5,13},{6,14},{7,15},{8,0},{9,1},... | collective-permute-start | bytes 589832 | tf_op jit(solution)/shard_map/ppermute | solution.py:279
  29.3 1.3 %arrange_left.1.left_ref = bf16[32,128,128]{2,1,0:T(8,128)(2,1)S(1)} custom-call(bf16[24,32,128]{2,1,0:T(8,128)(2,1)S(1)} %get-tuple-element.68.refs_0_, bf16[24,32,128]{2,1,0:T(8,128)(2,1)S(1)} %collective-permute-done.6.refs_1_, bf16[48,32,128]{2,1,0:T(8,128)(2,1)S(1)} %collective-permute-done.7.refs_2_), custom_call_target="tpu_custom_call" | custom-call | flops 1048576 | bytes 8388608 | tf_op jit(solution)/shard_map/arrange_left/pallas_call | solution.py:123
  30.6 0.0 collective-permute-done.10.refs_3_
  30.6 0.0 collective-permute-done.9.refs_2_
  30.6 0.0 copy-start
  30.6 0.0 copy-start.1
  30.6 7.8 %update_0.1.refs_4_ = f32[32,2,128,256]{3,2,1,0:T(8,128)S(1)} custom-call(bf16[32,128,128]{2,1,0:T(8,128)(2,1)S(1)} %arrange_left.1.left_ref, bf16[24,16,128]{2,1,0:T(8,128)(2,1)S(1)} %get-tuple-element.51.refs_0_, bf16[24,16,128]{2,1,0:T(8,128)(2,1)S(1)} %get-tuple-element.62.refs_1_, bf16[24,16,128]{2,1,0:T(8,128)(2,1)S(1)} %collective-permute-done.9.refs_2_, ...), custom_call_target="tpu_custom_call" | custom-call | flops 3758096384 | bytes 16777216 | tf_op jit(solution)/shard_map/update_0/pallas_call | solution.py:229
  38.5 1.1 %collective-permute-done.11.refs_2_ = bf16[48,16,128]{2,1,0:T(8,128)(2,1)S(1)} collective-permute-done((bf16[48,16,128]{2,1,0:T(8,128)(2,1)S(1)}, bf16[48,16,128]{2,1,0:T(8,128)(2,1)S(1)}, u32[]{:S(2)}, u32[]{:S(2)}) %collective-permute-start.11) | collective-permute-done | bytes 196640 | tf_op jit(solution)/shard_map/ppermute | solution.py:279
  39.5 0.0 copy-done
  39.5 0.0 copy-done.1
  39.5 9.4 %update_1.1 = bf16[4,32,128,128]{3,2,1,0:T(8,128)(2,1)} custom-call(bf16[32,128,128]{2,1,0:T(8,128)(2,1)S(1)} %arrange_left.1.left_ref, bf16[24,16,128]{2,1,0:T(8,128)(2,1)S(1)} %get-tuple-element.55.refs_0_, bf16[24,16,128]{2,1,0:T(8,128)(2,1)S(1)} %get-tuple-element.56.refs_1_, bf16[48,16,128]{2,1,0:T(8,128)(2,1)S(1)} %collective-permute-done.11.refs_2_, ...), custom_call_target="tpu_custom_call" | custom-call | flops 3758096384 | bytes 16777216 | tf_op jit(solution)/shard_map/update_1/pallas_call | solution.py:229
  (15 shorter events, 0.2 us)
Async XLA Ops:
  4.5 3.2 %collective-permute-start = (bf16[2,6,16,128]{3,2,1,0:T(8,128)(2,1)S(1)}, bf16[2,6,16,128]{3,2,1,0:T(8,128)(2,1)S(1)}, u32[]{:S(2)}, u32[]{:S(2)}) collective-permute-start(bf16[2,6,16,128]{3,2,1,0:T(8,128)(2,1)S(1)} %get-tuple-element.36), channel_id=1, source_target_pairs={{0,1},{1,0},{2,3},{3,2},{4,5},{5,4},{6,7},{7,6},{8,9},{9,8},{10,11... | collective-permute-start | bytes 147464 | tf_op jit(solution)/shard_map/ppermute | solution.py:279
  5.0 7.1 %collective-permute-start.2 = (bf16[2,6,16,128]{3,2,1,0:T(8,128)(2,1)S(1)}, bf16[2,6,16,128]{3,2,1,0:T(8,128)(2,1)S(1)}, u32[]{:S(2)}, u32[]{:S(2)}) collective-permute-start(bf16[2,6,16,128]{3,2,1,0:T(8,128)(2,1)S(1)} %get-tuple-element.41), channel_id=1, source_target_pairs={{0,2},{1,3},{2,0},{3,1},{4,6},{5,7},{6,4},{7,5},{8,10},{9,11},{10,... | collective-permute-start | bytes 147464 | tf_op jit(solution)/shard_map/ppermute | solution.py:279
  7.6 4.6 %collective-permute-start.3 = (bf16[2,6,16,128]{3,2,1,0:T(8,128)(2,1)S(1)}, bf16[2,6,16,128]{3,2,1,0:T(8,128)(2,1)S(1)}, u32[]{:S(2)}, u32[]{:S(2)}) collective-permute-start(bf16[2,6,16,128]{3,2,1,0:T(8,128)(2,1)S(1)} %get-tuple-element.42), channel_id=1, source_target_pairs={{0,3},{1,2},{2,1},{3,0},{4,7},{5,6},{6,5},{7,4},{8,11},{9,10},{10,... | collective-permute-start | bytes 147464 | tf_op jit(solution)/shard_map/ppermute | solution.py:279
  7.7 4.6 %collective-permute-start.1 = (bf16[6,32,128]{2,1,0:T(8,128)(2,1)S(1)}, bf16[6,32,128]{2,1,0:T(8,128)(2,1)S(1)}, u32[]{:S(2)}, u32[]{:S(2)}) collective-permute-start(bf16[6,32,128]{2,1,0:T(8,128)(2,1)S(1)} %get-tuple-element.38), channel_id=1, source_target_pairs={{0,4},{1,5},{2,6},{3,7},{4,0},{5,1},{6,2},{7,3},{8,12},{9,13},{10,... | collective-permute-start | bytes 147464 | tf_op jit(solution)/shard_map/ppermute | solution.py:279
  9.6 6.1 %collective-permute-start.4 = (bf16[6,32,128]{2,1,0:T(8,128)(2,1)S(1)}, bf16[6,32,128]{2,1,0:T(8,128)(2,1)S(1)}, u32[]{:S(2)}, u32[]{:S(2)}) collective-permute-start(bf16[6,32,128]{2,1,0:T(8,128)(2,1)S(1)} %get-tuple-element.44), channel_id=1, source_target_pairs={{0,8},{1,9},{2,10},{3,11},{4,12},{5,13},{6,14},{7,15},{8,0},{9,1},... | collective-permute-start | bytes 147464 | tf_op jit(solution)/shard_map/ppermute | solution.py:279
  12.2 5.9 %collective-permute-start.5 = (bf16[6,32,128]{2,1,0:T(8,128)(2,1)S(1)}, bf16[6,32,128]{2,1,0:T(8,128)(2,1)S(1)}, u32[]{:S(2)}, u32[]{:S(2)}) collective-permute-start(bf16[6,32,128]{2,1,0:T(8,128)(2,1)S(1)} %get-tuple-element.45), channel_id=1, source_target_pairs={{0,12},{1,13},{2,14},{3,15},{4,8},{5,9},{6,10},{7,11},{8,4},{9,5},... | collective-permute-start | bytes 147464 | tf_op jit(solution)/shard_map/ppermute | solution.py:279
  18.1 7.5 %collective-permute-start.8 = (bf16[2,24,16,128]{3,2,1,0:T(8,128)(2,1)S(1)}, bf16[2,24,16,128]{3,2,1,0:T(8,128)(2,1)S(1)}, u32[]{:S(2)}, u32[]{:S(2)}) collective-permute-start(bf16[2,24,16,128]{3,2,1,0:T(8,128)(2,1)S(1)} %pad_maximum_fusion), channel_id=1, source_target_pairs={{0,4},{1,5},{2,6},{3,7},{4,0},{5,1},{6,2},{7,3},{8,12},{9,13},{10,... | collective-permute-start | bytes 589832 | tf_op jit(solution)/shard_map/ppermute | solution.py:279
  18.2 8.4 %collective-permute-start.6 = (bf16[24,32,128]{2,1,0:T(8,128)(2,1)S(1)}, bf16[24,32,128]{2,1,0:T(8,128)(2,1)S(1)}, u32[]{:S(2)}, u32[]{:S(2)}) collective-permute-start(bf16[24,32,128]{2,1,0:T(8,128)(2,1)S(1)} %get-tuple-element.68.refs_0_), channel_id=1, source_target_pairs={{0,2},{1,3},{2,0},{3,1},{4,6},{5,7},{6,4},{7,5},{8,10},{9,11},{10,... | collective-permute-start | bytes 589832 | tf_op jit(solution)/shard_map/ppermute | solution.py:279
  19.8 10.8 %collective-permute-start.10 = (bf16[24,16,128]{2,1,0:T(8,128)(2,1)S(1)}, bf16[24,16,128]{2,1,0:T(8,128)(2,1)S(1)}, u32[]{:S(2)}, u32[]{:S(2)}) collective-permute-start(bf16[24,16,128]{2,1,0:T(8,128)(2,1)S(1)} %get-tuple-element.51.refs_0_), channel_id=1, source_target_pairs={{0,12},{1,13},{2,14},{3,15},{4,8},{5,9},{6,10},{7,11},{8,4},{9,5},... | collective-permute-start | bytes 294920 | tf_op jit(solution)/shard_map/ppermute | solution.py:279
  22.1 8.5 %collective-permute-start.9 = (bf16[24,16,128]{2,1,0:T(8,128)(2,1)S(1)}, bf16[24,16,128]{2,1,0:T(8,128)(2,1)S(1)}, u32[]{:S(2)}, u32[]{:S(2)}) collective-permute-start(bf16[24,16,128]{2,1,0:T(8,128)(2,1)S(1)} %get-tuple-element.51.refs_0_), channel_id=1, source_target_pairs={{0,8},{1,9},{2,10},{3,11},{4,12},{5,13},{6,14},{7,15},{8,0},{9,1},... | collective-permute-start | bytes 294920 | tf_op jit(solution)/shard_map/ppermute | solution.py:279
  26.6 1.8 %collective-permute-start.7 = (bf16[48,32,128]{2,1,0:T(8,128)(2,1)S(1)}, bf16[48,32,128]{2,1,0:T(8,128)(2,1)S(1)}, u32[]{:S(2)}, u32[]{:S(2)}) collective-permute-start(bf16[48,32,128]{2,1,0:T(8,128)(2,1)S(1)} %constant_dynamic-update-slice_fusion.4), channel_id=1, source_target_pairs={{0,1},{1,0},{2,3},{3,2},{4,5},{5,4},{6,7},{7,6},{8,9},{9,8},{10,11... | collective-permute-start | bytes 1179656 | tf_op jit(solution)/shard_map/ppermute | solution.py:279
  28.4 11.1 %collective-permute-start.11 = (bf16[48,16,128]{2,1,0:T(8,128)(2,1)S(1)}, bf16[48,16,128]{2,1,0:T(8,128)(2,1)S(1)}, u32[]{:S(2)}, u32[]{:S(2)}) collective-permute-start(bf16[48,16,128]{2,1,0:T(8,128)(2,1)S(1)} %pad_maximum_fusion.1), channel_id=1, source_target_pairs={{0,8},{1,9},{2,10},{3,11},{4,12},{5,13},{6,14},{7,15},{8,0},{9,1},... | collective-permute-start | bytes 589832 | tf_op jit(solution)/shard_map/ppermute | solution.py:279
  30.6 8.9 %copy-start = (bf16[1,128,128,128]{3,2,1,0:T(8,128)(2,1)S(1)}, bf16[1,128,128,128]{3,2,1,0:T(8,128)(2,1)}, u32[]{:S(2)}) copy-start(bf16[1,128,128,128]{3,2,1,0:T(8,128)(2,1)} %param.11) | copy-start | bytes 12582916
  30.6 8.9 %copy-start.1 = (f32[128]{0:T(128)S(1)}, f32[128]{0:T(128)}, u32[]{:S(2)}) copy-start(f32[128]{0:T(128)} %param.19) | copy-start | bytes 1540

commit v17 on v15

--- a/solution.py
+++ b/solution.py
@@ -46,16 +46,26 @@
         for h in range(pack)
     ]
     left_bias = jnp.concatenate([bl_ref[...]] * pack, axis=1)
+    ones = jnp.ones((chans, LANES), jnp.bfloat16)
     right_bias = jnp.broadcast_to(br_ref[...], (tile, width)).T
     for s in range(seqs):
         x_copies[s].wait()
         normed = normed_ref.at[s % 2]
-        x = x_ref[s].astype(jnp.float32)
-        center = x - jnp.mean(x, axis=-1, keepdims=True)
-        variance = jnp.mean(center * center, axis=-1, keepdims=True)
-        normed[...] = (
-            center * lax.rsqrt(variance + 1e-05) * gain_ref[...] + offset_ref[...]
-        ).astype(jnp.bfloat16)
+        mean = jnp.dot(x_ref[s], ones, preferred_element_type=jnp.float32) * (1.0 / chans)
+        center = [
+            x_ref[s, :, k : k + LANES].astype(jnp.float32) - mean for k in range(0, chans, LANES)
+        ]
+        square = jnp.concatenate([c * c for c in center], axis=1)
+        high = square.astype(jnp.bfloat16)
+        low = (square - high.astype(jnp.float32)).astype(jnp.bfloat16)
+        variance = (
+            jnp.dot(high, ones, preferred_element_type=jnp.float32)
+            + jnp.dot(low, ones, preferred_element_type=jnp.float32)
+        ) * (1.0 / chans)
+        scale = lax.rsqrt(variance + 1e-05)
+        for k, c in enumerate(center):
+            at = slice(k * LANES, (k + 1) * LANES)
+            normed[:, at] = (c * scale * gain_ref[:, at] + offset_ref[:, at]).astype(jnp.bfloat16)
         blocks = []
         for d in range(side):
             b = place_b ^ d
@@ -113,7 +123,7 @@
     if depth > seq_total:
         wide[seq_total * rows :] = jnp.zeros(((depth - seq_total) * rows, lanes), jnp.float32)
     for r in range(rows):
-        out_ref[r] = wide[pl.ds(r, depth, stride=rows), :].T.astype(jnp.bfloat16)
+        out_ref[r] = wide[pl.ds(r, depth, stride=rows), :].astype(jnp.bfloat16).T
 
 
 def arrange_left(lefts, tile):
@@ -139,7 +149,13 @@
         before_ref, refs = refs[0], refs[1:]
     if last:
         bias_ref, pair_ref, refs = refs[0], refs[1], refs[2:]
-    out_ref, right_wide, right_flat, outer = refs
+    out_ref, right_wide, right_flat, outer, *refs = refs
+    if last:
+        ready, sems = refs
+
+        def copy_out(row):
+            return pltpu.make_async_copy(ready.at[:, row], out_ref.at[:, row], sems.at[row])
+
     rows, lanes, depth = left_ref.shape
     _, some, tile = right_refs[0].shape
     halves = outer.shape[0] // group
@@ -198,13 +214,22 @@
                 h = 2 * g + k
                 share = update[:, k * tile : (k + 1) * tile].T * (1.0 / seq_total) + bias_ref[...]
                 old = pair_ref[h, at + q].astype(jnp.float32)
-                out_ref[h, q] = (old + share).astype(jnp.bfloat16)
+                ready[h, at + q] = (old + share).astype(jnp.bfloat16)
+        if last:
+            copy_out(at + q).start()
 
     for q in range(group + 1):
         if q < group:
             outer_products(q)
         if q > 0:
             project_back(q - 1)
+
+    if last:
+
+        @pl.when(pl.program_id(0) == pl.num_programs(0) - 1)
+        def _():
+            for row in range(rows):
+                copy_out(row).wait()
 
 
 def update_part(side, seqs, order, part, left, right, wt, before, bias, pair):
@@ -214,16 +239,25 @@
     pack = tile // rows
     width = lanes // pack
     halves = pack // 2
-    group = 8
+    group = 8 if part == PARTS - 1 else 16
     first, last = part == 0, part == PARTS - 1
     in_vmem = pl.BlockSpec(memory_space=pltpu.VMEM)
+    scratch = [
+        pltpu.VMEM((depth * some, tile), jnp.float32),
+        pltpu.VMEM((depth, some * tile), jnp.bfloat16),
+        pltpu.VMEM((group * halves, some * width, 2 * tile), jnp.bfloat16),
+    ]
     operands = [left] + list(right) + [wt[:, part * some * width : (part + 1) * some * width]]
     if not first:
         operands.append(before)
     if last:
         operands += [bias[None], pair.reshape(pack, rows, tile, chans)]
         out_shape = jax.ShapeDtypeStruct((pack, rows, tile, chans), jnp.bfloat16)
-        out_spec = pl.BlockSpec((pack, group, tile, chans), lambda g: (0, g, 0, 0))
+        out_spec = pl.BlockSpec(memory_space=pltpu.HBM)
+        scratch += [
+            pltpu.VMEM((pack, rows, tile, chans), jnp.bfloat16),
+            pltpu.SemaphoreType.DMA((rows,)),
+        ]
     else:
         out_shape, out_spec = pltpu.VMEM((rows, halves, chans, 2 * tile), jnp.float32), in_vmem
     return pl.pallas_call(
@@ -232,12 +266,8 @@
         in_specs=[in_vmem] * len(operands),
         out_specs=out_spec,
         out_shape=out_shape,
-        scratch_shapes=[
-            pltpu.VMEM((depth * some, tile), jnp.float32),
-            pltpu.VMEM((depth, some * tile), jnp.bfloat16),
-            pltpu.VMEM((group * halves, some * width, 2 * tile), jnp.bfloat16),
-        ],
-        compiler_params=pltpu.CompilerParams(vmem_limit_bytes=24 * MIB),
+        scratch_shapes=scratch,
+        compiler_params=pltpu.CompilerParams(vmem_limit_bytes=32 * MIB),
         cost_estimate=pl.CostEstimate(
             flops=2 * tile * tile * some * width * (side * side * seqs + chans),
             bytes_accessed=16 * MIB,
@@ -284,7 +314,6 @@
     mines = [jnp.concatenate([x[part] for x in right]) for part in range(PARTS)]
     stacked = jnp.stack(mines)
     left[1], mines[0] = lax.optimization_barrier((left[1], mines[0]))
-    *left, stacked = lax.optimization_barrier((*left, stacked))
     lefts = [jnp.concatenate(left)]
     order = [0]
     mask = side // 2
@@ -294,6 +323,7 @@
         mask //= 2
     near = swap(stacked, 1, 0)
     parts = [[mines[0], near[0]] + [swap(mines[0], d, 0) for d in range(2, side)]]
+    lefts[1], *mines[1:] = lax.optimization_barrier((lefts[1], *mines[1:]))
     for part in range(1, PARTS):
         pieces = [mines[part], near[part]]
         mask = 2

time: 50.4 us -> 53.9 us (1.069)
  waiting for transfers between devices: 10 us -> 14.3 us
  starting transfers between devices: 16.3 us -> 12.3 us
  Pallas kernels: 23.1 us -> 25.3 us
  local copies, waits for them, and re-layouts: 0.56 us -> 1.45 us
    ppermute x12, waiting for transfers between devices: 10 us -> 14.3 us  [swap(): lax.ppermute(x, 'row', [(i, i ^ da * side + db) for i in range(devices)])]
    ppermute x12, starting transfers between devices: 16.3 us -> 12.3 us  [swap(): lax.ppermute(x, 'row', [(i, i ^ da * side + db) for i in range(devices)])]
    pallas_call x1, Pallas kernels: 4.57 us -> 6.97 us  [project(): pl.pallas_call(functools.partial(project_kernel, side), in_specs=[pl.Bloc...]
    transpose x1, local copies, waits for them, and re-layouts: 0.11 us -> 1.06 us  [local(): final_matrix.reshape(width, width, -1).transpose(2, 1, 0)]
  transfers between devices with their start and end apart: 12 -> 12, of which waited for: 3 -> 5; matrix products, arithmetic and copies ran while one was open for 1% -> 3% of each run, Pallas kernels for 18% -> 16%
where the time goes in v17:
time: 53.9 us; the launch traced here: 53.7 us
  Pallas kernels  25.3 us (47%)
  waiting for transfers between devices  14.3 us (27%)
  starting transfers between devices  12.3 us (23%)
  local copies, waits for them, and re-layouts  1.45 us (3%)
    pallas_call x2, Pallas kernels, update_part(): pl.pallas_call(functools.partial(update_kernel, side, seqs, order, len(ri...  16.9 us
    ppermute x12, waiting for transfers between devices, swap(): lax.ppermute(x, 'row', [(i, i ^ da * side + db) for i in range(devices)])  14.3 us
    ppermute x12, starting transfers between devices, swap(): lax.ppermute(x, 'row', [(i, i ^ da * side + db) for i in range(devices)])  12.3 us
    pallas_call x1, Pallas kernels, project(): pl.pallas_call(functools.partial(project_kernel, side), in_specs=[pl.Bloc...  6.97 us
    pallas_call x1, Pallas kernels, arrange_left(): pl.pallas_call(functools.partial(arrange_kernel, seq_total), in_specs=[pl...  1.41 us
  transfers between devices with their start and end apart: 12, of which 5 were waited for; matrix products, arithmetic and copies ran while one was open for 3% of the time, Pallas kernels for 16%

profile of v17, /device:TPU:0, one launch (start us, length us, event | category | flops | bytes accessed | tf_op | source)
XLA Modules:
  0.0 53.7 jit_solution(2470764757941514742)
XLA Ops:
  0.0 7.0 %project.1 = (bf16[6,32,128]{2,1,0:T(8,128)(2,1)S(1)}, bf16[6,32,128]{2,1,0:T(8,128)(2,1)S(1)}, bf16[6,32,128]{2,1,0:T(8,128)(2,1)S(1)}, bf16[6,32,128]{2,1,0:T(...) custom-call(bf16[6,512,256]{2,1,0:T(8,128)(2,1)} %refs_0_.1, ...), custom_call_target="tpu_custom_call" | custom-call | tf_op jit(solution)/shard_map/project/pallas_call | solution.py:96
  7.0 0.5 collective-permute-start
  7.5 2.6 %collective-permute-start.2 = (bf16[2,6,16,128]{3,2,1,0:T(8,128)(2,1)S(1)}, bf16[2,6,16,128]{3,2,1,0:T(8,128)(2,1)S(1)}, u32[]{:S(2)}, u32[]{:S(2)}) collective-permute-start(bf16[2,6,16,128]{3,2,1,0:T(8,128)(2,1)S(1)} %get-tuple-element.36), channel_id=1, source_target_pairs={{0,2},{1,3},{2,0},{3,1},{4,6},{5,7},{6,4},{7,5},{8,10},{9,11},{10,... | collective-permute-start | bytes 147464 | tf_op jit(solution)/shard_map/ppermute | solution.py:309
  10.1 0.1 collective-permute-start.3
  10.2 0.0 collective-permute-done
  10.2 1.9 %collective-permute-start.1 = (bf16[6,32,128]{2,1,0:T(8,128)(2,1)S(1)}, bf16[6,32,128]{2,1,0:T(8,128)(2,1)S(1)}, u32[]{:S(2)}, u32[]{:S(2)}) collective-permute-start(bf16[6,32,128]{2,1,0:T(8,128)(2,1)S(1)} %get-tuple-element.33), channel_id=1, source_target_pairs={{0,4},{1,5},{2,6},{3,7},{4,0},{5,1},{6,2},{7,3},{8,12},{9,13},{10,... | collective-permute-start | bytes 147464 | tf_op jit(solution)/shard_map/ppermute | solution.py:309
  12.0 2.6 %collective-permute-start.4 = (bf16[6,32,128]{2,1,0:T(8,128)(2,1)S(1)}, bf16[6,32,128]{2,1,0:T(8,128)(2,1)S(1)}, u32[]{:S(2)}, u32[]{:S(2)}) collective-permute-start(bf16[6,32,128]{2,1,0:T(8,128)(2,1)S(1)} %get-tuple-element.39), channel_id=1, source_target_pairs={{0,8},{1,9},{2,10},{3,11},{4,12},{5,13},{6,14},{7,15},{8,0},{9,1},... | collective-permute-start | bytes 147464 | tf_op jit(solution)/shard_map/ppermute | solution.py:309
  14.6 0.0 collective-permute-start.5
  14.6 0.0 collective-permute-done.2
  14.6 0.0 collective-permute-done.3
  14.7 1.0 %collective-permute-start.8 = (bf16[2,24,16,128]{3,2,1,0:T(8,128)(2,1)S(1)}, bf16[2,24,16,128]{3,2,1,0:T(8,128)(2,1)S(1)}, u32[]{:S(2)}, u32[]{:S(2)}) collective-permute-start(bf16[2,24,16,128]{3,2,1,0:T(8,128)(2,1)S(1)} %pad_maximum_fusion), channel_id=1, source_target_pairs={{0,4},{1,5},{2,6},{3,7},{4,0},{5,1},{6,2},{7,3},{8,12},{9,13},{10,... | collective-permute-start | bytes 589832 | tf_op jit(solution)/shard_map/ppermute | solution.py:309
  15.7 0.0 collective-permute-done.1
  15.8 2.4 %collective-permute-done.4 = bf16[6,32,128]{2,1,0:T(8,128)(2,1)S(1)} collective-permute-done((bf16[6,32,128]{2,1,0:T(8,128)(2,1)S(1)}, bf16[6,32,128]{2,1,0:T(8,128)(2,1)S(1)}, u32[]{:S(2)}, u32[]{:S(2)}) %collective-permute-start.4) | collective-permute-done | bytes 49184 | tf_op jit(solution)/shard_map/ppermute | solution.py:309
  18.1 2.9 %collective-permute-done.5 = bf16[6,32,128]{2,1,0:T(8,128)(2,1)S(1)} collective-permute-done((bf16[6,32,128]{2,1,0:T(8,128)(2,1)S(1)}, bf16[6,32,128]{2,1,0:T(8,128)(2,1)S(1)}, u32[]{:S(2)}, u32[]{:S(2)}) %collective-permute-start.5) | collective-permute-done | bytes 49184 | tf_op jit(solution)/shard_map/ppermute | solution.py:309
  21.1 1.6 %collective-permute-start.6 = (bf16[24,32,128]{2,1,0:T(8,128)(2,1)S(1)}, bf16[24,32,128]{2,1,0:T(8,128)(2,1)S(1)}, u32[]{:S(2)}, u32[]{:S(2)}) collective-permute-start(bf16[24,32,128]{2,1,0:T(8,128)(2,1)S(1)} %get-tuple-element.58.refs_0_), channel_id=1, source_target_pairs={{0,2},{1,3},{2,0},{3,1},{4,6},{5,7},{6,4},{7,5},{8,10},{9,11},{10,... | collective-permute-start | bytes 589832 | tf_op jit(solution)/shard_map/ppermute | solution.py:309
  22.7 1.1 %collective-permute-start.10 = (bf16[24,16,128]{2,1,0:T(8,128)(2,1)S(1)}, bf16[24,16,128]{2,1,0:T(8,128)(2,1)S(1)}, u32[]{:S(2)}, u32[]{:S(2)}) collective-permute-start(bf16[24,16,128]{2,1,0:T(8,128)(2,1)S(1)} %get-tuple-element.42.refs_0_), channel_id=1, source_target_pairs={{0,12},{1,13},{2,14},{3,15},{4,8},{5,9},{6,10},{7,11},{8,4},{9,5},... | collective-permute-start | bytes 294920 | tf_op jit(solution)/shard_map/ppermute | solution.py:309
  23.7 0.0 collective-permute-start.9
  23.7 0.0 collective-permute-done.8
  23.7 1.1 %copy.14 = bf16[128,32,32]{0,2,1:T(8,128)(2,1)S(1)} copy(bf16[128,32,32]{0,1,2:T(8,128)(2,1)} %bitcast.40) | data formatting | bytes 524288 | tf_op jit(solution)/shard_map/transpose | solution.py:336
  24.8 2.0 %collective-permute-done.6.refs_1_ = bf16[24,32,128]{2,1,0:T(8,128)(2,1)S(1)} collective-permute-done((bf16[24,32,128]{2,1,0:T(8,128)(2,1)S(1)}, bf16[24,32,128]{2,1,0:T(8,128)(2,1)S(1)}, u32[]{:S(2)}, u32[]{:S(2)}) %collective-permute-start.6) | collective-permute-done | bytes 196640 | tf_op jit(solution)/shard_map/ppermute | solution.py:309
  26.9 0.1 collective-permute-start.7
  27.0 0.1 copy.18.refs_3_
  27.1 0.1 copy.17.refs_4_
  27.3 1.0 %collective-permute-start.11 = (bf16[48,16,128]{2,1,0:T(8,128)(2,1)S(1)}, bf16[48,16,128]{2,1,0:T(8,128)(2,1)S(1)}, u32[]{:S(2)}, u32[]{:S(2)}) collective-permute-start(bf16[48,16,128]{2,1,0:T(8,128)(2,1)S(1)} %pad_maximum_fusion.1), channel_id=1, source_target_pairs={{0,8},{1,9},{2,10},{3,11},{4,12},{5,13},{6,14},{7,15},{8,0},{9,1},... | collective-permute-start | bytes 589832 | tf_op jit(solution)/shard_map/ppermute | solution.py:309
  28.2 0.4 collective-permute-done.7.refs_2_
  28.6 1.4 %arrange_left.1.left_ref = bf16[32,128,128]{2,1,0:T(8,128)(2,1)S(1)} custom-call(bf16[24,32,128]{2,1,0:T(8,128)(2,1)S(1)} %get-tuple-element.58.refs_0_, bf16[24,32,128]{2,1,0:T(8,128)(2,1)S(1)} %collective-permute-done.6.refs_1_, bf16[48,32,128]{2,1,0:T(8,128)(2,1)S(1)} %collective-permute-done.7.refs_2_), custom_call_target="tpu_custom_call" | custom-call | flops 1048576 | bytes 8388608 | tf_op jit(solution)/shard_map/arrange_left/pallas_call | solution.py:133
  30.1 0.0 collective-permute-done.10.refs_3_
  30.1 6.6 %collective-permute-done.9.refs_2_ = bf16[24,16,128]{2,1,0:T(8,128)(2,1)S(1)} collective-permute-done((bf16[24,16,128]{2,1,0:T(8,128)(2,1)S(1)}, bf16[24,16,128]{2,1,0:T(8,128)(2,1)S(1)}, u32[]{:S(2)}, u32[]{:S(2)}) %collective-permute-start.9) | collective-permute-done | bytes 98336 | tf_op jit(solution)/shard_map/ppermute | solution.py:309
  36.6 0.0 copy-start
  36.6 0.0 copy-start.1
  36.7 7.4 %update_0.1.refs_4_ = f32[32,2,128,256]{3,2,1,0:T(8,128)S(1)} custom-call(bf16[32,128,128]{2,1,0:T(8,128)(2,1)S(1)} %arrange_left.1.left_ref, bf16[24,16,128]{2,1,0:T(8,128)(2,1)S(1)} %get-tuple-element.42.refs_0_, bf16[24,16,128]{2,1,0:T(8,128)(2,1)S(1)} %get-tuple-element.52.refs_1_, bf16[24,16,128]{2,1,0:T(8,128)(2,1)S(1)} %collective-permute-done.9.refs_2_, ...), custom_call_target="tpu_custom_call" | custom-call | flops 3758096384 | bytes 16777216 | tf_op jit(solution)/shard_map/update_0/pallas_call | solution.py:263
  44.0 0.0 collective-permute-done.11.refs_2_
  44.1 0.0 copy-done
  44.1 0.0 copy-done.1
  44.1 9.5 %update_1.1 = bf16[4,32,128,128]{3,2,1,0:T(8,128)(2,1)} custom-call(bf16[32,128,128]{2,1,0:T(8,128)(2,1)S(1)} %arrange_left.1.left_ref, bf16[24,16,128]{2,1,0:T(8,128)(2,1)S(1)} %get-tuple-element.45.refs_0_, bf16[24,16,128]{2,1,0:T(8,128)(2,1)S(1)} %get-tuple-element.46.refs_1_, bf16[48,16,128]{2,1,0:T(8,128)(2,1)S(1)} %collective-permute-done.11.refs_2_, ...), custom_call_target="tpu_custom_call" | custom-call | flops 3758096384 | bytes 16777216 | tf_op jit(solution)/shard_map/update_1/pallas_call | solution.py:263
  (15 shorter events, 0.2 us)
Async XLA Ops:
  7.0 3.2 %collective-permute-start = (bf16[2,6,16,128]{3,2,1,0:T(8,128)(2,1)S(1)}, bf16[2,6,16,128]{3,2,1,0:T(8,128)(2,1)S(1)}, u32[]{:S(2)}, u32[]{:S(2)}) collective-permute-start(bf16[2,6,16,128]{3,2,1,0:T(8,128)(2,1)S(1)} %get-tuple-element.31), channel_id=1, source_target_pairs={{0,1},{1,0},{2,3},{3,2},{4,5},{5,4},{6,7},{7,6},{8,9},{9,8},{10,11... | collective-permute-start | bytes 147464 | tf_op jit(solution)/shard_map/ppermute | solution.py:309
  7.5 7.1 %collective-permute-start.2 = (bf16[2,6,16,128]{3,2,1,0:T(8,128)(2,1)S(1)}, bf16[2,6,16,128]{3,2,1,0:T(8,128)(2,1)S(1)}, u32[]{:S(2)}, u32[]{:S(2)}) collective-permute-start(bf16[2,6,16,128]{3,2,1,0:T(8,128)(2,1)S(1)} %get-tuple-element.36), channel_id=1, source_target_pairs={{0,2},{1,3},{2,0},{3,1},{4,6},{5,7},{6,4},{7,5},{8,10},{9,11},{10,... | collective-permute-start | bytes 147464 | tf_op jit(solution)/shard_map/ppermute | solution.py:309
  10.1 4.6 %collective-permute-start.3 = (bf16[2,6,16,128]{3,2,1,0:T(8,128)(2,1)S(1)}, bf16[2,6,16,128]{3,2,1,0:T(8,128)(2,1)S(1)}, u32[]{:S(2)}, u32[]{:S(2)}) collective-permute-start(bf16[2,6,16,128]{3,2,1,0:T(8,128)(2,1)S(1)} %get-tuple-element.37), channel_id=1, source_target_pairs={{0,3},{1,2},{2,1},{3,0},{4,7},{5,6},{6,5},{7,4},{8,11},{9,10},{10,... | collective-permute-start | bytes 147464 | tf_op jit(solution)/shard_map/ppermute | solution.py:309
  10.2 5.5 %collective-permute-start.1 = (bf16[6,32,128]{2,1,0:T(8,128)(2,1)S(1)}, bf16[6,32,128]{2,1,0:T(8,128)(2,1)S(1)}, u32[]{:S(2)}, u32[]{:S(2)}) collective-permute-start(bf16[6,32,128]{2,1,0:T(8,128)(2,1)S(1)} %get-tuple-element.33), channel_id=1, source_target_pairs={{0,4},{1,5},{2,6},{3,7},{4,0},{5,1},{6,2},{7,3},{8,12},{9,13},{10,... | collective-permute-start | bytes 147464 | tf_op jit(solution)/shard_map/ppermute | solution.py:309
  12.0 6.1 %collective-permute-start.4 = (bf16[6,32,128]{2,1,0:T(8,128)(2,1)S(1)}, bf16[6,32,128]{2,1,0:T(8,128)(2,1)S(1)}, u32[]{:S(2)}, u32[]{:S(2)}) collective-permute-start(bf16[6,32,128]{2,1,0:T(8,128)(2,1)S(1)} %get-tuple-element.39), channel_id=1, source_target_pairs={{0,8},{1,9},{2,10},{3,11},{4,12},{5,13},{6,14},{7,15},{8,0},{9,1},... | collective-permute-start | bytes 147464 | tf_op jit(solution)/shard_map/ppermute | solution.py:309
  14.6 6.4 %collective-permute-start.5 = (bf16[6,32,128]{2,1,0:T(8,128)(2,1)S(1)}, bf16[6,32,128]{2,1,0:T(8,128)(2,1)S(1)}, u32[]{:S(2)}, u32[]{:S(2)}) collective-permute-start(bf16[6,32,128]{2,1,0:T(8,128)(2,1)S(1)} %get-tuple-element.40), channel_id=1, source_target_pairs={{0,12},{1,13},{2,14},{3,15},{4,8},{5,9},{6,10},{7,11},{8,4},{9,5},... | collective-permute-start | bytes 147464 | tf_op jit(solution)/shard_map/ppermute | solution.py:309
  14.7 9.0 %collective-permute-start.8 = (bf16[2,24,16,128]{3,2,1,0:T(8,128)(2,1)S(1)}, bf16[2,24,16,128]{3,2,1,0:T(8,128)(2,1)S(1)}, u32[]{:S(2)}, u32[]{:S(2)}) collective-permute-start(bf16[2,24,16,128]{3,2,1,0:T(8,128)(2,1)S(1)} %pad_maximum_fusion), channel_id=1, source_target_pairs={{0,4},{1,5},{2,6},{3,7},{4,0},{5,1},{6,2},{7,3},{8,12},{9,13},{10,... | collective-permute-start | bytes 589832 | tf_op jit(solution)/shard_map/ppermute | solution.py:309
  21.1 5.7 %collective-permute-start.6 = (bf16[24,32,128]{2,1,0:T(8,128)(2,1)S(1)}, bf16[24,32,128]{2,1,0:T(8,128)(2,1)S(1)}, u32[]{:S(2)}, u32[]{:S(2)}) collective-permute-start(bf16[24,32,128]{2,1,0:T(8,128)(2,1)S(1)} %get-tuple-element.58.refs_0_), channel_id=1, source_target_pairs={{0,2},{1,3},{2,0},{3,1},{4,6},{5,7},{6,4},{7,5},{8,10},{9,11},{10,... | collective-permute-start | bytes 589832 | tf_op jit(solution)/shard_map/ppermute | solution.py:309
  22.7 7.4 %collective-permute-start.10 = (bf16[24,16,128]{2,1,0:T(8,128)(2,1)S(1)}, bf16[24,16,128]{2,1,0:T(8,128)(2,1)S(1)}, u32[]{:S(2)}, u32[]{:S(2)}) collective-permute-start(bf16[24,16,128]{2,1,0:T(8,128)(2,1)S(1)} %get-tuple-element.42.refs_0_), channel_id=1, source_target_pairs={{0,12},{1,13},{2,14},{3,15},{4,8},{5,9},{6,10},{7,11},{8,4},{9,5},... | collective-permute-start | bytes 294920 | tf_op jit(solution)/shard_map/ppermute | solution.py:309
  23.7 12.9 %collective-permute-start.9 = (bf16[24,16,128]{2,1,0:T(8,128)(2,1)S(1)}, bf16[24,16,128]{2,1,0:T(8,128)(2,1)S(1)}, u32[]{:S(2)}, u32[]{:S(2)}) collective-permute-start(bf16[24,16,128]{2,1,0:T(8,128)(2,1)S(1)} %get-tuple-element.42.refs_0_), channel_id=1, source_target_pairs={{0,8},{1,9},{2,10},{3,11},{4,12},{5,13},{6,14},{7,15},{8,0},{9,1},... | collective-permute-start | bytes 294920 | tf_op jit(solution)/shard_map/ppermute | solution.py:309
  26.9 1.8 %collective-permute-start.7 = (bf16[48,32,128]{2,1,0:T(8,128)(2,1)S(1)}, bf16[48,32,128]{2,1,0:T(8,128)(2,1)S(1)}, u32[]{:S(2)}, u32[]{:S(2)}) collective-permute-start(bf16[48,32,128]{2,1,0:T(8,128)(2,1)S(1)} %constant_dynamic-update-slice_fusion.4), channel_id=1, source_target_pairs={{0,1},{1,0},{2,3},{3,2},{4,5},{5,4},{6,7},{7,6},{8,9},{9,8},{10,11... | collective-permute-start | bytes 1179656 | tf_op jit(solution)/shard_map/ppermute | solution.py:309
  27.3 16.8 %collective-permute-start.11 = (bf16[48,16,128]{2,1,0:T(8,128)(2,1)S(1)}, bf16[48,16,128]{2,1,0:T(8,128)(2,1)S(1)}, u32[]{:S(2)}, u32[]{:S(2)}) collective-permute-start(bf16[48,16,128]{2,1,0:T(8,128)(2,1)S(1)} %pad_maximum_fusion.1), channel_id=1, source_target_pairs={{0,8},{1,9},{2,10},{3,11},{4,12},{5,13},{6,14},{7,15},{8,0},{9,1},... | collective-permute-start | bytes 589832 | tf_op jit(solution)/shard_map/ppermute | solution.py:309
  36.6 7.4 %copy-start = (bf16[1,128,128,128]{3,2,1,0:T(8,128)(2,1)S(1)}, bf16[1,128,128,128]{3,2,1,0:T(8,128)(2,1)}, u32[]{:S(2)}) copy-start(bf16[1,128,128,128]{3,2,1,0:T(8,128)(2,1)} %param.11) | copy-start | bytes 12582916
  36.6 7.4 %copy-start.1 = (f32[128]{0:T(128)S(1)}, f32[128]{0:T(128)}, u32[]{:S(2)}) copy-start(f32[128]{0:T(128)} %param.19) | copy-start | bytes 1540

commit v18 on v16

--- a/solution.py
+++ b/solution.py
@@ -214,7 +214,7 @@
     pack = tile // rows
     width = lanes // pack
     halves = pack // 2
-    group = 8
+    group = 16 if part == 0 else 16
     first, last = part == 0, part == PARTS - 1
     in_vmem = pl.BlockSpec(memory_space=pltpu.VMEM)
     operands = [left] + list(right) + [wt[:, part * some * width : (part + 1) * some * width]]
@@ -283,13 +283,12 @@
     left = [left[0]] + [swap(left[d], d, 0) for d in range(1, side)]
     mines = [jnp.concatenate([x[part] for x in right]) for part in range(PARTS)]
     stacked = jnp.stack(mines)
-    left[1], mines[0] = lax.optimization_barrier((left[1], mines[0]))
-    *left, stacked = lax.optimization_barrier((*left, stacked))
+    left[3], mines[0] = lax.optimization_barrier((left[3], mines[0]))
     lefts = [jnp.concatenate(left)]
     order = [0]
     mask = side // 2
     while mask > 0:
-        lefts += [swap(jnp.concatenate(lefts), 0, mask)]
+        lefts += [swap(x, 0, mask) for x in lefts]
         order += [o ^ mask for o in order]
         mask //= 2
     near = swap(stacked, 1, 0)

time: 49.1 us -> 50.3 us (1.024)
  waiting for transfers between devices: 10.5 us -> 11.6 us
  starting transfers between devices: 13.6 us -> 14.3 us
    ppermute x12 -> x13, waiting for transfers between devices: 10.5 us -> 11.6 us  [swap(): lax.ppermute(x, 'row', [(i, i ^ da * side + db) for i in range(devices)])]
    ppermute x12 -> x13, starting transfers between devices: 13.6 us -> 14.3 us  [swap(): lax.ppermute(x, 'row', [(i, i ^ da * side + db) for i in range(devices)])]
  transfers between devices with their start and end apart: 12 -> 13, of which waited for: 5 -> 4; matrix products, arithmetic and copies ran while one was open for 3% -> 3% of each run, Pallas kernels for 19% -> 18%
where the time goes in v18:
time: 50.3 us; the launch traced here: 50.1 us
  Pallas kernels  22.6 us (45%)
  starting transfers between devices  14.3 us (28%)
  waiting for transfers between devices  11.6 us (23%)
  local copies, waits for them, and re-layouts  1.39 us (3%)
    pallas_call x2, Pallas kernels, update_part(): pl.pallas_call(functools.partial(update_kernel, side, seqs, order, len(ri...  16.8 us
    ppermute x13, starting transfers between devices, swap(): lax.ppermute(x, 'row', [(i, i ^ da * side + db) for i in range(devices)])  14.3 us
    ppermute x13, waiting for transfers between devices, swap(): lax.ppermute(x, 'row', [(i, i ^ da * side + db) for i in range(devices)])  11.6 us
    pallas_call x1, Pallas kernels, project(): pl.pallas_call(functools.partial(project_kernel, side), in_specs=[pl.Bloc...  4.52 us
    pallas_call x1, Pallas kernels, arrange_left(): pl.pallas_call(functools.partial(arrange_kernel, seq_total), in_specs=[pl...  1.33 us
    transpose x1, local copies, waits for them, and re-layouts, local(): final_matrix.reshape(width, width, -1).transpose(2, 1, 0)  1.05 us
  transfers between devices with their start and end apart: 13, of which 4 were waited for; matrix products, arithmetic and copies ran while one was open for 3% of the time, Pallas kernels for 18%

profile of v18, /device:TPU:0, one launch (start us, length us, event | category | flops | bytes accessed | tf_op | source)
XLA Modules:
  0.0 50.1 jit_solution(8268139454040739577)
XLA Ops:
  0.0 4.5 %project.1 = (bf16[6,32,128]{2,1,0:T(8,128)(2,1)S(1)}, bf16[6,32,128]{2,1,0:T(8,128)(2,1)S(1)}, bf16[6,32,128]{2,1,0:T(8,128)(2,1)S(1)}, bf16[6,32,128]{2,1,0:T(...) custom-call(bf16[6,512,256]{2,1,0:T(8,128)(2,1)} %refs_0_.1, ...), custom_call_target="tpu_custom_call" | custom-call | tf_op jit(solution)/shard_map/project/pallas_call | solution.py:86
  4.5 0.5 %collective-permute-start = (bf16[2,6,16,128]{3,2,1,0:T(8,128)(2,1)S(1)}, bf16[2,6,16,128]{3,2,1,0:T(8,128)(2,1)S(1)}, u32[]{:S(2)}, u32[]{:S(2)}) collective-permute-start(bf16[2,6,16,128]{3,2,1,0:T(8,128)(2,1)S(1)} %get-tuple-element.31), channel_id=1, source_target_pairs={{0,1},{1,0},{2,3},{3,2},{4,5},{5,4},{6,7},{7,6},{8,9},{9,8},{10,11... | collective-permute-start | bytes 147464 | tf_op jit(solution)/shard_map/ppermute | solution.py:279
  5.0 2.6 %collective-permute-start.4 = (bf16[2,6,16,128]{3,2,1,0:T(8,128)(2,1)S(1)}, bf16[2,6,16,128]{3,2,1,0:T(8,128)(2,1)S(1)}, u32[]{:S(2)}, u32[]{:S(2)}) collective-permute-start(bf16[2,6,16,128]{3,2,1,0:T(8,128)(2,1)S(1)} %get-tuple-element.38), channel_id=1, source_target_pairs={{0,2},{1,3},{2,0},{3,1},{4,6},{5,7},{6,4},{7,5},{8,10},{9,11},{10,... | collective-permute-start | bytes 147464 | tf_op jit(solution)/shard_map/ppermute | solution.py:279
  7.6 0.1 collective-permute-start.5
  7.7 0.0 collective-permute-done
  7.7 1.8 %collective-permute-start.1 = (bf16[6,32,128]{2,1,0:T(8,128)(2,1)S(1)}, bf16[6,32,128]{2,1,0:T(8,128)(2,1)S(1)}, u32[]{:S(2)}, u32[]{:S(2)}) collective-permute-start(bf16[6,32,128]{2,1,0:T(8,128)(2,1)S(1)} %get-tuple-element.33), channel_id=1, source_target_pairs={{0,4},{1,5},{2,6},{3,7},{4,0},{5,1},{6,2},{7,3},{8,12},{9,13},{10,... | collective-permute-start | bytes 147464 | tf_op jit(solution)/shard_map/ppermute | solution.py:279
  9.6 2.6 %collective-permute-start.2 = (bf16[6,32,128]{2,1,0:T(8,128)(2,1)S(1)}, bf16[6,32,128]{2,1,0:T(8,128)(2,1)S(1)}, u32[]{:S(2)}, u32[]{:S(2)}) collective-permute-start(bf16[6,32,128]{2,1,0:T(8,128)(2,1)S(1)} %get-tuple-element.34), channel_id=1, source_target_pairs={{0,8},{1,9},{2,10},{3,11},{4,12},{5,13},{6,14},{7,15},{8,0},{9,1},... | collective-permute-start | bytes 147464 | tf_op jit(solution)/shard_map/ppermute | solution.py:279
  12.2 0.0 collective-permute-start.3
  12.2 0.0 collective-permute-done.4
  12.2 0.0 collective-permute-done.5
  12.3 1.0 %collective-permute-start.9 = (bf16[2,24,16,128]{3,2,1,0:T(8,128)(2,1)S(1)}, bf16[2,24,16,128]{3,2,1,0:T(8,128)(2,1)S(1)}, u32[]{:S(2)}, u32[]{:S(2)}) collective-permute-start(bf16[2,24,16,128]{3,2,1,0:T(8,128)(2,1)S(1)} %pad_maximum_fusion), channel_id=1, source_target_pairs={{0,4},{1,5},{2,6},{3,7},{4,0},{5,1},{6,2},{7,3},{8,12},{9,13},{10,... | collective-permute-start | bytes 589832 | tf_op jit(solution)/shard_map/ppermute | solution.py:279
  13.3 5.3 %collective-permute-done.3 = bf16[6,32,128]{2,1,0:T(8,128)(2,1)S(1)} collective-permute-done((bf16[6,32,128]{2,1,0:T(8,128)(2,1)S(1)}, bf16[6,32,128]{2,1,0:T(8,128)(2,1)S(1)}, u32[]{:S(2)}, u32[]{:S(2)}) %collective-permute-start.3) | collective-permute-done | bytes 49184 | tf_op jit(solution)/shard_map/ppermute | solution.py:279
  18.6 1.0 %collective-permute-start.11 = (bf16[24,16,128]{2,1,0:T(8,128)(2,1)S(1)}, bf16[24,16,128]{2,1,0:T(8,128)(2,1)S(1)}, u32[]{:S(2)}, u32[]{:S(2)}) collective-permute-start(bf16[24,16,128]{2,1,0:T(8,128)(2,1)S(1)} %get-tuple-element.42.refs_0_), channel_id=1, source_target_pairs={{0,12},{1,13},{2,14},{3,15},{4,8},{5,9},{6,10},{7,11},{8,4},{9,5},... | collective-permute-start | bytes 294920 | tf_op jit(solution)/shard_map/ppermute | solution.py:279
  19.6 0.0 collective-permute-start.10
  19.6 0.0 collective-permute-done.1
  19.6 0.0 collective-permute-done.2
  19.7 0.1 collective-permute-start.7
  19.8 1.6 %collective-permute-start.6 = (bf16[24,32,128]{2,1,0:T(8,128)(2,1)S(1)}, bf16[24,32,128]{2,1,0:T(8,128)(2,1)S(1)}, u32[]{:S(2)}, u32[]{:S(2)}) collective-permute-start(bf16[24,32,128]{2,1,0:T(8,128)(2,1)S(1)} %constant_dynamic-update-slice_fusion.refs_0_), channel_id=1, source_target_pairs={{0,2},{1,3},{2,0},{3,1},{4,6},{5,7},{6,4},{7,5},{8,10},{9,11},{10,... | collective-permute-start | bytes 589832 | tf_op jit(solution)/shard_map/ppermute | solution.py:279
  21.4 0.0 collective-permute-done.9
  21.4 1.1 %copy.14 = bf16[128,32,32]{0,2,1:T(8,128)(2,1)S(1)} copy(bf16[128,32,32]{0,1,2:T(8,128)(2,1)} %bitcast.40) | data formatting | bytes 524288 | tf_op jit(solution)/shard_map/transpose | solution.py:306
  22.5 4.6 %collective-permute-done.6.refs_1_ = bf16[24,32,128]{2,1,0:T(8,128)(2,1)S(1)} collective-permute-done((bf16[24,32,128]{2,1,0:T(8,128)(2,1)S(1)}, bf16[24,32,128]{2,1,0:T(8,128)(2,1)S(1)}, u32[]{:S(2)}, u32[]{:S(2)}) %collective-permute-start.6) | collective-permute-done | bytes 196640 | tf_op jit(solution)/shard_map/ppermute | solution.py:279
  27.1 0.0 collective-permute-start.8
  27.1 0.1 copy.18.refs_3_
  27.2 0.1 copy.17.refs_4_
  27.3 1.2 %collective-permute-done.8.refs_3_ = bf16[24,32,128]{2,1,0:T(8,128)(2,1)S(1)} collective-permute-done((bf16[24,32,128]{2,1,0:T(8,128)(2,1)S(1)}, bf16[24,32,128]{2,1,0:T(8,128)(2,1)S(1)}, u32[]{:S(2)}, u32[]{:S(2)}) %collective-permute-start.8) | collective-permute-done | bytes 196640 | tf_op jit(solution)/shard_map/ppermute | solution.py:279
  28.5 3.0 %collective-permute-start.12 = (bf16[48,16,128]{2,1,0:T(8,128)(2,1)S(1)}, bf16[48,16,128]{2,1,0:T(8,128)(2,1)S(1)}, u32[]{:S(2)}, u32[]{:S(2)}) collective-permute-start(bf16[48,16,128]{2,1,0:T(8,128)(2,1)S(1)} %pad_maximum_fusion.1), channel_id=1, source_target_pairs={{0,8},{1,9},{2,10},{3,11},{4,12},{5,13},{6,14},{7,15},{8,0},{9,1},... | collective-permute-start | bytes 589832 | tf_op jit(solution)/shard_map/ppermute | solution.py:279
  31.5 0.0 collective-permute-done.7.refs_2_
  31.5 1.3 %arrange_left.1.left_ref = bf16[32,128,128]{2,1,0:T(8,128)(2,1)S(1)} custom-call(bf16[24,32,128]{2,1,0:T(8,128)(2,1)S(1)} %constant_dynamic-update-slice_fusion.refs_0_, bf16[24,32,128]{2,1,0:T(8,128)(2,1)S(1)} %collective-permute-done.6.refs_1_, bf16[24,32,128]{2,1,0:T(8,128)(2,1)S(1)} %collective-permute-done.7.refs_2_, ...), custom_call_target="tpu_custom_call" | custom-call | flops 1048576 | bytes 8388608 | tf_op jit(solution)/shard_map/arrange_left/pallas_call | solution.py:123
  32.9 0.0 collective-permute-done.11.refs_3_
  32.9 0.0 collective-permute-done.10.refs_2_
  32.9 0.0 copy-start
  32.9 0.0 copy-start.1
  32.9 7.6 %update_0.1.refs_4_ = f32[32,2,128,256]{3,2,1,0:T(8,128)S(1)} custom-call(bf16[32,128,128]{2,1,0:T(8,128)(2,1)S(1)} %arrange_left.1.left_ref, bf16[24,16,128]{2,1,0:T(8,128)(2,1)S(1)} %get-tuple-element.42.refs_0_, bf16[24,16,128]{2,1,0:T(8,128)(2,1)S(1)} %get-tuple-element.52.refs_1_, bf16[24,16,128]{2,1,0:T(8,128)(2,1)S(1)} %collective-permute-done.10.refs_2_, ...), custom_call_target="tpu_custom_call" | custom-call | flops 3758096384 | bytes 16777216 | tf_op jit(solution)/shard_map/update_0/pallas_call | solution.py:229
  40.5 0.4 collective-permute-done.12.refs_2_
  40.9 0.0 copy-done
  41.0 0.0 copy-done.1
  41.0 9.2 %update_1.1 = bf16[4,32,128,128]{3,2,1,0:T(8,128)(2,1)} custom-call(bf16[32,128,128]{2,1,0:T(8,128)(2,1)S(1)} %arrange_left.1.left_ref, bf16[24,16,128]{2,1,0:T(8,128)(2,1)S(1)} %get-tuple-element.45.refs_0_, bf16[24,16,128]{2,1,0:T(8,128)(2,1)S(1)} %get-tuple-element.46.refs_1_, bf16[48,16,128]{2,1,0:T(8,128)(2,1)S(1)} %collective-permute-done.12.refs_2_, ...), custom_call_target="tpu_custom_call" | custom-call | flops 3758096384 | bytes 16777216 | tf_op jit(solution)/shard_map/update_1/pallas_call | solution.py:229
  (14 shorter events, 0.2 us)
Async XLA Ops:
  4.5 3.2 %collective-permute-start = (bf16[2,6,16,128]{3,2,1,0:T(8,128)(2,1)S(1)}, bf16[2,6,16,128]{3,2,1,0:T(8,128)(2,1)S(1)}, u32[]{:S(2)}, u32[]{:S(2)}) collective-permute-start(bf16[2,6,16,128]{3,2,1,0:T(8,128)(2,1)S(1)} %get-tuple-element.31), channel_id=1, source_target_pairs={{0,1},{1,0},{2,3},{3,2},{4,5},{5,4},{6,7},{7,6},{8,9},{9,8},{10,11... | collective-permute-start | bytes 147464 | tf_op jit(solution)/shard_map/ppermute | solution.py:279
  5.0 7.1 %collective-permute-start.4 = (bf16[2,6,16,128]{3,2,1,0:T(8,128)(2,1)S(1)}, bf16[2,6,16,128]{3,2,1,0:T(8,128)(2,1)S(1)}, u32[]{:S(2)}, u32[]{:S(2)}) collective-permute-start(bf16[2,6,16,128]{3,2,1,0:T(8,128)(2,1)S(1)} %get-tuple-element.38), channel_id=1, source_target_pairs={{0,2},{1,3},{2,0},{3,1},{4,6},{5,7},{6,4},{7,5},{8,10},{9,11},{10,... | collective-permute-start | bytes 147464 | tf_op jit(solution)/shard_map/ppermute | solution.py:279
  7.6 4.6 %collective-permute-start.5 = (bf16[2,6,16,128]{3,2,1,0:T(8,128)(2,1)S(1)}, bf16[2,6,16,128]{3,2,1,0:T(8,128)(2,1)S(1)}, u32[]{:S(2)}, u32[]{:S(2)}) collective-permute-start(bf16[2,6,16,128]{3,2,1,0:T(8,128)(2,1)S(1)} %get-tuple-element.39), channel_id=1, source_target_pairs={{0,3},{1,2},{2,1},{3,0},{4,7},{5,6},{6,5},{7,4},{8,11},{9,10},{10,... | collective-permute-start | bytes 147464 | tf_op jit(solution)/shard_map/ppermute | solution.py:279
  7.7 11.9 %collective-permute-start.1 = (bf16[6,32,128]{2,1,0:T(8,128)(2,1)S(1)}, bf16[6,32,128]{2,1,0:T(8,128)(2,1)S(1)}, u32[]{:S(2)}, u32[]{:S(2)}) collective-permute-start(bf16[6,32,128]{2,1,0:T(8,128)(2,1)S(1)} %get-tuple-element.33), channel_id=1, source_target_pairs={{0,4},{1,5},{2,6},{3,7},{4,0},{5,1},{6,2},{7,3},{8,12},{9,13},{10,... | collective-permute-start | bytes 147464 | tf_op jit(solution)/shard_map/ppermute | solution.py:279
  9.6 10.1 %collective-permute-start.2 = (bf16[6,32,128]{2,1,0:T(8,128)(2,1)S(1)}, bf16[6,32,128]{2,1,0:T(8,128)(2,1)S(1)}, u32[]{:S(2)}, u32[]{:S(2)}) collective-permute-start(bf16[6,32,128]{2,1,0:T(8,128)(2,1)S(1)} %get-tuple-element.34), channel_id=1, source_target_pairs={{0,8},{1,9},{2,10},{3,11},{4,12},{5,13},{6,14},{7,15},{8,0},{9,1},... | collective-permute-start | bytes 147464 | tf_op jit(solution)/shard_map/ppermute | solution.py:279
  12.2 6.4 %collective-permute-start.3 = (bf16[6,32,128]{2,1,0:T(8,128)(2,1)S(1)}, bf16[6,32,128]{2,1,0:T(8,128)(2,1)S(1)}, u32[]{:S(2)}, u32[]{:S(2)}) collective-permute-start(bf16[6,32,128]{2,1,0:T(8,128)(2,1)S(1)} %get-tuple-element.35), channel_id=1, source_target_pairs={{0,12},{1,13},{2,14},{3,15},{4,8},{5,9},{6,10},{7,11},{8,4},{9,5},... | collective-permute-start | bytes 147464 | tf_op jit(solution)/shard_map/ppermute | solution.py:279
  12.3 9.1 %collective-permute-start.9 = (bf16[2,24,16,128]{3,2,1,0:T(8,128)(2,1)S(1)}, bf16[2,24,16,128]{3,2,1,0:T(8,128)(2,1)S(1)}, u32[]{:S(2)}, u32[]{:S(2)}) collective-permute-start(bf16[2,24,16,128]{3,2,1,0:T(8,128)(2,1)S(1)} %pad_maximum_fusion), channel_id=1, source_target_pairs={{0,4},{1,5},{2,6},{3,7},{4,0},{5,1},{6,2},{7,3},{8,12},{9,13},{10,... | collective-permute-start | bytes 589832 | tf_op jit(solution)/shard_map/ppermute | solution.py:279
  18.6 14.3 %collective-permute-start.11 = (bf16[24,16,128]{2,1,0:T(8,128)(2,1)S(1)}, bf16[24,16,128]{2,1,0:T(8,128)(2,1)S(1)}, u32[]{:S(2)}, u32[]{:S(2)}) collective-permute-start(bf16[24,16,128]{2,1,0:T(8,128)(2,1)S(1)} %get-tuple-element.42.refs_0_), channel_id=1, source_target_pairs={{0,12},{1,13},{2,14},{3,15},{4,8},{5,9},{6,10},{7,11},{8,4},{9,5},... | collective-permute-start | bytes 294920 | tf_op jit(solution)/shard_map/ppermute | solution.py:279
  19.6 13.3 %collective-permute-start.10 = (bf16[24,16,128]{2,1,0:T(8,128)(2,1)S(1)}, bf16[24,16,128]{2,1,0:T(8,128)(2,1)S(1)}, u32[]{:S(2)}, u32[]{:S(2)}) collective-permute-start(bf16[24,16,128]{2,1,0:T(8,128)(2,1)S(1)} %get-tuple-element.42.refs_0_), channel_id=1, source_target_pairs={{0,8},{1,9},{2,10},{3,11},{4,12},{5,13},{6,14},{7,15},{8,0},{9,1},... | collective-permute-start | bytes 294920 | tf_op jit(solution)/shard_map/ppermute | solution.py:279
  19.7 11.9 %collective-permute-start.7 = (bf16[24,32,128]{2,1,0:T(8,128)(2,1)S(1)}, bf16[24,32,128]{2,1,0:T(8,128)(2,1)S(1)}, u32[]{:S(2)}, u32[]{:S(2)}) collective-permute-start(bf16[24,32,128]{2,1,0:T(8,128)(2,1)S(1)} %constant_dynamic-update-slice_fusion.refs_0_), channel_id=1, source_target_pairs={{0,1},{1,0},{2,3},{3,2},{4,5},{5,4},{6,7},{7,6},{8,9},{9,8},{10,11... | collective-permute-start | bytes 589832 | tf_op jit(solution)/shard_map/ppermute | solution.py:279
  19.8 7.3 %collective-permute-start.6 = (bf16[24,32,128]{2,1,0:T(8,128)(2,1)S(1)}, bf16[24,32,128]{2,1,0:T(8,128)(2,1)S(1)}, u32[]{:S(2)}, u32[]{:S(2)}) collective-permute-start(bf16[24,32,128]{2,1,0:T(8,128)(2,1)S(1)} %constant_dynamic-update-slice_fusion.refs_0_), channel_id=1, source_target_pairs={{0,2},{1,3},{2,0},{3,1},{4,6},{5,7},{6,4},{7,5},{8,10},{9,11},{10,... | collective-permute-start | bytes 589832 | tf_op jit(solution)/shard_map/ppermute | solution.py:279
  27.1 1.4 %collective-permute-start.8 = (bf16[24,32,128]{2,1,0:T(8,128)(2,1)S(1)}, bf16[24,32,128]{2,1,0:T(8,128)(2,1)S(1)}, u32[]{:S(2)}, u32[]{:S(2)}) collective-permute-start(bf16[24,32,128]{2,1,0:T(8,128)(2,1)S(1)} %collective-permute-done.6.refs_1_), channel_id=1, source_target_pairs={{0,1},{1,0},{2,3},{3,2},{4,5},{5,4},{6,7},{7,6},{8,9},{9,8},{10,11... | collective-permute-start | bytes 589832 | tf_op jit(solution)/shard_map/ppermute | solution.py:279
  28.5 12.4 %collective-permute-start.12 = (bf16[48,16,128]{2,1,0:T(8,128)(2,1)S(1)}, bf16[48,16,128]{2,1,0:T(8,128)(2,1)S(1)}, u32[]{:S(2)}, u32[]{:S(2)}) collective-permute-start(bf16[48,16,128]{2,1,0:T(8,128)(2,1)S(1)} %pad_maximum_fusion.1), channel_id=1, source_target_pairs={{0,8},{1,9},{2,10},{3,11},{4,12},{5,13},{6,14},{7,15},{8,0},{9,1},... | collective-permute-start | bytes 589832 | tf_op jit(solution)/shard_map/ppermute | solution.py:279
  32.9 8.1 %copy-start = (bf16[1,128,128,128]{3,2,1,0:T(8,128)(2,1)S(1)}, bf16[1,128,128,128]{3,2,1,0:T(8,128)(2,1)}, u32[]{:S(2)}) copy-start(bf16[1,128,128,128]{3,2,1,0:T(8,128)(2,1)} %param.11) | copy-start | bytes 12582916
  32.9 8.1 %copy-start.1 = (f32[128]{0:T(128)S(1)}, f32[128]{0:T(128)}, u32[]{:S(2)}) copy-start(f32[128]{0:T(128)} %param.19) | copy-start | bytes 1540

commit v19 on v14

--- a/solution.py
+++ b/solution.py
@@ -170,41 +170,42 @@
                 pl.ds(e, depth, stride=some), :
             ].astype(jnp.bfloat16)
 
-    def outer_products(q):
-        for n in range(some // 2):
-            both = jnp.dot(
-                left_ref[at + q],
-                right_flat[:, 2 * n * tile : (2 * n + 2) * tile],
-                preferred_element_type=jnp.float32,
-            ).astype(jnp.bfloat16)
-            for k in range(2):
-                e = 2 * n + k
-                for h in range(pack):
-                    outer[
-                        q * halves + h // 2,
-                        e * width : (e + 1) * width,
-                        (h % 2) * tile : (h % 2 + 1) * tile,
-                    ] = both[h * width : (h + 1) * width, k * tile : (k + 1) * tile]
-
-    def project_back(q):
+    def outer_products(q, n):
+        both = jnp.dot(
+            left_ref[at + q],
+            right_flat[:, 2 * n * tile : (2 * n + 2) * tile],
+            preferred_element_type=jnp.float32,
+        ).astype(jnp.bfloat16)
+        for k in range(2):
+            e = 2 * n + k
+            for h in range(pack):
+                outer[
+                    q * halves + h // 2,
+                    e * width : (e + 1) * width,
+                    (h % 2) * tile : (h % 2 + 1) * tile,
+                ] = both[h * width : (h + 1) * width, k * tile : (k + 1) * tile]
+
+    def project_back(q, g):
+        update = jnp.dot(wt_ref[...], outer[q * halves + g], preferred_element_type=jnp.float32)
+        if not first:
+            update = update + before_ref[at + q, g]
+        if not last:
+            out_ref[at + q, g] = update
+            return
+        for k in range(2):
+            h = 2 * g + k
+            share = update[:, k * tile : (k + 1) * tile].T * (1.0 / seq_total) + bias_ref[...]
+            old = pair_ref[h, at + q].astype(jnp.float32)
+            out_ref[h, q] = (old + share).astype(jnp.bfloat16)
+
+    products = some // 2
+    for q in range(group + 1):
         for g in range(halves):
-            update = jnp.dot(wt_ref[...], outer[q * halves + g], preferred_element_type=jnp.float32)
-            if not first:
-                update = update + before_ref[at + q, g]
-            if not last:
-                out_ref[at + q, g] = update
-                continue
-            for k in range(2):
-                h = 2 * g + k
-                share = update[:, k * tile : (k + 1) * tile].T * (1.0 / seq_total) + bias_ref[...]
-                old = pair_ref[h, at + q].astype(jnp.float32)
-                out_ref[h, q] = (old + share).astype(jnp.bfloat16)
-
-    for q in range(group + 1):
-        if q < group:
-            outer_products(q)
-        if q > 0:
-            project_back(q - 1)
+            if q > 0:
+                project_back(q - 1, g)
+            if q < group:
+                for n in range(g * products // halves, (g + 1) * products // halves):
+                    outer_products(q, n)
 
 
 def update_part(side, seqs, order, part, left, right, wt, before, bias, pair):
@@ -214,7 +215,7 @@
     pack = tile // rows
     width = lanes // pack
     halves = pack // 2
-    group = 8
+    group = 16
     first, last = part == 0, part == PARTS - 1
     in_vmem = pl.BlockSpec(memory_space=pltpu.VMEM)
     operands = [left] + list(right) + [wt[:, part * some * width : (part + 1) * some * width]]

time: 47.9 us -> 52.7 us (1.10)
  Pallas kernels: 23 us -> 28.9 us
  waiting for transfers between devices: 10.7 us -> 9.66 us
    pallas_call x2, Pallas kernels: 17.2 us -> 23.1 us  [update_part(): pl.pallas_call(functools.partial(update_kernel, side, seqs, order, len(ri...]
    ppermute x12, waiting for transfers between devices: 10.7 us -> 9.66 us  [swap(): lax.ppermute(x, 'row', [(i, i ^ da * side + db) for i in range(devices)])]
  transfers between devices with their start and end apart: 12 -> 12, of which waited for: 6 -> 5; matrix products, arithmetic and copies ran while one was open for 3% -> 3% of each run, Pallas kernels for 19% -> 23%
where the time goes in v19:
time: 52.7 us; the launch traced here: 52.6 us
  Pallas kernels  28.9 us (55%)
  starting transfers between devices  12.3 us (23%)
  waiting for transfers between devices  9.66 us (18%)
  local copies, waits for them, and re-layouts  1.45 us (3%)
    pallas_call x2, Pallas kernels, update_part(): pl.pallas_call(functools.partial(update_kernel, side, seqs, order, len(ri...  23.1 us
    ppermute x12, starting transfers between devices, swap(): lax.ppermute(x, 'row', [(i, i ^ da * side + db) for i in range(devices)])  12.3 us
    ppermute x12, waiting for transfers between devices, swap(): lax.ppermute(x, 'row', [(i, i ^ da * side + db) for i in range(devices)])  9.66 us
    pallas_call x1, Pallas kernels, project(): pl.pallas_call(functools.partial(project_kernel, side), in_specs=[pl.Bloc...  4.52 us
    pallas_call x1, Pallas kernels, arrange_left(): pl.pallas_call(functools.partial(arrange_kernel, seq_total), in_specs=[pl...  1.33 us
    transpose x1, local copies, waits for them, and re-layouts, local(): final_matrix.reshape(width, width, -1).transpose(2, 1, 0)  1.06 us
  transfers between devices with their start and end apart: 12, of which 5 were waited for; matrix products, arithmetic and copies ran while one was open for 3% of the time, Pallas kernels for 23%

profile of v19, /device:TPU:0, one launch (start us, length us, event | category | flops | bytes accessed | tf_op | source)
XLA Modules:
  0.0 52.6 jit_solution(12098652581654064630)
XLA Ops:
  0.0 4.5 %project.1 = (bf16[6,32,128]{2,1,0:T(8,128)(2,1)S(1)}, bf16[6,32,128]{2,1,0:T(8,128)(2,1)S(1)}, bf16[6,32,128]{2,1,0:T(8,128)(2,1)S(1)}, bf16[6,32,128]{2,1,0:T(...) custom-call(bf16[6,512,256]{2,1,0:T(8,128)(2,1)} %refs_0_.1, ...), custom_call_target="tpu_custom_call" | custom-call | tf_op jit(solution)/shard_map/project/pallas_call | solution.py:86
  4.5 0.5 collective-permute-start
  5.0 2.6 %collective-permute-start.6 = (bf16[2,6,16,128]{3,2,1,0:T(8,128)(2,1)S(1)}, bf16[2,6,16,128]{3,2,1,0:T(8,128)(2,1)S(1)}, u32[]{:S(2)}, u32[]{:S(2)}) collective-permute-start(bf16[2,6,16,128]{3,2,1,0:T(8,128)(2,1)S(1)} %get-tuple-element.36), channel_id=1, source_target_pairs={{0,2},{1,3},{2,0},{3,1},{4,6},{5,7},{6,4},{7,5},{8,10},{9,11},{10,... | collective-permute-start | bytes 147464 | tf_op jit(solution)/shard_map/ppermute | solution.py:280
  7.6 0.1 collective-permute-start.7
  7.7 0.0 collective-permute-done
  7.7 1.8 %collective-permute-start.1 = (bf16[6,32,128]{2,1,0:T(8,128)(2,1)S(1)}, bf16[6,32,128]{2,1,0:T(8,128)(2,1)S(1)}, u32[]{:S(2)}, u32[]{:S(2)}) collective-permute-start(bf16[6,32,128]{2,1,0:T(8,128)(2,1)S(1)} %get-tuple-element.31), channel_id=1, source_target_pairs={{0,4},{1,5},{2,6},{3,7},{4,0},{5,1},{6,2},{7,3},{8,12},{9,13},{10,... | collective-permute-start | bytes 147464 | tf_op jit(solution)/shard_map/ppermute | solution.py:280
  9.6 2.6 %collective-permute-start.2 = (bf16[6,32,128]{2,1,0:T(8,128)(2,1)S(1)}, bf16[6,32,128]{2,1,0:T(8,128)(2,1)S(1)}, u32[]{:S(2)}, u32[]{:S(2)}) collective-permute-start(bf16[6,32,128]{2,1,0:T(8,128)(2,1)S(1)} %get-tuple-element.32), channel_id=1, source_target_pairs={{0,8},{1,9},{2,10},{3,11},{4,12},{5,13},{6,14},{7,15},{8,0},{9,1},... | collective-permute-start | bytes 147464 | tf_op jit(solution)/shard_map/ppermute | solution.py:280
  12.2 0.0 collective-permute-start.3
  12.2 0.0 collective-permute-done.6
  12.2 0.0 collective-permute-done.7
  12.3 1.0 %collective-permute-start.8 = (bf16[2,24,16,128]{3,2,1,0:T(8,128)(2,1)S(1)}, bf16[2,24,16,128]{3,2,1,0:T(8,128)(2,1)S(1)}, u32[]{:S(2)}, u32[]{:S(2)}) collective-permute-start(bf16[2,24,16,128]{3,2,1,0:T(8,128)(2,1)S(1)} %pad_maximum_fusion), channel_id=1, source_target_pairs={{0,4},{1,5},{2,6},{3,7},{4,0},{5,1},{6,2},{7,3},{8,12},{9,13},{10,... | collective-permute-start | bytes 589832 | tf_op jit(solution)/shard_map/ppermute | solution.py:280
  13.3 0.0 collective-permute-done.1
  13.3 2.4 %collective-permute-done.2 = bf16[6,32,128]{2,1,0:T(8,128)(2,1)S(1)} collective-permute-done((bf16[6,32,128]{2,1,0:T(8,128)(2,1)S(1)}, bf16[6,32,128]{2,1,0:T(8,128)(2,1)S(1)}, u32[]{:S(2)}, u32[]{:S(2)}) %collective-permute-start.2) | collective-permute-done | bytes 49184 | tf_op jit(solution)/shard_map/ppermute | solution.py:280
  15.7 2.9 %collective-permute-done.3 = bf16[6,32,128]{2,1,0:T(8,128)(2,1)S(1)} collective-permute-done((bf16[6,32,128]{2,1,0:T(8,128)(2,1)S(1)}, bf16[6,32,128]{2,1,0:T(8,128)(2,1)S(1)}, u32[]{:S(2)}, u32[]{:S(2)}) %collective-permute-start.3) | collective-permute-done | bytes 49184 | tf_op jit(solution)/shard_map/ppermute | solution.py:280
  18.6 1.6 %collective-permute-start.4 = (bf16[24,32,128]{2,1,0:T(8,128)(2,1)S(1)}, bf16[24,32,128]{2,1,0:T(8,128)(2,1)S(1)}, u32[]{:S(2)}, u32[]{:S(2)}) collective-permute-start(bf16[24,32,128]{2,1,0:T(8,128)(2,1)S(1)} %get-tuple-element.62.refs_0_), channel_id=1, source_target_pairs={{0,2},{1,3},{2,0},{3,1},{4,6},{5,7},{6,4},{7,5},{8,10},{9,11},{10,... | collective-permute-start | bytes 589832 | tf_op jit(solution)/shard_map/ppermute | solution.py:280
  20.2 1.1 %collective-permute-start.10 = (bf16[24,16,128]{2,1,0:T(8,128)(2,1)S(1)}, bf16[24,16,128]{2,1,0:T(8,128)(2,1)S(1)}, u32[]{:S(2)}, u32[]{:S(2)}) collective-permute-start(bf16[24,16,128]{2,1,0:T(8,128)(2,1)S(1)} %get-tuple-element.50.refs_0_), channel_id=1, source_target_pairs={{0,12},{1,13},{2,14},{3,15},{4,8},{5,9},{6,10},{7,11},{8,4},{9,5},... | collective-permute-start | bytes 294920 | tf_op jit(solution)/shard_map/ppermute | solution.py:280
  21.3 0.0 collective-permute-start.9
  21.3 0.0 collective-permute-done.8
  21.3 1.1 %copy.14 = bf16[128,32,32]{0,2,1:T(8,128)(2,1)S(1)} copy(bf16[128,32,32]{0,1,2:T(8,128)(2,1)} %bitcast.40) | data formatting | bytes 524288 | tf_op jit(solution)/shard_map/transpose | solution.py:306
  22.3 2.0 %collective-permute-done.4.refs_1_ = bf16[24,32,128]{2,1,0:T(8,128)(2,1)S(1)} collective-permute-done((bf16[24,32,128]{2,1,0:T(8,128)(2,1)S(1)}, bf16[24,32,128]{2,1,0:T(8,128)(2,1)S(1)}, u32[]{:S(2)}, u32[]{:S(2)}) %collective-permute-start.4) | collective-permute-done | bytes 196640 | tf_op jit(solution)/shard_map/ppermute | solution.py:280
  24.4 0.1 collective-permute-start.5
  24.5 0.1 copy.18.refs_3_
  24.6 0.1 copy.17.refs_4_
  24.8 1.4 %collective-permute-done.5.refs_2_ = bf16[48,32,128]{2,1,0:T(8,128)(2,1)S(1)} collective-permute-done((bf16[48,32,128]{2,1,0:T(8,128)(2,1)S(1)}, bf16[48,32,128]{2,1,0:T(8,128)(2,1)S(1)}, u32[]{:S(2)}, u32[]{:S(2)}) %collective-permute-start.5) | collective-permute-done | bytes 393248 | tf_op jit(solution)/shard_map/ppermute | solution.py:280
  26.2 1.0 %collective-permute-start.11 = (bf16[48,16,128]{2,1,0:T(8,128)(2,1)S(1)}, bf16[48,16,128]{2,1,0:T(8,128)(2,1)S(1)}, u32[]{:S(2)}, u32[]{:S(2)}) collective-permute-start(bf16[48,16,128]{2,1,0:T(8,128)(2,1)S(1)} %pad_maximum_fusion.1), channel_id=1, source_target_pairs={{0,8},{1,9},{2,10},{3,11},{4,12},{5,13},{6,14},{7,15},{8,0},{9,1},... | collective-permute-start | bytes 589832 | tf_op jit(solution)/shard_map/ppermute | solution.py:280
  27.2 1.3 %arrange_left.1.left_ref = bf16[32,128,128]{2,1,0:T(8,128)(2,1)S(1)} custom-call(bf16[24,32,128]{2,1,0:T(8,128)(2,1)S(1)} %get-tuple-element.62.refs_0_, bf16[24,32,128]{2,1,0:T(8,128)(2,1)S(1)} %collective-permute-done.4.refs_1_, bf16[48,32,128]{2,1,0:T(8,128)(2,1)S(1)} %collective-permute-done.5.refs_2_), custom_call_target="tpu_custom_call" | custom-call | flops 1048576 | bytes 8388608 | tf_op jit(solution)/shard_map/arrange_left/pallas_call | solution.py:123
  28.5 0.0 collective-permute-done.10.refs_3_
  28.5 0.9 %collective-permute-done.9.refs_2_ = bf16[24,16,128]{2,1,0:T(8,128)(2,1)S(1)} collective-permute-done((bf16[24,16,128]{2,1,0:T(8,128)(2,1)S(1)}, bf16[24,16,128]{2,1,0:T(8,128)(2,1)S(1)}, u32[]{:S(2)}, u32[]{:S(2)}) %collective-permute-start.9) | collective-permute-done | bytes 98336 | tf_op jit(solution)/shard_map/ppermute | solution.py:280
  29.4 0.0 copy-start
  29.5 0.0 copy-start.1
  29.5 10.8 %update_0.1.refs_4_ = f32[32,2,128,256]{3,2,1,0:T(8,128)S(1)} custom-call(bf16[32,128,128]{2,1,0:T(8,128)(2,1)S(1)} %arrange_left.1.left_ref, bf16[24,16,128]{2,1,0:T(8,128)(2,1)S(1)} %get-tuple-element.50.refs_0_, bf16[24,16,128]{2,1,0:T(8,128)(2,1)S(1)} %get-tuple-element.48.refs_1_, bf16[24,16,128]{2,1,0:T(8,128)(2,1)S(1)} %collective-permute-done.9.refs_2_, ...), custom_call_target="tpu_custom_call" | custom-call | flops 3758096384 | bytes 16777216 | tf_op jit(solution)/shard_map/update_0/pallas_call | solution.py:230
  40.3 0.0 collective-permute-done.11.refs_2_
  40.3 0.0 copy-done
  40.3 0.0 copy-done.1
  40.3 12.2 %update_1.1 = bf16[4,32,128,128]{3,2,1,0:T(8,128)(2,1)} custom-call(bf16[32,128,128]{2,1,0:T(8,128)(2,1)S(1)} %arrange_left.1.left_ref, bf16[24,16,128]{2,1,0:T(8,128)(2,1)S(1)} %get-tuple-element.41.refs_0_, bf16[24,16,128]{2,1,0:T(8,128)(2,1)S(1)} %get-tuple-element.42.refs_1_, bf16[48,16,128]{2,1,0:T(8,128)(2,1)S(1)} %collective-permute-done.11.refs_2_, ...), custom_call_target="tpu_custom_call" | custom-call | flops 3758096384 | bytes 16777216 | tf_op jit(solution)/shard_map/update_1/pallas_call | solution.py:230
  (15 shorter events, 0.2 us)
Async XLA Ops:
  4.5 3.2 %collective-permute-start = (bf16[2,6,16,128]{3,2,1,0:T(8,128)(2,1)S(1)}, bf16[2,6,16,128]{3,2,1,0:T(8,128)(2,1)S(1)}, u32[]{:S(2)}, u32[]{:S(2)}) collective-permute-start(bf16[2,6,16,128]{3,2,1,0:T(8,128)(2,1)S(1)} %get-tuple-element.29), channel_id=1, source_target_pairs={{0,1},{1,0},{2,3},{3,2},{4,5},{5,4},{6,7},{7,6},{8,9},{9,8},{10,11... | collective-permute-start | bytes 147464 | tf_op jit(solution)/shard_map/ppermute | solution.py:280
  5.0 7.1 %collective-permute-start.6 = (bf16[2,6,16,128]{3,2,1,0:T(8,128)(2,1)S(1)}, bf16[2,6,16,128]{3,2,1,0:T(8,128)(2,1)S(1)}, u32[]{:S(2)}, u32[]{:S(2)}) collective-permute-start(bf16[2,6,16,128]{3,2,1,0:T(8,128)(2,1)S(1)} %get-tuple-element.36), channel_id=1, source_target_pairs={{0,2},{1,3},{2,0},{3,1},{4,6},{5,7},{6,4},{7,5},{8,10},{9,11},{10,... | collective-permute-start | bytes 147464 | tf_op jit(solution)/shard_map/ppermute | solution.py:280
  7.6 4.6 %collective-permute-start.7 = (bf16[2,6,16,128]{3,2,1,0:T(8,128)(2,1)S(1)}, bf16[2,6,16,128]{3,2,1,0:T(8,128)(2,1)S(1)}, u32[]{:S(2)}, u32[]{:S(2)}) collective-permute-start(bf16[2,6,16,128]{3,2,1,0:T(8,128)(2,1)S(1)} %get-tuple-element.37), channel_id=1, source_target_pairs={{0,3},{1,2},{2,1},{3,0},{4,7},{5,6},{6,5},{7,4},{8,11},{9,10},{10,... | collective-permute-start | bytes 147464 | tf_op jit(solution)/shard_map/ppermute | solution.py:280
  7.7 5.5 %collective-permute-start.1 = (bf16[6,32,128]{2,1,0:T(8,128)(2,1)S(1)}, bf16[6,32,128]{2,1,0:T(8,128)(2,1)S(1)}, u32[]{:S(2)}, u32[]{:S(2)}) collective-permute-start(bf16[6,32,128]{2,1,0:T(8,128)(2,1)S(1)} %get-tuple-element.31), channel_id=1, source_target_pairs={{0,4},{1,5},{2,6},{3,7},{4,0},{5,1},{6,2},{7,3},{8,12},{9,13},{10,... | collective-permute-start | bytes 147464 | tf_op jit(solution)/shard_map/ppermute | solution.py:280
  9.6 6.1 %collective-permute-start.2 = (bf16[6,32,128]{2,1,0:T(8,128)(2,1)S(1)}, bf16[6,32,128]{2,1,0:T(8,128)(2,1)S(1)}, u32[]{:S(2)}, u32[]{:S(2)}) collective-permute-start(bf16[6,32,128]{2,1,0:T(8,128)(2,1)S(1)} %get-tuple-element.32), channel_id=1, source_target_pairs={{0,8},{1,9},{2,10},{3,11},{4,12},{5,13},{6,14},{7,15},{8,0},{9,1},... | collective-permute-start | bytes 147464 | tf_op jit(solution)/shard_map/ppermute | solution.py:280
  12.2 6.4 %collective-permute-start.3 = (bf16[6,32,128]{2,1,0:T(8,128)(2,1)S(1)}, bf16[6,32,128]{2,1,0:T(8,128)(2,1)S(1)}, u32[]{:S(2)}, u32[]{:S(2)}) collective-permute-start(bf16[6,32,128]{2,1,0:T(8,128)(2,1)S(1)} %get-tuple-element.33), channel_id=1, source_target_pairs={{0,12},{1,13},{2,14},{3,15},{4,8},{5,9},{6,10},{7,11},{8,4},{9,5},... | collective-permute-start | bytes 147464 | tf_op jit(solution)/shard_map/ppermute | solution.py:280
  12.3 9.0 %collective-permute-start.8 = (bf16[2,24,16,128]{3,2,1,0:T(8,128)(2,1)S(1)}, bf16[2,24,16,128]{3,2,1,0:T(8,128)(2,1)S(1)}, u32[]{:S(2)}, u32[]{:S(2)}) collective-permute-start(bf16[2,24,16,128]{3,2,1,0:T(8,128)(2,1)S(1)} %pad_maximum_fusion), channel_id=1, source_target_pairs={{0,4},{1,5},{2,6},{3,7},{4,0},{5,1},{6,2},{7,3},{8,12},{9,13},{10,... | collective-permute-start | bytes 589832 | tf_op jit(solution)/shard_map/ppermute | solution.py:280
  18.6 5.7 %collective-permute-start.4 = (bf16[24,32,128]{2,1,0:T(8,128)(2,1)S(1)}, bf16[24,32,128]{2,1,0:T(8,128)(2,1)S(1)}, u32[]{:S(2)}, u32[]{:S(2)}) collective-permute-start(bf16[24,32,128]{2,1,0:T(8,128)(2,1)S(1)} %get-tuple-element.62.refs_0_), channel_id=1, source_target_pairs={{0,2},{1,3},{2,0},{3,1},{4,6},{5,7},{6,4},{7,5},{8,10},{9,11},{10,... | collective-permute-start | bytes 589832 | tf_op jit(solution)/shard_map/ppermute | solution.py:280
  20.2 8.3 %collective-permute-start.10 = (bf16[24,16,128]{2,1,0:T(8,128)(2,1)S(1)}, bf16[24,16,128]{2,1,0:T(8,128)(2,1)S(1)}, u32[]{:S(2)}, u32[]{:S(2)}) collective-permute-start(bf16[24,16,128]{2,1,0:T(8,128)(2,1)S(1)} %get-tuple-element.50.refs_0_), channel_id=1, source_target_pairs={{0,12},{1,13},{2,14},{3,15},{4,8},{5,9},{6,10},{7,11},{8,4},{9,5},... | collective-permute-start | bytes 294920 | tf_op jit(solution)/shard_map/ppermute | solution.py:280
  21.3 8.2 %collective-permute-start.9 = (bf16[24,16,128]{2,1,0:T(8,128)(2,1)S(1)}, bf16[24,16,128]{2,1,0:T(8,128)(2,1)S(1)}, u32[]{:S(2)}, u32[]{:S(2)}) collective-permute-start(bf16[24,16,128]{2,1,0:T(8,128)(2,1)S(1)} %get-tuple-element.50.refs_0_), channel_id=1, source_target_pairs={{0,8},{1,9},{2,10},{3,11},{4,12},{5,13},{6,14},{7,15},{8,0},{9,1},... | collective-permute-start | bytes 294920 | tf_op jit(solution)/shard_map/ppermute | solution.py:280
  24.4 1.8 %collective-permute-start.5 = (bf16[48,32,128]{2,1,0:T(8,128)(2,1)S(1)}, bf16[48,32,128]{2,1,0:T(8,128)(2,1)S(1)}, u32[]{:S(2)}, u32[]{:S(2)}) collective-permute-start(bf16[48,32,128]{2,1,0:T(8,128)(2,1)S(1)} %constant_dynamic-update-slice_fusion.4), channel_id=1, source_target_pairs={{0,1},{1,0},{2,3},{3,2},{4,5},{5,4},{6,7},{7,6},{8,9},{9,8},{10,11... | collective-permute-start | bytes 1179656 | tf_op jit(solution)/shard_map/ppermute | solution.py:280
  26.2 14.1 %collective-permute-start.11 = (bf16[48,16,128]{2,1,0:T(8,128)(2,1)S(1)}, bf16[48,16,128]{2,1,0:T(8,128)(2,1)S(1)}, u32[]{:S(2)}, u32[]{:S(2)}) collective-permute-start(bf16[48,16,128]{2,1,0:T(8,128)(2,1)S(1)} %pad_maximum_fusion.1), channel_id=1, source_target_pairs={{0,8},{1,9},{2,10},{3,11},{4,12},{5,13},{6,14},{7,15},{8,0},{9,1},... | collective-permute-start | bytes 589832 | tf_op jit(solution)/shard_map/ppermute | solution.py:280
  29.4 10.9 %copy-start = (bf16[1,128,128,128]{3,2,1,0:T(8,128)(2,1)S(1)}, bf16[1,128,128,128]{3,2,1,0:T(8,128)(2,1)}, u32[]{:S(2)}) copy-start(bf16[1,128,128,128]{3,2,1,0:T(8,128)(2,1)} %param.11) | copy-start | bytes 12582916
  29.5 10.9 %copy-start.1 = (f32[128]{0:T(128)S(1)}, f32[128]{0:T(128)}, u32[]{:S(2)}) copy-start(f32[128]{0:T(128)} %param.19) | copy-start | bytes 1540

commit v20 on v14

--- a/solution.py
+++ b/solution.py
@@ -11,6 +11,7 @@
 LANES = 128
 PARTS = 2
 MIB = 1024 * 1024
+RUN = 4
 
 
 def in_hbm(x):
@@ -200,11 +201,13 @@
                 old = pair_ref[h, at + q].astype(jnp.float32)
                 out_ref[h, q] = (old + share).astype(jnp.bfloat16)
 
-    for q in range(group + 1):
-        if q < group:
-            outer_products(q)
-        if q > 0:
-            project_back(q - 1)
+    for start in range(0, group + RUN, RUN):
+        for q in range(start, start + RUN):
+            if q < group:
+                outer_products(q)
+        for q in range(start - RUN, start):
+            if q >= 0:
+                project_back(q)
 
 
 def update_part(side, seqs, order, part, left, right, wt, before, bias, pair):
@@ -214,7 +217,7 @@
     pack = tile // rows
     width = lanes // pack
     halves = pack // 2
-    group = 8
+    group = 16
     first, last = part == 0, part == PARTS - 1
     in_vmem = pl.BlockSpec(memory_space=pltpu.VMEM)
     operands = [left] + list(right) + [wt[:, part * some * width : (part + 1) * some * width]]

time: 47.9 us -> 47.8 us (level)
  Pallas kernels: 23 us -> 22.4 us
  waiting for transfers between devices: 10.7 us -> 11.2 us
    pallas_call x2, Pallas kernels: 17.2 us -> 16.6 us  [update_part(): pl.pallas_call(functools.partial(update_kernel, side, seqs, order, len(ri...]
    ppermute x12, waiting for transfers between devices: 10.7 us -> 11.2 us  [swap(): lax.ppermute(x, 'row', [(i, i ^ da * side + db) for i in range(devices)])]
  transfers between devices with their start and end apart: 12 -> 12, of which waited for: 6 -> 6; matrix products, arithmetic and copies ran while one was open for 3% -> 3% of each run, Pallas kernels for 19% -> 18%
where the time goes in v20:
time: 47.8 us; the launch traced here: 47.6 us
  Pallas kernels  22.4 us (47%)
  starting transfers between devices  12.3 us (26%)
  waiting for transfers between devices  11.2 us (23%)
  local copies, waits for them, and re-layouts  1.45 us (3%)
    pallas_call x2, Pallas kernels, update_part(): pl.pallas_call(functools.partial(update_kernel, side, seqs, order, len(ri...  16.6 us
    ppermute x12, starting transfers between devices, swap(): lax.ppermute(x, 'row', [(i, i ^ da * side + db) for i in range(devices)])  12.3 us
    ppermute x12, waiting for transfers between devices, swap(): lax.ppermute(x, 'row', [(i, i ^ da * side + db) for i in range(devices)])  11.2 us
    pallas_call x1, Pallas kernels, project(): pl.pallas_call(functools.partial(project_kernel, side), in_specs=[pl.Bloc...  4.52 us
    pallas_call x1, Pallas kernels, arrange_left(): pl.pallas_call(functools.partial(arrange_kernel, seq_total), in_specs=[pl...  1.33 us
    transpose x1, local copies, waits for them, and re-layouts, local(): final_matrix.reshape(width, width, -1).transpose(2, 1, 0)  1.06 us
  transfers between devices with their start and end apart: 12, of which 6 were waited for; matrix products, arithmetic and copies ran while one was open for 3% of the time, Pallas kernels for 18%

profile of v20, /device:TPU:0, one launch (start us, length us, event | category | flops | bytes accessed | tf_op | source)
XLA Modules:
  0.0 47.6 jit_solution(3461605642439775826)
XLA Ops:
  0.0 4.5 %project.1 = (bf16[6,32,128]{2,1,0:T(8,128)(2,1)S(1)}, bf16[6,32,128]{2,1,0:T(8,128)(2,1)S(1)}, bf16[6,32,128]{2,1,0:T(8,128)(2,1)S(1)}, bf16[6,32,128]{2,1,0:T(...) custom-call(bf16[6,512,256]{2,1,0:T(8,128)(2,1)} %refs_0_.1, ...), custom_call_target="tpu_custom_call" | custom-call | tf_op jit(solution)/shard_map/project/pallas_call | solution.py:87
  4.5 0.5 %collective-permute-start = (bf16[2,6,16,128]{3,2,1,0:T(8,128)(2,1)S(1)}, bf16[2,6,16,128]{3,2,1,0:T(8,128)(2,1)S(1)}, u32[]{:S(2)}, u32[]{:S(2)}) collective-permute-start(bf16[2,6,16,128]{3,2,1,0:T(8,128)(2,1)S(1)} %get-tuple-element.29), channel_id=1, source_target_pairs={{0,1},{1,0},{2,3},{3,2},{4,5},{5,4},{6,7},{7,6},{8,9},{9,8},{10,11... | collective-permute-start | bytes 147464 | tf_op jit(solution)/shard_map/ppermute | solution.py:282
  5.0 2.6 %collective-permute-start.6 = (bf16[2,6,16,128]{3,2,1,0:T(8,128)(2,1)S(1)}, bf16[2,6,16,128]{3,2,1,0:T(8,128)(2,1)S(1)}, u32[]{:S(2)}, u32[]{:S(2)}) collective-permute-start(bf16[2,6,16,128]{3,2,1,0:T(8,128)(2,1)S(1)} %get-tuple-element.36), channel_id=1, source_target_pairs={{0,2},{1,3},{2,0},{3,1},{4,6},{5,7},{6,4},{7,5},{8,10},{9,11},{10,... | collective-permute-start | bytes 147464 | tf_op jit(solution)/shard_map/ppermute | solution.py:282
  7.6 0.1 collective-permute-start.7
  7.7 0.0 collective-permute-done
  7.7 1.8 %collective-permute-start.1 = (bf16[6,32,128]{2,1,0:T(8,128)(2,1)S(1)}, bf16[6,32,128]{2,1,0:T(8,128)(2,1)S(1)}, u32[]{:S(2)}, u32[]{:S(2)}) collective-permute-start(bf16[6,32,128]{2,1,0:T(8,128)(2,1)S(1)} %get-tuple-element.31), channel_id=1, source_target_pairs={{0,4},{1,5},{2,6},{3,7},{4,0},{5,1},{6,2},{7,3},{8,12},{9,13},{10,... | collective-permute-start | bytes 147464 | tf_op jit(solution)/shard_map/ppermute | solution.py:282
  9.6 2.6 %collective-permute-start.2 = (bf16[6,32,128]{2,1,0:T(8,128)(2,1)S(1)}, bf16[6,32,128]{2,1,0:T(8,128)(2,1)S(1)}, u32[]{:S(2)}, u32[]{:S(2)}) collective-permute-start(bf16[6,32,128]{2,1,0:T(8,128)(2,1)S(1)} %get-tuple-element.32), channel_id=1, source_target_pairs={{0,8},{1,9},{2,10},{3,11},{4,12},{5,13},{6,14},{7,15},{8,0},{9,1},... | collective-permute-start | bytes 147464 | tf_op jit(solution)/shard_map/ppermute | solution.py:282
  12.2 0.0 collective-permute-start.3
  12.2 0.0 collective-permute-done.6
  12.2 0.0 collective-permute-done.7
  12.3 1.0 %collective-permute-start.8 = (bf16[2,24,16,128]{3,2,1,0:T(8,128)(2,1)S(1)}, bf16[2,24,16,128]{3,2,1,0:T(8,128)(2,1)S(1)}, u32[]{:S(2)}, u32[]{:S(2)}) collective-permute-start(bf16[2,24,16,128]{3,2,1,0:T(8,128)(2,1)S(1)} %pad_maximum_fusion), channel_id=1, source_target_pairs={{0,4},{1,5},{2,6},{3,7},{4,0},{5,1},{6,2},{7,3},{8,12},{9,13},{10,... | collective-permute-start | bytes 589832 | tf_op jit(solution)/shard_map/ppermute | solution.py:282
  13.3 0.0 collective-permute-done.1
  13.3 2.4 %collective-permute-done.2 = bf16[6,32,128]{2,1,0:T(8,128)(2,1)S(1)} collective-permute-done((bf16[6,32,128]{2,1,0:T(8,128)(2,1)S(1)}, bf16[6,32,128]{2,1,0:T(8,128)(2,1)S(1)}, u32[]{:S(2)}, u32[]{:S(2)}) %collective-permute-start.2) | collective-permute-done | bytes 49184 | tf_op jit(solution)/shard_map/ppermute | solution.py:282
  15.7 2.9 %collective-permute-done.3 = bf16[6,32,128]{2,1,0:T(8,128)(2,1)S(1)} collective-permute-done((bf16[6,32,128]{2,1,0:T(8,128)(2,1)S(1)}, bf16[6,32,128]{2,1,0:T(8,128)(2,1)S(1)}, u32[]{:S(2)}, u32[]{:S(2)}) %collective-permute-start.3) | collective-permute-done | bytes 49184 | tf_op jit(solution)/shard_map/ppermute | solution.py:282
  18.6 1.6 %collective-permute-start.4 = (bf16[24,32,128]{2,1,0:T(8,128)(2,1)S(1)}, bf16[24,32,128]{2,1,0:T(8,128)(2,1)S(1)}, u32[]{:S(2)}, u32[]{:S(2)}) collective-permute-start(bf16[24,32,128]{2,1,0:T(8,128)(2,1)S(1)} %get-tuple-element.62.refs_0_), channel_id=1, source_target_pairs={{0,2},{1,3},{2,0},{3,1},{4,6},{5,7},{6,4},{7,5},{8,10},{9,11},{10,... | collective-permute-start | bytes 589832 | tf_op jit(solution)/shard_map/ppermute | solution.py:282
  20.2 1.1 %collective-permute-start.10 = (bf16[24,16,128]{2,1,0:T(8,128)(2,1)S(1)}, bf16[24,16,128]{2,1,0:T(8,128)(2,1)S(1)}, u32[]{:S(2)}, u32[]{:S(2)}) collective-permute-start(bf16[24,16,128]{2,1,0:T(8,128)(2,1)S(1)} %get-tuple-element.50.refs_0_), channel_id=1, source_target_pairs={{0,12},{1,13},{2,14},{3,15},{4,8},{5,9},{6,10},{7,11},{8,4},{9,5},... | collective-permute-start | bytes 294920 | tf_op jit(solution)/shard_map/ppermute | solution.py:282
  21.3 0.0 collective-permute-start.9
  21.3 0.0 collective-permute-done.8
  21.3 1.1 %copy.14 = bf16[128,32,32]{0,2,1:T(8,128)(2,1)S(1)} copy(bf16[128,32,32]{0,1,2:T(8,128)(2,1)} %bitcast.40) | data formatting | bytes 524288 | tf_op jit(solution)/shard_map/transpose | solution.py:308
  22.3 2.0 %collective-permute-done.4.refs_1_ = bf16[24,32,128]{2,1,0:T(8,128)(2,1)S(1)} collective-permute-done((bf16[24,32,128]{2,1,0:T(8,128)(2,1)S(1)}, bf16[24,32,128]{2,1,0:T(8,128)(2,1)S(1)}, u32[]{:S(2)}, u32[]{:S(2)}) %collective-permute-start.4) | collective-permute-done | bytes 196640 | tf_op jit(solution)/shard_map/ppermute | solution.py:282
  24.4 0.1 collective-permute-start.5
  24.5 0.1 copy.18.refs_3_
  24.6 0.1 copy.17.refs_4_
  24.8 1.4 %collective-permute-done.5.refs_2_ = bf16[48,32,128]{2,1,0:T(8,128)(2,1)S(1)} collective-permute-done((bf16[48,32,128]{2,1,0:T(8,128)(2,1)S(1)}, bf16[48,32,128]{2,1,0:T(8,128)(2,1)S(1)}, u32[]{:S(2)}, u32[]{:S(2)}) %collective-permute-start.5) | collective-permute-done | bytes 393248 | tf_op jit(solution)/shard_map/ppermute | solution.py:282
  26.2 1.0 %collective-permute-start.11 = (bf16[48,16,128]{2,1,0:T(8,128)(2,1)S(1)}, bf16[48,16,128]{2,1,0:T(8,128)(2,1)S(1)}, u32[]{:S(2)}, u32[]{:S(2)}) collective-permute-start(bf16[48,16,128]{2,1,0:T(8,128)(2,1)S(1)} %pad_maximum_fusion.1), channel_id=1, source_target_pairs={{0,8},{1,9},{2,10},{3,11},{4,12},{5,13},{6,14},{7,15},{8,0},{9,1},... | collective-permute-start | bytes 589832 | tf_op jit(solution)/shard_map/ppermute | solution.py:282
  27.2 1.3 %arrange_left.1.left_ref = bf16[32,128,128]{2,1,0:T(8,128)(2,1)S(1)} custom-call(bf16[24,32,128]{2,1,0:T(8,128)(2,1)S(1)} %get-tuple-element.62.refs_0_, bf16[24,32,128]{2,1,0:T(8,128)(2,1)S(1)} %collective-permute-done.4.refs_1_, bf16[48,32,128]{2,1,0:T(8,128)(2,1)S(1)} %collective-permute-done.5.refs_2_), custom_call_target="tpu_custom_call" | custom-call | flops 1048576 | bytes 8388608 | tf_op jit(solution)/shard_map/arrange_left/pallas_call | solution.py:124
  28.5 0.0 collective-permute-done.10.refs_3_
  28.5 0.9 %collective-permute-done.9.refs_2_ = bf16[24,16,128]{2,1,0:T(8,128)(2,1)S(1)} collective-permute-done((bf16[24,16,128]{2,1,0:T(8,128)(2,1)S(1)}, bf16[24,16,128]{2,1,0:T(8,128)(2,1)S(1)}, u32[]{:S(2)}, u32[]{:S(2)}) %collective-permute-start.9) | collective-permute-done | bytes 98336 | tf_op jit(solution)/shard_map/ppermute | solution.py:282
  29.4 0.0 copy-start
  29.5 0.0 copy-start.1
  29.5 7.3 %update_0.1.refs_4_ = f32[32,2,128,256]{3,2,1,0:T(8,128)S(1)} custom-call(bf16[32,128,128]{2,1,0:T(8,128)(2,1)S(1)} %arrange_left.1.left_ref, bf16[24,16,128]{2,1,0:T(8,128)(2,1)S(1)} %get-tuple-element.50.refs_0_, bf16[24,16,128]{2,1,0:T(8,128)(2,1)S(1)} %get-tuple-element.48.refs_1_, bf16[24,16,128]{2,1,0:T(8,128)(2,1)S(1)} %collective-permute-done.9.refs_2_, ...), custom_call_target="tpu_custom_call" | custom-call | flops 3758096384 | bytes 16777216 | tf_op jit(solution)/shard_map/update_0/pallas_call | solution.py:232
  36.8 1.6 %collective-permute-done.11.refs_2_ = bf16[48,16,128]{2,1,0:T(8,128)(2,1)S(1)} collective-permute-done((bf16[48,16,128]{2,1,0:T(8,128)(2,1)S(1)}, bf16[48,16,128]{2,1,0:T(8,128)(2,1)S(1)}, u32[]{:S(2)}, u32[]{:S(2)}) %collective-permute-start.11) | collective-permute-done | bytes 196640 | tf_op jit(solution)/shard_map/ppermute | solution.py:282
  38.3 0.0 copy-done
  38.3 0.0 copy-done.1
  38.3 9.3 %update_1.1 = bf16[4,32,128,128]{3,2,1,0:T(8,128)(2,1)} custom-call(bf16[32,128,128]{2,1,0:T(8,128)(2,1)S(1)} %arrange_left.1.left_ref, bf16[24,16,128]{2,1,0:T(8,128)(2,1)S(1)} %get-tuple-element.41.refs_0_, bf16[24,16,128]{2,1,0:T(8,128)(2,1)S(1)} %get-tuple-element.42.refs_1_, bf16[48,16,128]{2,1,0:T(8,128)(2,1)S(1)} %collective-permute-done.11.refs_2_, ...), custom_call_target="tpu_custom_call" | custom-call | flops 3758096384 | bytes 16777216 | tf_op jit(solution)/shard_map/update_1/pallas_call | solution.py:232
  (15 shorter events, 0.2 us)
Async XLA Ops:
  4.5 3.2 %collective-permute-start = (bf16[2,6,16,128]{3,2,1,0:T(8,128)(2,1)S(1)}, bf16[2,6,16,128]{3,2,1,0:T(8,128)(2,1)S(1)}, u32[]{:S(2)}, u32[]{:S(2)}) collective-permute-start(bf16[2,6,16,128]{3,2,1,0:T(8,128)(2,1)S(1)} %get-tuple-element.29), channel_id=1, source_target_pairs={{0,1},{1,0},{2,3},{3,2},{4,5},{5,4},{6,7},{7,6},{8,9},{9,8},{10,11... | collective-permute-start | bytes 147464 | tf_op jit(solution)/shard_map/ppermute | solution.py:282
  5.0 7.1 %collective-permute-start.6 = (bf16[2,6,16,128]{3,2,1,0:T(8,128)(2,1)S(1)}, bf16[2,6,16,128]{3,2,1,0:T(8,128)(2,1)S(1)}, u32[]{:S(2)}, u32[]{:S(2)}) collective-permute-start(bf16[2,6,16,128]{3,2,1,0:T(8,128)(2,1)S(1)} %get-tuple-element.36), channel_id=1, source_target_pairs={{0,2},{1,3},{2,0},{3,1},{4,6},{5,7},{6,4},{7,5},{8,10},{9,11},{10,... | collective-permute-start | bytes 147464 | tf_op jit(solution)/shard_map/ppermute | solution.py:282
  7.6 4.6 %collective-permute-start.7 = (bf16[2,6,16,128]{3,2,1,0:T(8,128)(2,1)S(1)}, bf16[2,6,16,128]{3,2,1,0:T(8,128)(2,1)S(1)}, u32[]{:S(2)}, u32[]{:S(2)}) collective-permute-start(bf16[2,6,16,128]{3,2,1,0:T(8,128)(2,1)S(1)} %get-tuple-element.37), channel_id=1, source_target_pairs={{0,3},{1,2},{2,1},{3,0},{4,7},{5,6},{6,5},{7,4},{8,11},{9,10},{10,... | collective-permute-start | bytes 147464 | tf_op jit(solution)/shard_map/ppermute | solution.py:282
  7.7 5.5 %collective-permute-start.1 = (bf16[6,32,128]{2,1,0:T(8,128)(2,1)S(1)}, bf16[6,32,128]{2,1,0:T(8,128)(2,1)S(1)}, u32[]{:S(2)}, u32[]{:S(2)}) collective-permute-start(bf16[6,32,128]{2,1,0:T(8,128)(2,1)S(1)} %get-tuple-element.31), channel_id=1, source_target_pairs={{0,4},{1,5},{2,6},{3,7},{4,0},{5,1},{6,2},{7,3},{8,12},{9,13},{10,... | collective-permute-start | bytes 147464 | tf_op jit(solution)/shard_map/ppermute | solution.py:282
  9.6 6.1 %collective-permute-start.2 = (bf16[6,32,128]{2,1,0:T(8,128)(2,1)S(1)}, bf16[6,32,128]{2,1,0:T(8,128)(2,1)S(1)}, u32[]{:S(2)}, u32[]{:S(2)}) collective-permute-start(bf16[6,32,128]{2,1,0:T(8,128)(2,1)S(1)} %get-tuple-element.32), channel_id=1, source_target_pairs={{0,8},{1,9},{2,10},{3,11},{4,12},{5,13},{6,14},{7,15},{8,0},{9,1},... | collective-permute-start | bytes 147464 | tf_op jit(solution)/shard_map/ppermute | solution.py:282
  12.2 6.4 %collective-permute-start.3 = (bf16[6,32,128]{2,1,0:T(8,128)(2,1)S(1)}, bf16[6,32,128]{2,1,0:T(8,128)(2,1)S(1)}, u32[]{:S(2)}, u32[]{:S(2)}) collective-permute-start(bf16[6,32,128]{2,1,0:T(8,128)(2,1)S(1)} %get-tuple-element.33), channel_id=1, source_target_pairs={{0,12},{1,13},{2,14},{3,15},{4,8},{5,9},{6,10},{7,11},{8,4},{9,5},... | collective-permute-start | bytes 147464 | tf_op jit(solution)/shard_map/ppermute | solution.py:282
  12.3 9.0 %collective-permute-start.8 = (bf16[2,24,16,128]{3,2,1,0:T(8,128)(2,1)S(1)}, bf16[2,24,16,128]{3,2,1,0:T(8,128)(2,1)S(1)}, u32[]{:S(2)}, u32[]{:S(2)}) collective-permute-start(bf16[2,24,16,128]{3,2,1,0:T(8,128)(2,1)S(1)} %pad_maximum_fusion), channel_id=1, source_target_pairs={{0,4},{1,5},{2,6},{3,7},{4,0},{5,1},{6,2},{7,3},{8,12},{9,13},{10,... | collective-permute-start | bytes 589832 | tf_op jit(solution)/shard_map/ppermute | solution.py:282
  18.6 5.7 %collective-permute-start.4 = (bf16[24,32,128]{2,1,0:T(8,128)(2,1)S(1)}, bf16[24,32,128]{2,1,0:T(8,128)(2,1)S(1)}, u32[]{:S(2)}, u32[]{:S(2)}) collective-permute-start(bf16[24,32,128]{2,1,0:T(8,128)(2,1)S(1)} %get-tuple-element.62.refs_0_), channel_id=1, source_target_pairs={{0,2},{1,3},{2,0},{3,1},{4,6},{5,7},{6,4},{7,5},{8,10},{9,11},{10,... | collective-permute-start | bytes 589832 | tf_op jit(solution)/shard_map/ppermute | solution.py:282
  20.2 8.3 %collective-permute-start.10 = (bf16[24,16,128]{2,1,0:T(8,128)(2,1)S(1)}, bf16[24,16,128]{2,1,0:T(8,128)(2,1)S(1)}, u32[]{:S(2)}, u32[]{:S(2)}) collective-permute-start(bf16[24,16,128]{2,1,0:T(8,128)(2,1)S(1)} %get-tuple-element.50.refs_0_), channel_id=1, source_target_pairs={{0,12},{1,13},{2,14},{3,15},{4,8},{5,9},{6,10},{7,11},{8,4},{9,5},... | collective-permute-start | bytes 294920 | tf_op jit(solution)/shard_map/ppermute | solution.py:282
  21.3 8.2 %collective-permute-start.9 = (bf16[24,16,128]{2,1,0:T(8,128)(2,1)S(1)}, bf16[24,16,128]{2,1,0:T(8,128)(2,1)S(1)}, u32[]{:S(2)}, u32[]{:S(2)}) collective-permute-start(bf16[24,16,128]{2,1,0:T(8,128)(2,1)S(1)} %get-tuple-element.50.refs_0_), channel_id=1, source_target_pairs={{0,8},{1,9},{2,10},{3,11},{4,12},{5,13},{6,14},{7,15},{8,0},{9,1},... | collective-permute-start | bytes 294920 | tf_op jit(solution)/shard_map/ppermute | solution.py:282
  24.4 1.8 %collective-permute-start.5 = (bf16[48,32,128]{2,1,0:T(8,128)(2,1)S(1)}, bf16[48,32,128]{2,1,0:T(8,128)(2,1)S(1)}, u32[]{:S(2)}, u32[]{:S(2)}) collective-permute-start(bf16[48,32,128]{2,1,0:T(8,128)(2,1)S(1)} %constant_dynamic-update-slice_fusion.4), channel_id=1, source_target_pairs={{0,1},{1,0},{2,3},{3,2},{4,5},{5,4},{6,7},{7,6},{8,9},{9,8},{10,11... | collective-permute-start | bytes 1179656 | tf_op jit(solution)/shard_map/ppermute | solution.py:282
  26.2 12.1 %collective-permute-start.11 = (bf16[48,16,128]{2,1,0:T(8,128)(2,1)S(1)}, bf16[48,16,128]{2,1,0:T(8,128)(2,1)S(1)}, u32[]{:S(2)}, u32[]{:S(2)}) collective-permute-start(bf16[48,16,128]{2,1,0:T(8,128)(2,1)S(1)} %pad_maximum_fusion.1), channel_id=1, source_target_pairs={{0,8},{1,9},{2,10},{3,11},{4,12},{5,13},{6,14},{7,15},{8,0},{9,1},... | collective-permute-start | bytes 589832 | tf_op jit(solution)/shard_map/ppermute | solution.py:282
  29.4 8.9 %copy-start = (bf16[1,128,128,128]{3,2,1,0:T(8,128)(2,1)S(1)}, bf16[1,128,128,128]{3,2,1,0:T(8,128)(2,1)}, u32[]{:S(2)}) copy-start(bf16[1,128,128,128]{3,2,1,0:T(8,128)(2,1)} %param.11) | copy-start | bytes 12582916
  29.5 8.9 %copy-start.1 = (f32[128]{0:T(128)S(1)}, f32[128]{0:T(128)}, u32[]{:S(2)}) copy-start(f32[128]{0:T(128)} %param.19) | copy-start | bytes 1540

commit v21 on v20

--- a/solution.py
+++ b/solution.py
@@ -20,8 +20,8 @@
 
 def project_kernel(side, *refs):
     sources, refs = refs[:7], refs[7:]
-    left_out, right_out, refs = refs[:side], refs[side : 2 * side], refs[2 * side :]
-    buffers, normed_ref, sems, x_sems = refs[:7], refs[7], refs[8], refs[9]
+    left_out, right_out, refs = refs[0], refs[1], refs[2:]
+    buffers, sems, x_sems = refs[:7], refs[7], refs[8]
     x_ref, gain_ref, offset_ref, wl_ref, bl_ref, wr_ref, br_ref = buffers
     seqs, residues, chans = x_ref.shape
     width = wl_ref.shape[0]
@@ -50,32 +50,30 @@
     right_bias = jnp.broadcast_to(br_ref[...], (tile, width)).T
     for s in range(seqs):
         x_copies[s].wait()
-        normed = normed_ref.at[s % 2]
         x = x_ref[s].astype(jnp.float32)
         center = x - jnp.mean(x, axis=-1, keepdims=True)
         variance = jnp.mean(center * center, axis=-1, keepdims=True)
-        normed[...] = (
-            center * lax.rsqrt(variance + 1e-05) * gain_ref[...] + offset_ref[...]
-        ).astype(jnp.bfloat16)
-        blocks = []
-        for d in range(side):
-            b = place_b ^ d
-            block = normed[pl.ds(pl.multiple_of(b * tile, tile), tile), :]
-            right = lax.dot_general(wr_ref[...], block, nt, preferred_element_type=jnp.float32)
-            right_out[d][:, s] = (
-                (right + right_bias).astype(jnp.bfloat16).reshape(PARTS, width // PARTS, tile)
-            )
-            a = place_a ^ d
-            blocks.append(normed[pl.ds(pl.multiple_of(a * tile, tile), tile), :])
+        normed = (center * lax.rsqrt(variance + 1e-05) * gain_ref[...] + offset_ref[...]).astype(
+            jnp.bfloat16
+        )
+        right = lax.dot_general(wr_ref[...], normed, nt, preferred_element_type=jnp.float32)
         total = left_bias
         for h in range(pack):
-            picked = jnp.concatenate([block[h * rows : (h + 1) * rows] for block in blocks], axis=0)
+            picked = jnp.concatenate(
+                [normed[a * tile + h * rows : a * tile + (h + 1) * rows] for a in range(side)],
+                axis=0,
+            )
             total = total + lax.dot_general(
                 picked, placed[h], nt, preferred_element_type=jnp.float32
             )
         left = total.astype(jnp.bfloat16)
-        for d in range(side):
-            left_out[d][s] = left[d * rows : (d + 1) * rows]
+        for k in range(side):
+            left_out[place_a ^ k, s] = left[k * rows : (k + 1) * rows]
+            right_out[place_b ^ k, :, s] = (
+                (right[:, k * tile : (k + 1) * tile] + right_bias)
+                .astype(jnp.bfloat16)
+                .reshape(PARTS, width // PARTS, tile)
+            )
 
 
 def project(side, x, gain, offset, wl, bl, wr, br):
@@ -87,19 +85,20 @@
     out = pl.pallas_call(
         functools.partial(project_kernel, side),
         in_specs=[pl.BlockSpec(memory_space=pltpu.HBM)] * len(operands),
-        out_specs=[pl.BlockSpec(memory_space=pltpu.VMEM)] * (2 * side),
-        out_shape=[jax.ShapeDtypeStruct((seqs, rows, LANES), jnp.bfloat16)] * side
-        + [jax.ShapeDtypeStruct((PARTS, seqs, width // PARTS, tile), jnp.bfloat16)] * side,
+        out_specs=[pl.BlockSpec(memory_space=pltpu.VMEM)] * 2,
+        out_shape=[
+            jax.ShapeDtypeStruct((side, seqs, rows, LANES), jnp.bfloat16),
+            jax.ShapeDtypeStruct((side, PARTS, seqs, width // PARTS, tile), jnp.bfloat16),
+        ],
         scratch_shapes=[pltpu.VMEM(o.shape, o.dtype) for o in operands]
         + [
-            pltpu.VMEM((2, residues, chans), jnp.bfloat16),
             pltpu.SemaphoreType.DMA((len(operands),)),
             pltpu.SemaphoreType.DMA((seqs,)),
         ],
         compiler_params=pltpu.CompilerParams(vmem_limit_bytes=32 * MIB),
         name="project",
     )(*operands)
-    return out[:side], out[side:]
+    return list(out[0]), list(out[1])
 
 
 def arrange_kernel(seq_total, *refs):

time: 47.8 us -> 48.5 us (1.015)
  waiting for transfers between devices: 11.2 us -> 13.5 us
  local copies, waits for them, and re-layouts: 1.45 us -> 0.53 us
  starting transfers between devices: 12.3 us -> 11.7 us
    ppermute x12, waiting for transfers between devices: 11.2 us -> 13.5 us  [swap(): lax.ppermute(x, 'row', [(i, i ^ da * side + db) for i in range(devices)])]
    transpose x1, local copies, waits for them, and re-layouts: 1.06 us -> 0.11 us  [local(): final_matrix.reshape(width, width, -1).transpose(2, 1, 0)]
    ppermute x12, starting transfers between devices: 12.3 us -> 11.7 us  [swap(): lax.ppermute(x, 'row', [(i, i ^ da * side + db) for i in range(devices)])]
  transfers between devices with their start and end apart: 12 -> 12, of which waited for: 6 -> 7; matrix products, arithmetic and copies ran while one was open for 3% -> 1% of each run, Pallas kernels for 18% -> 18%
where the time goes in v21:
time: 48.5 us; the launch traced here: 48.3 us
  Pallas kernels  22.3 us (46%)
  waiting for transfers between devices  13.5 us (28%)
  starting transfers between devices  11.7 us (24%)
  local copies, waits for them, and re-layouts  0.53 us (1%)
    pallas_call x2, Pallas kernels, update_part(): pl.pallas_call(functools.partial(update_kernel, side, seqs, order, len(ri...  16.6 us
    ppermute x12, waiting for transfers between devices, swap(): lax.ppermute(x, 'row', [(i, i ^ da * side + db) for i in range(devices)])  13.5 us
    ppermute x12, starting transfers between devices, swap(): lax.ppermute(x, 'row', [(i, i ^ da * side + db) for i in range(devices)])  11.7 us
    pallas_call x1, Pallas kernels, project(): pl.pallas_call(functools.partial(project_kernel, side), in_specs=[pl.Bloc...  4.36 us
    pallas_call x1, Pallas kernels, arrange_left(): pl.pallas_call(functools.partial(arrange_kernel, seq_total), in_specs=[pl...  1.33 us
  transfers between devices with their start and end apart: 12, of which 7 were waited for; matrix products, arithmetic and copies ran while one was open for 1% of the time, Pallas kernels for 18%

profile of v21, /device:TPU:0, one launch (start us, length us, event | category | flops | bytes accessed | tf_op | source)
XLA Modules:
  0.0 48.3 jit_solution(5074571950236816115)
XLA Ops:
  0.0 0.0 copy-start.2
  0.0 4.4 %project.1 = (bf16[4,6,32,128]{3,2,1,0:T(8,128)(2,1)S(1)}, bf16[4,2,6,16,128]{4,3,2,1,0:T(8,128)(2,1)S(1)}) custom-call(bf16[6,512,256]{2,1,0:T(8,128)(2,1)} %refs_0_.1, f32[1,256]{1,0:T(1,128)} %bitcast.57, f32[1,256]{1,0:T(1,128)} %bitcast.58, bf16[32,256]{1,0:T(8,128)(2,1)} %bitcast.55, f32[1,32]{1,0:T(1,128)} %bitcast.59, bf16[32,256]{1,0:T(8,128)(2,1)} %bitcast.56, ...), custom_call_target="tpu_custom_call" | custom-call | tf_op jit(solution)/shard_map/project/pallas_call | solution.py:85
  4.4 3.0 %collective-permute-start.6 = (bf16[2,6,16,128]{3,2,1,0:T(8,128)(2,1)S(1)}, bf16[2,6,16,128]{3,2,1,0:T(8,128)(2,1)S(1)}, u32[]{:S(2)}, u32[]{:S(2)}) collective-permute-start(bf16[2,6,16,128]{3,2,1,0:T(8,128)(2,1)S(1)} %get-tuple-element.39), channel_id=1, source_target_pairs={{0,2},{1,3},{2,0},{3,1},{4,6},{5,7},{6,4},{7,5},{8,10},{9,11},{10,... | collective-permute-start | bytes 147464 | tf_op jit(solution)/shard_map/ppermute | solution.py:281
  7.4 0.0 collective-permute-start.7
  7.4 0.2 collective-permute-start
  7.6 1.0 %collective-permute-done = bf16[2,6,16,128]{3,2,1,0:T(8,128)(2,1)S(1)} collective-permute-done((bf16[2,6,16,128]{3,2,1,0:T(8,128)(2,1)S(1)}, bf16[2,6,16,128]{3,2,1,0:T(8,128)(2,1)S(1)}, u32[]{:S(2)}, u32[]{:S(2)}) %collective-permute-start) | collective-permute-done | bytes 49184 | tf_op jit(solution)/shard_map/ppermute | solution.py:281
  8.7 1.8 %collective-permute-start.1 = (bf16[6,32,128]{2,1,0:T(8,128)(2,1)S(1)}, bf16[6,32,128]{2,1,0:T(8,128)(2,1)S(1)}, u32[]{:S(2)}, u32[]{:S(2)}) collective-permute-start(bf16[6,32,128]{2,1,0:T(8,128)(2,1)S(1)} %get-tuple-element.22), channel_id=1, source_target_pairs={{0,4},{1,5},{2,6},{3,7},{4,0},{5,1},{6,2},{7,3},{8,12},{9,13},{10,... | collective-permute-start | bytes 147464 | tf_op jit(solution)/shard_map/ppermute | solution.py:281
  10.5 2.6 %collective-permute-start.2 = (bf16[6,32,128]{2,1,0:T(8,128)(2,1)S(1)}, bf16[6,32,128]{2,1,0:T(8,128)(2,1)S(1)}, u32[]{:S(2)}, u32[]{:S(2)}) collective-permute-start(bf16[6,32,128]{2,1,0:T(8,128)(2,1)S(1)} %get-tuple-element.23), channel_id=1, source_target_pairs={{0,8},{1,9},{2,10},{3,11},{4,12},{5,13},{6,14},{7,15},{8,0},{9,1},... | collective-permute-start | bytes 147464 | tf_op jit(solution)/shard_map/ppermute | solution.py:281
  13.1 0.0 collective-permute-start.3
  13.1 0.0 collective-permute-done.6
  13.1 0.0 collective-permute-done.7
  13.2 1.0 %collective-permute-start.8 = (bf16[2,24,16,128]{3,2,1,0:T(8,128)(2,1)S(1)}, bf16[2,24,16,128]{3,2,1,0:T(8,128)(2,1)S(1)}, u32[]{:S(2)}, u32[]{:S(2)}) collective-permute-start(bf16[2,24,16,128]{3,2,1,0:T(8,128)(2,1)S(1)} %pad_maximum_fusion), channel_id=1, source_target_pairs={{0,4},{1,5},{2,6},{3,7},{4,0},{5,1},{6,2},{7,3},{8,12},{9,13},{10,... | collective-permute-start | bytes 589832 | tf_op jit(solution)/shard_map/ppermute | solution.py:281
  14.2 0.0 collective-permute-done.1
  14.2 2.4 %collective-permute-done.2 = bf16[6,32,128]{2,1,0:T(8,128)(2,1)S(1)} collective-permute-done((bf16[6,32,128]{2,1,0:T(8,128)(2,1)S(1)}, bf16[6,32,128]{2,1,0:T(8,128)(2,1)S(1)}, u32[]{:S(2)}, u32[]{:S(2)}) %collective-permute-start.2) | collective-permute-done | bytes 49184 | tf_op jit(solution)/shard_map/ppermute | solution.py:281
  16.6 2.9 %collective-permute-done.3 = bf16[6,32,128]{2,1,0:T(8,128)(2,1)S(1)} collective-permute-done((bf16[6,32,128]{2,1,0:T(8,128)(2,1)S(1)}, bf16[6,32,128]{2,1,0:T(8,128)(2,1)S(1)}, u32[]{:S(2)}, u32[]{:S(2)}) %collective-permute-start.3) | collective-permute-done | bytes 49184 | tf_op jit(solution)/shard_map/ppermute | solution.py:281
  19.6 1.6 %collective-permute-start.4 = (bf16[24,32,128]{2,1,0:T(8,128)(2,1)S(1)}, bf16[24,32,128]{2,1,0:T(8,128)(2,1)S(1)}, u32[]{:S(2)}, u32[]{:S(2)}) collective-permute-start(bf16[24,32,128]{2,1,0:T(8,128)(2,1)S(1)} %get-tuple-element.57.refs_0_), channel_id=1, source_target_pairs={{0,2},{1,3},{2,0},{3,1},{4,6},{5,7},{6,4},{7,5},{8,10},{9,11},{10,... | collective-permute-start | bytes 589832 | tf_op jit(solution)/shard_map/ppermute | solution.py:281
  21.1 1.1 %collective-permute-start.10 = (bf16[24,16,128]{2,1,0:T(8,128)(2,1)S(1)}, bf16[24,16,128]{2,1,0:T(8,128)(2,1)S(1)}, u32[]{:S(2)}, u32[]{:S(2)}) collective-permute-start(bf16[24,16,128]{2,1,0:T(8,128)(2,1)S(1)} %get-tuple-element.47.refs_0_), channel_id=1, source_target_pairs={{0,12},{1,13},{2,14},{3,15},{4,8},{5,9},{6,10},{7,11},{8,4},{9,5},... | collective-permute-start | bytes 294920 | tf_op jit(solution)/shard_map/ppermute | solution.py:281
  22.2 0.0 collective-permute-start.9
  22.2 0.0 collective-permute-done.8
  22.2 0.0 copy-done.2
  22.2 0.1 copy.14
  22.3 3.0 %collective-permute-done.4.refs_1_ = bf16[24,32,128]{2,1,0:T(8,128)(2,1)S(1)} collective-permute-done((bf16[24,32,128]{2,1,0:T(8,128)(2,1)S(1)}, bf16[24,32,128]{2,1,0:T(8,128)(2,1)S(1)}, u32[]{:S(2)}, u32[]{:S(2)}) %collective-permute-start.4) | collective-permute-done | bytes 196640 | tf_op jit(solution)/shard_map/ppermute | solution.py:281
  25.3 0.1 collective-permute-start.5
  25.4 0.1 copy.18.refs_3_
  25.6 0.1 copy.17.refs_4_
  25.7 1.4 %collective-permute-done.5.refs_2_ = bf16[48,32,128]{2,1,0:T(8,128)(2,1)S(1)} collective-permute-done((bf16[48,32,128]{2,1,0:T(8,128)(2,1)S(1)}, bf16[48,32,128]{2,1,0:T(8,128)(2,1)S(1)}, u32[]{:S(2)}, u32[]{:S(2)}) %collective-permute-start.5) | collective-permute-done | bytes 393248 | tf_op jit(solution)/shard_map/ppermute | solution.py:281
  27.1 0.4 collective-permute-start.11
  27.5 1.3 %arrange_left.1.left_ref = bf16[32,128,128]{2,1,0:T(8,128)(2,1)S(1)} custom-call(bf16[24,32,128]{2,1,0:T(8,128)(2,1)S(1)} %get-tuple-element.57.refs_0_, bf16[24,32,128]{2,1,0:T(8,128)(2,1)S(1)} %collective-permute-done.4.refs_1_, bf16[48,32,128]{2,1,0:T(8,128)(2,1)S(1)} %collective-permute-done.5.refs_2_), custom_call_target="tpu_custom_call" | custom-call | flops 1048576 | bytes 8388608 | tf_op jit(solution)/shard_map/arrange_left/pallas_call | solution.py:123
  28.9 0.0 collective-permute-done.10.refs_3_
  28.9 1.5 %collective-permute-done.9.refs_2_ = bf16[24,16,128]{2,1,0:T(8,128)(2,1)S(1)} collective-permute-done((bf16[24,16,128]{2,1,0:T(8,128)(2,1)S(1)}, bf16[24,16,128]{2,1,0:T(8,128)(2,1)S(1)}, u32[]{:S(2)}, u32[]{:S(2)}) %collective-permute-start.9) | collective-permute-done | bytes 98336 | tf_op jit(solution)/shard_map/ppermute | solution.py:281
  30.4 0.0 copy-start
  30.4 0.0 copy-start.1
  30.4 7.3 %update_0.1.refs_4_ = f32[32,2,128,256]{3,2,1,0:T(8,128)S(1)} custom-call(bf16[32,128,128]{2,1,0:T(8,128)(2,1)S(1)} %arrange_left.1.left_ref, bf16[24,16,128]{2,1,0:T(8,128)(2,1)S(1)} %get-tuple-element.47.refs_0_, bf16[24,16,128]{2,1,0:T(8,128)(2,1)S(1)} %get-tuple-element.36.refs_1_, bf16[24,16,128]{2,1,0:T(8,128)(2,1)S(1)} %collective-permute-done.9.refs_2_, ...), custom_call_target="tpu_custom_call" | custom-call | flops 3758096384 | bytes 16777216 | tf_op jit(solution)/shard_map/update_0/pallas_call | solution.py:231
  37.7 1.3 %collective-permute-done.11.refs_2_ = bf16[48,16,128]{2,1,0:T(8,128)(2,1)S(1)} collective-permute-done((bf16[48,16,128]{2,1,0:T(8,128)(2,1)S(1)}, bf16[48,16,128]{2,1,0:T(8,128)(2,1)S(1)}, u32[]{:S(2)}, u32[]{:S(2)}) %collective-permute-start.11) | collective-permute-done | bytes 196640 | tf_op jit(solution)/shard_map/ppermute | solution.py:281
  39.1 0.0 copy-done
  39.1 0.0 copy-done.1
  39.1 9.3 %update_1.1 = bf16[4,32,128,128]{3,2,1,0:T(8,128)(2,1)} custom-call(bf16[32,128,128]{2,1,0:T(8,128)(2,1)S(1)} %arrange_left.1.left_ref, bf16[24,16,128]{2,1,0:T(8,128)(2,1)S(1)} %get-tuple-element.29.refs_0_, bf16[24,16,128]{2,1,0:T(8,128)(2,1)S(1)} %get-tuple-element.30.refs_1_, bf16[48,16,128]{2,1,0:T(8,128)(2,1)S(1)} %collective-permute-done.11.refs_2_, ...), custom_call_target="tpu_custom_call" | custom-call | flops 3758096384 | bytes 16777216 | tf_op jit(solution)/shard_map/update_1/pallas_call | solution.py:231
  (17 shorter events, 0.3 us)
Async XLA Ops:
  0.0 22.2 %copy-start.2 = (bf16[1024,128]{1,0:T(8,128)(2,1)S(1)}, bf16[1024,128]{1,0:T(8,128)(2,1)}, u32[]{:S(2)}) copy-start(bf16[1024,128]{1,0:T(8,128)(2,1)} %param.18) | copy-start | bytes 786436
  4.4 8.7 %collective-permute-start.6 = (bf16[2,6,16,128]{3,2,1,0:T(8,128)(2,1)S(1)}, bf16[2,6,16,128]{3,2,1,0:T(8,128)(2,1)S(1)}, u32[]{:S(2)}, u32[]{:S(2)}) collective-permute-start(bf16[2,6,16,128]{3,2,1,0:T(8,128)(2,1)S(1)} %get-tuple-element.39), channel_id=1, source_target_pairs={{0,2},{1,3},{2,0},{3,1},{4,6},{5,7},{6,4},{7,5},{8,10},{9,11},{10,... | collective-permute-start | bytes 147464 | tf_op jit(solution)/shard_map/ppermute | solution.py:281
  7.4 5.7 %collective-permute-start.7 = (bf16[2,6,16,128]{3,2,1,0:T(8,128)(2,1)S(1)}, bf16[2,6,16,128]{3,2,1,0:T(8,128)(2,1)S(1)}, u32[]{:S(2)}, u32[]{:S(2)}) collective-permute-start(bf16[2,6,16,128]{3,2,1,0:T(8,128)(2,1)S(1)} %get-tuple-element.40), channel_id=1, source_target_pairs={{0,3},{1,2},{2,1},{3,0},{4,7},{5,6},{6,5},{7,4},{8,11},{9,10},{10,... | collective-permute-start | bytes 147464 | tf_op jit(solution)/shard_map/ppermute | solution.py:281
  7.4 1.2 %collective-permute-start = (bf16[2,6,16,128]{3,2,1,0:T(8,128)(2,1)S(1)}, bf16[2,6,16,128]{3,2,1,0:T(8,128)(2,1)S(1)}, u32[]{:S(2)}, u32[]{:S(2)}) collective-permute-start(bf16[2,6,16,128]{3,2,1,0:T(8,128)(2,1)S(1)} %get-tuple-element.41), channel_id=1, source_target_pairs={{0,1},{1,0},{2,3},{3,2},{4,5},{5,4},{6,7},{7,6},{8,9},{9,8},{10,11... | collective-permute-start | bytes 147464 | tf_op jit(solution)/shard_map/ppermute | solution.py:281
  8.7 5.5 %collective-permute-start.1 = (bf16[6,32,128]{2,1,0:T(8,128)(2,1)S(1)}, bf16[6,32,128]{2,1,0:T(8,128)(2,1)S(1)}, u32[]{:S(2)}, u32[]{:S(2)}) collective-permute-start(bf16[6,32,128]{2,1,0:T(8,128)(2,1)S(1)} %get-tuple-element.22), channel_id=1, source_target_pairs={{0,4},{1,5},{2,6},{3,7},{4,0},{5,1},{6,2},{7,3},{8,12},{9,13},{10,... | collective-permute-start | bytes 147464 | tf_op jit(solution)/shard_map/ppermute | solution.py:281
  10.5 6.1 %collective-permute-start.2 = (bf16[6,32,128]{2,1,0:T(8,128)(2,1)S(1)}, bf16[6,32,128]{2,1,0:T(8,128)(2,1)S(1)}, u32[]{:S(2)}, u32[]{:S(2)}) collective-permute-start(bf16[6,32,128]{2,1,0:T(8,128)(2,1)S(1)} %get-tuple-element.23), channel_id=1, source_target_pairs={{0,8},{1,9},{2,10},{3,11},{4,12},{5,13},{6,14},{7,15},{8,0},{9,1},... | collective-permute-start | bytes 147464 | tf_op jit(solution)/shard_map/ppermute | solution.py:281
  13.1 6.4 %collective-permute-start.3 = (bf16[6,32,128]{2,1,0:T(8,128)(2,1)S(1)}, bf16[6,32,128]{2,1,0:T(8,128)(2,1)S(1)}, u32[]{:S(2)}, u32[]{:S(2)}) collective-permute-start(bf16[6,32,128]{2,1,0:T(8,128)(2,1)S(1)} %get-tuple-element.24), channel_id=1, source_target_pairs={{0,12},{1,13},{2,14},{3,15},{4,8},{5,9},{6,10},{7,11},{8,4},{9,5},... | collective-permute-start | bytes 147464 | tf_op jit(solution)/shard_map/ppermute | solution.py:281
  13.2 9.0 %collective-permute-start.8 = (bf16[2,24,16,128]{3,2,1,0:T(8,128)(2,1)S(1)}, bf16[2,24,16,128]{3,2,1,0:T(8,128)(2,1)S(1)}, u32[]{:S(2)}, u32[]{:S(2)}) collective-permute-start(bf16[2,24,16,128]{3,2,1,0:T(8,128)(2,1)S(1)} %pad_maximum_fusion), channel_id=1, source_target_pairs={{0,4},{1,5},{2,6},{3,7},{4,0},{5,1},{6,2},{7,3},{8,12},{9,13},{10,... | collective-permute-start | bytes 589832 | tf_op jit(solution)/shard_map/ppermute | solution.py:281
  19.6 5.7 %collective-permute-start.4 = (bf16[24,32,128]{2,1,0:T(8,128)(2,1)S(1)}, bf16[24,32,128]{2,1,0:T(8,128)(2,1)S(1)}, u32[]{:S(2)}, u32[]{:S(2)}) collective-permute-start(bf16[24,32,128]{2,1,0:T(8,128)(2,1)S(1)} %get-tuple-element.57.refs_0_), channel_id=1, source_target_pairs={{0,2},{1,3},{2,0},{3,1},{4,6},{5,7},{6,4},{7,5},{8,10},{9,11},{10,... | collective-permute-start | bytes 589832 | tf_op jit(solution)/shard_map/ppermute | solution.py:281
  21.1 7.7 %collective-permute-start.10 = (bf16[24,16,128]{2,1,0:T(8,128)(2,1)S(1)}, bf16[24,16,128]{2,1,0:T(8,128)(2,1)S(1)}, u32[]{:S(2)}, u32[]{:S(2)}) collective-permute-start(bf16[24,16,128]{2,1,0:T(8,128)(2,1)S(1)} %get-tuple-element.47.refs_0_), channel_id=1, source_target_pairs={{0,12},{1,13},{2,14},{3,15},{4,8},{5,9},{6,10},{7,11},{8,4},{9,5},... | collective-permute-start | bytes 294920 | tf_op jit(solution)/shard_map/ppermute | solution.py:281
  22.2 8.2 %collective-permute-start.9 = (bf16[24,16,128]{2,1,0:T(8,128)(2,1)S(1)}, bf16[24,16,128]{2,1,0:T(8,128)(2,1)S(1)}, u32[]{:S(2)}, u32[]{:S(2)}) collective-permute-start(bf16[24,16,128]{2,1,0:T(8,128)(2,1)S(1)} %get-tuple-element.47.refs_0_), channel_id=1, source_target_pairs={{0,8},{1,9},{2,10},{3,11},{4,12},{5,13},{6,14},{7,15},{8,0},{9,1},... | collective-permute-start | bytes 294920 | tf_op jit(solution)/shard_map/ppermute | solution.py:281
  25.3 1.8 %collective-permute-start.5 = (bf16[48,32,128]{2,1,0:T(8,128)(2,1)S(1)}, bf16[48,32,128]{2,1,0:T(8,128)(2,1)S(1)}, u32[]{:S(2)}, u32[]{:S(2)}) collective-permute-start(bf16[48,32,128]{2,1,0:T(8,128)(2,1)S(1)} %constant_dynamic-update-slice_fusion.4), channel_id=1, source_target_pairs={{0,1},{1,0},{2,3},{3,2},{4,5},{5,4},{6,7},{7,6},{8,9},{9,8},{10,11... | collective-permute-start | bytes 1179656 | tf_op jit(solution)/shard_map/ppermute | solution.py:281
  27.1 11.9 %collective-permute-start.11 = (bf16[48,16,128]{2,1,0:T(8,128)(2,1)S(1)}, bf16[48,16,128]{2,1,0:T(8,128)(2,1)S(1)}, u32[]{:S(2)}, u32[]{:S(2)}) collective-permute-start(bf16[48,16,128]{2,1,0:T(8,128)(2,1)S(1)} %pad_maximum_fusion.1), channel_id=1, source_target_pairs={{0,8},{1,9},{2,10},{3,11},{4,12},{5,13},{6,14},{7,15},{8,0},{9,1},... | collective-permute-start | bytes 589832 | tf_op jit(solution)/shard_map/ppermute | solution.py:281
  30.4 8.7 %copy-start = (bf16[1,128,128,128]{3,2,1,0:T(8,128)(2,1)S(1)}, bf16[1,128,128,128]{3,2,1,0:T(8,128)(2,1)}, u32[]{:S(2)}) copy-start(bf16[1,128,128,128]{3,2,1,0:T(8,128)(2,1)} %param.11) | copy-start | bytes 12582916
  30.4 8.7 %copy-start.1 = (f32[128]{0:T(128)S(1)}, f32[128]{0:T(128)}, u32[]{:S(2)}) copy-start(f32[128]{0:T(128)} %param.19) | copy-start | bytes 1540

commit v22 on v21

--- a/solution.py
+++ b/solution.py
@@ -20,8 +20,8 @@
 
 def project_kernel(side, *refs):
     sources, refs = refs[:7], refs[7:]
-    left_out, right_out, refs = refs[0], refs[1], refs[2:]
-    buffers, sems, x_sems = refs[:7], refs[7], refs[8]
+    left_out, right_out, refs = refs[:side], refs[side : 2 * side], refs[2 * side :]
+    buffers, left_all, right_all, sems, x_sems = refs[:7], refs[7], refs[8], refs[9], refs[10]
     x_ref, gain_ref, offset_ref, wl_ref, bl_ref, wr_ref, br_ref = buffers
     seqs, residues, chans = x_ref.shape
     width = wl_ref.shape[0]
@@ -40,14 +40,15 @@
         copy.wait()
     me = lax.axis_index("row")
     place_a, place_b = me // side, lax.rem(me, side)
-    nt = (((1,), (1,)), ((), ()))
-    wl = wl_ref[...]
-    placed = [
-        jnp.concatenate([wl if k == h else jnp.zeros_like(wl) for k in range(pack)], axis=0)
-        for h in range(pack)
-    ]
+    wl, wr = wl_ref[...], wr_ref[...]
+    blank = jnp.zeros_like(wl)
+    weights = []
+    for h in range(pack):
+        left_rows = jnp.concatenate([wl if k == h else blank for k in range(pack)], axis=0)
+        right_rows = jnp.concatenate([wr] + [blank] * (pack - 1), axis=0)
+        weights.append(jnp.concatenate([left_rows.T, right_rows.T], axis=1))
     left_bias = jnp.concatenate([bl_ref[...]] * pack, axis=1)
-    right_bias = jnp.broadcast_to(br_ref[...], (tile, width)).T
+    right_bias = jnp.concatenate([br_ref[...]] * pack, axis=1)
     for s in range(seqs):
         x_copies[s].wait()
         x = x_ref[s].astype(jnp.float32)
@@ -56,24 +57,24 @@
         normed = (center * lax.rsqrt(variance + 1e-05) * gain_ref[...] + offset_ref[...]).astype(
             jnp.bfloat16
         )
-        right = lax.dot_general(wr_ref[...], normed, nt, preferred_element_type=jnp.float32)
         total = left_bias
+        rights = []
         for h in range(pack):
             picked = jnp.concatenate(
                 [normed[a * tile + h * rows : a * tile + (h + 1) * rows] for a in range(side)],
                 axis=0,
             )
-            total = total + lax.dot_general(
-                picked, placed[h], nt, preferred_element_type=jnp.float32
-            )
+            both = jnp.dot(picked, weights[h], preferred_element_type=jnp.float32)
+            total = total + both[:, :LANES]
+            rights.append((both[:, LANES:] + right_bias).astype(jnp.bfloat16))
         left = total.astype(jnp.bfloat16)
         for k in range(side):
-            left_out[place_a ^ k, s] = left[k * rows : (k + 1) * rows]
-            right_out[place_b ^ k, :, s] = (
-                (right[:, k * tile : (k + 1) * tile] + right_bias)
-                .astype(jnp.bfloat16)
-                .reshape(PARTS, width // PARTS, tile)
-            )
+            left_all[place_a ^ k, s] = left[k * rows : (k + 1) * rows]
+            right = jnp.concatenate([r[k * rows : (k + 1) * rows] for r in rights], axis=0).T
+            right_all[place_b ^ k, :, s] = right[:width].reshape(PARTS, width // PARTS, tile)
+    for d in range(side):
+        left_out[d][...] = left_all[d]
+        right_out[d][...] = right_all[d]
 
 
 def project(side, x, gain, offset, wl, bl, wr, br):
@@ -85,20 +86,20 @@
     out = pl.pallas_call(
         functools.partial(project_kernel, side),
         in_specs=[pl.BlockSpec(memory_space=pltpu.HBM)] * len(operands),
-        out_specs=[pl.BlockSpec(memory_space=pltpu.VMEM)] * 2,
-        out_shape=[
-            jax.ShapeDtypeStruct((side, seqs, rows, LANES), jnp.bfloat16),
-            jax.ShapeDtypeStruct((side, PARTS, seqs, width // PARTS, tile), jnp.bfloat16),
-        ],
+        out_specs=[pl.BlockSpec(memory_space=pltpu.VMEM)] * (2 * side),
+        out_shape=[jax.ShapeDtypeStruct((seqs, rows, LANES), jnp.bfloat16)] * side
+        + [jax.ShapeDtypeStruct((PARTS, seqs, width // PARTS, tile), jnp.bfloat16)] * side,
         scratch_shapes=[pltpu.VMEM(o.shape, o.dtype) for o in operands]
         + [
+            pltpu.VMEM((side, seqs, rows, LANES), jnp.bfloat16),
+            pltpu.VMEM((side, PARTS, seqs, width // PARTS, tile), jnp.bfloat16),
             pltpu.SemaphoreType.DMA((len(operands),)),
             pltpu.SemaphoreType.DMA((seqs,)),
         ],
         compiler_params=pltpu.CompilerParams(vmem_limit_bytes=32 * MIB),
         name="project",
     )(*operands)
-    return list(out[0]), list(out[1])
+    return out[:side], out[side:]
 
 
 def arrange_kernel(seq_total, *refs):

time: 48.5 us -> 47.3 us (0.975)
  waiting for transfers between devices: 13.5 us -> 11.2 us
  local copies, waits for them, and re-layouts: 0.53 us -> 1.45 us
  starting transfers between devices: 11.7 us -> 12.3 us
    ppermute x12, waiting for transfers between devices: 13.5 us -> 11.2 us  [swap(): lax.ppermute(x, 'row', [(i, i ^ da * side + db) for i in range(devices)])]
    transpose x1, local copies, waits for them, and re-layouts: 0.11 us -> 1.06 us  [local(): final_matrix.reshape(width, width, -1).transpose(2, 1, 0)]
    ppermute x12, starting transfers between devices: 11.7 us -> 12.3 us  [swap(): lax.ppermute(x, 'row', [(i, i ^ da * side + db) for i in range(devices)])]
  transfers between devices with their start and end apart: 12 -> 12, of which waited for: 7 -> 6; matrix products, arithmetic and copies ran while one was open for 1% -> 3% of each run, Pallas kernels for 18% -> 18%
where the time goes in v22:
time: 47.3 us; the launch traced here: 47.2 us
  Pallas kernels  22 us (47%)
  starting transfers between devices  12.3 us (26%)
  waiting for transfers between devices  11.2 us (24%)
  local copies, waits for them, and re-layouts  1.45 us (3%)
    pallas_call x2, Pallas kernels, update_part(): pl.pallas_call(functools.partial(update_kernel, side, seqs, order, len(ri...  16.6 us
    ppermute x12, starting transfers between devices, swap(): lax.ppermute(x, 'row', [(i, i ^ da * side + db) for i in range(devices)])  12.3 us
    ppermute x12, waiting for transfers between devices, swap(): lax.ppermute(x, 'row', [(i, i ^ da * side + db) for i in range(devices)])  11.2 us
    pallas_call x1, Pallas kernels, project(): pl.pallas_call(functools.partial(project_kernel, side), in_specs=[pl.Bloc...  4.09 us
    pallas_call x1, Pallas kernels, arrange_left(): pl.pallas_call(functools.partial(arrange_kernel, seq_total), in_specs=[pl...  1.33 us
    transpose x1, local copies, waits for them, and re-layouts, local(): final_matrix.reshape(width, width, -1).transpose(2, 1, 0)  1.06 us
  transfers between devices with their start and end apart: 12, of which 6 were waited for; matrix products, arithmetic and copies ran while one was open for 3% of the time, Pallas kernels for 18%

profile of v22, /device:TPU:0, one launch (start us, length us, event | category | flops | bytes accessed | tf_op | source)
XLA Modules:
  0.0 47.2 jit_solution(9792968442330318876)
XLA Ops:
  0.0 4.1 %project.1 = (bf16[6,32,128]{2,1,0:T(8,128)(2,1)S(1)}, bf16[6,32,128]{2,1,0:T(8,128)(2,1)S(1)}, bf16[6,32,128]{2,1,0:T(8,128)(2,1)S(1)}, bf16[6,32,128]{2,1,0:T(...) custom-call(bf16[6,512,256]{2,1,0:T(8,128)(2,1)} %refs_0_.1, ...), custom_call_target="tpu_custom_call" | custom-call | tf_op jit(solution)/shard_map/project/pallas_call | solution.py:86
  4.1 0.5 %collective-permute-start = (bf16[2,6,16,128]{3,2,1,0:T(8,128)(2,1)S(1)}, bf16[2,6,16,128]{3,2,1,0:T(8,128)(2,1)S(1)}, u32[]{:S(2)}, u32[]{:S(2)}) collective-permute-start(bf16[2,6,16,128]{3,2,1,0:T(8,128)(2,1)S(1)} %get-tuple-element.29), channel_id=1, source_target_pairs={{0,1},{1,0},{2,3},{3,2},{4,5},{5,4},{6,7},{7,6},{8,9},{9,8},{10,11... | collective-permute-start | bytes 147464 | tf_op jit(solution)/shard_map/ppermute | solution.py:282
  4.6 2.6 %collective-permute-start.6 = (bf16[2,6,16,128]{3,2,1,0:T(8,128)(2,1)S(1)}, bf16[2,6,16,128]{3,2,1,0:T(8,128)(2,1)S(1)}, u32[]{:S(2)}, u32[]{:S(2)}) collective-permute-start(bf16[2,6,16,128]{3,2,1,0:T(8,128)(2,1)S(1)} %get-tuple-element.36), channel_id=1, source_target_pairs={{0,2},{1,3},{2,0},{3,1},{4,6},{5,7},{6,4},{7,5},{8,10},{9,11},{10,... | collective-permute-start | bytes 147464 | tf_op jit(solution)/shard_map/ppermute | solution.py:282
  7.2 0.1 collective-permute-start.7
  7.3 0.0 collective-permute-done
  7.3 1.8 %collective-permute-start.1 = (bf16[6,32,128]{2,1,0:T(8,128)(2,1)S(1)}, bf16[6,32,128]{2,1,0:T(8,128)(2,1)S(1)}, u32[]{:S(2)}, u32[]{:S(2)}) collective-permute-start(bf16[6,32,128]{2,1,0:T(8,128)(2,1)S(1)} %get-tuple-element.31), channel_id=1, source_target_pairs={{0,4},{1,5},{2,6},{3,7},{4,0},{5,1},{6,2},{7,3},{8,12},{9,13},{10,... | collective-permute-start | bytes 147464 | tf_op jit(solution)/shard_map/ppermute | solution.py:282
  9.1 2.6 %collective-permute-start.2 = (bf16[6,32,128]{2,1,0:T(8,128)(2,1)S(1)}, bf16[6,32,128]{2,1,0:T(8,128)(2,1)S(1)}, u32[]{:S(2)}, u32[]{:S(2)}) collective-permute-start(bf16[6,32,128]{2,1,0:T(8,128)(2,1)S(1)} %get-tuple-element.32), channel_id=1, source_target_pairs={{0,8},{1,9},{2,10},{3,11},{4,12},{5,13},{6,14},{7,15},{8,0},{9,1},... | collective-permute-start | bytes 147464 | tf_op jit(solution)/shard_map/ppermute | solution.py:282
  11.7 0.0 collective-permute-start.3
  11.8 0.0 collective-permute-done.6
  11.8 0.0 collective-permute-done.7
  11.9 0.9 %collective-permute-start.8 = (bf16[2,24,16,128]{3,2,1,0:T(8,128)(2,1)S(1)}, bf16[2,24,16,128]{3,2,1,0:T(8,128)(2,1)S(1)}, u32[]{:S(2)}, u32[]{:S(2)}) collective-permute-start(bf16[2,24,16,128]{3,2,1,0:T(8,128)(2,1)S(1)} %pad_maximum_fusion), channel_id=1, source_target_pairs={{0,4},{1,5},{2,6},{3,7},{4,0},{5,1},{6,2},{7,3},{8,12},{9,13},{10,... | collective-permute-start | bytes 589832 | tf_op jit(solution)/shard_map/ppermute | solution.py:282
  12.8 0.0 collective-permute-done.1
  12.9 2.4 %collective-permute-done.2 = bf16[6,32,128]{2,1,0:T(8,128)(2,1)S(1)} collective-permute-done((bf16[6,32,128]{2,1,0:T(8,128)(2,1)S(1)}, bf16[6,32,128]{2,1,0:T(8,128)(2,1)S(1)}, u32[]{:S(2)}, u32[]{:S(2)}) %collective-permute-start.2) | collective-permute-done | bytes 49184 | tf_op jit(solution)/shard_map/ppermute | solution.py:282
  15.3 2.9 %collective-permute-done.3 = bf16[6,32,128]{2,1,0:T(8,128)(2,1)S(1)} collective-permute-done((bf16[6,32,128]{2,1,0:T(8,128)(2,1)S(1)}, bf16[6,32,128]{2,1,0:T(8,128)(2,1)S(1)}, u32[]{:S(2)}, u32[]{:S(2)}) %collective-permute-start.3) | collective-permute-done | bytes 49184 | tf_op jit(solution)/shard_map/ppermute | solution.py:282
  18.2 1.6 %collective-permute-start.4 = (bf16[24,32,128]{2,1,0:T(8,128)(2,1)S(1)}, bf16[24,32,128]{2,1,0:T(8,128)(2,1)S(1)}, u32[]{:S(2)}, u32[]{:S(2)}) collective-permute-start(bf16[24,32,128]{2,1,0:T(8,128)(2,1)S(1)} %get-tuple-element.62.refs_0_), channel_id=1, source_target_pairs={{0,2},{1,3},{2,0},{3,1},{4,6},{5,7},{6,4},{7,5},{8,10},{9,11},{10,... | collective-permute-start | bytes 589832 | tf_op jit(solution)/shard_map/ppermute | solution.py:282
  19.8 1.1 %collective-permute-start.10 = (bf16[24,16,128]{2,1,0:T(8,128)(2,1)S(1)}, bf16[24,16,128]{2,1,0:T(8,128)(2,1)S(1)}, u32[]{:S(2)}, u32[]{:S(2)}) collective-permute-start(bf16[24,16,128]{2,1,0:T(8,128)(2,1)S(1)} %get-tuple-element.50.refs_0_), channel_id=1, source_target_pairs={{0,12},{1,13},{2,14},{3,15},{4,8},{5,9},{6,10},{7,11},{8,4},{9,5},... | collective-permute-start | bytes 294920 | tf_op jit(solution)/shard_map/ppermute | solution.py:282
  20.8 0.0 collective-permute-start.9
  20.9 0.0 collective-permute-done.8
  20.9 1.1 %copy.14 = bf16[128,32,32]{0,2,1:T(8,128)(2,1)S(1)} copy(bf16[128,32,32]{0,1,2:T(8,128)(2,1)} %bitcast.40) | data formatting | bytes 524288 | tf_op jit(solution)/shard_map/transpose | solution.py:308
  21.9 2.0 %collective-permute-done.4.refs_1_ = bf16[24,32,128]{2,1,0:T(8,128)(2,1)S(1)} collective-permute-done((bf16[24,32,128]{2,1,0:T(8,128)(2,1)S(1)}, bf16[24,32,128]{2,1,0:T(8,128)(2,1)S(1)}, u32[]{:S(2)}, u32[]{:S(2)}) %collective-permute-start.4) | collective-permute-done | bytes 196640 | tf_op jit(solution)/shard_map/ppermute | solution.py:282
  24.0 0.1 collective-permute-start.5
  24.1 0.1 copy.18.refs_3_
  24.2 0.1 copy.17.refs_4_
  24.3 1.4 %collective-permute-done.5.refs_2_ = bf16[48,32,128]{2,1,0:T(8,128)(2,1)S(1)} collective-permute-done((bf16[48,32,128]{2,1,0:T(8,128)(2,1)S(1)}, bf16[48,32,128]{2,1,0:T(8,128)(2,1)S(1)}, u32[]{:S(2)}, u32[]{:S(2)}) %collective-permute-start.5) | collective-permute-done | bytes 393248 | tf_op jit(solution)/shard_map/ppermute | solution.py:282
  25.8 1.0 %collective-permute-start.11 = (bf16[48,16,128]{2,1,0:T(8,128)(2,1)S(1)}, bf16[48,16,128]{2,1,0:T(8,128)(2,1)S(1)}, u32[]{:S(2)}, u32[]{:S(2)}) collective-permute-start(bf16[48,16,128]{2,1,0:T(8,128)(2,1)S(1)} %pad_maximum_fusion.1), channel_id=1, source_target_pairs={{0,8},{1,9},{2,10},{3,11},{4,12},{5,13},{6,14},{7,15},{8,0},{9,1},... | collective-permute-start | bytes 589832 | tf_op jit(solution)/shard_map/ppermute | solution.py:282
  26.8 1.3 %arrange_left.1.left_ref = bf16[32,128,128]{2,1,0:T(8,128)(2,1)S(1)} custom-call(bf16[24,32,128]{2,1,0:T(8,128)(2,1)S(1)} %get-tuple-element.62.refs_0_, bf16[24,32,128]{2,1,0:T(8,128)(2,1)S(1)} %collective-permute-done.4.refs_1_, bf16[48,32,128]{2,1,0:T(8,128)(2,1)S(1)} %collective-permute-done.5.refs_2_), custom_call_target="tpu_custom_call" | custom-call | flops 1048576 | bytes 8388608 | tf_op jit(solution)/shard_map/arrange_left/pallas_call | solution.py:124
  28.1 0.0 collective-permute-done.10.refs_3_
  28.1 0.9 %collective-permute-done.9.refs_2_ = bf16[24,16,128]{2,1,0:T(8,128)(2,1)S(1)} collective-permute-done((bf16[24,16,128]{2,1,0:T(8,128)(2,1)S(1)}, bf16[24,16,128]{2,1,0:T(8,128)(2,1)S(1)}, u32[]{:S(2)}, u32[]{:S(2)}) %collective-permute-start.9) | collective-permute-done | bytes 98336 | tf_op jit(solution)/shard_map/ppermute | solution.py:282
  29.0 0.0 copy-start
  29.0 0.0 copy-start.1
  29.0 7.3 %update_0.1.refs_4_ = f32[32,2,128,256]{3,2,1,0:T(8,128)S(1)} custom-call(bf16[32,128,128]{2,1,0:T(8,128)(2,1)S(1)} %arrange_left.1.left_ref, bf16[24,16,128]{2,1,0:T(8,128)(2,1)S(1)} %get-tuple-element.50.refs_0_, bf16[24,16,128]{2,1,0:T(8,128)(2,1)S(1)} %get-tuple-element.48.refs_1_, bf16[24,16,128]{2,1,0:T(8,128)(2,1)S(1)} %collective-permute-done.9.refs_2_, ...), custom_call_target="tpu_custom_call" | custom-call | flops 3758096384 | bytes 16777216 | tf_op jit(solution)/shard_map/update_0/pallas_call | solution.py:232
  36.3 1.6 %collective-permute-done.11.refs_2_ = bf16[48,16,128]{2,1,0:T(8,128)(2,1)S(1)} collective-permute-done((bf16[48,16,128]{2,1,0:T(8,128)(2,1)S(1)}, bf16[48,16,128]{2,1,0:T(8,128)(2,1)S(1)}, u32[]{:S(2)}, u32[]{:S(2)}) %collective-permute-start.11) | collective-permute-done | bytes 196640 | tf_op jit(solution)/shard_map/ppermute | solution.py:282
  37.9 0.0 copy-done
  37.9 0.0 copy-done.1
  37.9 9.3 %update_1.1 = bf16[4,32,128,128]{3,2,1,0:T(8,128)(2,1)} custom-call(bf16[32,128,128]{2,1,0:T(8,128)(2,1)S(1)} %arrange_left.1.left_ref, bf16[24,16,128]{2,1,0:T(8,128)(2,1)S(1)} %get-tuple-element.41.refs_0_, bf16[24,16,128]{2,1,0:T(8,128)(2,1)S(1)} %get-tuple-element.42.refs_1_, bf16[48,16,128]{2,1,0:T(8,128)(2,1)S(1)} %collective-permute-done.11.refs_2_, ...), custom_call_target="tpu_custom_call" | custom-call | flops 3758096384 | bytes 16777216 | tf_op jit(solution)/shard_map/update_1/pallas_call | solution.py:232
  (15 shorter events, 0.2 us)
Async XLA Ops:
  4.1 3.2 %collective-permute-start = (bf16[2,6,16,128]{3,2,1,0:T(8,128)(2,1)S(1)}, bf16[2,6,16,128]{3,2,1,0:T(8,128)(2,1)S(1)}, u32[]{:S(2)}, u32[]{:S(2)}) collective-permute-start(bf16[2,6,16,128]{3,2,1,0:T(8,128)(2,1)S(1)} %get-tuple-element.29), channel_id=1, source_target_pairs={{0,1},{1,0},{2,3},{3,2},{4,5},{5,4},{6,7},{7,6},{8,9},{9,8},{10,11... | collective-permute-start | bytes 147464 | tf_op jit(solution)/shard_map/ppermute | solution.py:282
  4.6 7.1 %collective-permute-start.6 = (bf16[2,6,16,128]{3,2,1,0:T(8,128)(2,1)S(1)}, bf16[2,6,16,128]{3,2,1,0:T(8,128)(2,1)S(1)}, u32[]{:S(2)}, u32[]{:S(2)}) collective-permute-start(bf16[2,6,16,128]{3,2,1,0:T(8,128)(2,1)S(1)} %get-tuple-element.36), channel_id=1, source_target_pairs={{0,2},{1,3},{2,0},{3,1},{4,6},{5,7},{6,4},{7,5},{8,10},{9,11},{10,... | collective-permute-start | bytes 147464 | tf_op jit(solution)/shard_map/ppermute | solution.py:282
  7.2 4.6 %collective-permute-start.7 = (bf16[2,6,16,128]{3,2,1,0:T(8,128)(2,1)S(1)}, bf16[2,6,16,128]{3,2,1,0:T(8,128)(2,1)S(1)}, u32[]{:S(2)}, u32[]{:S(2)}) collective-permute-start(bf16[2,6,16,128]{3,2,1,0:T(8,128)(2,1)S(1)} %get-tuple-element.37), channel_id=1, source_target_pairs={{0,3},{1,2},{2,1},{3,0},{4,7},{5,6},{6,5},{7,4},{8,11},{9,10},{10,... | collective-permute-start | bytes 147464 | tf_op jit(solution)/shard_map/ppermute | solution.py:282
  7.3 5.5 %collective-permute-start.1 = (bf16[6,32,128]{2,1,0:T(8,128)(2,1)S(1)}, bf16[6,32,128]{2,1,0:T(8,128)(2,1)S(1)}, u32[]{:S(2)}, u32[]{:S(2)}) collective-permute-start(bf16[6,32,128]{2,1,0:T(8,128)(2,1)S(1)} %get-tuple-element.31), channel_id=1, source_target_pairs={{0,4},{1,5},{2,6},{3,7},{4,0},{5,1},{6,2},{7,3},{8,12},{9,13},{10,... | collective-permute-start | bytes 147464 | tf_op jit(solution)/shard_map/ppermute | solution.py:282
  9.1 6.1 %collective-permute-start.2 = (bf16[6,32,128]{2,1,0:T(8,128)(2,1)S(1)}, bf16[6,32,128]{2,1,0:T(8,128)(2,1)S(1)}, u32[]{:S(2)}, u32[]{:S(2)}) collective-permute-start(bf16[6,32,128]{2,1,0:T(8,128)(2,1)S(1)} %get-tuple-element.32), channel_id=1, source_target_pairs={{0,8},{1,9},{2,10},{3,11},{4,12},{5,13},{6,14},{7,15},{8,0},{9,1},... | collective-permute-start | bytes 147464 | tf_op jit(solution)/shard_map/ppermute | solution.py:282
  11.7 6.4 %collective-permute-start.3 = (bf16[6,32,128]{2,1,0:T(8,128)(2,1)S(1)}, bf16[6,32,128]{2,1,0:T(8,128)(2,1)S(1)}, u32[]{:S(2)}, u32[]{:S(2)}) collective-permute-start(bf16[6,32,128]{2,1,0:T(8,128)(2,1)S(1)} %get-tuple-element.33), channel_id=1, source_target_pairs={{0,12},{1,13},{2,14},{3,15},{4,8},{5,9},{6,10},{7,11},{8,4},{9,5},... | collective-permute-start | bytes 147464 | tf_op jit(solution)/shard_map/ppermute | solution.py:282
  11.9 9.0 %collective-permute-start.8 = (bf16[2,24,16,128]{3,2,1,0:T(8,128)(2,1)S(1)}, bf16[2,24,16,128]{3,2,1,0:T(8,128)(2,1)S(1)}, u32[]{:S(2)}, u32[]{:S(2)}) collective-permute-start(bf16[2,24,16,128]{3,2,1,0:T(8,128)(2,1)S(1)} %pad_maximum_fusion), channel_id=1, source_target_pairs={{0,4},{1,5},{2,6},{3,7},{4,0},{5,1},{6,2},{7,3},{8,12},{9,13},{10,... | collective-permute-start | bytes 589832 | tf_op jit(solution)/shard_map/ppermute | solution.py:282
  18.2 5.7 %collective-permute-start.4 = (bf16[24,32,128]{2,1,0:T(8,128)(2,1)S(1)}, bf16[24,32,128]{2,1,0:T(8,128)(2,1)S(1)}, u32[]{:S(2)}, u32[]{:S(2)}) collective-permute-start(bf16[24,32,128]{2,1,0:T(8,128)(2,1)S(1)} %get-tuple-element.62.refs_0_), channel_id=1, source_target_pairs={{0,2},{1,3},{2,0},{3,1},{4,6},{5,7},{6,4},{7,5},{8,10},{9,11},{10,... | collective-permute-start | bytes 589832 | tf_op jit(solution)/shard_map/ppermute | solution.py:282
  19.8 8.3 %collective-permute-start.10 = (bf16[24,16,128]{2,1,0:T(8,128)(2,1)S(1)}, bf16[24,16,128]{2,1,0:T(8,128)(2,1)S(1)}, u32[]{:S(2)}, u32[]{:S(2)}) collective-permute-start(bf16[24,16,128]{2,1,0:T(8,128)(2,1)S(1)} %get-tuple-element.50.refs_0_), channel_id=1, source_target_pairs={{0,12},{1,13},{2,14},{3,15},{4,8},{5,9},{6,10},{7,11},{8,4},{9,5},... | collective-permute-start | bytes 294920 | tf_op jit(solution)/shard_map/ppermute | solution.py:282
  20.8 8.2 %collective-permute-start.9 = (bf16[24,16,128]{2,1,0:T(8,128)(2,1)S(1)}, bf16[24,16,128]{2,1,0:T(8,128)(2,1)S(1)}, u32[]{:S(2)}, u32[]{:S(2)}) collective-permute-start(bf16[24,16,128]{2,1,0:T(8,128)(2,1)S(1)} %get-tuple-element.50.refs_0_), channel_id=1, source_target_pairs={{0,8},{1,9},{2,10},{3,11},{4,12},{5,13},{6,14},{7,15},{8,0},{9,1},... | collective-permute-start | bytes 294920 | tf_op jit(solution)/shard_map/ppermute | solution.py:282
  24.0 1.8 %collective-permute-start.5 = (bf16[48,32,128]{2,1,0:T(8,128)(2,1)S(1)}, bf16[48,32,128]{2,1,0:T(8,128)(2,1)S(1)}, u32[]{:S(2)}, u32[]{:S(2)}) collective-permute-start(bf16[48,32,128]{2,1,0:T(8,128)(2,1)S(1)} %constant_dynamic-update-slice_fusion.4), channel_id=1, source_target_pairs={{0,1},{1,0},{2,3},{3,2},{4,5},{5,4},{6,7},{7,6},{8,9},{9,8},{10,11... | collective-permute-start | bytes 1179656 | tf_op jit(solution)/shard_map/ppermute | solution.py:282
  25.8 12.1 %collective-permute-start.11 = (bf16[48,16,128]{2,1,0:T(8,128)(2,1)S(1)}, bf16[48,16,128]{2,1,0:T(8,128)(2,1)S(1)}, u32[]{:S(2)}, u32[]{:S(2)}) collective-permute-start(bf16[48,16,128]{2,1,0:T(8,128)(2,1)S(1)} %pad_maximum_fusion.1), channel_id=1, source_target_pairs={{0,8},{1,9},{2,10},{3,11},{4,12},{5,13},{6,14},{7,15},{8,0},{9,1},... | collective-permute-start | bytes 589832 | tf_op jit(solution)/shard_map/ppermute | solution.py:282
  29.0 8.9 %copy-start = (bf16[1,128,128,128]{3,2,1,0:T(8,128)(2,1)S(1)}, bf16[1,128,128,128]{3,2,1,0:T(8,128)(2,1)}, u32[]{:S(2)}) copy-start(bf16[1,128,128,128]{3,2,1,0:T(8,128)(2,1)} %param.11) | copy-start | bytes 12582916
  29.0 8.9 %copy-start.1 = (f32[128]{0:T(128)S(1)}, f32[128]{0:T(128)}, u32[]{:S(2)}) copy-start(f32[128]{0:T(128)} %param.19) | copy-start | bytes 1540

commit v23 on v22

--- a/solution.py
+++ b/solution.py
@@ -143,8 +143,7 @@
     out_ref, right_wide, right_flat, outer = refs
     rows, lanes, depth = left_ref.shape
     _, some, tile = right_refs[0].shape
-    halves = outer.shape[0] // group
-    pack = 2 * halves
+    pack = outer.shape[2] // tile
     width = lanes // pack
     seq_total = side * side * seqs
     at = pl.program_id(0) * group
@@ -181,25 +180,19 @@
             for k in range(2):
                 e = 2 * n + k
                 for h in range(pack):
-                    outer[
-                        q * halves + h // 2,
-                        e * width : (e + 1) * width,
-                        (h % 2) * tile : (h % 2 + 1) * tile,
-                    ] = both[h * width : (h + 1) * width, k * tile : (k + 1) * tile]
+                    outer[q, e * width : (e + 1) * width, h * tile : (h + 1) * tile] = both[h * width : (h + 1) * width, k * tile : (k + 1) * tile]
 
     def project_back(q):
-        for g in range(halves):
-            update = jnp.dot(wt_ref[...], outer[q * halves + g], preferred_element_type=jnp.float32)
-            if not first:
-                update = update + before_ref[at + q, g]
-            if not last:
-                out_ref[at + q, g] = update
-                continue
-            for k in range(2):
-                h = 2 * g + k
-                share = update[:, k * tile : (k + 1) * tile].T * (1.0 / seq_total) + bias_ref[...]
-                old = pair_ref[h, at + q].astype(jnp.float32)
-                out_ref[h, q] = (old + share).astype(jnp.bfloat16)
+        update = jnp.dot(wt_ref[...], outer[q], preferred_element_type=jnp.float32)
+        if not first:
+            update = update + before_ref[at + q]
+        if not last:
+            out_ref[at + q] = update
+            return
+        for h in range(pack):
+            share = update[:, h * tile : (h + 1) * tile].T * (1.0 / seq_total) + bias_ref[...]
+            old = pair_ref[h, at + q].astype(jnp.float32)
+            out_ref[h, q] = (old + share).astype(jnp.bfloat16)
 
     for start in range(0, group + RUN, RUN):
         for q in range(start, start + RUN):
@@ -216,7 +209,6 @@
     chans = wt.shape[0]
     pack = tile // rows
     width = lanes // pack
-    halves = pack // 2
     group = 16
     first, last = part == 0, part == PARTS - 1
     in_vmem = pl.BlockSpec(memory_space=pltpu.VMEM)
@@ -228,7 +220,7 @@
         out_shape = jax.ShapeDtypeStruct((pack, rows, tile, chans), jnp.bfloat16)
         out_spec = pl.BlockSpec((pack, group, tile, chans), lambda g: (0, g, 0, 0))
     else:
-        out_shape, out_spec = pltpu.VMEM((rows, halves, chans, 2 * tile), jnp.float32), in_vmem
+        out_shape, out_spec = pltpu.VMEM((rows, chans, pack * tile), jnp.float32), in_vmem
     return pl.pallas_call(
         functools.partial(update_kernel, side, seqs, order, len(right), group, first, last),
         grid=(rows // group,),
@@ -238,7 +230,7 @@
         scratch_shapes=[
             pltpu.VMEM((depth * some, tile), jnp.float32),
             pltpu.VMEM((depth, some * tile), jnp.bfloat16),
-            pltpu.VMEM((group * halves, some * width, 2 * tile), jnp.bfloat16),
+            pltpu.VMEM((group, some * width, pack * tile), jnp.bfloat16),
         ],
         compiler_params=pltpu.CompilerParams(vmem_limit_bytes=24 * MIB),
         cost_estimate=pl.CostEstimate(

time: 47.3 us -> 47.4 us (level)
  no operation moved by 1% of the time
where the time goes in v23:
time: 47.4 us; the launch traced here: 47.2 us
  Pallas kernels  22 us (46%)
  starting transfers between devices  12.3 us (26%)
  waiting for transfers between devices  11.2 us (24%)
  local copies, waits for them, and re-layouts  1.45 us (3%)
    pallas_call x2, Pallas kernels, update_part(): pl.pallas_call(functools.partial(update_kernel, side, seqs, order, len(ri...  16.6 us
    ppermute x12, starting transfers between devices, swap(): lax.ppermute(x, 'row', [(i, i ^ da * side + db) for i in range(devices)])  12.3 us
    ppermute x12, waiting for transfers between devices, swap(): lax.ppermute(x, 'row', [(i, i ^ da * side + db) for i in range(devices)])  11.2 us
    pallas_call x1, Pallas kernels, project(): pl.pallas_call(functools.partial(project_kernel, side), in_specs=[pl.Bloc...  4.09 us
    pallas_call x1, Pallas kernels, arrange_left(): pl.pallas_call(functools.partial(arrange_kernel, seq_total), in_specs=[pl...  1.33 us
    transpose x1, local copies, waits for them, and re-layouts, local(): final_matrix.reshape(width, width, -1).transpose(2, 1, 0)  1.06 us
  transfers between devices with their start and end apart: 12, of which 6 were waited for; matrix products, arithmetic and copies ran while one was open for 3% of the time, Pallas kernels for 18%

profile of v23, /device:TPU:0, one launch (start us, length us, event | category | flops | bytes accessed | tf_op | source)
XLA Modules:
  0.0 47.2 jit_solution(7272991357067006287)
XLA Ops:
  0.0 4.1 %project.1 = (bf16[6,32,128]{2,1,0:T(8,128)(2,1)S(1)}, bf16[6,32,128]{2,1,0:T(8,128)(2,1)S(1)}, bf16[6,32,128]{2,1,0:T(8,128)(2,1)S(1)}, bf16[6,32,128]{2,1,0:T(...) custom-call(bf16[6,512,256]{2,1,0:T(8,128)(2,1)} %refs_0_.1, ...), custom_call_target="tpu_custom_call" | custom-call | tf_op jit(solution)/shard_map/project/pallas_call | solution.py:86
  4.1 0.5 %collective-permute-start = (bf16[2,6,16,128]{3,2,1,0:T(8,128)(2,1)S(1)}, bf16[2,6,16,128]{3,2,1,0:T(8,128)(2,1)S(1)}, u32[]{:S(2)}, u32[]{:S(2)}) collective-permute-start(bf16[2,6,16,128]{3,2,1,0:T(8,128)(2,1)S(1)} %get-tuple-element.29), channel_id=1, source_target_pairs={{0,1},{1,0},{2,3},{3,2},{4,5},{5,4},{6,7},{7,6},{8,9},{9,8},{10,11... | collective-permute-start | bytes 147464 | tf_op jit(solution)/shard_map/ppermute | solution.py:274
  4.6 2.6 %collective-permute-start.6 = (bf16[2,6,16,128]{3,2,1,0:T(8,128)(2,1)S(1)}, bf16[2,6,16,128]{3,2,1,0:T(8,128)(2,1)S(1)}, u32[]{:S(2)}, u32[]{:S(2)}) collective-permute-start(bf16[2,6,16,128]{3,2,1,0:T(8,128)(2,1)S(1)} %get-tuple-element.36), channel_id=1, source_target_pairs={{0,2},{1,3},{2,0},{3,1},{4,6},{5,7},{6,4},{7,5},{8,10},{9,11},{10,... | collective-permute-start | bytes 147464 | tf_op jit(solution)/shard_map/ppermute | solution.py:274
  7.2 0.1 collective-permute-start.7
  7.3 0.0 collective-permute-done
  7.3 1.8 %collective-permute-start.1 = (bf16[6,32,128]{2,1,0:T(8,128)(2,1)S(1)}, bf16[6,32,128]{2,1,0:T(8,128)(2,1)S(1)}, u32[]{:S(2)}, u32[]{:S(2)}) collective-permute-start(bf16[6,32,128]{2,1,0:T(8,128)(2,1)S(1)} %get-tuple-element.31), channel_id=1, source_target_pairs={{0,4},{1,5},{2,6},{3,7},{4,0},{5,1},{6,2},{7,3},{8,12},{9,13},{10,... | collective-permute-start | bytes 147464 | tf_op jit(solution)/shard_map/ppermute | solution.py:274
  9.1 2.6 %collective-permute-start.2 = (bf16[6,32,128]{2,1,0:T(8,128)(2,1)S(1)}, bf16[6,32,128]{2,1,0:T(8,128)(2,1)S(1)}, u32[]{:S(2)}, u32[]{:S(2)}) collective-permute-start(bf16[6,32,128]{2,1,0:T(8,128)(2,1)S(1)} %get-tuple-element.32), channel_id=1, source_target_pairs={{0,8},{1,9},{2,10},{3,11},{4,12},{5,13},{6,14},{7,15},{8,0},{9,1},... | collective-permute-start | bytes 147464 | tf_op jit(solution)/shard_map/ppermute | solution.py:274
  11.7 0.0 collective-permute-start.3
  11.8 0.0 collective-permute-done.6
  11.8 0.0 collective-permute-done.7
  11.9 0.9 %collective-permute-start.8 = (bf16[2,24,16,128]{3,2,1,0:T(8,128)(2,1)S(1)}, bf16[2,24,16,128]{3,2,1,0:T(8,128)(2,1)S(1)}, u32[]{:S(2)}, u32[]{:S(2)}) collective-permute-start(bf16[2,24,16,128]{3,2,1,0:T(8,128)(2,1)S(1)} %pad_maximum_fusion), channel_id=1, source_target_pairs={{0,4},{1,5},{2,6},{3,7},{4,0},{5,1},{6,2},{7,3},{8,12},{9,13},{10,... | collective-permute-start | bytes 589832 | tf_op jit(solution)/shard_map/ppermute | solution.py:274
  12.8 0.0 collective-permute-done.1
  12.9 2.4 %collective-permute-done.2 = bf16[6,32,128]{2,1,0:T(8,128)(2,1)S(1)} collective-permute-done((bf16[6,32,128]{2,1,0:T(8,128)(2,1)S(1)}, bf16[6,32,128]{2,1,0:T(8,128)(2,1)S(1)}, u32[]{:S(2)}, u32[]{:S(2)}) %collective-permute-start.2) | collective-permute-done | bytes 49184 | tf_op jit(solution)/shard_map/ppermute | solution.py:274
  15.3 2.9 %collective-permute-done.3 = bf16[6,32,128]{2,1,0:T(8,128)(2,1)S(1)} collective-permute-done((bf16[6,32,128]{2,1,0:T(8,128)(2,1)S(1)}, bf16[6,32,128]{2,1,0:T(8,128)(2,1)S(1)}, u32[]{:S(2)}, u32[]{:S(2)}) %collective-permute-start.3) | collective-permute-done | bytes 49184 | tf_op jit(solution)/shard_map/ppermute | solution.py:274
  18.2 1.6 %collective-permute-start.4 = (bf16[24,32,128]{2,1,0:T(8,128)(2,1)S(1)}, bf16[24,32,128]{2,1,0:T(8,128)(2,1)S(1)}, u32[]{:S(2)}, u32[]{:S(2)}) collective-permute-start(bf16[24,32,128]{2,1,0:T(8,128)(2,1)S(1)} %get-tuple-element.62.refs_0_), channel_id=1, source_target_pairs={{0,2},{1,3},{2,0},{3,1},{4,6},{5,7},{6,4},{7,5},{8,10},{9,11},{10,... | collective-permute-start | bytes 589832 | tf_op jit(solution)/shard_map/ppermute | solution.py:274
  19.8 1.1 %collective-permute-start.10 = (bf16[24,16,128]{2,1,0:T(8,128)(2,1)S(1)}, bf16[24,16,128]{2,1,0:T(8,128)(2,1)S(1)}, u32[]{:S(2)}, u32[]{:S(2)}) collective-permute-start(bf16[24,16,128]{2,1,0:T(8,128)(2,1)S(1)} %get-tuple-element.50.refs_0_), channel_id=1, source_target_pairs={{0,12},{1,13},{2,14},{3,15},{4,8},{5,9},{6,10},{7,11},{8,4},{9,5},... | collective-permute-start | bytes 294920 | tf_op jit(solution)/shard_map/ppermute | solution.py:274
  20.8 0.0 collective-permute-start.9
  20.9 0.0 collective-permute-done.8
  20.9 1.1 %copy.14 = bf16[128,32,32]{0,2,1:T(8,128)(2,1)S(1)} copy(bf16[128,32,32]{0,1,2:T(8,128)(2,1)} %bitcast.40) | data formatting | bytes 524288 | tf_op jit(solution)/shard_map/transpose | solution.py:300
  21.9 2.0 %collective-permute-done.4.refs_1_ = bf16[24,32,128]{2,1,0:T(8,128)(2,1)S(1)} collective-permute-done((bf16[24,32,128]{2,1,0:T(8,128)(2,1)S(1)}, bf16[24,32,128]{2,1,0:T(8,128)(2,1)S(1)}, u32[]{:S(2)}, u32[]{:S(2)}) %collective-permute-start.4) | collective-permute-done | bytes 196640 | tf_op jit(solution)/shard_map/ppermute | solution.py:274
  24.0 0.1 collective-permute-start.5
  24.1 0.1 copy.18.refs_3_
  24.2 0.1 copy.17.refs_4_
  24.3 1.4 %collective-permute-done.5.refs_2_ = bf16[48,32,128]{2,1,0:T(8,128)(2,1)S(1)} collective-permute-done((bf16[48,32,128]{2,1,0:T(8,128)(2,1)S(1)}, bf16[48,32,128]{2,1,0:T(8,128)(2,1)S(1)}, u32[]{:S(2)}, u32[]{:S(2)}) %collective-permute-start.5) | collective-permute-done | bytes 393248 | tf_op jit(solution)/shard_map/ppermute | solution.py:274
  25.8 1.0 %collective-permute-start.11 = (bf16[48,16,128]{2,1,0:T(8,128)(2,1)S(1)}, bf16[48,16,128]{2,1,0:T(8,128)(2,1)S(1)}, u32[]{:S(2)}, u32[]{:S(2)}) collective-permute-start(bf16[48,16,128]{2,1,0:T(8,128)(2,1)S(1)} %pad_maximum_fusion.1), channel_id=1, source_target_pairs={{0,8},{1,9},{2,10},{3,11},{4,12},{5,13},{6,14},{7,15},{8,0},{9,1},... | collective-permute-start | bytes 589832 | tf_op jit(solution)/shard_map/ppermute | solution.py:274
  26.8 1.3 %arrange_left.1.left_ref = bf16[32,128,128]{2,1,0:T(8,128)(2,1)S(1)} custom-call(bf16[24,32,128]{2,1,0:T(8,128)(2,1)S(1)} %get-tuple-element.62.refs_0_, bf16[24,32,128]{2,1,0:T(8,128)(2,1)S(1)} %collective-permute-done.4.refs_1_, bf16[48,32,128]{2,1,0:T(8,128)(2,1)S(1)} %collective-permute-done.5.refs_2_), custom_call_target="tpu_custom_call" | custom-call | flops 1048576 | bytes 8388608 | tf_op jit(solution)/shard_map/arrange_left/pallas_call | solution.py:124
  28.1 0.0 collective-permute-done.10.refs_3_
  28.1 0.9 %collective-permute-done.9.refs_2_ = bf16[24,16,128]{2,1,0:T(8,128)(2,1)S(1)} collective-permute-done((bf16[24,16,128]{2,1,0:T(8,128)(2,1)S(1)}, bf16[24,16,128]{2,1,0:T(8,128)(2,1)S(1)}, u32[]{:S(2)}, u32[]{:S(2)}) %collective-permute-start.9) | collective-permute-done | bytes 98336 | tf_op jit(solution)/shard_map/ppermute | solution.py:274
  29.0 0.0 copy-start
  29.0 0.0 copy-start.1
  29.0 7.3 %update_0.1.refs_4_ = f32[32,128,512]{2,1,0:T(8,128)S(1)} custom-call(bf16[32,128,128]{2,1,0:T(8,128)(2,1)S(1)} %arrange_left.1.left_ref, bf16[24,16,128]{2,1,0:T(8,128)(2,1)S(1)} %get-tuple-element.50.refs_0_, bf16[24,16,128]{2,1,0:T(8,128)(2,1)S(1)} %get-tuple-element.48.refs_1_, bf16[24,16,128]{2,1,0:T(8,128)(2,1)S(1)} %collective-permute-done.9.refs_2_, ...), custom_call_target="tpu_custom_call" | custom-call | flops 3758096384 | bytes 16777216 | tf_op jit(solution)/shard_map/update_0/pallas_call | solution.py:224
  36.3 1.6 %collective-permute-done.11.refs_2_ = bf16[48,16,128]{2,1,0:T(8,128)(2,1)S(1)} collective-permute-done((bf16[48,16,128]{2,1,0:T(8,128)(2,1)S(1)}, bf16[48,16,128]{2,1,0:T(8,128)(2,1)S(1)}, u32[]{:S(2)}, u32[]{:S(2)}) %collective-permute-start.11) | collective-permute-done | bytes 196640 | tf_op jit(solution)/shard_map/ppermute | solution.py:274
  37.9 0.0 copy-done
  37.9 0.0 copy-done.1
  37.9 9.3 %update_1.1 = bf16[4,32,128,128]{3,2,1,0:T(8,128)(2,1)} custom-call(bf16[32,128,128]{2,1,0:T(8,128)(2,1)S(1)} %arrange_left.1.left_ref, bf16[24,16,128]{2,1,0:T(8,128)(2,1)S(1)} %get-tuple-element.41.refs_0_, bf16[24,16,128]{2,1,0:T(8,128)(2,1)S(1)} %get-tuple-element.42.refs_1_, bf16[48,16,128]{2,1,0:T(8,128)(2,1)S(1)} %collective-permute-done.11.refs_2_, ...), custom_call_target="tpu_custom_call" | custom-call | flops 3758096384 | bytes 16777216 | tf_op jit(solution)/shard_map/update_1/pallas_call | solution.py:224
  (15 shorter events, 0.2 us)
Async XLA Ops:
  4.1 3.2 %collective-permute-start = (bf16[2,6,16,128]{3,2,1,0:T(8,128)(2,1)S(1)}, bf16[2,6,16,128]{3,2,1,0:T(8,128)(2,1)S(1)}, u32[]{:S(2)}, u32[]{:S(2)}) collective-permute-start(bf16[2,6,16,128]{3,2,1,0:T(8,128)(2,1)S(1)} %get-tuple-element.29), channel_id=1, source_target_pairs={{0,1},{1,0},{2,3},{3,2},{4,5},{5,4},{6,7},{7,6},{8,9},{9,8},{10,11... | collective-permute-start | bytes 147464 | tf_op jit(solution)/shard_map/ppermute | solution.py:274
  4.6 7.1 %collective-permute-start.6 = (bf16[2,6,16,128]{3,2,1,0:T(8,128)(2,1)S(1)}, bf16[2,6,16,128]{3,2,1,0:T(8,128)(2,1)S(1)}, u32[]{:S(2)}, u32[]{:S(2)}) collective-permute-start(bf16[2,6,16,128]{3,2,1,0:T(8,128)(2,1)S(1)} %get-tuple-element.36), channel_id=1, source_target_pairs={{0,2},{1,3},{2,0},{3,1},{4,6},{5,7},{6,4},{7,5},{8,10},{9,11},{10,... | collective-permute-start | bytes 147464 | tf_op jit(solution)/shard_map/ppermute | solution.py:274
  7.2 4.6 %collective-permute-start.7 = (bf16[2,6,16,128]{3,2,1,0:T(8,128)(2,1)S(1)}, bf16[2,6,16,128]{3,2,1,0:T(8,128)(2,1)S(1)}, u32[]{:S(2)}, u32[]{:S(2)}) collective-permute-start(bf16[2,6,16,128]{3,2,1,0:T(8,128)(2,1)S(1)} %get-tuple-element.37), channel_id=1, source_target_pairs={{0,3},{1,2},{2,1},{3,0},{4,7},{5,6},{6,5},{7,4},{8,11},{9,10},{10,... | collective-permute-start | bytes 147464 | tf_op jit(solution)/shard_map/ppermute | solution.py:274
  7.3 5.5 %collective-permute-start.1 = (bf16[6,32,128]{2,1,0:T(8,128)(2,1)S(1)}, bf16[6,32,128]{2,1,0:T(8,128)(2,1)S(1)}, u32[]{:S(2)}, u32[]{:S(2)}) collective-permute-start(bf16[6,32,128]{2,1,0:T(8,128)(2,1)S(1)} %get-tuple-element.31), channel_id=1, source_target_pairs={{0,4},{1,5},{2,6},{3,7},{4,0},{5,1},{6,2},{7,3},{8,12},{9,13},{10,... | collective-permute-start | bytes 147464 | tf_op jit(solution)/shard_map/ppermute | solution.py:274
  9.1 6.1 %collective-permute-start.2 = (bf16[6,32,128]{2,1,0:T(8,128)(2,1)S(1)}, bf16[6,32,128]{2,1,0:T(8,128)(2,1)S(1)}, u32[]{:S(2)}, u32[]{:S(2)}) collective-permute-start(bf16[6,32,128]{2,1,0:T(8,128)(2,1)S(1)} %get-tuple-element.32), channel_id=1, source_target_pairs={{0,8},{1,9},{2,10},{3,11},{4,12},{5,13},{6,14},{7,15},{8,0},{9,1},... | collective-permute-start | bytes 147464 | tf_op jit(solution)/shard_map/ppermute | solution.py:274
  11.7 6.4 %collective-permute-start.3 = (bf16[6,32,128]{2,1,0:T(8,128)(2,1)S(1)}, bf16[6,32,128]{2,1,0:T(8,128)(2,1)S(1)}, u32[]{:S(2)}, u32[]{:S(2)}) collective-permute-start(bf16[6,32,128]{2,1,0:T(8,128)(2,1)S(1)} %get-tuple-element.33), channel_id=1, source_target_pairs={{0,12},{1,13},{2,14},{3,15},{4,8},{5,9},{6,10},{7,11},{8,4},{9,5},... | collective-permute-start | bytes 147464 | tf_op jit(solution)/shard_map/ppermute | solution.py:274
  11.9 9.0 %collective-permute-start.8 = (bf16[2,24,16,128]{3,2,1,0:T(8,128)(2,1)S(1)}, bf16[2,24,16,128]{3,2,1,0:T(8,128)(2,1)S(1)}, u32[]{:S(2)}, u32[]{:S(2)}) collective-permute-start(bf16[2,24,16,128]{3,2,1,0:T(8,128)(2,1)S(1)} %pad_maximum_fusion), channel_id=1, source_target_pairs={{0,4},{1,5},{2,6},{3,7},{4,0},{5,1},{6,2},{7,3},{8,12},{9,13},{10,... | collective-permute-start | bytes 589832 | tf_op jit(solution)/shard_map/ppermute | solution.py:274
  18.2 5.7 %collective-permute-start.4 = (bf16[24,32,128]{2,1,0:T(8,128)(2,1)S(1)}, bf16[24,32,128]{2,1,0:T(8,128)(2,1)S(1)}, u32[]{:S(2)}, u32[]{:S(2)}) collective-permute-start(bf16[24,32,128]{2,1,0:T(8,128)(2,1)S(1)} %get-tuple-element.62.refs_0_), channel_id=1, source_target_pairs={{0,2},{1,3},{2,0},{3,1},{4,6},{5,7},{6,4},{7,5},{8,10},{9,11},{10,... | collective-permute-start | bytes 589832 | tf_op jit(solution)/shard_map/ppermute | solution.py:274
  19.8 8.3 %collective-permute-start.10 = (bf16[24,16,128]{2,1,0:T(8,128)(2,1)S(1)}, bf16[24,16,128]{2,1,0:T(8,128)(2,1)S(1)}, u32[]{:S(2)}, u32[]{:S(2)}) collective-permute-start(bf16[24,16,128]{2,1,0:T(8,128)(2,1)S(1)} %get-tuple-element.50.refs_0_), channel_id=1, source_target_pairs={{0,12},{1,13},{2,14},{3,15},{4,8},{5,9},{6,10},{7,11},{8,4},{9,5},... | collective-permute-start | bytes 294920 | tf_op jit(solution)/shard_map/ppermute | solution.py:274
  20.8 8.2 %collective-permute-start.9 = (bf16[24,16,128]{2,1,0:T(8,128)(2,1)S(1)}, bf16[24,16,128]{2,1,0:T(8,128)(2,1)S(1)}, u32[]{:S(2)}, u32[]{:S(2)}) collective-permute-start(bf16[24,16,128]{2,1,0:T(8,128)(2,1)S(1)} %get-tuple-element.50.refs_0_), channel_id=1, source_target_pairs={{0,8},{1,9},{2,10},{3,11},{4,12},{5,13},{6,14},{7,15},{8,0},{9,1},... | collective-permute-start | bytes 294920 | tf_op jit(solution)/shard_map/ppermute | solution.py:274
  24.0 1.8 %collective-permute-start.5 = (bf16[48,32,128]{2,1,0:T(8,128)(2,1)S(1)}, bf16[48,32,128]{2,1,0:T(8,128)(2,1)S(1)}, u32[]{:S(2)}, u32[]{:S(2)}) collective-permute-start(bf16[48,32,128]{2,1,0:T(8,128)(2,1)S(1)} %constant_dynamic-update-slice_fusion.4), channel_id=1, source_target_pairs={{0,1},{1,0},{2,3},{3,2},{4,5},{5,4},{6,7},{7,6},{8,9},{9,8},{10,11... | collective-permute-start | bytes 1179656 | tf_op jit(solution)/shard_map/ppermute | solution.py:274
  25.8 12.1 %collective-permute-start.11 = (bf16[48,16,128]{2,1,0:T(8,128)(2,1)S(1)}, bf16[48,16,128]{2,1,0:T(8,128)(2,1)S(1)}, u32[]{:S(2)}, u32[]{:S(2)}) collective-permute-start(bf16[48,16,128]{2,1,0:T(8,128)(2,1)S(1)} %pad_maximum_fusion.1), channel_id=1, source_target_pairs={{0,8},{1,9},{2,10},{3,11},{4,12},{5,13},{6,14},{7,15},{8,0},{9,1},... | collective-permute-start | bytes 589832 | tf_op jit(solution)/shard_map/ppermute | solution.py:274
  29.0 8.9 %copy-start = (bf16[1,128,128,128]{3,2,1,0:T(8,128)(2,1)S(1)}, bf16[1,128,128,128]{3,2,1,0:T(8,128)(2,1)}, u32[]{:S(2)}) copy-start(bf16[1,128,128,128]{3,2,1,0:T(8,128)(2,1)} %param.11) | copy-start | bytes 12582916
  29.0 8.9 %copy-start.1 = (f32[128]{0:T(128)S(1)}, f32[128]{0:T(128)}, u32[]{:S(2)}) copy-start(f32[128]{0:T(128)} %param.19) | copy-start | bytes 1540

commit v24 on v22

--- a/solution.py
+++ b/solution.py
@@ -140,7 +140,13 @@
         before_ref, refs = refs[0], refs[1:]
     if last:
         bias_ref, pair_ref, refs = refs[0], refs[1], refs[2:]
-    out_ref, right_wide, right_flat, outer = refs
+    out_ref, right_wide, right_flat, outer, *refs = refs
+    if last:
+        ready, sems = refs
+
+        def copy_out(row):
+            return pltpu.make_async_copy(ready.at[:, row], out_ref.at[:, row], sems.at[row])
+
     rows, lanes, depth = left_ref.shape
     _, some, tile = right_refs[0].shape
     halves = outer.shape[0] // group
@@ -199,7 +205,9 @@
                 h = 2 * g + k
                 share = update[:, k * tile : (k + 1) * tile].T * (1.0 / seq_total) + bias_ref[...]
                 old = pair_ref[h, at + q].astype(jnp.float32)
-                out_ref[h, q] = (old + share).astype(jnp.bfloat16)
+                ready[h, at + q] = (old + share).astype(jnp.bfloat16)
+        if last:
+            copy_out(at + q).start()
 
     for start in range(0, group + RUN, RUN):
         for q in range(start, start + RUN):
@@ -209,6 +217,13 @@
             if q >= 0:
                 project_back(q)
 
+    if last:
+
+        @pl.when(pl.program_id(0) == pl.num_programs(0) - 1)
+        def _():
+            for row in range(rows):
+                copy_out(row).wait()
+
 
 def update_part(side, seqs, order, part, left, right, wt, before, bias, pair):
     rows, lanes, depth = left.shape
@@ -217,16 +232,25 @@
     pack = tile // rows
     width = lanes // pack
     halves = pack // 2
-    group = 16
+    group = 16 if part < PARTS - 1 else rows
     first, last = part == 0, part == PARTS - 1
     in_vmem = pl.BlockSpec(memory_space=pltpu.VMEM)
+    scratch = [
+        pltpu.VMEM((depth * some, tile), jnp.float32),
+        pltpu.VMEM((depth, some * tile), jnp.bfloat16),
+        pltpu.VMEM((group * halves, some * width, 2 * tile), jnp.bfloat16),
+    ]
     operands = [left] + list(right) + [wt[:, part * some * width : (part + 1) * some * width]]
     if not first:
         operands.append(before)
     if last:
         operands += [bias[None], pair.reshape(pack, rows, tile, chans)]
         out_shape = jax.ShapeDtypeStruct((pack, rows, tile, chans), jnp.bfloat16)
-        out_spec = pl.BlockSpec((pack, group, tile, chans), lambda g: (0, g, 0, 0))
+        out_spec = pl.BlockSpec(memory_space=pltpu.HBM)
+        scratch += [
+            pltpu.VMEM((pack, rows, tile, chans), jnp.bfloat16),
+            pltpu.SemaphoreType.DMA((rows,)),
+        ]
     else:
         out_shape, out_spec = pltpu.VMEM((rows, halves, chans, 2 * tile), jnp.float32), in_vmem
     return pl.pallas_call(
@@ -235,12 +259,8 @@
         in_specs=[in_vmem] * len(operands),
         out_specs=out_spec,
         out_shape=out_shape,
-        scratch_shapes=[
-            pltpu.VMEM((depth * some, tile), jnp.float32),
-            pltpu.VMEM((depth, some * tile), jnp.bfloat16),
-            pltpu.VMEM((group * halves, some * width, 2 * tile), jnp.bfloat16),
-        ],
-        compiler_params=pltpu.CompilerParams(vmem_limit_bytes=24 * MIB),
+        scratch_shapes=scratch,
+        compiler_params=pltpu.CompilerParams(vmem_limit_bytes=32 * MIB),
         cost_estimate=pl.CostEstimate(
             flops=2 * tile * tile * some * width * (side * side * seqs + chans),
             bytes_accessed=16 * MIB,

time: 47.3 us -> 46.9 us (level)
  Pallas kernels: 22 us -> 21.4 us
    pallas_call x2, Pallas kernels: 16.6 us -> 16 us  [update_part(): pl.pallas_call(functools.partial(update_kernel, side, seqs, order, len(ri...]
where the time goes in v24:
time: 46.9 us; the launch traced here: 46.7 us
  Pallas kernels  21.4 us (46%)
  starting transfers between devices  12.3 us (26%)
  waiting for transfers between devices  11.2 us (24%)
  local copies, waits for them, and re-layouts  1.45 us (3%)
    pallas_call x2, Pallas kernels, update_part(): pl.pallas_call(functools.partial(update_kernel, side, seqs, order, len(ri...  16 us
    ppermute x12, starting transfers between devices, swap(): lax.ppermute(x, 'row', [(i, i ^ da * side + db) for i in range(devices)])  12.3 us
    ppermute x12, waiting for transfers between devices, swap(): lax.ppermute(x, 'row', [(i, i ^ da * side + db) for i in range(devices)])  11.2 us
    pallas_call x1, Pallas kernels, project(): pl.pallas_call(functools.partial(project_kernel, side), in_specs=[pl.Bloc...  4.09 us
    pallas_call x1, Pallas kernels, arrange_left(): pl.pallas_call(functools.partial(arrange_kernel, seq_total), in_specs=[pl...  1.33 us
    transpose x1, local copies, waits for them, and re-layouts, local(): final_matrix.reshape(width, width, -1).transpose(2, 1, 0)  1.06 us
  transfers between devices with their start and end apart: 12, of which 6 were waited for; matrix products, arithmetic and copies ran while one was open for 3% of the time, Pallas kernels for 18%

profile of v24, /device:TPU:0, one launch (start us, length us, event | category | flops | bytes accessed | tf_op | source)
XLA Modules:
  0.0 46.7 jit_solution(15331442363541680902)
XLA Ops:
  0.0 4.1 %project.1 = (bf16[6,32,128]{2,1,0:T(8,128)(2,1)S(1)}, bf16[6,32,128]{2,1,0:T(8,128)(2,1)S(1)}, bf16[6,32,128]{2,1,0:T(8,128)(2,1)S(1)}, bf16[6,32,128]{2,1,0:T(...) custom-call(bf16[6,512,256]{2,1,0:T(8,128)(2,1)} %refs_0_.1, ...), custom_call_target="tpu_custom_call" | custom-call | tf_op jit(solution)/shard_map/project/pallas_call | solution.py:86
  4.1 0.5 %collective-permute-start = (bf16[2,6,16,128]{3,2,1,0:T(8,128)(2,1)S(1)}, bf16[2,6,16,128]{3,2,1,0:T(8,128)(2,1)S(1)}, u32[]{:S(2)}, u32[]{:S(2)}) collective-permute-start(bf16[2,6,16,128]{3,2,1,0:T(8,128)(2,1)S(1)} %get-tuple-element.29), channel_id=1, source_target_pairs={{0,1},{1,0},{2,3},{3,2},{4,5},{5,4},{6,7},{7,6},{8,9},{9,8},{10,11... | collective-permute-start | bytes 147464 | tf_op jit(solution)/shard_map/ppermute | solution.py:302
  4.6 2.6 %collective-permute-start.6 = (bf16[2,6,16,128]{3,2,1,0:T(8,128)(2,1)S(1)}, bf16[2,6,16,128]{3,2,1,0:T(8,128)(2,1)S(1)}, u32[]{:S(2)}, u32[]{:S(2)}) collective-permute-start(bf16[2,6,16,128]{3,2,1,0:T(8,128)(2,1)S(1)} %get-tuple-element.36), channel_id=1, source_target_pairs={{0,2},{1,3},{2,0},{3,1},{4,6},{5,7},{6,4},{7,5},{8,10},{9,11},{10,... | collective-permute-start | bytes 147464 | tf_op jit(solution)/shard_map/ppermute | solution.py:302
  7.2 0.1 collective-permute-start.7
  7.3 0.0 collective-permute-done
  7.3 1.8 %collective-permute-start.1 = (bf16[6,32,128]{2,1,0:T(8,128)(2,1)S(1)}, bf16[6,32,128]{2,1,0:T(8,128)(2,1)S(1)}, u32[]{:S(2)}, u32[]{:S(2)}) collective-permute-start(bf16[6,32,128]{2,1,0:T(8,128)(2,1)S(1)} %get-tuple-element.31), channel_id=1, source_target_pairs={{0,4},{1,5},{2,6},{3,7},{4,0},{5,1},{6,2},{7,3},{8,12},{9,13},{10,... | collective-permute-start | bytes 147464 | tf_op jit(solution)/shard_map/ppermute | solution.py:302
  9.1 2.6 %collective-permute-start.2 = (bf16[6,32,128]{2,1,0:T(8,128)(2,1)S(1)}, bf16[6,32,128]{2,1,0:T(8,128)(2,1)S(1)}, u32[]{:S(2)}, u32[]{:S(2)}) collective-permute-start(bf16[6,32,128]{2,1,0:T(8,128)(2,1)S(1)} %get-tuple-element.32), channel_id=1, source_target_pairs={{0,8},{1,9},{2,10},{3,11},{4,12},{5,13},{6,14},{7,15},{8,0},{9,1},... | collective-permute-start | bytes 147464 | tf_op jit(solution)/shard_map/ppermute | solution.py:302
  11.7 0.0 collective-permute-start.3
  11.8 0.0 collective-permute-done.6
  11.8 0.0 collective-permute-done.7
  11.9 0.9 %collective-permute-start.8 = (bf16[2,24,16,128]{3,2,1,0:T(8,128)(2,1)S(1)}, bf16[2,24,16,128]{3,2,1,0:T(8,128)(2,1)S(1)}, u32[]{:S(2)}, u32[]{:S(2)}) collective-permute-start(bf16[2,24,16,128]{3,2,1,0:T(8,128)(2,1)S(1)} %pad_maximum_fusion), channel_id=1, source_target_pairs={{0,4},{1,5},{2,6},{3,7},{4,0},{5,1},{6,2},{7,3},{8,12},{9,13},{10,... | collective-permute-start | bytes 589832 | tf_op jit(solution)/shard_map/ppermute | solution.py:302
  12.8 0.0 collective-permute-done.1
  12.9 2.4 %collective-permute-done.2 = bf16[6,32,128]{2,1,0:T(8,128)(2,1)S(1)} collective-permute-done((bf16[6,32,128]{2,1,0:T(8,128)(2,1)S(1)}, bf16[6,32,128]{2,1,0:T(8,128)(2,1)S(1)}, u32[]{:S(2)}, u32[]{:S(2)}) %collective-permute-start.2) | collective-permute-done | bytes 49184 | tf_op jit(solution)/shard_map/ppermute | solution.py:302
  15.3 2.9 %collective-permute-done.3 = bf16[6,32,128]{2,1,0:T(8,128)(2,1)S(1)} collective-permute-done((bf16[6,32,128]{2,1,0:T(8,128)(2,1)S(1)}, bf16[6,32,128]{2,1,0:T(8,128)(2,1)S(1)}, u32[]{:S(2)}, u32[]{:S(2)}) %collective-permute-start.3) | collective-permute-done | bytes 49184 | tf_op jit(solution)/shard_map/ppermute | solution.py:302
  18.2 1.6 %collective-permute-start.4 = (bf16[24,32,128]{2,1,0:T(8,128)(2,1)S(1)}, bf16[24,32,128]{2,1,0:T(8,128)(2,1)S(1)}, u32[]{:S(2)}, u32[]{:S(2)}) collective-permute-start(bf16[24,32,128]{2,1,0:T(8,128)(2,1)S(1)} %get-tuple-element.62.refs_0_), channel_id=1, source_target_pairs={{0,2},{1,3},{2,0},{3,1},{4,6},{5,7},{6,4},{7,5},{8,10},{9,11},{10,... | collective-permute-start | bytes 589832 | tf_op jit(solution)/shard_map/ppermute | solution.py:302
  19.8 1.1 %collective-permute-start.10 = (bf16[24,16,128]{2,1,0:T(8,128)(2,1)S(1)}, bf16[24,16,128]{2,1,0:T(8,128)(2,1)S(1)}, u32[]{:S(2)}, u32[]{:S(2)}) collective-permute-start(bf16[24,16,128]{2,1,0:T(8,128)(2,1)S(1)} %get-tuple-element.50.refs_0_), channel_id=1, source_target_pairs={{0,12},{1,13},{2,14},{3,15},{4,8},{5,9},{6,10},{7,11},{8,4},{9,5},... | collective-permute-start | bytes 294920 | tf_op jit(solution)/shard_map/ppermute | solution.py:302
  20.8 0.0 collective-permute-start.9
  20.9 0.0 collective-permute-done.8
  20.9 1.1 %copy.14 = bf16[128,32,32]{0,2,1:T(8,128)(2,1)S(1)} copy(bf16[128,32,32]{0,1,2:T(8,128)(2,1)} %bitcast.40) | data formatting | bytes 524288 | tf_op jit(solution)/shard_map/transpose | solution.py:328
  21.9 2.0 %collective-permute-done.4.refs_1_ = bf16[24,32,128]{2,1,0:T(8,128)(2,1)S(1)} collective-permute-done((bf16[24,32,128]{2,1,0:T(8,128)(2,1)S(1)}, bf16[24,32,128]{2,1,0:T(8,128)(2,1)S(1)}, u32[]{:S(2)}, u32[]{:S(2)}) %collective-permute-start.4) | collective-permute-done | bytes 196640 | tf_op jit(solution)/shard_map/ppermute | solution.py:302
  24.0 0.1 collective-permute-start.5
  24.1 0.1 copy.18.refs_3_
  24.2 0.1 copy.17.refs_4_
  24.3 1.4 %collective-permute-done.5.refs_2_ = bf16[48,32,128]{2,1,0:T(8,128)(2,1)S(1)} collective-permute-done((bf16[48,32,128]{2,1,0:T(8,128)(2,1)S(1)}, bf16[48,32,128]{2,1,0:T(8,128)(2,1)S(1)}, u32[]{:S(2)}, u32[]{:S(2)}) %collective-permute-start.5) | collective-permute-done | bytes 393248 | tf_op jit(solution)/shard_map/ppermute | solution.py:302
  25.8 1.0 %collective-permute-start.11 = (bf16[48,16,128]{2,1,0:T(8,128)(2,1)S(1)}, bf16[48,16,128]{2,1,0:T(8,128)(2,1)S(1)}, u32[]{:S(2)}, u32[]{:S(2)}) collective-permute-start(bf16[48,16,128]{2,1,0:T(8,128)(2,1)S(1)} %pad_maximum_fusion.1), channel_id=1, source_target_pairs={{0,8},{1,9},{2,10},{3,11},{4,12},{5,13},{6,14},{7,15},{8,0},{9,1},... | collective-permute-start | bytes 589832 | tf_op jit(solution)/shard_map/ppermute | solution.py:302
  26.8 1.3 %arrange_left.1.left_ref = bf16[32,128,128]{2,1,0:T(8,128)(2,1)S(1)} custom-call(bf16[24,32,128]{2,1,0:T(8,128)(2,1)S(1)} %get-tuple-element.62.refs_0_, bf16[24,32,128]{2,1,0:T(8,128)(2,1)S(1)} %collective-permute-done.4.refs_1_, bf16[48,32,128]{2,1,0:T(8,128)(2,1)S(1)} %collective-permute-done.5.refs_2_), custom_call_target="tpu_custom_call" | custom-call | flops 1048576 | bytes 8388608 | tf_op jit(solution)/shard_map/arrange_left/pallas_call | solution.py:124
  28.1 0.0 collective-permute-done.10.refs_3_
  28.1 0.9 %collective-permute-done.9.refs_2_ = bf16[24,16,128]{2,1,0:T(8,128)(2,1)S(1)} collective-permute-done((bf16[24,16,128]{2,1,0:T(8,128)(2,1)S(1)}, bf16[24,16,128]{2,1,0:T(8,128)(2,1)S(1)}, u32[]{:S(2)}, u32[]{:S(2)}) %collective-permute-start.9) | collective-permute-done | bytes 98336 | tf_op jit(solution)/shard_map/ppermute | solution.py:302
  29.0 0.0 copy-start
  29.0 0.0 copy-start.1
  29.0 7.3 %update_0.1.refs_4_ = f32[32,2,128,256]{3,2,1,0:T(8,128)S(1)} custom-call(bf16[32,128,128]{2,1,0:T(8,128)(2,1)S(1)} %arrange_left.1.left_ref, bf16[24,16,128]{2,1,0:T(8,128)(2,1)S(1)} %get-tuple-element.50.refs_0_, bf16[24,16,128]{2,1,0:T(8,128)(2,1)S(1)} %get-tuple-element.48.refs_1_, bf16[24,16,128]{2,1,0:T(8,128)(2,1)S(1)} %collective-permute-done.9.refs_2_, ...), custom_call_target="tpu_custom_call" | custom-call | flops 3758096384 | bytes 16777216 | tf_op jit(solution)/shard_map/update_0/pallas_call | solution.py:256
  36.3 1.6 %collective-permute-done.11.refs_2_ = bf16[48,16,128]{2,1,0:T(8,128)(2,1)S(1)} collective-permute-done((bf16[48,16,128]{2,1,0:T(8,128)(2,1)S(1)}, bf16[48,16,128]{2,1,0:T(8,128)(2,1)S(1)}, u32[]{:S(2)}, u32[]{:S(2)}) %collective-permute-start.11) | collective-permute-done | bytes 196640 | tf_op jit(solution)/shard_map/ppermute | solution.py:302
  37.9 0.0 copy-done
  37.9 0.0 copy-done.1
  37.9 8.7 %update_1.1 = bf16[4,32,128,128]{3,2,1,0:T(8,128)(2,1)} custom-call(bf16[32,128,128]{2,1,0:T(8,128)(2,1)S(1)} %arrange_left.1.left_ref, bf16[24,16,128]{2,1,0:T(8,128)(2,1)S(1)} %get-tuple-element.41.refs_0_, bf16[24,16,128]{2,1,0:T(8,128)(2,1)S(1)} %get-tuple-element.42.refs_1_, bf16[48,16,128]{2,1,0:T(8,128)(2,1)S(1)} %collective-permute-done.11.refs_2_, ...), custom_call_target="tpu_custom_call" | custom-call | flops 3758096384 | bytes 16777216 | tf_op jit(solution)/shard_map/update_1/pallas_call | solution.py:256
  (15 shorter events, 0.2 us)
Async XLA Ops:
  4.1 3.2 %collective-permute-start = (bf16[2,6,16,128]{3,2,1,0:T(8,128)(2,1)S(1)}, bf16[2,6,16,128]{3,2,1,0:T(8,128)(2,1)S(1)}, u32[]{:S(2)}, u32[]{:S(2)}) collective-permute-start(bf16[2,6,16,128]{3,2,1,0:T(8,128)(2,1)S(1)} %get-tuple-element.29), channel_id=1, source_target_pairs={{0,1},{1,0},{2,3},{3,2},{4,5},{5,4},{6,7},{7,6},{8,9},{9,8},{10,11... | collective-permute-start | bytes 147464 | tf_op jit(solution)/shard_map/ppermute | solution.py:302
  4.6 7.1 %collective-permute-start.6 = (bf16[2,6,16,128]{3,2,1,0:T(8,128)(2,1)S(1)}, bf16[2,6,16,128]{3,2,1,0:T(8,128)(2,1)S(1)}, u32[]{:S(2)}, u32[]{:S(2)}) collective-permute-start(bf16[2,6,16,128]{3,2,1,0:T(8,128)(2,1)S(1)} %get-tuple-element.36), channel_id=1, source_target_pairs={{0,2},{1,3},{2,0},{3,1},{4,6},{5,7},{6,4},{7,5},{8,10},{9,11},{10,... | collective-permute-start | bytes 147464 | tf_op jit(solution)/shard_map/ppermute | solution.py:302
  7.2 4.6 %collective-permute-start.7 = (bf16[2,6,16,128]{3,2,1,0:T(8,128)(2,1)S(1)}, bf16[2,6,16,128]{3,2,1,0:T(8,128)(2,1)S(1)}, u32[]{:S(2)}, u32[]{:S(2)}) collective-permute-start(bf16[2,6,16,128]{3,2,1,0:T(8,128)(2,1)S(1)} %get-tuple-element.37), channel_id=1, source_target_pairs={{0,3},{1,2},{2,1},{3,0},{4,7},{5,6},{6,5},{7,4},{8,11},{9,10},{10,... | collective-permute-start | bytes 147464 | tf_op jit(solution)/shard_map/ppermute | solution.py:302
  7.3 5.5 %collective-permute-start.1 = (bf16[6,32,128]{2,1,0:T(8,128)(2,1)S(1)}, bf16[6,32,128]{2,1,0:T(8,128)(2,1)S(1)}, u32[]{:S(2)}, u32[]{:S(2)}) collective-permute-start(bf16[6,32,128]{2,1,0:T(8,128)(2,1)S(1)} %get-tuple-element.31), channel_id=1, source_target_pairs={{0,4},{1,5},{2,6},{3,7},{4,0},{5,1},{6,2},{7,3},{8,12},{9,13},{10,... | collective-permute-start | bytes 147464 | tf_op jit(solution)/shard_map/ppermute | solution.py:302
  9.1 6.1 %collective-permute-start.2 = (bf16[6,32,128]{2,1,0:T(8,128)(2,1)S(1)}, bf16[6,32,128]{2,1,0:T(8,128)(2,1)S(1)}, u32[]{:S(2)}, u32[]{:S(2)}) collective-permute-start(bf16[6,32,128]{2,1,0:T(8,128)(2,1)S(1)} %get-tuple-element.32), channel_id=1, source_target_pairs={{0,8},{1,9},{2,10},{3,11},{4,12},{5,13},{6,14},{7,15},{8,0},{9,1},... | collective-permute-start | bytes 147464 | tf_op jit(solution)/shard_map/ppermute | solution.py:302
  11.7 6.4 %collective-permute-start.3 = (bf16[6,32,128]{2,1,0:T(8,128)(2,1)S(1)}, bf16[6,32,128]{2,1,0:T(8,128)(2,1)S(1)}, u32[]{:S(2)}, u32[]{:S(2)}) collective-permute-start(bf16[6,32,128]{2,1,0:T(8,128)(2,1)S(1)} %get-tuple-element.33), channel_id=1, source_target_pairs={{0,12},{1,13},{2,14},{3,15},{4,8},{5,9},{6,10},{7,11},{8,4},{9,5},... | collective-permute-start | bytes 147464 | tf_op jit(solution)/shard_map/ppermute | solution.py:302
  11.9 9.0 %collective-permute-start.8 = (bf16[2,24,16,128]{3,2,1,0:T(8,128)(2,1)S(1)}, bf16[2,24,16,128]{3,2,1,0:T(8,128)(2,1)S(1)}, u32[]{:S(2)}, u32[]{:S(2)}) collective-permute-start(bf16[2,24,16,128]{3,2,1,0:T(8,128)(2,1)S(1)} %pad_maximum_fusion), channel_id=1, source_target_pairs={{0,4},{1,5},{2,6},{3,7},{4,0},{5,1},{6,2},{7,3},{8,12},{9,13},{10,... | collective-permute-start | bytes 589832 | tf_op jit(solution)/shard_map/ppermute | solution.py:302
  18.2 5.7 %collective-permute-start.4 = (bf16[24,32,128]{2,1,0:T(8,128)(2,1)S(1)}, bf16[24,32,128]{2,1,0:T(8,128)(2,1)S(1)}, u32[]{:S(2)}, u32[]{:S(2)}) collective-permute-start(bf16[24,32,128]{2,1,0:T(8,128)(2,1)S(1)} %get-tuple-element.62.refs_0_), channel_id=1, source_target_pairs={{0,2},{1,3},{2,0},{3,1},{4,6},{5,7},{6,4},{7,5},{8,10},{9,11},{10,... | collective-permute-start | bytes 589832 | tf_op jit(solution)/shard_map/ppermute | solution.py:302
  19.8 8.3 %collective-permute-start.10 = (bf16[24,16,128]{2,1,0:T(8,128)(2,1)S(1)}, bf16[24,16,128]{2,1,0:T(8,128)(2,1)S(1)}, u32[]{:S(2)}, u32[]{:S(2)}) collective-permute-start(bf16[24,16,128]{2,1,0:T(8,128)(2,1)S(1)} %get-tuple-element.50.refs_0_), channel_id=1, source_target_pairs={{0,12},{1,13},{2,14},{3,15},{4,8},{5,9},{6,10},{7,11},{8,4},{9,5},... | collective-permute-start | bytes 294920 | tf_op jit(solution)/shard_map/ppermute | solution.py:302
  20.8 8.2 %collective-permute-start.9 = (bf16[24,16,128]{2,1,0:T(8,128)(2,1)S(1)}, bf16[24,16,128]{2,1,0:T(8,128)(2,1)S(1)}, u32[]{:S(2)}, u32[]{:S(2)}) collective-permute-start(bf16[24,16,128]{2,1,0:T(8,128)(2,1)S(1)} %get-tuple-element.50.refs_0_), channel_id=1, source_target_pairs={{0,8},{1,9},{2,10},{3,11},{4,12},{5,13},{6,14},{7,15},{8,0},{9,1},... | collective-permute-start | bytes 294920 | tf_op jit(solution)/shard_map/ppermute | solution.py:302
  24.0 1.8 %collective-permute-start.5 = (bf16[48,32,128]{2,1,0:T(8,128)(2,1)S(1)}, bf16[48,32,128]{2,1,0:T(8,128)(2,1)S(1)}, u32[]{:S(2)}, u32[]{:S(2)}) collective-permute-start(bf16[48,32,128]{2,1,0:T(8,128)(2,1)S(1)} %constant_dynamic-update-slice_fusion.4), channel_id=1, source_target_pairs={{0,1},{1,0},{2,3},{3,2},{4,5},{5,4},{6,7},{7,6},{8,9},{9,8},{10,11... | collective-permute-start | bytes 1179656 | tf_op jit(solution)/shard_map/ppermute | solution.py:302
  25.8 12.1 %collective-permute-start.11 = (bf16[48,16,128]{2,1,0:T(8,128)(2,1)S(1)}, bf16[48,16,128]{2,1,0:T(8,128)(2,1)S(1)}, u32[]{:S(2)}, u32[]{:S(2)}) collective-permute-start(bf16[48,16,128]{2,1,0:T(8,128)(2,1)S(1)} %pad_maximum_fusion.1), channel_id=1, source_target_pairs={{0,8},{1,9},{2,10},{3,11},{4,12},{5,13},{6,14},{7,15},{8,0},{9,1},... | collective-permute-start | bytes 589832 | tf_op jit(solution)/shard_map/ppermute | solution.py:302
  29.0 8.9 %copy-start = (bf16[1,128,128,128]{3,2,1,0:T(8,128)(2,1)S(1)}, bf16[1,128,128,128]{3,2,1,0:T(8,128)(2,1)}, u32[]{:S(2)}) copy-start(bf16[1,128,128,128]{3,2,1,0:T(8,128)(2,1)} %param.11) | copy-start | bytes 12582916
  29.0 8.9 %copy-start.1 = (f32[128]{0:T(128)S(1)}, f32[128]{0:T(128)}, u32[]{:S(2)}) copy-start(f32[128]{0:T(128)} %param.19) | copy-start | bytes 1540

commit v25 on v24

--- a/solution.py
+++ b/solution.py
@@ -11,7 +11,7 @@
 LANES = 128
 PARTS = 2
 MIB = 1024 * 1024
-RUN = 4
+RUN = 8
 
 
 def in_hbm(x):

time: 46.9 us -> 46.9 us (level)
  no operation moved by 1% of the time
where the time goes in v25:
time: 46.9 us; the launch traced here: 46.7 us
  Pallas kernels  21.4 us (46%)
  starting transfers between devices  12.3 us (26%)
  waiting for transfers between devices  11.2 us (24%)
  local copies, waits for them, and re-layouts  1.45 us (3%)
    pallas_call x2, Pallas kernels, update_part(): pl.pallas_call(functools.partial(update_kernel, side, seqs, order, len(ri...  15.9 us
    ppermute x12, starting transfers between devices, swap(): lax.ppermute(x, 'row', [(i, i ^ da * side + db) for i in range(devices)])  12.3 us
    ppermute x12, waiting for transfers between devices, swap(): lax.ppermute(x, 'row', [(i, i ^ da * side + db) for i in range(devices)])  11.2 us
    pallas_call x1, Pallas kernels, project(): pl.pallas_call(functools.partial(project_kernel, side), in_specs=[pl.Bloc...  4.09 us
    pallas_call x1, Pallas kernels, arrange_left(): pl.pallas_call(functools.partial(arrange_kernel, seq_total), in_specs=[pl...  1.33 us
    transpose x1, local copies, waits for them, and re-layouts, local(): final_matrix.reshape(width, width, -1).transpose(2, 1, 0)  1.06 us
  transfers between devices with their start and end apart: 12, of which 6 were waited for; matrix products, arithmetic and copies ran while one was open for 3% of the time, Pallas kernels for 18%

profile of v25, /device:TPU:0, one launch (start us, length us, event | category | flops | bytes accessed | tf_op | source)
XLA Modules:
  0.0 46.7 jit_solution(15418812336531511336)
XLA Ops:
  0.0 4.1 %project.1 = (bf16[6,32,128]{2,1,0:T(8,128)(2,1)S(1)}, bf16[6,32,128]{2,1,0:T(8,128)(2,1)S(1)}, bf16[6,32,128]{2,1,0:T(8,128)(2,1)S(1)}, bf16[6,32,128]{2,1,0:T(...) custom-call(bf16[6,512,256]{2,1,0:T(8,128)(2,1)} %refs_0_.1, ...), custom_call_target="tpu_custom_call" | custom-call | tf_op jit(solution)/shard_map/project/pallas_call | solution.py:86
  4.1 0.5 %collective-permute-start = (bf16[2,6,16,128]{3,2,1,0:T(8,128)(2,1)S(1)}, bf16[2,6,16,128]{3,2,1,0:T(8,128)(2,1)S(1)}, u32[]{:S(2)}, u32[]{:S(2)}) collective-permute-start(bf16[2,6,16,128]{3,2,1,0:T(8,128)(2,1)S(1)} %get-tuple-element.29), channel_id=1, source_target_pairs={{0,1},{1,0},{2,3},{3,2},{4,5},{5,4},{6,7},{7,6},{8,9},{9,8},{10,11... | collective-permute-start | bytes 147464 | tf_op jit(solution)/shard_map/ppermute | solution.py:302
  4.6 2.6 %collective-permute-start.6 = (bf16[2,6,16,128]{3,2,1,0:T(8,128)(2,1)S(1)}, bf16[2,6,16,128]{3,2,1,0:T(8,128)(2,1)S(1)}, u32[]{:S(2)}, u32[]{:S(2)}) collective-permute-start(bf16[2,6,16,128]{3,2,1,0:T(8,128)(2,1)S(1)} %get-tuple-element.36), channel_id=1, source_target_pairs={{0,2},{1,3},{2,0},{3,1},{4,6},{5,7},{6,4},{7,5},{8,10},{9,11},{10,... | collective-permute-start | bytes 147464 | tf_op jit(solution)/shard_map/ppermute | solution.py:302
  7.2 0.1 collective-permute-start.7
  7.3 0.0 collective-permute-done
  7.3 1.8 %collective-permute-start.1 = (bf16[6,32,128]{2,1,0:T(8,128)(2,1)S(1)}, bf16[6,32,128]{2,1,0:T(8,128)(2,1)S(1)}, u32[]{:S(2)}, u32[]{:S(2)}) collective-permute-start(bf16[6,32,128]{2,1,0:T(8,128)(2,1)S(1)} %get-tuple-element.31), channel_id=1, source_target_pairs={{0,4},{1,5},{2,6},{3,7},{4,0},{5,1},{6,2},{7,3},{8,12},{9,13},{10,... | collective-permute-start | bytes 147464 | tf_op jit(solution)/shard_map/ppermute | solution.py:302
  9.1 2.6 %collective-permute-start.2 = (bf16[6,32,128]{2,1,0:T(8,128)(2,1)S(1)}, bf16[6,32,128]{2,1,0:T(8,128)(2,1)S(1)}, u32[]{:S(2)}, u32[]{:S(2)}) collective-permute-start(bf16[6,32,128]{2,1,0:T(8,128)(2,1)S(1)} %get-tuple-element.32), channel_id=1, source_target_pairs={{0,8},{1,9},{2,10},{3,11},{4,12},{5,13},{6,14},{7,15},{8,0},{9,1},... | collective-permute-start | bytes 147464 | tf_op jit(solution)/shard_map/ppermute | solution.py:302
  11.7 0.0 collective-permute-start.3
  11.8 0.0 collective-permute-done.6
  11.8 0.0 collective-permute-done.7
  11.9 0.9 %collective-permute-start.8 = (bf16[2,24,16,128]{3,2,1,0:T(8,128)(2,1)S(1)}, bf16[2,24,16,128]{3,2,1,0:T(8,128)(2,1)S(1)}, u32[]{:S(2)}, u32[]{:S(2)}) collective-permute-start(bf16[2,24,16,128]{3,2,1,0:T(8,128)(2,1)S(1)} %pad_maximum_fusion), channel_id=1, source_target_pairs={{0,4},{1,5},{2,6},{3,7},{4,0},{5,1},{6,2},{7,3},{8,12},{9,13},{10,... | collective-permute-start | bytes 589832 | tf_op jit(solution)/shard_map/ppermute | solution.py:302
  12.8 0.0 collective-permute-done.1
  12.9 2.4 %collective-permute-done.2 = bf16[6,32,128]{2,1,0:T(8,128)(2,1)S(1)} collective-permute-done((bf16[6,32,128]{2,1,0:T(8,128)(2,1)S(1)}, bf16[6,32,128]{2,1,0:T(8,128)(2,1)S(1)}, u32[]{:S(2)}, u32[]{:S(2)}) %collective-permute-start.2) | collective-permute-done | bytes 49184 | tf_op jit(solution)/shard_map/ppermute | solution.py:302
  15.3 2.9 %collective-permute-done.3 = bf16[6,32,128]{2,1,0:T(8,128)(2,1)S(1)} collective-permute-done((bf16[6,32,128]{2,1,0:T(8,128)(2,1)S(1)}, bf16[6,32,128]{2,1,0:T(8,128)(2,1)S(1)}, u32[]{:S(2)}, u32[]{:S(2)}) %collective-permute-start.3) | collective-permute-done | bytes 49184 | tf_op jit(solution)/shard_map/ppermute | solution.py:302
  18.2 1.6 %collective-permute-start.4 = (bf16[24,32,128]{2,1,0:T(8,128)(2,1)S(1)}, bf16[24,32,128]{2,1,0:T(8,128)(2,1)S(1)}, u32[]{:S(2)}, u32[]{:S(2)}) collective-permute-start(bf16[24,32,128]{2,1,0:T(8,128)(2,1)S(1)} %get-tuple-element.62.refs_0_), channel_id=1, source_target_pairs={{0,2},{1,3},{2,0},{3,1},{4,6},{5,7},{6,4},{7,5},{8,10},{9,11},{10,... | collective-permute-start | bytes 589832 | tf_op jit(solution)/shard_map/ppermute | solution.py:302
  19.8 1.1 %collective-permute-start.10 = (bf16[24,16,128]{2,1,0:T(8,128)(2,1)S(1)}, bf16[24,16,128]{2,1,0:T(8,128)(2,1)S(1)}, u32[]{:S(2)}, u32[]{:S(2)}) collective-permute-start(bf16[24,16,128]{2,1,0:T(8,128)(2,1)S(1)} %get-tuple-element.50.refs_0_), channel_id=1, source_target_pairs={{0,12},{1,13},{2,14},{3,15},{4,8},{5,9},{6,10},{7,11},{8,4},{9,5},... | collective-permute-start | bytes 294920 | tf_op jit(solution)/shard_map/ppermute | solution.py:302
  20.8 0.0 collective-permute-start.9
  20.9 0.0 collective-permute-done.8
  20.9 1.1 %copy.14 = bf16[128,32,32]{0,2,1:T(8,128)(2,1)S(1)} copy(bf16[128,32,32]{0,1,2:T(8,128)(2,1)} %bitcast.40) | data formatting | bytes 524288 | tf_op jit(solution)/shard_map/transpose | solution.py:328
  21.9 2.0 %collective-permute-done.4.refs_1_ = bf16[24,32,128]{2,1,0:T(8,128)(2,1)S(1)} collective-permute-done((bf16[24,32,128]{2,1,0:T(8,128)(2,1)S(1)}, bf16[24,32,128]{2,1,0:T(8,128)(2,1)S(1)}, u32[]{:S(2)}, u32[]{:S(2)}) %collective-permute-start.4) | collective-permute-done | bytes 196640 | tf_op jit(solution)/shard_map/ppermute | solution.py:302
  24.0 0.1 collective-permute-start.5
  24.1 0.1 copy.18.refs_3_
  24.2 0.1 copy.17.refs_4_
  24.3 1.4 %collective-permute-done.5.refs_2_ = bf16[48,32,128]{2,1,0:T(8,128)(2,1)S(1)} collective-permute-done((bf16[48,32,128]{2,1,0:T(8,128)(2,1)S(1)}, bf16[48,32,128]{2,1,0:T(8,128)(2,1)S(1)}, u32[]{:S(2)}, u32[]{:S(2)}) %collective-permute-start.5) | collective-permute-done | bytes 393248 | tf_op jit(solution)/shard_map/ppermute | solution.py:302
  25.8 1.0 %collective-permute-start.11 = (bf16[48,16,128]{2,1,0:T(8,128)(2,1)S(1)}, bf16[48,16,128]{2,1,0:T(8,128)(2,1)S(1)}, u32[]{:S(2)}, u32[]{:S(2)}) collective-permute-start(bf16[48,16,128]{2,1,0:T(8,128)(2,1)S(1)} %pad_maximum_fusion.1), channel_id=1, source_target_pairs={{0,8},{1,9},{2,10},{3,11},{4,12},{5,13},{6,14},{7,15},{8,0},{9,1},... | collective-permute-start | bytes 589832 | tf_op jit(solution)/shard_map/ppermute | solution.py:302
  26.8 1.3 %arrange_left.1.left_ref = bf16[32,128,128]{2,1,0:T(8,128)(2,1)S(1)} custom-call(bf16[24,32,128]{2,1,0:T(8,128)(2,1)S(1)} %get-tuple-element.62.refs_0_, bf16[24,32,128]{2,1,0:T(8,128)(2,1)S(1)} %collective-permute-done.4.refs_1_, bf16[48,32,128]{2,1,0:T(8,128)(2,1)S(1)} %collective-permute-done.5.refs_2_), custom_call_target="tpu_custom_call" | custom-call | flops 1048576 | bytes 8388608 | tf_op jit(solution)/shard_map/arrange_left/pallas_call | solution.py:124
  28.1 0.0 collective-permute-done.10.refs_3_
  28.1 0.9 %collective-permute-done.9.refs_2_ = bf16[24,16,128]{2,1,0:T(8,128)(2,1)S(1)} collective-permute-done((bf16[24,16,128]{2,1,0:T(8,128)(2,1)S(1)}, bf16[24,16,128]{2,1,0:T(8,128)(2,1)S(1)}, u32[]{:S(2)}, u32[]{:S(2)}) %collective-permute-start.9) | collective-permute-done | bytes 98336 | tf_op jit(solution)/shard_map/ppermute | solution.py:302
  29.0 0.0 copy-start
  29.0 0.0 copy-start.1
  29.0 7.3 %update_0.1.refs_4_ = f32[32,2,128,256]{3,2,1,0:T(8,128)S(1)} custom-call(bf16[32,128,128]{2,1,0:T(8,128)(2,1)S(1)} %arrange_left.1.left_ref, bf16[24,16,128]{2,1,0:T(8,128)(2,1)S(1)} %get-tuple-element.50.refs_0_, bf16[24,16,128]{2,1,0:T(8,128)(2,1)S(1)} %get-tuple-element.48.refs_1_, bf16[24,16,128]{2,1,0:T(8,128)(2,1)S(1)} %collective-permute-done.9.refs_2_, ...), custom_call_target="tpu_custom_call" | custom-call | flops 3758096384 | bytes 16777216 | tf_op jit(solution)/shard_map/update_0/pallas_call | solution.py:256
  36.3 1.6 %collective-permute-done.11.refs_2_ = bf16[48,16,128]{2,1,0:T(8,128)(2,1)S(1)} collective-permute-done((bf16[48,16,128]{2,1,0:T(8,128)(2,1)S(1)}, bf16[48,16,128]{2,1,0:T(8,128)(2,1)S(1)}, u32[]{:S(2)}, u32[]{:S(2)}) %collective-permute-start.11) | collective-permute-done | bytes 196640 | tf_op jit(solution)/shard_map/ppermute | solution.py:302
  37.9 0.0 copy-done
  37.9 0.0 copy-done.1
  37.9 8.6 %update_1.1 = bf16[4,32,128,128]{3,2,1,0:T(8,128)(2,1)} custom-call(bf16[32,128,128]{2,1,0:T(8,128)(2,1)S(1)} %arrange_left.1.left_ref, bf16[24,16,128]{2,1,0:T(8,128)(2,1)S(1)} %get-tuple-element.41.refs_0_, bf16[24,16,128]{2,1,0:T(8,128)(2,1)S(1)} %get-tuple-element.42.refs_1_, bf16[48,16,128]{2,1,0:T(8,128)(2,1)S(1)} %collective-permute-done.11.refs_2_, ...), custom_call_target="tpu_custom_call" | custom-call | flops 3758096384 | bytes 16777216 | tf_op jit(solution)/shard_map/update_1/pallas_call | solution.py:256
  (15 shorter events, 0.2 us)
Async XLA Ops:
  4.1 3.2 %collective-permute-start = (bf16[2,6,16,128]{3,2,1,0:T(8,128)(2,1)S(1)}, bf16[2,6,16,128]{3,2,1,0:T(8,128)(2,1)S(1)}, u32[]{:S(2)}, u32[]{:S(2)}) collective-permute-start(bf16[2,6,16,128]{3,2,1,0:T(8,128)(2,1)S(1)} %get-tuple-element.29), channel_id=1, source_target_pairs={{0,1},{1,0},{2,3},{3,2},{4,5},{5,4},{6,7},{7,6},{8,9},{9,8},{10,11... | collective-permute-start | bytes 147464 | tf_op jit(solution)/shard_map/ppermute | solution.py:302
  4.6 7.1 %collective-permute-start.6 = (bf16[2,6,16,128]{3,2,1,0:T(8,128)(2,1)S(1)}, bf16[2,6,16,128]{3,2,1,0:T(8,128)(2,1)S(1)}, u32[]{:S(2)}, u32[]{:S(2)}) collective-permute-start(bf16[2,6,16,128]{3,2,1,0:T(8,128)(2,1)S(1)} %get-tuple-element.36), channel_id=1, source_target_pairs={{0,2},{1,3},{2,0},{3,1},{4,6},{5,7},{6,4},{7,5},{8,10},{9,11},{10,... | collective-permute-start | bytes 147464 | tf_op jit(solution)/shard_map/ppermute | solution.py:302
  7.2 4.6 %collective-permute-start.7 = (bf16[2,6,16,128]{3,2,1,0:T(8,128)(2,1)S(1)}, bf16[2,6,16,128]{3,2,1,0:T(8,128)(2,1)S(1)}, u32[]{:S(2)}, u32[]{:S(2)}) collective-permute-start(bf16[2,6,16,128]{3,2,1,0:T(8,128)(2,1)S(1)} %get-tuple-element.37), channel_id=1, source_target_pairs={{0,3},{1,2},{2,1},{3,0},{4,7},{5,6},{6,5},{7,4},{8,11},{9,10},{10,... | collective-permute-start | bytes 147464 | tf_op jit(solution)/shard_map/ppermute | solution.py:302
  7.3 5.5 %collective-permute-start.1 = (bf16[6,32,128]{2,1,0:T(8,128)(2,1)S(1)}, bf16[6,32,128]{2,1,0:T(8,128)(2,1)S(1)}, u32[]{:S(2)}, u32[]{:S(2)}) collective-permute-start(bf16[6,32,128]{2,1,0:T(8,128)(2,1)S(1)} %get-tuple-element.31), channel_id=1, source_target_pairs={{0,4},{1,5},{2,6},{3,7},{4,0},{5,1},{6,2},{7,3},{8,12},{9,13},{10,... | collective-permute-start | bytes 147464 | tf_op jit(solution)/shard_map/ppermute | solution.py:302
  9.1 6.1 %collective-permute-start.2 = (bf16[6,32,128]{2,1,0:T(8,128)(2,1)S(1)}, bf16[6,32,128]{2,1,0:T(8,128)(2,1)S(1)}, u32[]{:S(2)}, u32[]{:S(2)}) collective-permute-start(bf16[6,32,128]{2,1,0:T(8,128)(2,1)S(1)} %get-tuple-element.32), channel_id=1, source_target_pairs={{0,8},{1,9},{2,10},{3,11},{4,12},{5,13},{6,14},{7,15},{8,0},{9,1},... | collective-permute-start | bytes 147464 | tf_op jit(solution)/shard_map/ppermute | solution.py:302
  11.7 6.4 %collective-permute-start.3 = (bf16[6,32,128]{2,1,0:T(8,128)(2,1)S(1)}, bf16[6,32,128]{2,1,0:T(8,128)(2,1)S(1)}, u32[]{:S(2)}, u32[]{:S(2)}) collective-permute-start(bf16[6,32,128]{2,1,0:T(8,128)(2,1)S(1)} %get-tuple-element.33), channel_id=1, source_target_pairs={{0,12},{1,13},{2,14},{3,15},{4,8},{5,9},{6,10},{7,11},{8,4},{9,5},... | collective-permute-start | bytes 147464 | tf_op jit(solution)/shard_map/ppermute | solution.py:302
  11.9 9.0 %collective-permute-start.8 = (bf16[2,24,16,128]{3,2,1,0:T(8,128)(2,1)S(1)}, bf16[2,24,16,128]{3,2,1,0:T(8,128)(2,1)S(1)}, u32[]{:S(2)}, u32[]{:S(2)}) collective-permute-start(bf16[2,24,16,128]{3,2,1,0:T(8,128)(2,1)S(1)} %pad_maximum_fusion), channel_id=1, source_target_pairs={{0,4},{1,5},{2,6},{3,7},{4,0},{5,1},{6,2},{7,3},{8,12},{9,13},{10,... | collective-permute-start | bytes 589832 | tf_op jit(solution)/shard_map/ppermute | solution.py:302
  18.2 5.7 %collective-permute-start.4 = (bf16[24,32,128]{2,1,0:T(8,128)(2,1)S(1)}, bf16[24,32,128]{2,1,0:T(8,128)(2,1)S(1)}, u32[]{:S(2)}, u32[]{:S(2)}) collective-permute-start(bf16[24,32,128]{2,1,0:T(8,128)(2,1)S(1)} %get-tuple-element.62.refs_0_), channel_id=1, source_target_pairs={{0,2},{1,3},{2,0},{3,1},{4,6},{5,7},{6,4},{7,5},{8,10},{9,11},{10,... | collective-permute-start | bytes 589832 | tf_op jit(solution)/shard_map/ppermute | solution.py:302
  19.8 8.3 %collective-permute-start.10 = (bf16[24,16,128]{2,1,0:T(8,128)(2,1)S(1)}, bf16[24,16,128]{2,1,0:T(8,128)(2,1)S(1)}, u32[]{:S(2)}, u32[]{:S(2)}) collective-permute-start(bf16[24,16,128]{2,1,0:T(8,128)(2,1)S(1)} %get-tuple-element.50.refs_0_), channel_id=1, source_target_pairs={{0,12},{1,13},{2,14},{3,15},{4,8},{5,9},{6,10},{7,11},{8,4},{9,5},... | collective-permute-start | bytes 294920 | tf_op jit(solution)/shard_map/ppermute | solution.py:302
  20.8 8.2 %collective-permute-start.9 = (bf16[24,16,128]{2,1,0:T(8,128)(2,1)S(1)}, bf16[24,16,128]{2,1,0:T(8,128)(2,1)S(1)}, u32[]{:S(2)}, u32[]{:S(2)}) collective-permute-start(bf16[24,16,128]{2,1,0:T(8,128)(2,1)S(1)} %get-tuple-element.50.refs_0_), channel_id=1, source_target_pairs={{0,8},{1,9},{2,10},{3,11},{4,12},{5,13},{6,14},{7,15},{8,0},{9,1},... | collective-permute-start | bytes 294920 | tf_op jit(solution)/shard_map/ppermute | solution.py:302
  24.0 1.8 %collective-permute-start.5 = (bf16[48,32,128]{2,1,0:T(8,128)(2,1)S(1)}, bf16[48,32,128]{2,1,0:T(8,128)(2,1)S(1)}, u32[]{:S(2)}, u32[]{:S(2)}) collective-permute-start(bf16[48,32,128]{2,1,0:T(8,128)(2,1)S(1)} %constant_dynamic-update-slice_fusion.4), channel_id=1, source_target_pairs={{0,1},{1,0},{2,3},{3,2},{4,5},{5,4},{6,7},{7,6},{8,9},{9,8},{10,11... | collective-permute-start | bytes 1179656 | tf_op jit(solution)/shard_map/ppermute | solution.py:302
  25.8 12.1 %collective-permute-start.11 = (bf16[48,16,128]{2,1,0:T(8,128)(2,1)S(1)}, bf16[48,16,128]{2,1,0:T(8,128)(2,1)S(1)}, u32[]{:S(2)}, u32[]{:S(2)}) collective-permute-start(bf16[48,16,128]{2,1,0:T(8,128)(2,1)S(1)} %pad_maximum_fusion.1), channel_id=1, source_target_pairs={{0,8},{1,9},{2,10},{3,11},{4,12},{5,13},{6,14},{7,15},{8,0},{9,1},... | collective-permute-start | bytes 589832 | tf_op jit(solution)/shard_map/ppermute | solution.py:302
  29.0 8.9 %copy-start = (bf16[1,128,128,128]{3,2,1,0:T(8,128)(2,1)S(1)}, bf16[1,128,128,128]{3,2,1,0:T(8,128)(2,1)}, u32[]{:S(2)}) copy-start(bf16[1,128,128,128]{3,2,1,0:T(8,128)(2,1)} %param.11) | copy-start | bytes 12582916
  29.0 8.9 %copy-start.1 = (f32[128]{0:T(128)S(1)}, f32[128]{0:T(128)}, u32[]{:S(2)}) copy-start(f32[128]{0:T(128)} %param.19) | copy-start | bytes 1540
